TPU v7x, 32 devices: a whole 2x2x4 slice. The times are simulated.
32 devices in a mesh: parts: 2 (over y), tile: 4 (over z), slab: 2 (over x), rep: 2 (over core).
Axes of the slice: x: 2, y: 2, z: 4, core: 2. Of those that a mesh axis runs over, the one named last changes fastest.
Arguments:
- volume: float32 [16, 16384], P(('parts', 'slab'), 'tile'), parts along dimension 0, may hold values from -6 to 6
- split_var: float32 [3, 16, 16384], P(None, ('parts', 'slab'), 'tile'), parts along dimension 1, may hold values from -6 to 6
- dual_var: float32 [3, 16, 16384], P(None, ('parts', 'slab'), 'tile'), parts along dimension 1, may hold values from -6 to 6
- sinogram: float32 [32, 16, 128], P(('tile', 'rep'), ('parts', 'slab')), parts along dimension 1, may hold values from -6 to 6
- proj_tiles: bfloat16 [2048, 64, 128], P(('tile', 'rep')), may hold values from -0.125 to 0.125
- ray_index: int32 [2048], P(('tile', 'rep')), may hold values from 0 to 31
- voxel_index: int32 [2048], P(('tile', 'rep')), may hold values from 0 to 63
- tile_count: int32 [8], P(('tile', 'rep')), may hold values from 1 to 256, 1024 in all
- rho: float32 [1], replicated, may hold values from 0.5 to 2
Outputs:
- new_volume: float32 [16, 16384], P(('parts', 'slab'), 'tile'), parts along dimension 0
- new_split: float32 [3, 16, 16384], P(None, ('parts', 'slab'), 'tile'), parts along dimension 1
- new_dual: float32 [3, 16, 16384], P(None, ('parts', 'slab'), 'tile'), parts along dimension 1
There are 2 independent parts, one for each index of `parts`. A program takes and returns all parts, laid end to end along the dimension named above; an argument that names none is the same for every part. Nothing has to cross between parts.
Inputs may be any that keep to these rules, and one draw needn't show every extreme that they name: `tile_count`: slots at or beyond a device's count are unused; some device uses all 256 slots.
All inputs are finite; a program needn't handle non-finite values.
Results may differ from a plain program's by a relative error of at most 0.0017.
Values may be sent and summed in bfloat16 or wider, within the bound.
No kernel may reach another device: no remote copies, remote signals or barrier semaphores. Data moves between devices by JAX's collectives and lax.ppermute only.
A program may use at most 64 MiB of HBM per device.

v0:
```python
import jax
import jax.numpy as jnp
from jax import lax
from jax.sharding import PartitionSpec as P

TV = 64


TAU = 0.5


def passed_along(array, axis, by):
    devices = lax.axis_size(axis)
    pairs = [(i, i + by) for i in range(devices) if 0 <= i + by < devices]
    return lax.ppermute(array, axis, pairs)


def plane_grad(field):
    cells = field.reshape(field.shape[:-1] + (-1, 8, 8))
    across = jnp.concatenate(
        [cells[..., 1:, :] - cells[..., :-1, :], jnp.zeros_like(cells[..., :1, :])], axis=-2
    )
    along = jnp.concatenate(
        [cells[..., :, 1:] - cells[..., :, :-1], jnp.zeros_like(cells[..., :, :1])], axis=-1
    )
    return (across.reshape(field.shape), along.reshape(field.shape))


def plane_masks(width):
    place = jnp.arange(width, dtype=jnp.int32) % TV
    return (place // 8 < 7, place % 8 < 7)


def plane_adjoint(across, along):
    shape = across.shape
    cells_a = across.reshape(shape[:-1] + (-1, 8, 8))
    cells_b = along.reshape(shape[:-1] + (-1, 8, 8))
    part_a = (
        jnp.concatenate([jnp.zeros_like(cells_a[..., :1, :]), cells_a[..., :-1, :]], axis=-2)
        - cells_a
    )
    part_b = (
        jnp.concatenate([jnp.zeros_like(cells_b[..., :, :1]), cells_b[..., :, :-1]], axis=-1)
        - cells_b
    )
    return (part_a + part_b).reshape(shape)


def tv_parts(field):
    slices = field.shape[0]
    following = passed_along(field[:1], "slab", -1)
    extended = jnp.concatenate([field, following], axis=0)
    at_end = lax.axis_index("slab") == lax.axis_size("slab") - 1
    keep = jnp.logical_or(jnp.arange(slices, dtype=jnp.int32) < slices - 1, jnp.logical_not(at_end))
    depth = jnp.where(keep[:, None], extended[1:] - extended[:-1], 0.0)
    across, along = plane_grad(field)
    return (depth, across, along, keep)


def advance(volume, split_var, dual_var, grad, penalty):
    depth, across, along, keep = tv_parts(volume)
    row_mask, col_mask = plane_masks(volume.shape[-1])
    w_depth = jnp.where(keep[:, None], depth - split_var[0] + dual_var[0], 0.0)
    w_across = jnp.where(row_mask, across - split_var[1] + dual_var[1], 0.0)
    w_along = jnp.where(col_mask, along - split_var[2] + dual_var[2], 0.0)
    previous = passed_along(w_depth[-1:], "slab", 1)
    adjoint = jnp.concatenate([previous, w_depth[:-1]], axis=0) - w_depth
    adjoint = adjoint + plane_adjoint(w_across, w_along)
    new_volume = volume - TAU * (grad + penalty * adjoint)
    depth2, across2, along2, unused = tv_parts(new_volume)
    mixed = jnp.stack([depth2, across2, along2]) + dual_var
    limit = 1.0 / penalty
    new_dual = jnp.clip(mixed, -limit, limit)
    new_split = mixed - new_dual
    return (new_volume, new_split, new_dual)


def shards(
    volume, split_var, dual_var, sinogram, proj_tiles, ray_index, voxel_index, tile_count, rho
):
    penalty = rho[0]
    slices = volume.shape[0]
    tiles_dev = volume.shape[1] // TV
    slots = ray_index.shape[0]
    owned_rays = sinogram.shape[0]
    used = (jnp.arange(slots, dtype=jnp.int32) < tile_count[0]).astype(jnp.float32)
    vol_b = volume.astype(jnp.bfloat16)
    picked = vol_b.reshape(slices, tiles_dev, TV)[:, voxel_index]
    forward = jnp.einsum("snv,nvr->nsr", picked, proj_tiles, preferred_element_type=jnp.float32)
    forward = forward * used[:, None, None]
    count = lax.axis_size(("tile", "rep")) * owned_rays
    inside = jnp.logical_and(ray_index >= 0, ray_index < count)
    target = jnp.where(inside, ray_index, count)
    owned = lax.psum_scatter(
        jax.ops.segment_sum(forward, target, num_segments=count + 1)[:count],
        ("tile", "rep"),
        scatter_dimension=0,
        tiled=True,
    )
    resid = (owned - sinogram).astype(jnp.bfloat16)
    resid_all = lax.all_gather(resid, ("tile", "rep"), axis=0, tiled=True)
    rows = resid_all[ray_index]
    backward = jnp.einsum("nsr,nvr->nsv", rows, proj_tiles, preferred_element_type=jnp.float32)
    backward = backward * used[:, None, None]
    grad_tiles = jax.ops.segment_sum(backward, voxel_index, num_segments=tiles_dev)
    grad_part = grad_tiles.transpose(1, 0, 2).reshape(slices, tiles_dev * TV)
    grad = lax.psum(grad_part, "rep")
    return advance(volume, split_var, dual_var, grad, penalty)


def solution(mesh):
    return jax.shard_map(
        shards,
        mesh=mesh,
        in_specs=(
            P(("parts", "slab"), "tile"),
            P(None, ("parts", "slab"), "tile"),
            P(None, ("parts", "slab"), "tile"),
            P(("tile", "rep"), ("parts", "slab"), None),
            P(("tile", "rep"), None, None),
            P(("tile", "rep")),
            P(("tile", "rep")),
            P(("tile", "rep")),
            P(),
        ),
        out_specs=(
            P(("parts", "slab"), "tile"),
            P(None, ("parts", "slab"), "tile"),
            P(None, ("parts", "slab"), "tile"),
        ),
        check_vma=False,
    )
```

profile of v0, /device:TPU:0, one launch (start us, length us, event | category | flops | bytes accessed | tf_op | source)
XLA Modules:
  0.0 158.7 jit_solution(6437925864608319065)
XLA Ops:
  7.2 1.5 slice.70
  8.7 1.4 collective-permute-start
  10.1 1.4 reshape.51
  11.9 1.1 slice_subtract_fusion.3
  13.5 1.6 %squeeze.28 = f32[4,64,8,8]{3,2,1,0:T(8,128)} reshape(f32[1,4,4096]{2,1,0:T(4,128)S(1)} %get-tuple-element.5) | data formatting | bytes 131072 | tf_op jit(solution)/shard_map/squeeze | solution.py:64
  15.1 1.6 squeeze.29
  16.7 1.6 %squeeze.30 = f32[4,64,8,8]{3,2,1,0:T(8,128)} reshape(f32[1,4,4096]{2,1,0:T(4,128)S(1)} %get-tuple-element.6) | data formatting | bytes 131072 | tf_op jit(solution)/shard_map/squeeze | solution.py:65
  18.3 1.6 squeeze.31
  22.3 2.9 %add_select_fusion = (f32[4,64,8,8]{3,2,1,0:T(8,128)S(1)}, f32[4,64,8,8]{3,2,1,0:T(8,128)S(1)}) fusion(f32[4,64,8,8]{3,2,1,0:T(8,128)} %squeeze.31, f32[4,64,8,8]{3,2,1,0:T(8,128)} %squeeze.30, f32[4,64,8,7]{3,2,1,0:T(8,128)S(1)} %slice_subtract_fusion.2, pred[64,8,8]{2,1,0:T(8,128)(4,1)S(1)} %fusion.1, f32[4,64,8,8]{3,2,1,0:T(8,128)} %squeeze.29, ...), kind=kLoop, calls=%fused_computation.11 | loop fusion | flops 98304 | bytes 516096 | tf_op jit(solution)/shard_map/jit(_where)/select_n | solution.py:65
  25.2 0.9 fusion.15
  26.4 1.1 gather_fusion
  27.5 3.4 %convolution_multiply_fusion.1 = f32[256,4,128]{2,1,0:T(4,128)S(1)} fusion(bf16[256,64,128]{2,1,0:T(8,128)(2,1)} %param.13, bf16[256,4,64]{2,1,0:T(4,128)(2,1)S(1)} %gather_fusion, f32[256]{0:T(256)} %compare_convert_fusion), kind=kOutput, calls=%fused_computation.5 | convolution fusion | flops 16908288 | bytes 4850688 | tf_op jit(solution)/shard_map/snv,nvr->nsr/dot_general | solution.py:89
  30.9 8.4 %scatter_fusion = f32[33,4,128]{2,1,0:T(4,128)S(1)} fusion(f32[33,4,128]{2,1,0:T(4,128)S(1)} %broadcast_in_dim.59, s32[256]{0:T(256)S(1)} %copy-done.6, f32[256,4,128]{2,1,0:T(4,128)S(1)} %convolution_multiply_fusion.1), kind=kCustom, calls=%fused_computation.2 | custom fusion | flops 131072 | bytes 1573888 | tf_op jit(solution)/shard_map/scatter-add | solution.py:95
  41.4 4.8 %collective-permute-start.1 = (f32[1,4096]{1,0:T(1,128)S(1)}, f32[1,4096]{1,0:T(1,128)S(1)}, u32[]{:S(2)}, u32[]{:S(2)}) collective-permute-start(f32[1,4096]{1,0:T(1,128)S(1)} %slice.97), channel_id=1, source_target_pairs={{0,2},{1,3},{4,6},{5,7},{8,10},{9,11},{12,14},{13,15},{16,18},{17,... | collective-permute-start | bytes 49160 | tf_op jit(solution)/shard_map/ppermute | solution.py:15
  46.2 51.4 %all-reduce.12.cloned.1.call-done = f32[32,4,128]{2,1,0:T(4,128)} async-done(((f32[32,4,128]{2,1,0:T(4,128)}), f32[32,4,128]{2,1,0:T(4,128)}) %all-reduce.12.cloned.1.call-update) | async-done | bytes 65552
  98.4 14.0 %all_gather.3 = bf16[32,4,128]{2,1,0:T(4,128)(2,1)S(1)} all-gather(bf16[4,4,128]{2,1,0:T(4,128)(2,1)S(1)} %fusion.21), channel_id=1, replica_groups=mesh['parts'=2,'tile'=4,'slab'=2,'rep'=2] {'tile','rep'}, dimensions={0}, use_global_device_ids=true | all-gather | bytes 36864 | tf_op jit(solution)/shard_map/all_gather | solution.py:101
  112.3 1.0 gather_fusion.1
  113.3 4.4 %convolution_multiply_fusion = f32[256,4,64]{2,1,0:T(4,128)S(1)} fusion(bf16[256,4,128]{2,1,0:T(4,128)(2,1)S(1)} %gather_fusion.1, bf16[256,64,128]{2,1,0:T(8,128)(2,1)} %param.13, f32[256]{0:T(256)S(1)} %copy-done.9), kind=kOutput, calls=%fused_computation.4 | convolution fusion | flops 16842752 | bytes 4719616 | tf_op jit(solution)/shard_map/nsr,nvr->nsv/dot_general | solution.py:103
  117.8 8.4 %scatter_fusion.1 = f32[64,4,64]{2,1,0:T(4,128)S(1)} fusion(f32[64,4,64]{2,1,0:T(4,128)S(1)} %broadcast_in_dim.57, s32[256]{0:T(256)S(1)} %copy-done.8, f32[256,4,64]{2,1,0:T(4,128)S(1)} %convolution_multiply_fusion), kind=kCustom, calls=%fused_computation.3 | custom fusion | flops 65536 | bytes 787456 | tf_op jit(solution)/shard_map/scatter-add | solution.py:105
  128.7 15.2 %all-reduce.10.cloned.1.call-done = f32[4,4096]{1,0:T(4,128)} async-done(((f32[4,4096]{1,0:T(4,128)}), f32[4,4096]{1,0:T(4,128)}) %all-reduce.10.cloned.1.call-update) | async-done | bytes 65552 | tf_op jit(solution)/shard_map/psum | solution.py:107
  143.8 0.9 fusion.20
  145.4 1.3 collective-permute-start.2
  148.4 2.6 %collective-permute-done.2 = f32[1,4096]{1,0:T(1,128)S(1)} collective-permute-done((f32[1,4096]{1,0:T(1,128)S(1)}, f32[1,4096]{1,0:T(1,128)S(1)}, u32[]{:S(2)}, u32[]{:S(2)}) %collective-permute-start.2) | collective-permute-done | bytes 16416 | tf_op jit(solution)/shard_map/ppermute | solution.py:15
  151.1 0.8 fusion.22
  (62 shorter events, 9.0 us)
Async XLA Ops:
  7.2 6.3 %copy-start.3 = (f32[3,4,4096]{2,1,0:T(4,128)S(1)}, f32[3,4,4096]{2,1,0:T(4,128)}, u32[]{:S(2)}) copy-start(f32[3,4,4096]{2,1,0:T(4,128)} %param.10) | copy-start | bytes 589828
  7.2 90.5 %all-reduce.12.cloned.1.call-start = ((), (), s32[]{:S(2)}) async-start(), calls=%async_computation.1 | async-start | bytes 131072
  8.7 6.4 %copy-start = (f32[3,4,4096]{2,1,0:T(4,128)S(1)}, f32[3,4,4096]{2,1,0:T(4,128)}, u32[]{:S(2)}) copy-start(f32[3,4,4096]{2,1,0:T(4,128)} %param.11) | copy-start | bytes 589828
  8.7 16.5 %collective-permute-start = (f32[1,4096]{1,0:T(1,128)}, f32[1,4096]{1,0:T(1,128)S(1)}, u32[]{:S(2)}, u32[]{:S(2)}) collective-permute-start(f32[1,4096]{1,0:T(1,128)} %slice.70), channel_id=1, source_target_pairs={{2,0},{3,1},{6,4},{7,5},{10,8},{11,9},{14,12},{15,13},{18,16},{19,... | collective-permute-start | bytes 49160 | tf_op jit(solution)/shard_map/ppermute | solution.py:15
  11.9 8.0 %copy-start.7 = (s32[256]{0:T(256)S(1)}, s32[256]{0:T(256)}, u32[]{:S(2)}) copy-start(s32[256]{0:T(256)} %param.15) | copy-start | bytes 3076
  11.9 9.8 %copy-start.10 = (s32[256]{0:T(256)S(1)}, s32[256]{0:T(256)}, u32[]{:S(2)}) copy-start(s32[256]{0:T(256)} %param.14) | copy-start | bytes 3076
  22.3 2.9 %copy-start.1 = (f32[4,4096]{1,0:T(4,128)S(1)}, f32[4,4096]{1,0:T(4,128)}, u32[]{:S(2)}) copy-start(f32[4,4096]{1,0:T(4,128)} %param.9) | copy-start | bytes 196612
  25.2 5.8 %copy-start.6 = (s32[256]{0:T(256)S(1)}, s32[256]{0:T(256)}, u32[]{:S(2)}) copy-start(s32[256]{0:T(256)} %get-tuple-element.12) | copy-start | bytes 3076
  25.2 14.9 %copy-start.5 = (s32[256]{0:T(256)S(1)}, s32[256]{0:T(256)}, u32[]{:S(2)}) copy-start(s32[256]{0:T(256)} %get-tuple-element.11) | copy-start | bytes 3076
  25.2 14.9 %copy-start.11 = (u32[32]{0:T(128)S(1)}, u32[32]{0:T(128)}, u32[]{:S(2)}) copy-start(u32[32]{0:T(128)} %constant.82) | copy-start | bytes 388
  25.2 72.4 %copy-start.4 = (f32[4,4,128]{2,1,0:T(4,128)S(1)}, f32[4,4,128]{2,1,0:T(4,128)}, u32[]{:S(2)}) copy-start(f32[4,4,128]{2,1,0:T(4,128)} %param.12) | copy-start | bytes 24580
  26.2 87.1 %copy-start.9 = (f32[256]{0:T(256)S(1)}, f32[256]{0:T(256)}, u32[]{:S(2)}) copy-start(f32[256]{0:T(256)} %compare_convert_fusion) | copy-start | bytes 3076
  30.9 86.9 %copy-start.8 = (s32[256]{0:T(256)S(1)}, s32[256]{0:T(256)}, u32[]{:S(2)}) copy-start(s32[256]{0:T(256)} %param.15) | copy-start | bytes 3076
  40.0 103.8 %all-reduce.10.cloned.1.call-start = ((), (), s32[]{:S(2)}) async-start(), calls=%async_computation | async-start | bytes 131072 | tf_op jit(solution)/shard_map/psum | solution.py:107
  41.4 87.3 %collective-permute-start.1 = (f32[1,4096]{1,0:T(1,128)S(1)}, f32[1,4096]{1,0:T(1,128)S(1)}, u32[]{:S(2)}, u32[]{:S(2)}) collective-permute-start(f32[1,4096]{1,0:T(1,128)S(1)} %slice.97), channel_id=1, source_target_pairs={{0,2},{1,3},{4,6},{5,7},{8,10},{9,11},{12,14},{13,15},{16,18},{17,... | collective-permute-start | bytes 49160 | tf_op jit(solution)/shard_map/ppermute | solution.py:15
  144.7 6.3 %copy-start.2 = (f32[4,4096]{1,0:T(4,128)}, f32[4,4096]{1,0:T(4,128)S(1)}, u32[]{:S(2)}) copy-start(f32[4,4096]{1,0:T(4,128)S(1)} %fusion.20) | copy-start | bytes 196612
  145.4 5.6 %collective-permute-start.2 = (f32[1,4096]{1,0:T(1,128)S(1)}, f32[1,4096]{1,0:T(1,128)S(1)}, u32[]{:S(2)}, u32[]{:S(2)}) collective-permute-start(f32[1,4096]{1,0:T(1,128)S(1)} %slice.105), channel_id=1, source_target_pairs={{2,0},{3,1},{6,4},{7,5},{10,8},{11,9},{14,12},{15,13},{18,16},{19,... | collective-permute-start | bytes 49160 | tf_op jit(solution)/shard_map/ppermute | solution.py:15
Sparse Core Ops, SparseCore 0:
  40.2 57.4 all-reduce.11
  127.1 16.6 all-reduce.9
where the time goes:
time: 159 us
  waiting for transfers between devices  69.2 us (44%)
  other arithmetic  27.6 us (17%)
  between operations  16.4 us (10%)
  local copies, waits for them, and re-layouts  16.1 us (10%)
  blocking collectives  14 us (9%)
  matrix products  7.83 us (5%)
  starting transfers between devices  7.62 us (5%)
    unnamed x3, waiting for transfers between devices  51.4 us
    psum x1, waiting for transfers between devices, shards(): grad = lax.psum(grad_part, 'rep')  15.2 us
    all_gather x1, blocking collectives, shards(): resid_all = lax.all_gather(resid, ('tile', 'rep'), axis=0, tiled=True)  14 us
    scatter-add x1, other arithmetic, shards(): jax.ops.segment_sum(forward, target, num_segments=count + 1)[:count]  8.45 us
    scatter-add x1, other arithmetic, shards(): jax.ops.segment_sum(backward, voxel_index, num_segments=tiles_dev)  8.39 us
    ppermute x3, starting transfers between devices, passed_along(): return lax.ppermute(array, axis, pairs)  7.54 us
    dot_general x1, matrix products, shards(): jnp.einsum('nsr,nvr->nsv', rows, proj_tiles, preferred_element_type=jnp.f...  4.45 us
    dot_general x1, matrix products, shards(): jnp.einsum('snv,nvr->nsr', picked, proj_tiles, preferred_element_type=jnp...  3.38 us
  transfers between devices with their start and end apart: 5, of which 3 were waited for; matrix products, arithmetic and copies ran while one was open for 21% of the time, Pallas kernels for 0%

commit v1 on v0

v1 whole, which is shorter than its diff:
```python
import jax
import jax.numpy as jnp
from jax import lax
from jax.experimental import pallas as pl
from jax.experimental.pallas import tpu as pltpu
from jax.sharding import PartitionSpec as P

TV = 64
TR = 128
TAU = 0.5
GROUP = 4
CHUNKS = 8
VMEM_LIMIT = 48 * 1024 * 1024


def iotas(shape):
    row = lax.broadcasted_iota(jnp.int32, shape, 0)
    lane = lax.broadcasted_iota(jnp.int32, shape, 1)
    return row, lane


def start_tiles(proj_hbm, tiles, sems):
    per = proj_hbm.shape[0] // CHUNKS
    copies = []
    for c in range(CHUNKS):
        part = pl.ds(c * per, per)
        copy = pltpu.make_async_copy(proj_hbm.at[part], tiles.at[part], sems.at[c])
        copy.start()
        copies.append(copy)
    return copies


def plane_masks(lane):
    return (lane % TV) // 8 < 7, lane % 8 < 7


def forward_kernel(
    count, ray, voxel, rho, vol_hbm, split_hbm, dual_hbm, proj_hbm,
    partial_out, base_out, halo_out,
    vol, split, dual, tiles, double, table, acc0, acc1, acc2, acc3, sems, tile_sems,
):
    slots = proj_hbm.shape[0]
    rays = acc0.shape[0] - 1
    width = vol.shape[1]
    loads = [
        pltpu.make_async_copy(vol_hbm, vol, sems.at[0]),
        pltpu.make_async_copy(split_hbm, split, sems.at[1]),
        pltpu.make_async_copy(dual_hbm, dual, sems.at[2]),
    ]
    for load in loads:
        load.start()
    copies = start_tiles(proj_hbm, tiles, tile_sems)
    accs = (acc0, acc1, acc2, acc3)
    for acc in accs:
        acc[...] = jnp.zeros_like(acc)
    row, lane = iotas((8, 128))
    low, top = lane < TV, row < 4

    loads[0].wait()
    field = vol[...]
    double[0:4, :] = field
    double[4:8, :] = field
    for j in range(width // 128):
        x = double[:, 128 * j:128 * j + 128].astype(jnp.bfloat16).astype(jnp.float32)
        turned = pltpu.roll(x, TV, axis=1)
        zero = jnp.zeros_like(x)
        first = jnp.where(jnp.logical_and(top, low), x, zero)
        second = jnp.where(jnp.logical_and(top, low), turned, zero)
        other = jnp.logical_not(jnp.logical_or(top, low))
        table[2 * j] = jnp.where(other, turned, first)
        table[2 * j + 1] = jnp.where(other, x, second)

    loads[1].wait()
    loads[2].wait()
    factor = TAU * rho[0]
    row_mask, col_mask = plane_masks(lane)
    for j in range(width // 128):
        at = slice(128 * j, 128 * j + 128)
        x = double[:, at]
        gap = [
            jnp.concatenate([dual[k, :, at] - split[k, :, at]] * 2, axis=0) for k in range(3)
        ]
        depth = jnp.where(row < 3, pltpu.roll(x, 7, axis=0) - x + gap[0], 0.0)
        across = jnp.where(row_mask, pltpu.roll(x, 120, axis=1) - x + gap[1], 0.0)
        along = jnp.where(col_mask, pltpu.roll(x, 127, axis=1) - x + gap[2], 0.0)
        adjoint = pltpu.roll(depth, 1, axis=0) - depth
        adjoint += jnp.where((lane % TV) >= 8, pltpu.roll(across, 8, axis=1), 0.0) - across
        adjoint += jnp.where(lane % 8 >= 1, pltpu.roll(along, 1, axis=1), 0.0) - along
        base = x - factor * adjoint
        base_out[:, at] = base[0:4]
        halo_out[0:1, at] = (x - gap[0])[3:4]
        halo_out[1:2, at] = x[0:1]
        halo_out[2:3, at] = base[0:1]
        halo_out[3:4, at] = base[0:1]

    used = count[0]
    per = slots // CHUNKS
    for g in range(slots // GROUP):
        if GROUP * g % per == 0:
            copies[GROUP * g // per].wait()
        n = GROUP * g
        pairs = [
            jnp.where(top, table[voxel[n + 2 * i]], table[voxel[n + 2 * i + 1]]) for i in range(2)
        ]
        zero = jnp.zeros_like(pairs[0])
        left = jnp.concatenate([pairs[0], zero], axis=0).astype(jnp.bfloat16)
        right = jnp.concatenate([zero, pairs[1]], axis=0).astype(jnp.bfloat16)
        sums = jnp.dot(
            jnp.concatenate([left, right], axis=1),
            tiles[n:n + GROUP].reshape(GROUP * TV, TR),
            preferred_element_type=jnp.float32,
        )
        for i in range(GROUP):
            at = jnp.where(n + i < used, ray[n + i], rays)
            accs[i][at] += sums[8 * (i // 2):8 * (i // 2) + 8]
    for q in range(rays // 4):
        halves = []
        for r in (4 * q, 4 * q + 2):
            even = [acc0[r + k] + acc2[r + k] for k in range(2)]
            odd = [acc1[r + k] + acc3[r + k] for k in range(2)]
            halves.append(
                jnp.where(top, even[0], odd[1])
                + pltpu.roll(jnp.where(top, even[1], odd[0]), 4, axis=0)
            )
        partial_out[16 * q:16 * q + 16, :] = jnp.concatenate(halves, axis=0).astype(jnp.bfloat16)


def resid_kernel(parts, sinogram, out, total):
    total[...] = jnp.sum(parts[...].astype(jnp.float32), axis=0)
    for r in range(sinogram.shape[0]):
        at = pl.ds(4 * r, 4)
        total[at, :] = total[at, :] - sinogram[r]
    resid = total[...].astype(jnp.bfloat16)
    for copy in range(out.shape[0]):
        out[copy] = resid


def backward_kernel(
    count, ray, voxel, here, resid, proj_hbm, out,
    tiles, table, acc0, acc1, acc2, acc3, tile_sems,
):
    slots = proj_hbm.shape[0]
    rays = table.shape[0]
    voxel_tiles = acc0.shape[0] - 1
    copies = start_tiles(proj_hbm, tiles, tile_sems)
    accs = (acc0, acc1, acc2, acc3)
    for acc in accs:
        acc[...] = jnp.zeros_like(acc)
    row, lane = iotas((8, 128))
    low, top = lane < TV, row < 4
    mine = here[0]
    for q in range(rays // 4):
        own = resid[mine, 16 * q:16 * q + 16, :].astype(jnp.float32)
        following = resid[1 - mine, 16 * q:16 * q + 16, :].astype(jnp.float32)
        for k in range(2):
            a, b = own[8 * k:8 * k + 8], following[8 * k:8 * k + 8]
            table[4 * q + 2 * k] = jnp.where(top, a, pltpu.roll(b, 4, axis=0))
            table[4 * q + 2 * k + 1] = jnp.where(top, pltpu.roll(a, 4, axis=0), b)
    used = count[0]
    per = slots // CHUNKS
    for g in range(slots // GROUP):
        if GROUP * g % per == 0:
            copies[GROUP * g // per].wait()
        n = GROUP * g
        rows = jnp.concatenate([table[ray[n + i]] for i in range(GROUP)], axis=0)
        back = lax.dot_general(
            rows.astype(jnp.bfloat16),
            tiles[n:n + GROUP].reshape(GROUP * TV, TR),
            (((1,), (1,)), ((), ())),
            preferred_element_type=jnp.float32,
        )
        for i in range(GROUP):
            at = jnp.where(n + i < used, voxel[n + i], voxel_tiles)
            half = 128 * (i // 2)
            accs[i][at] += back[8 * i:8 * i + 8, half:half + 128]
    for j in range(voxel_tiles // 2):
        even = [acc0[2 * j + k] + acc2[2 * j + k] for k in range(2)]
        odd = [acc1[2 * j + k] + acc3[2 * j + k] for k in range(2)]
        out[:, 128 * j:128 * j + 128] = jnp.where(low, even[0], odd[1]) + pltpu.roll(
            jnp.where(low, even[1], odd[0]), TV, axis=1
        )


def update_kernel(
    rho, grad, grad_other, base, dual, halo, from_next, from_previous,
    new_volume, new_split, new_dual,
):
    slab, slabs = lax.axis_index("slab"), lax.axis_size("slab")
    first, last = slab == 0, slab == slabs - 1
    penalty = rho[0]
    factor = TAU * penalty
    limit = 1.0 / penalty
    row, lane = iotas((8, 128))
    row_mask, col_mask = plane_masks(lane)
    inner = jnp.logical_or(row < 3, jnp.logical_not(last))
    for j in range(dual.shape[2] // 128):
        at = slice(128 * j, 128 * j + 128)
        above = jnp.where(last, 0.0, factor * (from_next[1:2, at] - halo[0:1, at]))
        below = jnp.where(first, 0.0, factor * (halo[1:2, at] - from_previous[0:1, at]))
        own = jnp.concatenate([base[:, at]] * 2, axis=0)
        field = jnp.where(row < 4, own, from_next[2:3, at])
        field += jnp.where(
            row == 0, -below, jnp.where(row == 3, above, jnp.where(row == 4, -above, 0.0))
        )
        field -= TAU * (grad[:, at] + grad_other[:, at])
        new_volume[:, at] = field[0:4]
        steps = (
            jnp.where(inner, pltpu.roll(field, 7, axis=0) - field, 0.0),
            jnp.where(row_mask, pltpu.roll(field, 120, axis=1) - field, 0.0),
            jnp.where(col_mask, pltpu.roll(field, 127, axis=1) - field, 0.0),
        )
        for k in range(3):
            mixed = steps[k][0:4] + dual[k, :, at]
            clipped = jnp.clip(mixed, -limit, limit)
            new_dual[k, :, at] = clipped
            new_split[k, :, at] = mixed - clipped


def vmem():
    return pl.BlockSpec(memory_space=pltpu.VMEM)


def smem():
    return pl.BlockSpec(memory_space=pltpu.SMEM)


def anywhere():
    return pl.BlockSpec(memory_space=pl.ANY)


def params():
    return pltpu.CompilerParams(vmem_limit_bytes=VMEM_LIMIT)


def shards(
    volume, split_var, dual_var, sinogram, proj_tiles, ray_index, voxel_index, tile_count, rho
):
    f32, bf16 = jnp.float32, jnp.bfloat16
    slices, width = volume.shape
    slots = ray_index.shape[0]
    owned = sinogram.shape[0]
    group = lax.axis_size(("tile", "rep"))
    slabs = lax.axis_size("slab")
    rays = owned * group
    voxel_tiles = width // TV
    block = owned * slices

    partial, base, halo = pl.pallas_call(
        forward_kernel,
        out_shape=(
            jax.ShapeDtypeStruct((rays * slices, TR), bf16),
            jax.ShapeDtypeStruct((slices, width), f32),
            jax.ShapeDtypeStruct((4, width), f32),
        ),
        in_specs=[smem()] * 4 + [anywhere()] * 4,
        out_specs=(vmem(), vmem(), vmem()),
        scratch_shapes=[
            pltpu.VMEM((slices, width), f32),
            pltpu.VMEM((3, slices, width), f32),
            pltpu.VMEM((3, slices, width), f32),
            pltpu.VMEM(proj_tiles.shape, bf16),
            pltpu.VMEM((8, width), f32),
            pltpu.VMEM((voxel_tiles, 8, 128), f32),
        ]
        + [pltpu.VMEM((rays + 1, 8, 128), f32)] * 4
        + [pltpu.SemaphoreType.DMA((3,)), pltpu.SemaphoreType.DMA((CHUNKS,))],
        compiler_params=params(),
        name="forward",
    )(tile_count, ray_index, voxel_index, rho, volume, split_var, dual_var, proj_tiles)

    if slabs == 2:
        from_next = from_previous = lax.ppermute(halo, "slab", [(0, 1), (1, 0)])
    else:
        from_next = lax.ppermute(halo, "slab", [(i, i - 1) for i in range(1, slabs)])
        from_previous = lax.ppermute(halo, "slab", [(i, i + 1) for i in range(slabs - 1)])

    parts = lax.all_to_all(
        partial.reshape(group, block, TR), ("tile", "rep"), 0, 0, tiled=True
    )
    copies = group * (2 if slabs == 2 else 1)
    resid = pl.pallas_call(
        resid_kernel,
        out_shape=jax.ShapeDtypeStruct((copies, block, TR), bf16),
        in_specs=[vmem(), vmem()],
        out_specs=vmem(),
        scratch_shapes=[pltpu.VMEM((block, TR), f32)],
        compiler_params=params(),
        name="residual",
    )(parts, sinogram)
    if slabs == 2:
        both = lax.all_to_all(resid, ("slab", "tile", "rep"), 0, 0, tiled=True)
        both = both.reshape(2, rays * slices, TR)
        here = lax.axis_index("slab").reshape(1)
    else:
        own = lax.all_to_all(resid, ("tile", "rep"), 0, 0, tiled=True)
        following = lax.ppermute(own, "slab", [(i, i - 1) for i in range(1, slabs)])
        both = jnp.stack([own, following]).reshape(2, rays * slices, TR)
        here = jnp.zeros((1,), jnp.int32)

    grad = pl.pallas_call(
        backward_kernel,
        out_shape=jax.ShapeDtypeStruct((8, width), f32),
        in_specs=[smem()] * 4 + [vmem(), anywhere()],
        out_specs=vmem(),
        scratch_shapes=[
            pltpu.VMEM(proj_tiles.shape, bf16),
            pltpu.VMEM((rays, 8, 128), f32),
        ]
        + [pltpu.VMEM((voxel_tiles + 1, 8, 128), f32)] * 4
        + [pltpu.SemaphoreType.DMA((CHUNKS,))],
        compiler_params=params(),
        name="backward",
    )(tile_count, ray_index, voxel_index, here.astype(jnp.int32), both, proj_tiles)
    grad_other = lax.ppermute(grad, "rep", [(0, 1), (1, 0)])

    return pl.pallas_call(
        update_kernel,
        out_shape=(
            jax.ShapeDtypeStruct((slices, width), f32),
            jax.ShapeDtypeStruct((3, slices, width), f32),
            jax.ShapeDtypeStruct((3, slices, width), f32),
        ),
        in_specs=[smem()] + [vmem()] * 7,
        out_specs=(vmem(), vmem(), vmem()),
        compiler_params=params(),
        name="update",
    )(rho, grad, grad_other, base, dual_var, halo, from_next, from_previous)


def solution(mesh):
    return jax.shard_map(
        shards,
        mesh=mesh,
        in_specs=(
            P(("parts", "slab"), "tile"),
            P(None, ("parts", "slab"), "tile"),
            P(None, ("parts", "slab"), "tile"),
            P(("tile", "rep"), ("parts", "slab"), None),
            P(("tile", "rep"), None, None),
            P(("tile", "rep")),
            P(("tile", "rep")),
            P(("tile", "rep")),
            P(),
        ),
        out_specs=(
            P(("parts", "slab"), "tile"),
            P(None, ("parts", "slab"), "tile"),
            P(None, ("parts", "slab"), "tile"),
        ),
        check_vma=False,
    )
```

time: 159 us -> 46.3 us (0.29)
  waiting for transfers between devices: 69.2 us -> 10.8 us
  other arithmetic: 27.6 us -> 0 us
  between operations: 16.4 us -> 2.02 us
  Pallas kernels: 0 us -> 8.54 us
  matrix products: 7.83 us -> 0 us
  local copies, waits for them, and re-layouts: 16.1 us -> 8.44 us
  starting transfers between devices: 7.62 us -> 4.15 us
  blocking collectives: 14 us -> 11.9 us
    unnamed x3 -> x0, waiting for transfers between devices: 51.4 us -> none
    scatter-add x2 -> x0, other arithmetic: 16.8 us -> none  [the longest x1 8.45 us: shards(): jax.ops.segment_sum(forward, target, num_segments=count + 1)[:count]]
    psum x1 -> x0, waiting for transfers between devices: 15.2 us -> none  [shards(): grad = lax.psum(grad_part, 'rep')]
    all_gather x1 -> x0, blocking collectives: 14 us -> none  [shards(): resid_all = lax.all_gather(resid, ('tile', 'rep'), axis=0, tiled=True)]
    all_to_all x0 -> x1, blocking collectives: none -> 11.9 us  [shards(): lax.all_to_all(partial.reshape(group, block, TR), ('tile', 'rep'), 0, 0,...]
    pallas_call x0 -> x4, Pallas kernels: none -> 8.54 us  [the longest x1 3.53 us: shards(): pl.pallas_call(forward_kernel, out_shape=(jax.ShapeDtypeStruct((rays * sl...]
    dot_general x2 -> x0, matrix products: 7.83 us -> none  [the longest x1 4.45 us: shards(): jnp.einsum('nsr,nvr->nsv', rows, proj_tiles, preferred_element_type=jnp.f...]
    unnamed x25 -> x22, local copies, waits for them, and re-layouts: 0.65 us -> 8.44 us
  transfers between devices with their start and end apart: 5 -> 3, of which waited for: 3 -> 2; matrix products, arithmetic and copies ran while one was open for 21% -> 0% of each run, Pallas kernels for 0% -> 0%
where the time goes in v1:
time: 46.3 us; the launch traced here: 45.8 us
  blocking collectives  11.9 us (26%)
  waiting for transfers between devices  10.8 us (23%)
  Pallas kernels  8.54 us (18%)
  local copies, waits for them, and re-layouts  8.44 us (18%)
  starting transfers between devices  4.15 us (9%)
  between operations  2.02 us (4%)
    all_to_all x1, blocking collectives, shards(): lax.all_to_all(partial.reshape(group, block, TR), ('tile', 'rep'), 0, 0,...  11.9 us
    unnamed x22, local copies, waits for them, and re-layouts  8.44 us
    all_to_all x1, waiting for transfers between devices, shards(): both = lax.all_to_all(resid, ('slab', 'tile', 'rep'), 0, 0, tiled=True)  6.85 us
    ppermute x1, waiting for transfers between devices, shards(): from_next = from_previous = lax.ppermute(halo, 'slab', [(0, 1), (1, 0)])  3.93 us
    pallas_call x1, Pallas kernels, shards(): pl.pallas_call(forward_kernel, out_shape=(jax.ShapeDtypeStruct((rays * sl...  3.53 us
    all_to_all x1, starting transfers between devices, shards(): both = lax.all_to_all(resid, ('slab', 'tile', 'rep'), 0, 0, tiled=True)  3.5 us
    pallas_call x1, Pallas kernels, shards(): pl.pallas_call(backward_kernel, out_shape=jax.ShapeDtypeStruct((8, width)...  3.41 us
    pallas_call x1, Pallas kernels, shards(): pl.pallas_call(update_kernel, out_shape=(jax.ShapeDtypeStruct((slices, wi...  0.94 us
  transfers between devices with their start and end apart: 3, of which 2 were waited for; matrix products, arithmetic and copies ran while one was open for 0% of the time, Pallas kernels for 0%

profile of v1, /device:TPU:0, one launch (start us, length us, event | category | flops | bytes accessed | tf_op | source)
XLA Modules:
  0.0 45.8 jit_solution(8750616455557468212)
XLA Ops:
  0.6 0.0 copy-start.10
  0.6 0.0 copy-start.8
  2.0 0.0 copy-start
  2.0 2.2 %copy-done = bf16[256,64,128]{2,1,0:T(8,128)(2,1)S(1)} copy-done((bf16[256,64,128]{2,1,0:T(8,128)(2,1)S(1)}, bf16[256,64,128]{2,1,0:T(8,128)(2,1)}, u32[]{:S(2)}) %copy-start) | copy-done | bytes 4194328
  4.2 0.9 %copy-done.2 = f32[3,4,4096]{2,1,0:T(4,128)S(1)} copy-done((f32[3,4,4096]{2,1,0:T(4,128)S(1)}, f32[3,4,4096]{2,1,0:T(4,128)}, u32[]{:S(2)}) %copy-start.2) | copy-done | bytes 196632
  5.1 0.9 %copy-done.4 = f32[3,4,4096]{2,1,0:T(4,128)S(1)} copy-done((f32[3,4,4096]{2,1,0:T(4,128)S(1)}, f32[3,4,4096]{2,1,0:T(4,128)}, u32[]{:S(2)}) %copy-start.4) | copy-done | bytes 196632
  6.0 0.8 %copy-done.5 = f32[4,4096]{1,0:T(4,128)S(1)} copy-done((f32[4,4096]{1,0:T(4,128)S(1)}, f32[4,4096]{1,0:T(4,128)}, u32[]{:S(2)}) %copy-start.5) | copy-done | bytes 65560
  6.9 0.7 %copy-done.7 = s32[256]{0:T(256)S(1)} copy-done((s32[256]{0:T(256)S(1)}, s32[256]{0:T(256)}, u32[]{:S(2)}) %copy-start.7) | copy-done | bytes 1048
  7.5 0.7 %copy-done.9 = s32[256]{0:T(256)S(1)} copy-done((s32[256]{0:T(256)S(1)}, s32[256]{0:T(256)}, u32[]{:S(2)}) %copy-start.9) | copy-done | bytes 1048
  8.2 3.5 %forward.1 = (bf16[128,128]{1,0:T(8,128)(2,1)S(1)}, f32[4,4096]{1,0:T(4,128)S(1)}, f32[4,4096]{1,0:T(4,128)S(1)}) custom-call(s32[1]{0:T(128)S(6)} %copy.12.count, s32[256]{0:T(256)S(1)} %copy-done.7, s32[256]{0:T(256)S(1)} %copy-done.9, f32[1]{0:T(128)S(6)} %copy.13.rho, f32[4,4096]{1,0:T(4,128)S(1)} %copy-done.5, f32[3,4,4096]{2,1,0:T(4,128)S(1)} %copy-done.4, ...), custom_call_target="tpu_custom_call" | custom-call | tf_op jit(solution)/shard_map/forward/pallas_call | solution.py:248
  11.7 11.9 %all_to_all.10.parts = bf16[8,16,128]{2,1,0:T(8,128)(2,1)S(1)} all-to-all(bf16[8,16,128]{2,1,0:T(8,128)(2,1)S(1)} %bitcast.4), channel_id=1, replica_groups=mesh['parts'=2,'tile'=4,'slab'=2,'rep'=2] {'tile','rep'}, dimensions={0} | all-to-all | bytes 65536 | tf_op jit(solution)/shard_map/all_to_all | solution.py:277
  23.6 0.0 copy-done.6
  23.6 0.7 %residual.1 = bf16[16,16,128]{2,1,0:T(8,128)(2,1)} custom-call(bf16[8,16,128]{2,1,0:T(8,128)(2,1)S(1)} %all_to_all.10.parts, f32[4,4,128]{2,1,0:T(4,128)S(1)} %copy-done.6), custom_call_target="tpu_custom_call" | custom-call | tf_op jit(solution)/shard_map/residual/pallas_call | solution.py:281
  24.3 3.5 %all-to-all-start.1 = ((bf16[16,16,128]{2,1,0:T(8,128)(2,1)}), bf16[16,16,128]{2,1,0:T(8,128)(2,1)S(1)}, u32[]{:S(2)}, u32[]{:S(2)}) async-start(bf16[16,16,128]{2,1,0:T(8,128)(2,1)} %residual.1), calls=%async_computation.1 | async-start | bytes 131072 | tf_op jit(solution)/shard_map/all_to_all | solution.py:291
  27.8 6.9 %all-to-all-done.1 = bf16[16,16,128]{2,1,0:T(8,128)(2,1)S(1)} async-done(((bf16[16,16,128]{2,1,0:T(8,128)(2,1)}), bf16[16,16,128]{2,1,0:T(8,128)(2,1)S(1)}, u32[]{:S(2)}, u32[]{:S(2)}) %all-to-all-start.1) | async-done | bytes 65568 | tf_op jit(solution)/shard_map/all_to_all | solution.py:291
  34.7 0.0 copy-done.10
  34.7 0.0 copy-done.8
  34.7 2.2 %copy-done.1 = bf16[256,64,128]{2,1,0:T(8,128)(2,1)S(1)} copy-done((bf16[256,64,128]{2,1,0:T(8,128)(2,1)S(1)}, bf16[256,64,128]{2,1,0:T(8,128)(2,1)}, u32[]{:S(2)}) %copy-start.1) | copy-done | bytes 4194328
  36.9 3.4 %backward.1.grad = f32[8,4096]{1,0:T(8,128)S(1)} custom-call(s32[1]{0:T(128)S(6)} %copy.12.count, s32[256]{0:T(256)S(1)} %copy-done.8, s32[256]{0:T(256)S(1)} %copy-done.10, s32[1]{0:T(128)} %bitcast.here, bf16[2,128,128]{2,1,0:T(8,128)(2,1)S(1)} %bitcast.3, bf16[256,64,128]{2,1,0:T(8,128)(2,1)S(1)} %copy-done.1), custom_call_target="tpu_custom_call" | custom-call | tf_op jit(solution)/shard_map/backward/pallas_call | solution.py:300
  40.3 0.1 collective-permute-start
  40.4 0.6 %collective-permute-start.1 = (f32[4,4096]{1,0:T(4,128)S(1)}, f32[4,4096]{1,0:T(4,128)S(1)}, u32[]{:S(2)}, u32[]{:S(2)}) collective-permute-start(f32[4,4096]{1,0:T(4,128)S(1)} %get-tuple-element.8.halo), channel_id=1, source_target_pairs={{0,2},{2,0},{1,3},{3,1},{4,6},{6,4},{5,7},{7,5},{8,10},{10,8},{9,1... | collective-permute-start | bytes 196616 | tf_op jit(solution)/shard_map/ppermute | solution.py:272
  40.9 3.9 %collective-permute-done.1.from_next.from_previous = f32[4,4096]{1,0:T(4,128)S(1)} collective-permute-done((f32[4,4096]{1,0:T(4,128)S(1)}, f32[4,4096]{1,0:T(4,128)S(1)}, u32[]{:S(2)}, u32[]{:S(2)}) %collective-permute-start.1) | collective-permute-done | bytes 65568 | tf_op jit(solution)/shard_map/ppermute | solution.py:272
  44.9 0.0 collective-permute-done.grad_other
  44.9 0.9 %update.1 = (f32[4,4096]{1,0:T(4,128)}, f32[3,4,4096]{2,1,0:T(4,128)}, f32[3,4,4096]{2,1,0:T(4,128)}) custom-call(f32[1]{0:T(128)S(6)} %copy.13.rho, f32[8,4096]{1,0:T(8,128)S(1)} %backward.1.grad, f32[8,4096]{1,0:T(8,128)S(1)} %collective-permute-done.grad_other, f32[4,4096]{1,0:T(4,128)S(1)} %get-tuple-element.7.base, f32[3,4,4096]{2,1,0:T(4,128)S(1)} %copy-done.3, ...), custom_call_target="tpu_custom_call" | custom-call | tf_op jit(solution)/shard_map/update/pallas_call | solution.py:316
  (9 shorter events, 0.0 us)
Async XLA Ops:
  0.6 34.0 %copy-start.10 = (s32[256]{0:T(256)S(1)}, s32[256]{0:T(256)}, u32[]{:S(2)}) copy-start(s32[256]{0:T(256)} %voxel.3) | copy-start | bytes 3076
  0.6 34.0 %copy-start.8 = (s32[256]{0:T(256)S(1)}, s32[256]{0:T(256)}, u32[]{:S(2)}) copy-start(s32[256]{0:T(256)} %ray.3) | copy-start | bytes 3076
  2.0 2.2 %copy-start = (bf16[256,64,128]{2,1,0:T(8,128)(2,1)S(1)}, bf16[256,64,128]{2,1,0:T(8,128)(2,1)}, u32[]{:S(2)}) copy-start(bf16[256,64,128]{2,1,0:T(8,128)(2,1)} %proj_hbm.3) | copy-start | bytes 12582916
  4.2 0.9 %copy-start.2 = (f32[3,4,4096]{2,1,0:T(4,128)S(1)}, f32[3,4,4096]{2,1,0:T(4,128)}, u32[]{:S(2)}) copy-start(f32[3,4,4096]{2,1,0:T(4,128)} %dual.1) | copy-start | bytes 589828
  5.1 0.9 %copy-start.4 = (f32[3,4,4096]{2,1,0:T(4,128)S(1)}, f32[3,4,4096]{2,1,0:T(4,128)}, u32[]{:S(2)}) copy-start(f32[3,4,4096]{2,1,0:T(4,128)} %split_hbm.1) | copy-start | bytes 589828
  6.0 0.8 %copy-start.5 = (f32[4,4096]{1,0:T(4,128)S(1)}, f32[4,4096]{1,0:T(4,128)}, u32[]{:S(2)}) copy-start(f32[4,4096]{1,0:T(4,128)} %vol_hbm.1) | copy-start | bytes 196612
  6.8 0.7 %copy-start.7 = (s32[256]{0:T(256)S(1)}, s32[256]{0:T(256)}, u32[]{:S(2)}) copy-start(s32[256]{0:T(256)} %ray.3) | copy-start | bytes 3076
  7.5 0.7 %copy-start.9 = (s32[256]{0:T(256)S(1)}, s32[256]{0:T(256)}, u32[]{:S(2)}) copy-start(s32[256]{0:T(256)} %voxel.3) | copy-start | bytes 3076
  8.2 15.4 %copy-start.6 = (f32[4,4,128]{2,1,0:T(4,128)S(1)}, f32[4,4,128]{2,1,0:T(4,128)}, u32[]{:S(2)}) copy-start(f32[4,4,128]{2,1,0:T(4,128)} %sinogram.1) | copy-start | bytes 24580
  8.2 36.7 %copy-start.3 = (f32[3,4,4096]{2,1,0:T(4,128)S(1)}, f32[3,4,4096]{2,1,0:T(4,128)}, u32[]{:S(2)}) copy-start(f32[3,4,4096]{2,1,0:T(4,128)} %dual.1) | copy-start | bytes 589828
  24.3 10.4 %all-to-all-start.1 = ((bf16[16,16,128]{2,1,0:T(8,128)(2,1)}), bf16[16,16,128]{2,1,0:T(8,128)(2,1)S(1)}, u32[]{:S(2)}, u32[]{:S(2)}) async-start(bf16[16,16,128]{2,1,0:T(8,128)(2,1)} %residual.1), calls=%async_computation.1 | async-start | bytes 131072 | tf_op jit(solution)/shard_map/all_to_all | solution.py:291
  34.7 2.2 %copy-start.1 = (bf16[256,64,128]{2,1,0:T(8,128)(2,1)S(1)}, bf16[256,64,128]{2,1,0:T(8,128)(2,1)}, u32[]{:S(2)}) copy-start(bf16[256,64,128]{2,1,0:T(8,128)(2,1)} %proj_hbm.3) | copy-start | bytes 12582916
  40.3 4.6 %collective-permute-start = (f32[8,4096]{1,0:T(8,128)S(1)}, f32[8,4096]{1,0:T(8,128)S(1)}, u32[]{:S(2)}, u32[]{:S(2)}) collective-permute-start(f32[8,4096]{1,0:T(8,128)S(1)} %backward.1.grad), channel_id=1, source_target_pairs={{0,1},{1,0},{2,3},{3,2},{4,5},{5,4},{6,7},{7,6},{8,9},{9,8},{10,11... | collective-permute-start | bytes 393224 | tf_op jit(solution)/shard_map/ppermute | solution.py:314
  40.4 4.5 %collective-permute-start.1 = (f32[4,4096]{1,0:T(4,128)S(1)}, f32[4,4096]{1,0:T(4,128)S(1)}, u32[]{:S(2)}, u32[]{:S(2)}) collective-permute-start(f32[4,4096]{1,0:T(4,128)S(1)} %get-tuple-element.8.halo), channel_id=1, source_target_pairs={{0,2},{2,0},{1,3},{3,1},{4,6},{6,4},{5,7},{7,5},{8,10},{10,8},{9,1... | collective-permute-start | bytes 196616 | tf_op jit(solution)/shard_map/ppermute | solution.py:272

commit v2 on v1

--- a/solution.py
+++ b/solution.py
@@ -1,3 +1,5 @@
+import functools
+
 import jax
 import jax.numpy as jnp
 from jax import lax
@@ -10,7 +12,7 @@
 TAU = 0.5
 GROUP = 4
 CHUNKS = 8
-VMEM_LIMIT = 48 * 1024 * 1024
+VMEM_LIMIT = 16 * 1024 * 1024
 
 
 def iotas(shape):
@@ -35,17 +37,23 @@
 
 
 def forward_kernel(
-    count, ray, voxel, rho, vol_hbm, split_hbm, dual_hbm, proj_hbm,
+    count, rho, ray_hbm, voxel_hbm, vol_hbm, split_hbm, dual_hbm, sino_hbm, proj_hbm,
     partial_out, base_out, halo_out,
-    vol, split, dual, tiles, double, table, acc0, acc1, acc2, acc3, sems, tile_sems,
+    ray, voxel, vol, split, dual, sino, tiles, double, table, acc0, acc1, acc2, acc3,
+    sems, tile_sems,
 ):
     slots = proj_hbm.shape[0]
     rays = acc0.shape[0] - 1
+    owned = sino.shape[0]
     width = vol.shape[1]
     loads = [
-        pltpu.make_async_copy(vol_hbm, vol, sems.at[0]),
-        pltpu.make_async_copy(split_hbm, split, sems.at[1]),
-        pltpu.make_async_copy(dual_hbm, dual, sems.at[2]),
+        pltpu.make_async_copy(source, target, sems.at[i])
+        for i, (source, target) in enumerate(
+            [
+                (vol_hbm, vol), (voxel_hbm, voxel), (ray_hbm, ray), (sino_hbm, sino),
+                (split_hbm, split), (dual_hbm, dual),
+            ]
+        )
     ]
     for load in loads:
         load.start()
@@ -70,8 +78,11 @@
         table[2 * j] = jnp.where(other, turned, first)
         table[2 * j + 1] = jnp.where(other, x, second)
 
-    loads[1].wait()
-    loads[2].wait()
+    for load in loads[1:]:
+        load.wait()
+    mine = (lax.axis_index("tile") * lax.axis_size("rep") + lax.axis_index("rep")) * owned
+    for r in range(owned):
+        acc0[mine + r, 0:4, :] = -sino[r]
     factor = TAU * rho[0]
     row_mask, col_mask = plane_masks(lane)
     for j in range(width // 128):
@@ -125,44 +136,73 @@
         partial_out[16 * q:16 * q + 16, :] = jnp.concatenate(halves, axis=0).astype(jnp.bfloat16)
 
 
-def resid_kernel(parts, sinogram, out, total):
-    total[...] = jnp.sum(parts[...].astype(jnp.float32), axis=0)
-    for r in range(sinogram.shape[0]):
-        at = pl.ds(4 * r, 4)
-        total[at, :] = total[at, :] - sinogram[r]
-    resid = total[...].astype(jnp.bfloat16)
-    for copy in range(out.shape[0]):
-        out[copy] = resid
-
-
-def backward_kernel(
-    count, ray, voxel, here, resid, proj_hbm, out,
-    tiles, table, acc0, acc1, acc2, acc3, tile_sems,
-):
+def backward_kernel(parts_in, *refs):
+    count, rho, ray_hbm, voxel_hbm, proj_hbm = refs[:5]
+    parts = refs[5:5 + parts_in]
+    base, halo, from_next, from_previous = refs[5 + parts_in:9 + parts_in]
+    grad_out, first_out, base_out = refs[9 + parts_in:12 + parts_in]
+    (
+        ray, voxel, tiles, table, acc0, acc1, acc2, acc3, sems, tile_sems
+    ) = refs[12 + parts_in:]
     slots = proj_hbm.shape[0]
     rays = table.shape[0]
     voxel_tiles = acc0.shape[0] - 1
+    loads = [
+        pltpu.make_async_copy(source, target, sems.at[i])
+        for i, (source, target) in enumerate(
+            [(voxel_hbm, voxel), (ray_hbm, ray)]
+        )
+    ]
+    for load in loads:
+        load.start()
     copies = start_tiles(proj_hbm, tiles, tile_sems)
     accs = (acc0, acc1, acc2, acc3)
     for acc in accs:
         acc[...] = jnp.zeros_like(acc)
     row, lane = iotas((8, 128))
     low, top = lane < TV, row < 4
-    mine = here[0]
     for q in range(rays // 4):
-        own = resid[mine, 16 * q:16 * q + 16, :].astype(jnp.float32)
-        following = resid[1 - mine, 16 * q:16 * q + 16, :].astype(jnp.float32)
+        at = slice(16 * q, 16 * q + 16)
+        total = parts[0][at, :].astype(jnp.float32)
+        for part in parts[1:]:
+            total += part[at, :].astype(jnp.float32)
         for k in range(2):
-            a, b = own[8 * k:8 * k + 8], following[8 * k:8 * k + 8]
-            table[4 * q + 2 * k] = jnp.where(top, a, pltpu.roll(b, 4, axis=0))
-            table[4 * q + 2 * k + 1] = jnp.where(top, pltpu.roll(a, 4, axis=0), b)
+            x = total[8 * k:8 * k + 8]
+            turned = pltpu.roll(x, 4, axis=0)
+            table[4 * q + 2 * k] = jnp.where(top, x, turned)
+            table[4 * q + 2 * k + 1] = jnp.where(top, turned, x)
+
+    for load in loads:
+        load.wait()
+    slab, slabs = lax.axis_index("slab"), lax.axis_size("slab")
+    factor = TAU * rho[0]
+    limit = 1.0 / rho[0]
+    for j in range(voxel_tiles // 2):
+        at = slice(128 * j, 128 * j + 128)
+        above = factor * (from_next[1:2, at] - halo[0:1, at])
+        above = jnp.where(slab == slabs - 1, 0.0, above)
+        below = factor * (halo[1:2, at] - from_previous[0:1, at])
+        below = jnp.where(slab == 0, 0.0, below)
+        own = jnp.concatenate([base[:, at]] * 2, axis=0)
+        field = jnp.where(top, own, from_next[2:3, at])
+        field += jnp.where(
+            row == 0, -below, jnp.where(row == 3, above, jnp.where(row == 4, -above, 0.0))
+        )
+        base_out[:, at] = jnp.where(row < 5, field, limit)
+
     used = count[0]
     per = slots // CHUNKS
     for g in range(slots // GROUP):
         if GROUP * g % per == 0:
             copies[GROUP * g // per].wait()
         n = GROUP * g
-        rows = jnp.concatenate([table[ray[n + i]] for i in range(GROUP)], axis=0)
+        rows = jnp.concatenate(
+            [
+                jnp.where(top, table[ray[n + 2 * i]], table[ray[n + 2 * i + 1]])
+                for i in range(GROUP // 2)
+            ],
+            axis=0,
+        )
         back = lax.dot_general(
             rows.astype(jnp.bfloat16),
             tiles[n:n + GROUP].reshape(GROUP * TV, TR),
@@ -171,38 +211,33 @@
         )
         for i in range(GROUP):
             at = jnp.where(n + i < used, voxel[n + i], voxel_tiles)
-            half = 128 * (i // 2)
-            accs[i][at] += back[8 * i:8 * i + 8, half:half + 128]
+            k = i // 2
+            accs[i][at] += back[8 * k:8 * k + 8, 128 * k:128 * k + 128]
     for j in range(voxel_tiles // 2):
+        at = slice(128 * j, 128 * j + 128)
         even = [acc0[2 * j + k] + acc2[2 * j + k] for k in range(2)]
         odd = [acc1[2 * j + k] + acc3[2 * j + k] for k in range(2)]
-        out[:, 128 * j:128 * j + 128] = jnp.where(low, even[0], odd[1]) + pltpu.roll(
-            jnp.where(low, even[1], odd[0]), TV, axis=1
-        )
+        turned = pltpu.roll(jnp.where(top, even[1], odd[0]), TV, axis=1)
+        both = jnp.where(top == low, jnp.where(top, even[0], odd[1]), turned)
+        grad = (both + pltpu.roll(both, 4, axis=0))[0:4]
+        grad_out[:, at] = grad
+        first_out[:, at] = grad[0:1]
 
 
 def update_kernel(
-    rho, grad, grad_other, base, dual, halo, from_next, from_previous,
+    grad, grad_other, first_next, first_cross, base, dual,
     new_volume, new_split, new_dual,
 ):
-    slab, slabs = lax.axis_index("slab"), lax.axis_size("slab")
-    first, last = slab == 0, slab == slabs - 1
-    penalty = rho[0]
-    factor = TAU * penalty
-    limit = 1.0 / penalty
+    last = lax.axis_index("slab") == lax.axis_size("slab") - 1
     row, lane = iotas((8, 128))
     row_mask, col_mask = plane_masks(lane)
     inner = jnp.logical_or(row < 3, jnp.logical_not(last))
     for j in range(dual.shape[2] // 128):
         at = slice(128 * j, 128 * j + 128)
-        above = jnp.where(last, 0.0, factor * (from_next[1:2, at] - halo[0:1, at]))
-        below = jnp.where(first, 0.0, factor * (halo[1:2, at] - from_previous[0:1, at]))
-        own = jnp.concatenate([base[:, at]] * 2, axis=0)
-        field = jnp.where(row < 4, own, from_next[2:3, at])
-        field += jnp.where(
-            row == 0, -below, jnp.where(row == 3, above, jnp.where(row == 4, -above, 0.0))
-        )
-        field -= TAU * (grad[:, at] + grad_other[:, at])
+        slope = jnp.concatenate([grad[:, at] + grad_other[:, at]] * 2, axis=0)
+        slope = jnp.where(row < 4, slope, first_next[:, at] + first_cross[:, at])
+        limit = base[5:6, at]
+        field = base[:, at] - TAU * slope
         new_volume[:, at] = field[0:4]
         steps = (
             jnp.where(inner, pltpu.roll(field, 7, axis=0) - field, 0.0),
@@ -224,8 +259,8 @@
     return pl.BlockSpec(memory_space=pltpu.SMEM)
 
 
-def anywhere():
-    return pl.BlockSpec(memory_space=pl.ANY)
+def hbm():
+    return pl.BlockSpec(memory_space=pltpu.HBM)
 
 
 def params():
@@ -240,10 +275,17 @@
     slots = ray_index.shape[0]
     owned = sinogram.shape[0]
     group = lax.axis_size(("tile", "rep"))
+    reps = lax.axis_size("rep")
     slabs = lax.axis_size("slab")
     rays = owned * group
     voxel_tiles = width // TV
-    block = owned * slices
+    dual_here = dual_var
+    volume, split_var, dual_var, sinogram, proj_tiles, ray_index, voxel_index = (
+        pltpu.with_memory_space_constraint(x, pltpu.HBM)
+        for x in (
+            volume, split_var, dual_var, sinogram, proj_tiles, ray_index, voxel_index
+        )
+    )
 
     partial, base, halo = pl.pallas_call(
         forward_kernel,
@@ -252,66 +294,67 @@
             jax.ShapeDtypeStruct((slices, width), f32),
             jax.ShapeDtypeStruct((4, width), f32),
         ),
-        in_specs=[smem()] * 4 + [anywhere()] * 4,
+        in_specs=[smem()] * 2 + [hbm()] * 7,
         out_specs=(vmem(), vmem(), vmem()),
         scratch_shapes=[
+            pltpu.SMEM((slots,), jnp.int32),
+            pltpu.SMEM((slots,), jnp.int32),
             pltpu.VMEM((slices, width), f32),
             pltpu.VMEM((3, slices, width), f32),
             pltpu.VMEM((3, slices, width), f32),
+            pltpu.VMEM(sinogram.shape, f32),
             pltpu.VMEM(proj_tiles.shape, bf16),
             pltpu.VMEM((8, width), f32),
             pltpu.VMEM((voxel_tiles, 8, 128), f32),
         ]
         + [pltpu.VMEM((rays + 1, 8, 128), f32)] * 4
-        + [pltpu.SemaphoreType.DMA((3,)), pltpu.SemaphoreType.DMA((CHUNKS,))],
+        + [pltpu.SemaphoreType.DMA((6,)), pltpu.SemaphoreType.DMA((CHUNKS,))],
         compiler_params=params(),
         name="forward",
-    )(tile_count, ray_index, voxel_index, rho, volume, split_var, dual_var, proj_tiles)
-
+    )(
+        tile_count, rho, ray_index, voxel_index, volume, split_var, dual_var, sinogram, proj_tiles
+    )
+
+    down = [(i, i - 1) for i in range(1, slabs)]
     if slabs == 2:
         from_next = from_previous = lax.ppermute(halo, "slab", [(0, 1), (1, 0)])
     else:
-        from_next = lax.ppermute(halo, "slab", [(i, i - 1) for i in range(1, slabs)])
-        from_previous = lax.ppermute(halo, "slab", [(i, i + 1) for i in range(slabs - 1)])
-
-    parts = lax.all_to_all(
-        partial.reshape(group, block, TR), ("tile", "rep"), 0, 0, tiled=True
-    )
-    copies = group * (2 if slabs == 2 else 1)
-    resid = pl.pallas_call(
-        resid_kernel,
-        out_shape=jax.ShapeDtypeStruct((copies, block, TR), bf16),
-        in_specs=[vmem(), vmem()],
-        out_specs=vmem(),
-        scratch_shapes=[pltpu.VMEM((block, TR), f32)],
-        compiler_params=params(),
-        name="residual",
-    )(parts, sinogram)
-    if slabs == 2:
-        both = lax.all_to_all(resid, ("slab", "tile", "rep"), 0, 0, tiled=True)
-        both = both.reshape(2, rays * slices, TR)
-        here = lax.axis_index("slab").reshape(1)
-    else:
-        own = lax.all_to_all(resid, ("tile", "rep"), 0, 0, tiled=True)
-        following = lax.ppermute(own, "slab", [(i, i - 1) for i in range(1, slabs)])
-        both = jnp.stack([own, following]).reshape(2, rays * slices, TR)
-        here = jnp.zeros((1,), jnp.int32)
-
-    grad = pl.pallas_call(
-        backward_kernel,
-        out_shape=jax.ShapeDtypeStruct((8, width), f32),
-        in_specs=[smem()] * 4 + [vmem(), anywhere()],
-        out_specs=vmem(),
+        from_next = lax.ppermute(halo, "slab", down)
+        from_previous = lax.ppermute(halo, "slab", [(i - 1, i) for i in range(1, slabs)])
+    parts = [partial] + [
+        lax.ppermute(partial, ("tile", "rep"), [(i, i ^ k) for i in range(group)])
+        for k in reversed(range(1, group))
+    ]
+
+    grad, first, base = pl.pallas_call(
+        functools.partial(backward_kernel, len(parts)),
+        out_shape=(
+            jax.ShapeDtypeStruct((slices, width), f32),
+            jax.ShapeDtypeStruct((1, width), f32),
+            jax.ShapeDtypeStruct((8, width), f32),
+        ),
+        in_specs=[smem()] * 2 + [hbm()] * 3 + [vmem()] * (len(parts) + 4),
+        out_specs=(vmem(), vmem(), vmem()),
         scratch_shapes=[
+            pltpu.SMEM((slots,), jnp.int32),
+            pltpu.SMEM((slots,), jnp.int32),
             pltpu.VMEM(proj_tiles.shape, bf16),
             pltpu.VMEM((rays, 8, 128), f32),
         ]
         + [pltpu.VMEM((voxel_tiles + 1, 8, 128), f32)] * 4
-        + [pltpu.SemaphoreType.DMA((CHUNKS,))],
+        + [pltpu.SemaphoreType.DMA((2,)), pltpu.SemaphoreType.DMA((CHUNKS,))],
         compiler_params=params(),
         name="backward",
-    )(tile_count, ray_index, voxel_index, here.astype(jnp.int32), both, proj_tiles)
-    grad_other = lax.ppermute(grad, "rep", [(0, 1), (1, 0)])
+    )(
+        tile_count, rho, ray_index, voxel_index, proj_tiles,
+        *parts, base, halo, from_next, from_previous,
+    )
+    grad_other = lax.ppermute(grad, "rep", [(i, i ^ 1) for i in range(reps)])
+    first_next = lax.ppermute(first, "slab", down)
+    first_cross = lax.ppermute(
+        first, ("slab", "rep"),
+        [(i * reps + k, j * reps + 1 - k) for i, j in down for k in range(reps)],
+    )
 
     return pl.pallas_call(
         update_kernel,
@@ -320,11 +363,11 @@
             jax.ShapeDtypeStruct((3, slices, width), f32),
             jax.ShapeDtypeStruct((3, slices, width), f32),
         ),
-        in_specs=[smem()] + [vmem()] * 7,
+        in_specs=[vmem()] * 6,
         out_specs=(vmem(), vmem(), vmem()),
         compiler_params=params(),
         name="update",
-    )(rho, grad, grad_other, base, dual_var, halo, from_next, from_previous)
+    )(grad, grad_other, first_next, first_cross, base, dual_here)
 
 
 def solution(mesh):

time: 46.3 us -> 34 us (0.73)
  blocking collectives: 11.9 us -> 0 us
  starting transfers between devices: 4.15 us -> 14.3 us
  local copies, waits for them, and re-layouts: 8.44 us -> 0.01 us
  waiting for transfers between devices: 10.8 us -> 9.08 us
    ppermute x1 -> x10, starting transfers between devices: 0.07 us -> 12.7 us  [the longest x7 9.57 us: shards(): lax.ppermute(partial, ('tile', 'rep'), [(i, i ^ k) for i in range(group)])]
    all_to_all x1 -> x0, blocking collectives: 11.9 us -> none  [shards(): lax.all_to_all(partial.reshape(group, block, TR), ('tile', 'rep'), 0, 0,...]
    ppermute x1 -> x10, waiting for transfers between devices: 0.01 us -> 9.08 us  [the longest x7 4.74 us: shards(): lax.ppermute(partial, ('tile', 'rep'), [(i, i ^ k) for i in range(group)])]
    unnamed x22 -> x2, local copies, waits for them, and re-layouts: 8.44 us -> 0.01 us
    all_to_all x1 -> x0, waiting for transfers between devices: 6.85 us -> none  [shards(): both = lax.all_to_all(resid, ('slab', 'tile', 'rep'), 0, 0, tiled=True)]
    ppermute x1, waiting for transfers between devices: 3.93 us -> 0.01 us  [shards(): from_next = from_previous = lax.ppermute(halo, 'slab', [(0, 1), (1, 0)])]
    all_to_all x1 -> x0, starting transfers between devices: 3.5 us -> none  [shards(): both = lax.all_to_all(resid, ('slab', 'tile', 'rep'), 0, 0, tiled=True)]
    ppermute x1, starting transfers between devices: 0.57 us -> 1.64 us  [shards(): from_next = from_previous = lax.ppermute(halo, 'slab', [(0, 1), (1, 0)])]
  transfers between devices with their start and end apart: 3 -> 11, of which waited for: 2 -> 5; matrix products, arithmetic and copies ran while one was open for 0% -> 0% of each run, Pallas kernels for 0% -> 0%
where the time goes in v2:
time: 34 us; the launch traced here: 33.8 us
  starting transfers between devices  14.3 us (42%)
  waiting for transfers between devices  9.08 us (27%)
  Pallas kernels  8.37 us (25%)
  between operations  1.98 us (6%)
    ppermute x7, starting transfers between devices, shards(): lax.ppermute(partial, ('tile', 'rep'), [(i, i ^ k) for i in range(group)])  9.57 us
    ppermute x7, waiting for transfers between devices, shards(): lax.ppermute(partial, ('tile', 'rep'), [(i, i ^ k) for i in range(group)])  4.74 us
    pallas_call x1, Pallas kernels, shards(): pl.pallas_call(forward_kernel, out_shape=(jax.ShapeDtypeStruct((rays * sl...  4.15 us
    pallas_call x1, Pallas kernels, shards(): pl.pallas_call(functools.partial(backward_kernel, len(parts)), out_shape=...  3.33 us
    ppermute x1, waiting for transfers between devices, shards(): lax.ppermute(first, ('slab', 'rep'), [(i * reps + k, j * reps + 1 - k) fo...  2.46 us
    ppermute x1, waiting for transfers between devices, shards(): first_next = lax.ppermute(first, 'slab', down)  1.87 us
    ppermute x1, starting transfers between devices, shards(): from_next = from_previous = lax.ppermute(halo, 'slab', [(0, 1), (1, 0)])  1.64 us
    ppermute x1, starting transfers between devices, shards(): first_next = lax.ppermute(first, 'slab', down)  1.29 us
  transfers between devices with their start and end apart: 11, of which 5 were waited for; matrix products, arithmetic and copies ran while one was open for 0% of the time, Pallas kernels for 0%

profile of v2, /device:TPU:0, one launch (start us, length us, event | category | flops | bytes accessed | tf_op | source)
XLA Modules:
  0.0 33.8 jit_solution(18341492684894288175)
XLA Ops:
  1.9 4.1 %forward.1 = (bf16[128,128]{1,0:T(8,128)(2,1)S(1)}, f32[4,4096]{1,0:T(4,128)S(1)}, f32[4,4096]{1,0:T(4,128)S(1)}) custom-call(s32[1]{0:T(128)S(6)} %copy.12.count.refs_0_, f32[1]{0:T(128)S(6)} %copy.13.rho.refs_1_, s32[256]{0:T(256)} %refs_2_.1, s32[256]{0:T(256)} %refs_3_.1, f32[4,4096]{1,0:T(4,128)} %vol_hbm.1, f32[3,4,4096]{2,1,0:T(4,128)} %split_hbm.1, ...), custom_call_target="tpu_custom_call" | custom-call | tf_op jit(solution)/shard_map/forward/pallas_call | solution.py:290
  6.1 0.5 %collective-permute-start.6 = (bf16[128,128]{1,0:T(8,128)(2,1)S(1)}, bf16[128,128]{1,0:T(8,128)(2,1)S(1)}, u32[]{:S(2)}, u32[]{:S(2)}) collective-permute-start(bf16[128,128]{1,0:T(8,128)(2,1)S(1)} %get-tuple-element.9.refs_5_), channel_id=1, source_target_pairs={{0,1},{1,0},{4,5},{5,4},{8,9},{9,8},{12,13},{13,12},{2,3},{3,2},{6... | collective-permute-start | bytes 98312 | tf_op jit(solution)/shard_map/ppermute | solution.py:325
  6.6 2.6 %collective-permute-start.5 = (bf16[128,128]{1,0:T(8,128)(2,1)S(1)}, bf16[128,128]{1,0:T(8,128)(2,1)S(1)}, u32[]{:S(2)}, u32[]{:S(2)}) collective-permute-start(bf16[128,128]{1,0:T(8,128)(2,1)S(1)} %get-tuple-element.9.refs_5_), channel_id=1, source_target_pairs={{0,4},{1,5},{4,0},{5,1},{8,12},{9,13},{12,8},{13,9},{2,6},{3,7},{6... | collective-permute-start | bytes 98312 | tf_op jit(solution)/shard_map/ppermute | solution.py:325
  9.3 0.1 collective-permute-start.4
  9.3 1.6 %collective-permute-start.7 = (f32[4,4096]{1,0:T(4,128)S(1)}, f32[4,4096]{1,0:T(4,128)S(1)}, u32[]{:S(2)}, u32[]{:S(2)}) collective-permute-start(f32[4,4096]{1,0:T(4,128)S(1)} %get-tuple-element.11.refs_14_), channel_id=1, source_target_pairs={{0,2},{2,0},{1,3},{3,1},{4,6},{6,4},{5,7},{7,5},{8,10},{10,8},{9,1... | collective-permute-start | bytes 196616 | tf_op jit(solution)/shard_map/ppermute | solution.py:320
  11.0 2.6 %collective-permute-start.3 = (bf16[128,128]{1,0:T(8,128)(2,1)S(1)}, bf16[128,128]{1,0:T(8,128)(2,1)S(1)}, u32[]{:S(2)}, u32[]{:S(2)}) collective-permute-start(bf16[128,128]{1,0:T(8,128)(2,1)S(1)} %get-tuple-element.9.refs_5_), channel_id=1, source_target_pairs={{0,8},{1,9},{4,12},{5,13},{8,0},{9,1},{12,4},{13,5},{2,10},{3,11},... | collective-permute-start | bytes 98312 | tf_op jit(solution)/shard_map/ppermute | solution.py:325
  13.6 0.0 collective-permute-done.6.refs_12_
  13.6 0.0 collective-permute-start.2
  13.6 0.0 collective-permute-done.5.refs_11_
  13.6 3.3 %collective-permute-start.1 = (bf16[128,128]{1,0:T(8,128)(2,1)S(1)}, bf16[128,128]{1,0:T(8,128)(2,1)S(1)}, u32[]{:S(2)}, u32[]{:S(2)}) collective-permute-start(bf16[128,128]{1,0:T(8,128)(2,1)S(1)} %get-tuple-element.9.refs_5_), channel_id=1, source_target_pairs={{0,12},{1,13},{4,8},{5,9},{8,4},{9,5},{12,0},{13,1},{2,14},{3,15},... | collective-permute-start | bytes 98312 | tf_op jit(solution)/shard_map/ppermute | solution.py:325
  16.9 0.0 collective-permute-done.4.refs_10_
  16.9 0.4 %collective-permute-start = (bf16[128,128]{1,0:T(8,128)(2,1)S(1)}, bf16[128,128]{1,0:T(8,128)(2,1)S(1)}, u32[]{:S(2)}, u32[]{:S(2)}) collective-permute-start(bf16[128,128]{1,0:T(8,128)(2,1)S(1)} %get-tuple-element.9.refs_5_), channel_id=1, source_target_pairs={{0,13},{1,12},{4,9},{5,8},{8,5},{9,4},{12,1},{13,0},{2,15},{3,14},... | collective-permute-start | bytes 98312 | tf_op jit(solution)/shard_map/ppermute | solution.py:325
  17.3 0.8 %collective-permute-done.2.refs_8_ = bf16[128,128]{1,0:T(8,128)(2,1)S(1)} collective-permute-done((bf16[128,128]{1,0:T(8,128)(2,1)S(1)}, bf16[128,128]{1,0:T(8,128)(2,1)S(1)}, u32[]{:S(2)}, u32[]{:S(2)}) %collective-permute-start.2) | collective-permute-done | bytes 32800 | tf_op jit(solution)/shard_map/ppermute | solution.py:325
  18.1 1.8 %collective-permute-done.1.refs_7_ = bf16[128,128]{1,0:T(8,128)(2,1)S(1)} collective-permute-done((bf16[128,128]{1,0:T(8,128)(2,1)S(1)}, bf16[128,128]{1,0:T(8,128)(2,1)S(1)}, u32[]{:S(2)}, u32[]{:S(2)}) %collective-permute-start.1) | collective-permute-done | bytes 32800 | tf_op jit(solution)/shard_map/ppermute | solution.py:325
  19.9 2.1 %collective-permute-done.refs_6_ = bf16[128,128]{1,0:T(8,128)(2,1)S(1)} collective-permute-done((bf16[128,128]{1,0:T(8,128)(2,1)S(1)}, bf16[128,128]{1,0:T(8,128)(2,1)S(1)}, u32[]{:S(2)}, u32[]{:S(2)}) %collective-permute-start) | collective-permute-done | bytes 32800 | tf_op jit(solution)/shard_map/ppermute | solution.py:325
  22.1 0.0 collective-permute-done.7.refs_15_.refs_16_
  22.1 3.3 %backward.1 = (f32[4,4096]{1,0:T(4,128)S(1)}, f32[1,4096]{1,0:T(1,128)S(1)}, f32[8,4096]{1,0:T(8,128)S(1)}) custom-call(s32[1]{0:T(128)S(6)} %copy.12.count.refs_0_, f32[1]{0:T(128)S(6)} %copy.13.rho.refs_1_, s32[256]{0:T(256)} %refs_2_.1, s32[256]{0:T(256)} %refs_3_.1, bf16[256,64,128]{2,1,0:T(8,128)(2,1)} %refs_4_.1, ...), custom_call_target="tpu_custom_call" | custom-call | tf_op jit(solution)/shard_map/backward/pallas_call | solution.py:329
  25.4 0.5 %collective-permute-start.8 = (f32[4,4096]{1,0:T(4,128)S(1)}, f32[4,4096]{1,0:T(4,128)S(1)}, u32[]{:S(2)}, u32[]{:S(2)}) collective-permute-start(f32[4,4096]{1,0:T(4,128)S(1)} %get-tuple-element.12.grad), channel_id=1, source_target_pairs={{0,1},{1,0},{2,3},{3,2},{4,5},{5,4},{6,7},{7,6},{8,9},{9,8},{10,11... | collective-permute-start | bytes 196616 | tf_op jit(solution)/shard_map/ppermute | solution.py:352
  25.9 1.3 %collective-permute-start.10 = (f32[1,4096]{1,0:T(1,128)S(1)}, f32[1,4096]{1,0:T(1,128)S(1)}, u32[]{:S(2)}, u32[]{:S(2)}) collective-permute-start(f32[1,4096]{1,0:T(1,128)S(1)} %get-tuple-element.13), channel_id=1, source_target_pairs={{2,1},{3,0},{6,5},{7,4},{10,9},{11,8},{14,13},{15,12},{18,17},{19,... | collective-permute-start | bytes 49160 | tf_op jit(solution)/shard_map/ppermute | solution.py:354
  27.2 1.3 %collective-permute-start.9 = (f32[1,4096]{1,0:T(1,128)S(1)}, f32[1,4096]{1,0:T(1,128)S(1)}, u32[]{:S(2)}, u32[]{:S(2)}) collective-permute-start(f32[1,4096]{1,0:T(1,128)S(1)} %get-tuple-element.13), channel_id=1, source_target_pairs={{2,0},{3,1},{6,4},{7,5},{10,8},{11,9},{14,12},{15,13},{18,16},{19,... | collective-permute-start | bytes 49160 | tf_op jit(solution)/shard_map/ppermute | solution.py:353
  28.5 2.5 %collective-permute-done.10.first_cross = f32[1,4096]{1,0:T(1,128)S(1)} collective-permute-done((f32[1,4096]{1,0:T(1,128)S(1)}, f32[1,4096]{1,0:T(1,128)S(1)}, u32[]{:S(2)}, u32[]{:S(2)}) %collective-permute-start.10) | collective-permute-done | bytes 16416 | tf_op jit(solution)/shard_map/ppermute | solution.py:354
  31.0 1.9 %collective-permute-done.9.first_next = f32[1,4096]{1,0:T(1,128)S(1)} collective-permute-done((f32[1,4096]{1,0:T(1,128)S(1)}, f32[1,4096]{1,0:T(1,128)S(1)}, u32[]{:S(2)}, u32[]{:S(2)}) %collective-permute-start.9) | collective-permute-done | bytes 16416 | tf_op jit(solution)/shard_map/ppermute | solution.py:353
  32.9 0.0 collective-permute-done.8.grad_other
  32.9 0.9 %update.1 = (f32[4,4096]{1,0:T(4,128)}, f32[3,4,4096]{2,1,0:T(4,128)}, f32[3,4,4096]{2,1,0:T(4,128)}) custom-call(f32[4,4096]{1,0:T(4,128)S(1)} %get-tuple-element.12.grad, f32[4,4096]{1,0:T(4,128)S(1)} %collective-permute-done.8.grad_other, f32[1,4096]{1,0:T(1,128)S(1)} %collective-permute-done.9.first_next, ...), custom_call_target="tpu_custom_call" | custom-call | tf_op jit(solution)/shard_map/update/pallas_call | solution.py:359
  (3 shorter events, 0.0 us)
Async XLA Ops:
  1.9 30.9 %copy-start = (f32[3,4,4096]{2,1,0:T(4,128)S(1)}, f32[3,4,4096]{2,1,0:T(4,128)}, u32[]{:S(2)}) copy-start(f32[3,4,4096]{2,1,0:T(4,128)} %dual.1) | copy-start | bytes 589828
  6.1 7.5 %collective-permute-start.6 = (bf16[128,128]{1,0:T(8,128)(2,1)S(1)}, bf16[128,128]{1,0:T(8,128)(2,1)S(1)}, u32[]{:S(2)}, u32[]{:S(2)}) collective-permute-start(bf16[128,128]{1,0:T(8,128)(2,1)S(1)} %get-tuple-element.9.refs_5_), channel_id=1, source_target_pairs={{0,1},{1,0},{4,5},{5,4},{8,9},{9,8},{12,13},{13,12},{2,3},{3,2},{6... | collective-permute-start | bytes 98312 | tf_op jit(solution)/shard_map/ppermute | solution.py:325
  6.6 7.0 %collective-permute-start.5 = (bf16[128,128]{1,0:T(8,128)(2,1)S(1)}, bf16[128,128]{1,0:T(8,128)(2,1)S(1)}, u32[]{:S(2)}, u32[]{:S(2)}) collective-permute-start(bf16[128,128]{1,0:T(8,128)(2,1)S(1)} %get-tuple-element.9.refs_5_), channel_id=1, source_target_pairs={{0,4},{1,5},{4,0},{5,1},{8,12},{9,13},{12,8},{13,9},{2,6},{3,7},{6... | collective-permute-start | bytes 98312 | tf_op jit(solution)/shard_map/ppermute | solution.py:325
  9.3 7.7 %collective-permute-start.4 = (bf16[128,128]{1,0:T(8,128)(2,1)S(1)}, bf16[128,128]{1,0:T(8,128)(2,1)S(1)}, u32[]{:S(2)}, u32[]{:S(2)}) collective-permute-start(bf16[128,128]{1,0:T(8,128)(2,1)S(1)} %get-tuple-element.9.refs_5_), channel_id=1, source_target_pairs={{0,5},{1,4},{4,1},{5,0},{8,13},{9,12},{12,9},{13,8},{2,7},{3,6},{6... | collective-permute-start | bytes 98312 | tf_op jit(solution)/shard_map/ppermute | solution.py:325
  9.3 12.7 %collective-permute-start.7 = (f32[4,4096]{1,0:T(4,128)S(1)}, f32[4,4096]{1,0:T(4,128)S(1)}, u32[]{:S(2)}, u32[]{:S(2)}) collective-permute-start(f32[4,4096]{1,0:T(4,128)S(1)} %get-tuple-element.11.refs_14_), channel_id=1, source_target_pairs={{0,2},{2,0},{1,3},{3,1},{4,6},{6,4},{5,7},{7,5},{8,10},{10,8},{9,1... | collective-permute-start | bytes 196616 | tf_op jit(solution)/shard_map/ppermute | solution.py:320
  11.0 6.4 %collective-permute-start.3 = (bf16[128,128]{1,0:T(8,128)(2,1)S(1)}, bf16[128,128]{1,0:T(8,128)(2,1)S(1)}, u32[]{:S(2)}, u32[]{:S(2)}) collective-permute-start(bf16[128,128]{1,0:T(8,128)(2,1)S(1)} %get-tuple-element.9.refs_5_), channel_id=1, source_target_pairs={{0,8},{1,9},{4,12},{5,13},{8,0},{9,1},{12,4},{13,5},{2,10},{3,11},... | collective-permute-start | bytes 98312 | tf_op jit(solution)/shard_map/ppermute | solution.py:325
  13.6 4.6 %collective-permute-start.2 = (bf16[128,128]{1,0:T(8,128)(2,1)S(1)}, bf16[128,128]{1,0:T(8,128)(2,1)S(1)}, u32[]{:S(2)}, u32[]{:S(2)}) collective-permute-start(bf16[128,128]{1,0:T(8,128)(2,1)S(1)} %get-tuple-element.9.refs_5_), channel_id=1, source_target_pairs={{0,9},{1,8},{4,13},{5,12},{8,1},{9,0},{12,5},{13,4},{2,11},{3,10},... | collective-permute-start | bytes 98312 | tf_op jit(solution)/shard_map/ppermute | solution.py:325
  13.6 6.3 %collective-permute-start.1 = (bf16[128,128]{1,0:T(8,128)(2,1)S(1)}, bf16[128,128]{1,0:T(8,128)(2,1)S(1)}, u32[]{:S(2)}, u32[]{:S(2)}) collective-permute-start(bf16[128,128]{1,0:T(8,128)(2,1)S(1)} %get-tuple-element.9.refs_5_), channel_id=1, source_target_pairs={{0,12},{1,13},{4,8},{5,9},{8,4},{9,5},{12,0},{13,1},{2,14},{3,15},... | collective-permute-start | bytes 98312 | tf_op jit(solution)/shard_map/ppermute | solution.py:325
  16.9 5.1 %collective-permute-start = (bf16[128,128]{1,0:T(8,128)(2,1)S(1)}, bf16[128,128]{1,0:T(8,128)(2,1)S(1)}, u32[]{:S(2)}, u32[]{:S(2)}) collective-permute-start(bf16[128,128]{1,0:T(8,128)(2,1)S(1)} %get-tuple-element.9.refs_5_), channel_id=1, source_target_pairs={{0,13},{1,12},{4,9},{5,8},{8,5},{9,4},{12,1},{13,0},{2,15},{3,14},... | collective-permute-start | bytes 98312 | tf_op jit(solution)/shard_map/ppermute | solution.py:325
  25.4 7.5 %collective-permute-start.8 = (f32[4,4096]{1,0:T(4,128)S(1)}, f32[4,4096]{1,0:T(4,128)S(1)}, u32[]{:S(2)}, u32[]{:S(2)}) collective-permute-start(f32[4,4096]{1,0:T(4,128)S(1)} %get-tuple-element.12.grad), channel_id=1, source_target_pairs={{0,1},{1,0},{2,3},{3,2},{4,5},{5,4},{6,7},{7,6},{8,9},{9,8},{10,11... | collective-permute-start | bytes 196616 | tf_op jit(solution)/shard_map/ppermute | solution.py:352
  25.9 5.0 %collective-permute-start.10 = (f32[1,4096]{1,0:T(1,128)S(1)}, f32[1,4096]{1,0:T(1,128)S(1)}, u32[]{:S(2)}, u32[]{:S(2)}) collective-permute-start(f32[1,4096]{1,0:T(1,128)S(1)} %get-tuple-element.13), channel_id=1, source_target_pairs={{2,1},{3,0},{6,5},{7,4},{10,9},{11,8},{14,13},{15,12},{18,17},{19,... | collective-permute-start | bytes 49160 | tf_op jit(solution)/shard_map/ppermute | solution.py:354
  27.2 5.6 %collective-permute-start.9 = (f32[1,4096]{1,0:T(1,128)S(1)}, f32[1,4096]{1,0:T(1,128)S(1)}, u32[]{:S(2)}, u32[]{:S(2)}) collective-permute-start(f32[1,4096]{1,0:T(1,128)S(1)} %get-tuple-element.13), channel_id=1, source_target_pairs={{2,0},{3,1},{6,4},{7,5},{10,8},{11,9},{14,12},{15,13},{18,16},{19,... | collective-permute-start | bytes 49160 | tf_op jit(solution)/shard_map/ppermute | solution.py:353

commit v3 on v2

--- a/solution.py
+++ b/solution.py
@@ -37,8 +37,8 @@
 
 
 def forward_kernel(
-    count, rho, ray_hbm, voxel_hbm, vol_hbm, split_hbm, dual_hbm, sino_hbm, proj_hbm,
-    partial_out, base_out, halo_out,
+    count, ray_hbm, voxel_hbm, vol_hbm, split_hbm, dual_hbm, sino_hbm, proj_hbm,
+    partial_out, adjoint_out, halo_out,
     ray, voxel, vol, split, dual, sino, tiles, double, table, acc0, acc1, acc2, acc3,
     sems, tile_sems,
 ):
@@ -83,7 +83,6 @@
     mine = (lax.axis_index("tile") * lax.axis_size("rep") + lax.axis_index("rep")) * owned
     for r in range(owned):
         acc0[mine + r, 0:4, :] = -sino[r]
-    factor = TAU * rho[0]
     row_mask, col_mask = plane_masks(lane)
     for j in range(width // 128):
         at = slice(128 * j, 128 * j + 128)
@@ -97,12 +96,11 @@
         adjoint = pltpu.roll(depth, 1, axis=0) - depth
         adjoint += jnp.where((lane % TV) >= 8, pltpu.roll(across, 8, axis=1), 0.0) - across
         adjoint += jnp.where(lane % 8 >= 1, pltpu.roll(along, 1, axis=1), 0.0) - along
-        base = x - factor * adjoint
-        base_out[:, at] = base[0:4]
+        adjoint_out[:, at] = adjoint[0:4]
         halo_out[0:1, at] = (x - gap[0])[3:4]
         halo_out[1:2, at] = x[0:1]
-        halo_out[2:3, at] = base[0:1]
-        halo_out[3:4, at] = base[0:1]
+        halo_out[2:3, at] = adjoint[0:1]
+        halo_out[3:4, at] = adjoint[0:1]
 
     used = count[0]
     per = slots // CHUNKS
@@ -139,11 +137,11 @@
 def backward_kernel(parts_in, *refs):
     count, rho, ray_hbm, voxel_hbm, proj_hbm = refs[:5]
     parts = refs[5:5 + parts_in]
-    base, halo, from_next, from_previous = refs[5 + parts_in:9 + parts_in]
-    grad_out, first_out, base_out = refs[9 + parts_in:12 + parts_in]
+    vol, adjoint, halo, from_next, from_previous = refs[5 + parts_in:10 + parts_in]
+    grad_out, first_out, base_out = refs[10 + parts_in:13 + parts_in]
     (
         ray, voxel, tiles, table, acc0, acc1, acc2, acc3, sems, tile_sems
-    ) = refs[12 + parts_in:]
+    ) = refs[13 + parts_in:]
     slots = proj_hbm.shape[0]
     rays = table.shape[0]
     voxel_tiles = acc0.shape[0] - 1
@@ -179,15 +177,14 @@
     limit = 1.0 / rho[0]
     for j in range(voxel_tiles // 2):
         at = slice(128 * j, 128 * j + 128)
-        above = factor * (from_next[1:2, at] - halo[0:1, at])
-        above = jnp.where(slab == slabs - 1, 0.0, above)
-        below = factor * (halo[1:2, at] - from_previous[0:1, at])
-        below = jnp.where(slab == 0, 0.0, below)
-        own = jnp.concatenate([base[:, at]] * 2, axis=0)
-        field = jnp.where(top, own, from_next[2:3, at])
-        field += jnp.where(
-            row == 0, -below, jnp.where(row == 3, above, jnp.where(row == 4, -above, 0.0))
-        )
+        above = jnp.where(slab == slabs - 1, 0.0, from_next[1:2, at] - halo[0:1, at])
+        below = jnp.where(slab == 0, 0.0, halo[1:2, at] - from_previous[0:1, at])
+        turn = jnp.where(top, jnp.concatenate([adjoint[:, at]] * 2, axis=0), from_next[2:3, at])
+        turn += jnp.where(
+            row == 0, below, jnp.where(row == 3, -above, jnp.where(row == 4, above, 0.0))
+        )
+        field = jnp.where(top, jnp.concatenate([vol[:, at]] * 2, axis=0), from_next[1:2, at])
+        field -= factor * turn
         base_out[:, at] = jnp.where(row < 5, field, limit)
 
     used = count[0]
@@ -279,7 +276,7 @@
     slabs = lax.axis_size("slab")
     rays = owned * group
     voxel_tiles = width // TV
-    dual_here = dual_var
+    volume_here, dual_here = volume, dual_var
     volume, split_var, dual_var, sinogram, proj_tiles, ray_index, voxel_index = (
         pltpu.with_memory_space_constraint(x, pltpu.HBM)
         for x in (
@@ -287,14 +284,14 @@
         )
     )
 
-    partial, base, halo = pl.pallas_call(
+    partial, adjoint, halo = pl.pallas_call(
         forward_kernel,
         out_shape=(
             jax.ShapeDtypeStruct((rays * slices, TR), bf16),
             jax.ShapeDtypeStruct((slices, width), f32),
             jax.ShapeDtypeStruct((4, width), f32),
         ),
-        in_specs=[smem()] * 2 + [hbm()] * 7,
+        in_specs=[smem()] + [hbm()] * 7,
         out_specs=(vmem(), vmem(), vmem()),
         scratch_shapes=[
             pltpu.SMEM((slots,), jnp.int32),
@@ -312,7 +309,7 @@
         compiler_params=params(),
         name="forward",
     )(
-        tile_count, rho, ray_index, voxel_index, volume, split_var, dual_var, sinogram, proj_tiles
+        tile_count, ray_index, voxel_index, volume, split_var, dual_var, sinogram, proj_tiles
     )
 
     down = [(i, i - 1) for i in range(1, slabs)]
@@ -321,10 +318,14 @@
     else:
         from_next = lax.ppermute(halo, "slab", down)
         from_previous = lax.ppermute(halo, "slab", [(i - 1, i) for i in range(1, slabs)])
-    parts = [partial] + [
-        lax.ppermute(partial, ("tile", "rep"), [(i, i ^ k) for i in range(group)])
-        for k in reversed(range(1, group))
-    ]
+    step = 1
+    while True:
+        moved = lax.ppermute(partial, ("tile", "rep"), [(i, i ^ step) for i in range(group)])
+        step *= 2
+        if step == group:
+            break
+        partial = (partial.astype(f32) + moved.astype(f32)).astype(bf16)
+    parts = [partial, moved]
 
     grad, first, base = pl.pallas_call(
         functools.partial(backward_kernel, len(parts)),
@@ -333,7 +334,7 @@
             jax.ShapeDtypeStruct((1, width), f32),
             jax.ShapeDtypeStruct((8, width), f32),
         ),
-        in_specs=[smem()] * 2 + [hbm()] * 3 + [vmem()] * (len(parts) + 4),
+        in_specs=[smem()] * 2 + [hbm()] * 3 + [vmem()] * (len(parts) + 5),
         out_specs=(vmem(), vmem(), vmem()),
         scratch_shapes=[
             pltpu.SMEM((slots,), jnp.int32),
@@ -347,14 +348,11 @@
         name="backward",
     )(
         tile_count, rho, ray_index, voxel_index, proj_tiles,
-        *parts, base, halo, from_next, from_previous,
+        *parts, volume_here, adjoint, halo, from_next, from_previous,
     )
     grad_other = lax.ppermute(grad, "rep", [(i, i ^ 1) for i in range(reps)])
     first_next = lax.ppermute(first, "slab", down)
-    first_cross = lax.ppermute(
-        first, ("slab", "rep"),
-        [(i * reps + k, j * reps + 1 - k) for i, j in down for k in range(reps)],
-    )
+    first_cross = lax.ppermute(first_next, "rep", [(i, i ^ 1) for i in range(reps)])
 
     return pl.pallas_call(
         update_kernel,

time: 34 us -> 28.1 us (0.83)
  starting transfers between devices: 14.3 us -> 9.46 us
  waiting for transfers between devices: 9.08 us -> 8.01 us
    ppermute x8 -> x4, starting transfers between devices: 10.9 us -> 6.6 us  [the longest x3 6.6 us: shards(): lax.ppermute(partial, ('tile', 'rep'), [(i, i ^ step) for i in range(grou...]
    ppermute x8 -> x4, waiting for transfers between devices: 7.2 us -> 3.68 us  [the longest x3 2.5 us: shards(): lax.ppermute(partial, ('tile', 'rep'), [(i, i ^ step) for i in range(grou...]
    ppermute x1, waiting for transfers between devices: 1.87 us -> 4.33 us  [shards(): first_next = lax.ppermute(first, 'slab', down)]
    ppermute x1, starting transfers between devices: 0.54 us -> 0.07 us  [shards(): grad_other = lax.ppermute(grad, 'rep', [(i, i ^ 1) for i in range(reps)])]
  transfers between devices with their start and end apart: 11 -> 7, of which waited for: 5 -> 5; matrix products, arithmetic and copies ran while one was open for 0% -> 0% of each run, Pallas kernels for 0% -> 0%
where the time goes in v3:
time: 28.1 us; the launch traced here: 27.9 us
  starting transfers between devices  9.46 us (34%)
  Pallas kernels  8.4 us (30%)
  waiting for transfers between devices  8.01 us (29%)
  between operations  2.03 us (7%)
    ppermute x3, starting transfers between devices, shards(): lax.ppermute(partial, ('tile', 'rep'), [(i, i ^ step) for i in range(grou...  6.6 us
    ppermute x1, waiting for transfers between devices, shards(): first_next = lax.ppermute(first, 'slab', down)  4.33 us
    pallas_call x1, Pallas kernels, shards(): pl.pallas_call(forward_kernel, out_shape=(jax.ShapeDtypeStruct((rays * sl...  4.16 us
    pallas_call x1, Pallas kernels, shards(): pl.pallas_call(functools.partial(backward_kernel, len(parts)), out_shape=...  3.34 us
    ppermute x3, waiting for transfers between devices, shards(): lax.ppermute(partial, ('tile', 'rep'), [(i, i ^ step) for i in range(grou...  2.5 us
    ppermute x1, starting transfers between devices, shards(): from_next = from_previous = lax.ppermute(halo, 'slab', [(0, 1), (1, 0)])  1.49 us
    ppermute x1, starting transfers between devices, shards(): first_next = lax.ppermute(first, 'slab', down)  1.29 us
    ppermute x1, waiting for transfers between devices, shards(): lax.ppermute(first_next, 'rep', [(i, i ^ 1) for i in range(reps)])  1.18 us
  transfers between devices with their start and end apart: 7, of which 5 were waited for; matrix products, arithmetic and copies ran while one was open for 0% of the time, Pallas kernels for 0%

profile of v3, /device:TPU:0, one launch (start us, length us, event | category | flops | bytes accessed | tf_op | source)
XLA Modules:
  0.0 27.9 jit_solution(12069442746601071069)
XLA Ops:
  0.6 0.0 copy-start.1
  1.3 0.0 copy-start
  1.3 4.2 %forward.1 = (bf16[128,128]{1,0:T(8,128)(2,1)S(1)}, f32[4,4096]{1,0:T(4,128)S(1)}, f32[4,4096]{1,0:T(4,128)S(1)}) custom-call(s32[1]{0:T(128)S(6)} %copy.12.count.refs_0_, s32[256]{0:T(256)} %refs_2_.1, s32[256]{0:T(256)} %refs_3_.1, f32[4,4096]{1,0:T(4,128)} %refs_7_.1, f32[3,4,4096]{2,1,0:T(4,128)} %split_hbm.1, f32[3,4,4096]{2,1,0:T(4,128)} %dual.1, ...), custom_call_target="tpu_custom_call" | custom-call | tf_op jit(solution)/shard_map/forward/pallas_call | solution.py:287
  5.5 0.5 %collective-permute-start = (bf16[128,128]{1,0:T(8,128)(2,1)S(1)}, bf16[128,128]{1,0:T(8,128)(2,1)S(1)}, u32[]{:S(2)}, u32[]{:S(2)}) collective-permute-start(bf16[128,128]{1,0:T(8,128)(2,1)S(1)} %get-tuple-element.9), channel_id=1, source_target_pairs={{0,1},{1,0},{4,5},{5,4},{8,9},{9,8},{12,13},{13,12},{2,3},{3,2},{6... | collective-permute-start | bytes 98312 | tf_op jit(solution)/shard_map/ppermute | solution.py:323
  6.0 0.9 %collective-permute-done = bf16[128,128]{1,0:T(8,128)(2,1)S(1)} collective-permute-done((bf16[128,128]{1,0:T(8,128)(2,1)S(1)}, bf16[128,128]{1,0:T(8,128)(2,1)S(1)}, u32[]{:S(2)}, u32[]{:S(2)}) %collective-permute-start) | collective-permute-done | bytes 32800 | tf_op jit(solution)/shard_map/ppermute | solution.py:323
  6.9 3.0 %collective-permute-start.1 = (bf16[128,128]{1,0:T(8,128)(2,1)S(1)}, bf16[128,128]{1,0:T(8,128)(2,1)S(1)}, u32[]{:S(2)}, u32[]{:S(2)}) collective-permute-start(bf16[128,128]{1,0:T(8,128)(2,1)S(1)} %add_convert_fusion.1), channel_id=1, source_target_pairs={{0,4},{1,5},{4,0},{5,1},{8,12},{9,13},{12,8},{13,9},{2,6},{3,7},{6... | collective-permute-start | bytes 98312 | tf_op jit(solution)/shard_map/ppermute | solution.py:323
  9.9 1.5 %collective-permute-start.3 = (f32[4,4096]{1,0:T(4,128)S(1)}, f32[4,4096]{1,0:T(4,128)S(1)}, u32[]{:S(2)}, u32[]{:S(2)}) collective-permute-start(f32[4,4096]{1,0:T(4,128)S(1)} %get-tuple-element.11.refs_9_), channel_id=1, source_target_pairs={{0,2},{2,0},{1,3},{3,1},{4,6},{6,4},{5,7},{7,5},{8,10},{10,8},{9,1... | collective-permute-start | bytes 196616 | tf_op jit(solution)/shard_map/ppermute | solution.py:317
  11.4 0.4 %collective-permute-done.1 = bf16[128,128]{1,0:T(8,128)(2,1)S(1)} collective-permute-done((bf16[128,128]{1,0:T(8,128)(2,1)S(1)}, bf16[128,128]{1,0:T(8,128)(2,1)S(1)}, u32[]{:S(2)}, u32[]{:S(2)}) %collective-permute-start.1) | collective-permute-done | bytes 32800 | tf_op jit(solution)/shard_map/ppermute | solution.py:323
  11.8 3.1 %collective-permute-start.2 = (bf16[128,128]{1,0:T(8,128)(2,1)S(1)}, bf16[128,128]{1,0:T(8,128)(2,1)S(1)}, u32[]{:S(2)}, u32[]{:S(2)}) collective-permute-start(bf16[128,128]{1,0:T(8,128)(2,1)S(1)} %add_convert_fusion.refs_5_), channel_id=1, source_target_pairs={{0,8},{1,9},{4,12},{5,13},{8,0},{9,1},{12,4},{13,5},{2,10},{3,11},... | collective-permute-start | bytes 98312 | tf_op jit(solution)/shard_map/ppermute | solution.py:323
  15.5 0.0 collective-permute-done.3.refs_10_.refs_11_
  15.5 1.2 %collective-permute-done.2.refs_6_ = bf16[128,128]{1,0:T(8,128)(2,1)S(1)} collective-permute-done((bf16[128,128]{1,0:T(8,128)(2,1)S(1)}, bf16[128,128]{1,0:T(8,128)(2,1)S(1)}, u32[]{:S(2)}, u32[]{:S(2)}) %collective-permute-start.2) | collective-permute-done | bytes 32800 | tf_op jit(solution)/shard_map/ppermute | solution.py:323
  16.8 0.0 copy-done.1
  16.8 3.3 %backward.1 = (f32[4,4096]{1,0:T(4,128)S(1)}, f32[1,4096]{1,0:T(1,128)S(1)}, f32[8,4096]{1,0:T(8,128)S(1)}) custom-call(s32[1]{0:T(128)S(6)} %copy.12.count.refs_0_, f32[1]{0:T(128)S(6)} %copy.13.refs_1_, s32[256]{0:T(256)} %refs_2_.1, s32[256]{0:T(256)} %refs_3_.1, bf16[256,64,128]{2,1,0:T(8,128)(2,1)} %refs_4_.1, ...), custom_call_target="tpu_custom_call" | custom-call | tf_op jit(solution)/shard_map/backward/pallas_call | solution.py:330
  20.1 0.1 collective-permute-start.4
  20.2 1.3 %collective-permute-start.5 = (f32[1,4096]{1,0:T(1,128)S(1)}, f32[1,4096]{1,0:T(1,128)S(1)}, u32[]{:S(2)}, u32[]{:S(2)}) collective-permute-start(f32[1,4096]{1,0:T(1,128)S(1)} %get-tuple-element.13), channel_id=1, source_target_pairs={{2,0},{3,1},{6,4},{7,5},{10,8},{11,9},{14,12},{15,13},{18,16},{19,... | collective-permute-start | bytes 49160 | tf_op jit(solution)/shard_map/ppermute | solution.py:354
  21.5 4.3 %collective-permute-done.5.first_next = f32[1,4096]{1,0:T(1,128)S(1)} collective-permute-done((f32[1,4096]{1,0:T(1,128)S(1)}, f32[1,4096]{1,0:T(1,128)S(1)}, u32[]{:S(2)}, u32[]{:S(2)}) %collective-permute-start.5) | collective-permute-done | bytes 16416 | tf_op jit(solution)/shard_map/ppermute | solution.py:354
  25.8 0.0 collective-permute-start.6
  25.8 1.2 %collective-permute-done.6.first_cross = f32[1,4096]{1,0:T(1,128)S(1)} collective-permute-done((f32[1,4096]{1,0:T(1,128)S(1)}, f32[1,4096]{1,0:T(1,128)S(1)}, u32[]{:S(2)}, u32[]{:S(2)}) %collective-permute-start.6) | collective-permute-done | bytes 16416 | tf_op jit(solution)/shard_map/ppermute | solution.py:355
  27.0 0.0 collective-permute-done.4.grad_other
  27.0 0.0 copy-done
  27.0 0.9 %update.1 = (f32[4,4096]{1,0:T(4,128)}, f32[3,4,4096]{2,1,0:T(4,128)}, f32[3,4,4096]{2,1,0:T(4,128)}) custom-call(f32[4,4096]{1,0:T(4,128)S(1)} %get-tuple-element.12.grad, f32[4,4096]{1,0:T(4,128)S(1)} %collective-permute-done.4.grad_other, f32[1,4096]{1,0:T(1,128)S(1)} %collective-permute-done.5.first_next, ...), custom_call_target="tpu_custom_call" | custom-call | tf_op jit(solution)/shard_map/update/pallas_call | solution.py:357
  (2 shorter events, 0.0 us)
Async XLA Ops:
  0.6 16.2 %copy-start.1 = (f32[4,4096]{1,0:T(4,128)S(1)}, f32[4,4096]{1,0:T(4,128)}, u32[]{:S(2)}) copy-start(f32[4,4096]{1,0:T(4,128)} %refs_7_.1) | copy-start | bytes 196612
  1.3 25.7 %copy-start = (f32[3,4,4096]{2,1,0:T(4,128)S(1)}, f32[3,4,4096]{2,1,0:T(4,128)}, u32[]{:S(2)}) copy-start(f32[3,4,4096]{2,1,0:T(4,128)} %dual.1) | copy-start | bytes 589828
  5.5 1.4 %collective-permute-start = (bf16[128,128]{1,0:T(8,128)(2,1)S(1)}, bf16[128,128]{1,0:T(8,128)(2,1)S(1)}, u32[]{:S(2)}, u32[]{:S(2)}) collective-permute-start(bf16[128,128]{1,0:T(8,128)(2,1)S(1)} %get-tuple-element.9), channel_id=1, source_target_pairs={{0,1},{1,0},{4,5},{5,4},{8,9},{9,8},{12,13},{13,12},{2,3},{3,2},{6... | collective-permute-start | bytes 98312 | tf_op jit(solution)/shard_map/ppermute | solution.py:323
  6.9 4.9 %collective-permute-start.1 = (bf16[128,128]{1,0:T(8,128)(2,1)S(1)}, bf16[128,128]{1,0:T(8,128)(2,1)S(1)}, u32[]{:S(2)}, u32[]{:S(2)}) collective-permute-start(bf16[128,128]{1,0:T(8,128)(2,1)S(1)} %add_convert_fusion.1), channel_id=1, source_target_pairs={{0,4},{1,5},{4,0},{5,1},{8,12},{9,13},{12,8},{13,9},{2,6},{3,7},{6... | collective-permute-start | bytes 98312 | tf_op jit(solution)/shard_map/ppermute | solution.py:323
  9.9 5.7 %collective-permute-start.3 = (f32[4,4096]{1,0:T(4,128)S(1)}, f32[4,4096]{1,0:T(4,128)S(1)}, u32[]{:S(2)}, u32[]{:S(2)}) collective-permute-start(f32[4,4096]{1,0:T(4,128)S(1)} %get-tuple-element.11.refs_9_), channel_id=1, source_target_pairs={{0,2},{2,0},{1,3},{3,1},{4,6},{6,4},{5,7},{7,5},{8,10},{10,8},{9,1... | collective-permute-start | bytes 196616 | tf_op jit(solution)/shard_map/ppermute | solution.py:317
  11.8 5.0 %collective-permute-start.2 = (bf16[128,128]{1,0:T(8,128)(2,1)S(1)}, bf16[128,128]{1,0:T(8,128)(2,1)S(1)}, u32[]{:S(2)}, u32[]{:S(2)}) collective-permute-start(bf16[128,128]{1,0:T(8,128)(2,1)S(1)} %add_convert_fusion.refs_5_), channel_id=1, source_target_pairs={{0,8},{1,9},{4,12},{5,13},{8,0},{9,1},{12,4},{13,5},{2,10},{3,11},... | collective-permute-start | bytes 98312 | tf_op jit(solution)/shard_map/ppermute | solution.py:323
  20.1 6.9 %collective-permute-start.4 = (f32[4,4096]{1,0:T(4,128)S(1)}, f32[4,4096]{1,0:T(4,128)S(1)}, u32[]{:S(2)}, u32[]{:S(2)}) collective-permute-start(f32[4,4096]{1,0:T(4,128)S(1)} %get-tuple-element.12.grad), channel_id=1, source_target_pairs={{0,1},{1,0},{2,3},{3,2},{4,5},{5,4},{6,7},{7,6},{8,9},{9,8},{10,11... | collective-permute-start | bytes 196616 | tf_op jit(solution)/shard_map/ppermute | solution.py:353
  20.2 5.6 %collective-permute-start.5 = (f32[1,4096]{1,0:T(1,128)S(1)}, f32[1,4096]{1,0:T(1,128)S(1)}, u32[]{:S(2)}, u32[]{:S(2)}) collective-permute-start(f32[1,4096]{1,0:T(1,128)S(1)} %get-tuple-element.13), channel_id=1, source_target_pairs={{2,0},{3,1},{6,4},{7,5},{10,8},{11,9},{14,12},{15,13},{18,16},{19,... | collective-permute-start | bytes 49160 | tf_op jit(solution)/shard_map/ppermute | solution.py:354
  25.8 1.2 %collective-permute-start.6 = (f32[1,4096]{1,0:T(1,128)S(1)}, f32[1,4096]{1,0:T(1,128)S(1)}, u32[]{:S(2)}, u32[]{:S(2)}) collective-permute-start(f32[1,4096]{1,0:T(1,128)S(1)} %collective-permute-done.5.first_next), channel_id=1, source_target_pairs={{0,1},{1,0},{2,3},{3,2},{4,5},{5,4},{6,7},{7,6},{8,9},{9,8},{10,11... | collective-permute-start | bytes 49160 | tf_op jit(solution)/shard_map/ppermute | solution.py:355

commit v4 on v3

--- a/solution.py
+++ b/solution.py
@@ -1,5 +1,3 @@
-import functools
-
 import jax
 import jax.numpy as jnp
 from jax import lax
@@ -38,7 +36,7 @@
 
 def forward_kernel(
     count, ray_hbm, voxel_hbm, vol_hbm, split_hbm, dual_hbm, sino_hbm, proj_hbm,
-    partial_out, adjoint_out, halo_out,
+    partial_out, adjoint_out, edge_out, first_out,
     ray, voxel, vol, split, dual, sino, tiles, double, table, acc0, acc1, acc2, acc3,
     sems, tile_sems,
 ):
@@ -97,10 +95,8 @@
         adjoint += jnp.where((lane % TV) >= 8, pltpu.roll(across, 8, axis=1), 0.0) - across
         adjoint += jnp.where(lane % 8 >= 1, pltpu.roll(along, 1, axis=1), 0.0) - along
         adjoint_out[:, at] = adjoint[0:4]
-        halo_out[0:1, at] = (x - gap[0])[3:4]
-        halo_out[1:2, at] = x[0:1]
-        halo_out[2:3, at] = adjoint[0:1]
-        halo_out[3:4, at] = adjoint[0:1]
+        edge_out[:, at] = (x - gap[0])[3:4]
+        first_out[:, at] = x[0:1]
 
     used = count[0]
     per = slots // CHUNKS
@@ -134,14 +130,12 @@
         partial_out[16 * q:16 * q + 16, :] = jnp.concatenate(halves, axis=0).astype(jnp.bfloat16)
 
 
-def backward_kernel(parts_in, *refs):
-    count, rho, ray_hbm, voxel_hbm, proj_hbm = refs[:5]
-    parts = refs[5:5 + parts_in]
-    vol, adjoint, halo, from_next, from_previous = refs[5 + parts_in:10 + parts_in]
-    grad_out, first_out, base_out = refs[10 + parts_in:13 + parts_in]
-    (
-        ray, voxel, tiles, table, acc0, acc1, acc2, acc3, sems, tile_sems
-    ) = refs[13 + parts_in:]
+def backward_kernel(
+    count, rho, ray_hbm, voxel_hbm, proj_hbm,
+    total, shared, vol, adjoint, edge, from_next, from_previous,
+    grad_out, base_out, limit_out,
+    ray, voxel, tiles, table, acc0, acc1, acc2, acc3, sems, tile_sems,
+):
     slots = proj_hbm.shape[0]
     rays = table.shape[0]
     voxel_tiles = acc0.shape[0] - 1
@@ -159,13 +153,12 @@
         acc[...] = jnp.zeros_like(acc)
     row, lane = iotas((8, 128))
     low, top = lane < TV, row < 4
+    holder = lax.axis_index("rep") == lax.axis_size("rep") - 1
     for q in range(rays // 4):
         at = slice(16 * q, 16 * q + 16)
-        total = parts[0][at, :].astype(jnp.float32)
-        for part in parts[1:]:
-            total += part[at, :].astype(jnp.float32)
+        both = jnp.where(holder, total[at, :].astype(jnp.float32), shared[at, :].astype(jnp.float32))
         for k in range(2):
-            x = total[8 * k:8 * k + 8]
+            x = both[8 * k:8 * k + 8]
             turned = pltpu.roll(x, 4, axis=0)
             table[4 * q + 2 * k] = jnp.where(top, x, turned)
             table[4 * q + 2 * k + 1] = jnp.where(top, turned, x)
@@ -175,17 +168,15 @@
     slab, slabs = lax.axis_index("slab"), lax.axis_size("slab")
     factor = TAU * rho[0]
     limit = 1.0 / rho[0]
+    short = lax.broadcasted_iota(jnp.int32, (4, 128), 0)
     for j in range(voxel_tiles // 2):
         at = slice(128 * j, 128 * j + 128)
-        above = jnp.where(slab == slabs - 1, 0.0, from_next[1:2, at] - halo[0:1, at])
-        below = jnp.where(slab == 0, 0.0, halo[1:2, at] - from_previous[0:1, at])
-        turn = jnp.where(top, jnp.concatenate([adjoint[:, at]] * 2, axis=0), from_next[2:3, at])
-        turn += jnp.where(
-            row == 0, below, jnp.where(row == 3, -above, jnp.where(row == 4, above, 0.0))
-        )
-        field = jnp.where(top, jnp.concatenate([vol[:, at]] * 2, axis=0), from_next[1:2, at])
-        field -= factor * turn
-        base_out[:, at] = jnp.where(row < 5, field, limit)
+        field = vol[:, at]
+        above = jnp.where(slab == slabs - 1, 0.0, from_next[:, at] - edge[:, at])
+        below = jnp.where(slab == 0, 0.0, field[0:1] - from_previous[:, at])
+        turn = adjoint[:, at] + jnp.where(short == 0, below, jnp.where(short == 3, -above, 0.0))
+        base_out[:, at] = field - factor * turn
+        limit_out[:, at] = jnp.full((1, 128), limit, jnp.float32)
 
     used = count[0]
     per = slots // CHUNKS
@@ -218,11 +209,10 @@
         both = jnp.where(top == low, jnp.where(top, even[0], odd[1]), turned)
         grad = (both + pltpu.roll(both, 4, axis=0))[0:4]
         grad_out[:, at] = grad
-        first_out[:, at] = grad[0:1]
 
 
 def update_kernel(
-    grad, grad_other, first_next, first_cross, base, dual,
+    grad, grad_other, first_next, base, dual, limits,
     new_volume, new_split, new_dual,
 ):
     last = lax.axis_index("slab") == lax.axis_size("slab") - 1
@@ -231,11 +221,10 @@
     inner = jnp.logical_or(row < 3, jnp.logical_not(last))
     for j in range(dual.shape[2] // 128):
         at = slice(128 * j, 128 * j + 128)
-        slope = jnp.concatenate([grad[:, at] + grad_other[:, at]] * 2, axis=0)
-        slope = jnp.where(row < 4, slope, first_next[:, at] + first_cross[:, at])
-        limit = base[5:6, at]
-        field = base[:, at] - TAU * slope
-        new_volume[:, at] = field[0:4]
+        limit = limits[:, at]
+        own = base[:, at] - TAU * (grad[:, at] + grad_other[:, at])
+        field = jnp.where(row < 4, jnp.concatenate([own] * 2, axis=0), first_next[:, at])
+        new_volume[:, at] = own
         steps = (
             jnp.where(inner, pltpu.roll(field, 7, axis=0) - field, 0.0),
             jnp.where(row_mask, pltpu.roll(field, 120, axis=1) - field, 0.0),
@@ -284,15 +273,16 @@
         )
     )
 
-    partial, adjoint, halo = pl.pallas_call(
+    partial, adjoint, edge, first = pl.pallas_call(
         forward_kernel,
         out_shape=(
             jax.ShapeDtypeStruct((rays * slices, TR), bf16),
             jax.ShapeDtypeStruct((slices, width), f32),
-            jax.ShapeDtypeStruct((4, width), f32),
+            jax.ShapeDtypeStruct((1, width), f32),
+            jax.ShapeDtypeStruct((1, width), f32),
         ),
         in_specs=[smem()] + [hbm()] * 7,
-        out_specs=(vmem(), vmem(), vmem()),
+        out_specs=(vmem(),) * 4,
         scratch_shapes=[
             pltpu.SMEM((slots,), jnp.int32),
             pltpu.SMEM((slots,), jnp.int32),
@@ -314,27 +304,35 @@
 
     down = [(i, i - 1) for i in range(1, slabs)]
     if slabs == 2:
+        halo = jnp.where(lax.axis_index("slab") == 0, edge, first)
         from_next = from_previous = lax.ppermute(halo, "slab", [(0, 1), (1, 0)])
     else:
-        from_next = lax.ppermute(halo, "slab", down)
-        from_previous = lax.ppermute(halo, "slab", [(i - 1, i) for i in range(1, slabs)])
-    step = 1
-    while True:
-        moved = lax.ppermute(partial, ("tile", "rep"), [(i, i ^ step) for i in range(group)])
+        from_next = lax.ppermute(first, "slab", down)
+        from_previous = lax.ppermute(edge, "slab", [(i - 1, i) for i in range(1, slabs)])
+
+    both = ("tile", "rep")
+    holders = range(reps - 1, group, reps)
+    moved = lax.ppermute(partial, "rep", [(0, 1)])
+    total = (partial.astype(f32) + moved.astype(f32)).astype(bf16)
+    step = reps
+    while step < group:
+        moved = lax.ppermute(total, both, [(i, i ^ step) for i in holders])
+        if step == reps:
+            moved, from_next, from_previous = lax.optimization_barrier(
+                (moved, from_next, from_previous)
+            )
+        total = (total.astype(f32) + moved.astype(f32)).astype(bf16)
         step *= 2
-        if step == group:
-            break
-        partial = (partial.astype(f32) + moved.astype(f32)).astype(bf16)
-    parts = [partial, moved]
-
-    grad, first, base = pl.pallas_call(
-        functools.partial(backward_kernel, len(parts)),
+    shared = lax.ppermute(total, "rep", [(1, 0)])
+
+    grad, base, limits = pl.pallas_call(
+        backward_kernel,
         out_shape=(
             jax.ShapeDtypeStruct((slices, width), f32),
+            jax.ShapeDtypeStruct((slices, width), f32),
             jax.ShapeDtypeStruct((1, width), f32),
-            jax.ShapeDtypeStruct((8, width), f32),
-        ),
-        in_specs=[smem()] * 2 + [hbm()] * 3 + [vmem()] * (len(parts) + 5),
+        ),
+        in_specs=[smem()] * 2 + [hbm()] * 3 + [vmem()] * 7,
         out_specs=(vmem(), vmem(), vmem()),
         scratch_shapes=[
             pltpu.SMEM((slots,), jnp.int32),
@@ -348,11 +346,11 @@
         name="backward",
     )(
         tile_count, rho, ray_index, voxel_index, proj_tiles,
-        *parts, volume_here, adjoint, halo, from_next, from_previous,
+        total, shared, volume_here, adjoint, edge, from_next, from_previous,
     )
     grad_other = lax.ppermute(grad, "rep", [(i, i ^ 1) for i in range(reps)])
-    first_next = lax.ppermute(first, "slab", down)
-    first_cross = lax.ppermute(first_next, "rep", [(i, i ^ 1) for i in range(reps)])
+    new_first = base[0:1] - TAU * (grad[0:1] + grad_other[0:1])
+    first_next = lax.ppermute(new_first, "slab", down)
 
     return pl.pallas_call(
         update_kernel,
@@ -365,7 +363,7 @@
         out_specs=(vmem(), vmem(), vmem()),
         compiler_params=params(),
         name="update",
-    )(grad, grad_other, first_next, first_cross, base, dual_here)
+    )(grad, grad_other, first_next, base, dual_here, limits)
 
 
 def solution(mesh):

time: 28.1 us -> 35 us (1.25)
  waiting for transfers between devices: 8.01 us -> 15.4 us
  starting transfers between devices: 9.46 us -> 8.89 us
    ppermute x5, waiting for transfers between devices: 8.01 us -> 12.5 us  [the longest x1 7.37 us: shards(): shared = lax.ppermute(total, 'rep', [(1, 0)])]
    ppermute x1, waiting for transfers between devices: 0.01 us -> 1.72 us  [shards(): from_next = from_previous = lax.ppermute(halo, 'slab', [(0, 1), (1, 0)])]
    ppermute x5, starting transfers between devices: 7.89 us -> 6.27 us  [the longest x1 2.36 us: shards(): moved = lax.ppermute(partial, 'rep', [(0, 1)])]
    ppermute x1, waiting for transfers between devices: 0.01 us -> 1.09 us  [shards(): grad_other = lax.ppermute(grad, 'rep', [(i, i ^ 1) for i in range(reps)])]
    ppermute x1, starting transfers between devices: 1.49 us -> 2.39 us  [shards(): from_next = from_previous = lax.ppermute(halo, 'slab', [(0, 1), (1, 0)])]
where the time goes in v4:
time: 35 us; the launch traced here: 34.8 us
  waiting for transfers between devices  15.4 us (44%)
  starting transfers between devices  8.89 us (25%)
  Pallas kernels  8.37 us (24%)
  between operations  2.07 us (6%)
    ppermute x1, waiting for transfers between devices, shards(): shared = lax.ppermute(total, 'rep', [(1, 0)])  7.37 us
    ppermute x1, waiting for transfers between devices, shards(): first_next = lax.ppermute(new_first, 'slab', down)  4.33 us
    pallas_call x1, Pallas kernels, shards(): pl.pallas_call(forward_kernel, out_shape=(jax.ShapeDtypeStruct((rays * sl...  4.15 us
    pallas_call x1, Pallas kernels, shards(): pl.pallas_call(backward_kernel, out_shape=(jax.ShapeDtypeStruct((slices,...  3.33 us
    ppermute x1, starting transfers between devices, shards(): from_next = from_previous = lax.ppermute(halo, 'slab', [(0, 1), (1, 0)])  2.39 us
    ppermute x1, starting transfers between devices, shards(): moved = lax.ppermute(partial, 'rep', [(0, 1)])  2.36 us
    ppermute x1, waiting for transfers between devices, shards(): from_next = from_previous = lax.ppermute(halo, 'slab', [(0, 1), (1, 0)])  1.72 us
    ppermute x2, starting transfers between devices, shards(): moved = lax.ppermute(total, both, [(i, i ^ step) for i in holders])  1.33 us
  transfers between devices with their start and end apart: 7, of which 5 were waited for; matrix products, arithmetic and copies ran while one was open for 0% of the time, Pallas kernels for 0%

profile of v4, /device:TPU:0, one launch (start us, length us, event | category | flops | bytes accessed | tf_op | source)
XLA Modules:
  0.0 34.8 jit_solution(17933166153953854697)
XLA Ops:
  0.6 0.0 copy-start.1
  1.3 0.0 copy-start
  1.3 4.2 %forward.1 = (bf16[128,128]{1,0:T(8,128)(2,1)S(1)}, f32[4,4096]{1,0:T(4,128)S(1)}, f32[1,4096]{1,0:T(1,128)S(1)}, f32[1,4096]{1,0:T(1,128)S(1)}) custom-call(s32[1]{0:T(128)S(6)} %copy.12.count, s32[256]{0:T(256)} %ray_hbm.3, s32[256]{0:T(256)} %voxel_hbm.3, f32[4,4096]{1,0:T(4,128)} %vol.1, f32[3,4,4096]{2,1,0:T(4,128)} %split_hbm.1, f32[3,4,4096]{2,1,0:T(4,128)} %dual.1, ...), custom_call_target="tpu_custom_call" | custom-call | tf_op jit(solution)/shard_map/forward/pallas_call | solution.py:276
  5.5 2.4 %collective-permute-start = (bf16[128,128]{1,0:T(8,128)(2,1)S(1)}, bf16[128,128]{1,0:T(8,128)(2,1)S(1)}, u32[]{:S(2)}, u32[]{:S(2)}) collective-permute-start(bf16[128,128]{1,0:T(8,128)(2,1)S(1)} %get-tuple-element.13), channel_id=1, source_target_pairs={{0,1},{2,3},{4,5},{6,7},{8,9},{10,11},{12,13},{14,15},{16,17},{18,... | collective-permute-start | bytes 98312 | tf_op jit(solution)/shard_map/ppermute | solution.py:315
  7.9 0.8 %collective-permute-done = bf16[128,128]{1,0:T(8,128)(2,1)S(1)} collective-permute-done((bf16[128,128]{1,0:T(8,128)(2,1)S(1)}, bf16[128,128]{1,0:T(8,128)(2,1)S(1)}, u32[]{:S(2)}, u32[]{:S(2)}) %collective-permute-start) | collective-permute-done | bytes 32800 | tf_op jit(solution)/shard_map/ppermute | solution.py:315
  8.7 0.7 %collective-permute-start.1 = (bf16[128,128]{1,0:T(8,128)(2,1)S(1)}, bf16[128,128]{1,0:T(8,128)(2,1)S(1)}, u32[]{:S(2)}, u32[]{:S(2)}) collective-permute-start(bf16[128,128]{1,0:T(8,128)(2,1)S(1)} %add_convert_fusion.2), channel_id=1, source_target_pairs={{1,5},{5,1},{9,13},{13,9},{3,7},{7,3},{11,15},{15,11},{17,21},{21,... | collective-permute-start | bytes 98312 | tf_op jit(solution)/shard_map/ppermute | solution.py:319
  9.4 2.4 %collective-permute-start.2 = (f32[1,4096]{1,0:T(1,128)S(1)}, f32[1,4096]{1,0:T(1,128)S(1)}, u32[]{:S(2)}, u32[]{:S(2)}) collective-permute-start(f32[1,4096]{1,0:T(1,128)S(1)} %broadcast_select_fusion), channel_id=1, source_target_pairs={{0,2},{2,0},{1,3},{3,1},{4,6},{6,4},{5,7},{7,5},{8,10},{10,8},{9,1... | collective-permute-start | bytes 49160 | tf_op jit(solution)/shard_map/ppermute | solution.py:308
  11.8 1.7 %collective-permute-done.2.from_next.from_previous = f32[1,4096]{1,0:T(1,128)S(1)} collective-permute-done((f32[1,4096]{1,0:T(1,128)S(1)}, f32[1,4096]{1,0:T(1,128)S(1)}, u32[]{:S(2)}, u32[]{:S(2)}) %collective-permute-start.2) | collective-permute-done | bytes 16416 | tf_op jit(solution)/shard_map/ppermute | solution.py:308
  13.5 0.0 collective-permute-done.1
  13.5 0.7 %collective-permute-start.3 = (bf16[128,128]{1,0:T(8,128)(2,1)S(1)}, bf16[128,128]{1,0:T(8,128)(2,1)S(1)}, u32[]{:S(2)}, u32[]{:S(2)}) collective-permute-start(bf16[128,128]{1,0:T(8,128)(2,1)S(1)} %add_convert_fusion.1), channel_id=1, source_target_pairs={{1,9},{5,13},{9,1},{13,5},{3,11},{7,15},{11,3},{15,7},{17,25},{21,... | collective-permute-start | bytes 98312 | tf_op jit(solution)/shard_map/ppermute | solution.py:319
  14.2 0.0 collective-permute-done.3
  14.2 1.3 %collective-permute-start.4 = (bf16[128,128]{1,0:T(8,128)(2,1)S(1)}, bf16[128,128]{1,0:T(8,128)(2,1)S(1)}, u32[]{:S(2)}, u32[]{:S(2)}) collective-permute-start(bf16[128,128]{1,0:T(8,128)(2,1)S(1)} %add_convert_fusion.total), channel_id=1, source_target_pairs={{1,0},{3,2},{5,4},{7,6},{9,8},{11,10},{13,12},{15,14},{17,16},{19,... | collective-permute-start | bytes 98312 | tf_op jit(solution)/shard_map/ppermute | solution.py:326
  16.2 7.4 %collective-permute-done.4.shared = bf16[128,128]{1,0:T(8,128)(2,1)S(1)} collective-permute-done((bf16[128,128]{1,0:T(8,128)(2,1)S(1)}, bf16[128,128]{1,0:T(8,128)(2,1)S(1)}, u32[]{:S(2)}, u32[]{:S(2)}) %collective-permute-start.4) | collective-permute-done | bytes 32800 | tf_op jit(solution)/shard_map/ppermute | solution.py:326
  23.6 0.0 copy-done.1
  23.6 3.3 %backward.1 = (f32[4,4096]{1,0:T(4,128)S(1)}, f32[4,4096]{1,0:T(4,128)S(1)}, f32[1,4096]{1,0:T(1,128)S(1)}) custom-call(s32[1]{0:T(128)S(6)} %copy.12.count, f32[1]{0:T(128)S(6)} %copy.13.rho, s32[256]{0:T(256)} %ray_hbm.3, s32[256]{0:T(256)} %voxel_hbm.3, bf16[256,64,128]{2,1,0:T(8,128)(2,1)} %proj_hbm.3, bf16[128,128]{1,0:T(8,128)(2,1)S(1)} %add_convert_fusion.total, ...), custom_call_target="tpu_custom_call" | custom-call | tf_op jit(solution)/shard_map/backward/pallas_call | solution.py:328
  26.9 0.2 collective-permute-start.5
  27.1 1.1 %collective-permute-done.5.grad_other = f32[4,4096]{1,0:T(4,128)S(1)} collective-permute-done((f32[4,4096]{1,0:T(4,128)S(1)}, f32[4,4096]{1,0:T(4,128)S(1)}, u32[]{:S(2)}, u32[]{:S(2)}) %collective-permute-start.5) | collective-permute-done | bytes 65568 | tf_op jit(solution)/shard_map/ppermute | solution.py:351
  28.3 1.3 %collective-permute-start.6 = (f32[1,4096]{1,0:T(1,128)S(1)}, f32[1,4096]{1,0:T(1,128)S(1)}, u32[]{:S(2)}, u32[]{:S(2)}) collective-permute-start(f32[1,4096]{1,0:T(1,128)S(1)} %fusion.1), channel_id=1, source_target_pairs={{2,0},{3,1},{6,4},{7,5},{10,8},{11,9},{14,12},{15,13},{18,16},{19,... | collective-permute-start | bytes 49160 | tf_op jit(solution)/shard_map/ppermute | solution.py:353
  29.6 4.3 %collective-permute-done.6.first_next = f32[1,4096]{1,0:T(1,128)S(1)} collective-permute-done((f32[1,4096]{1,0:T(1,128)S(1)}, f32[1,4096]{1,0:T(1,128)S(1)}, u32[]{:S(2)}, u32[]{:S(2)}) %collective-permute-start.6) | collective-permute-done | bytes 16416 | tf_op jit(solution)/shard_map/ppermute | solution.py:353
  33.9 0.0 copy-done
  33.9 0.9 %update.1 = (f32[4,4096]{1,0:T(4,128)}, f32[3,4,4096]{2,1,0:T(4,128)}, f32[3,4,4096]{2,1,0:T(4,128)}) custom-call(f32[4,4096]{1,0:T(4,128)S(1)} %get-tuple-element.20.grad, f32[4,4096]{1,0:T(4,128)S(1)} %collective-permute-done.5.grad_other, f32[1,4096]{1,0:T(1,128)S(1)} %collective-permute-done.6.first_next, f32[4,4096]{1,0:T(4,128)S(1)} %get-tuple-element.21.base, ...), custom_call_target="tpu_custom_call" | custom-call | tf_op jit(solution)/shard_map/update/pallas_call | solution.py:355
  (5 shorter events, 0.1 us)
Async XLA Ops:
  0.6 22.9 %copy-start.1 = (f32[4,4096]{1,0:T(4,128)S(1)}, f32[4,4096]{1,0:T(4,128)}, u32[]{:S(2)}) copy-start(f32[4,4096]{1,0:T(4,128)} %vol.1) | copy-start | bytes 196612
  1.3 32.6 %copy-start = (f32[3,4,4096]{2,1,0:T(4,128)S(1)}, f32[3,4,4096]{2,1,0:T(4,128)}, u32[]{:S(2)}) copy-start(f32[3,4,4096]{2,1,0:T(4,128)} %dual.1) | copy-start | bytes 589828
  5.5 3.2 %collective-permute-start = (bf16[128,128]{1,0:T(8,128)(2,1)S(1)}, bf16[128,128]{1,0:T(8,128)(2,1)S(1)}, u32[]{:S(2)}, u32[]{:S(2)}) collective-permute-start(bf16[128,128]{1,0:T(8,128)(2,1)S(1)} %get-tuple-element.13), channel_id=1, source_target_pairs={{0,1},{2,3},{4,5},{6,7},{8,9},{10,11},{12,13},{14,15},{16,17},{18,... | collective-permute-start | bytes 98312 | tf_op jit(solution)/shard_map/ppermute | solution.py:315
  8.7 4.8 %collective-permute-start.1 = (bf16[128,128]{1,0:T(8,128)(2,1)S(1)}, bf16[128,128]{1,0:T(8,128)(2,1)S(1)}, u32[]{:S(2)}, u32[]{:S(2)}) collective-permute-start(bf16[128,128]{1,0:T(8,128)(2,1)S(1)} %add_convert_fusion.2), channel_id=1, source_target_pairs={{1,5},{5,1},{9,13},{13,9},{3,7},{7,3},{11,15},{15,11},{17,21},{21,... | collective-permute-start | bytes 98312 | tf_op jit(solution)/shard_map/ppermute | solution.py:319
  9.4 4.1 %collective-permute-start.2 = (f32[1,4096]{1,0:T(1,128)S(1)}, f32[1,4096]{1,0:T(1,128)S(1)}, u32[]{:S(2)}, u32[]{:S(2)}) collective-permute-start(f32[1,4096]{1,0:T(1,128)S(1)} %broadcast_select_fusion), channel_id=1, source_target_pairs={{0,2},{2,0},{1,3},{3,1},{4,6},{6,4},{5,7},{7,5},{8,10},{10,8},{9,1... | collective-permute-start | bytes 49160 | tf_op jit(solution)/shard_map/ppermute | solution.py:308
  13.5 0.7 %collective-permute-start.3 = (bf16[128,128]{1,0:T(8,128)(2,1)S(1)}, bf16[128,128]{1,0:T(8,128)(2,1)S(1)}, u32[]{:S(2)}, u32[]{:S(2)}) collective-permute-start(bf16[128,128]{1,0:T(8,128)(2,1)S(1)} %add_convert_fusion.1), channel_id=1, source_target_pairs={{1,9},{5,13},{9,1},{13,5},{3,11},{7,15},{11,3},{15,7},{17,25},{21,... | collective-permute-start | bytes 98312 | tf_op jit(solution)/shard_map/ppermute | solution.py:319
  14.2 9.3 %collective-permute-start.4 = (bf16[128,128]{1,0:T(8,128)(2,1)S(1)}, bf16[128,128]{1,0:T(8,128)(2,1)S(1)}, u32[]{:S(2)}, u32[]{:S(2)}) collective-permute-start(bf16[128,128]{1,0:T(8,128)(2,1)S(1)} %add_convert_fusion.total), channel_id=1, source_target_pairs={{1,0},{3,2},{5,4},{7,6},{9,8},{11,10},{13,12},{15,14},{17,16},{19,... | collective-permute-start | bytes 98312 | tf_op jit(solution)/shard_map/ppermute | solution.py:326
  26.9 1.3 %collective-permute-start.5 = (f32[4,4096]{1,0:T(4,128)S(1)}, f32[4,4096]{1,0:T(4,128)S(1)}, u32[]{:S(2)}, u32[]{:S(2)}) collective-permute-start(f32[4,4096]{1,0:T(4,128)S(1)} %get-tuple-element.20.grad), channel_id=1, source_target_pairs={{0,1},{1,0},{2,3},{3,2},{4,5},{5,4},{6,7},{7,6},{8,9},{9,8},{10,11... | collective-permute-start | bytes 196616 | tf_op jit(solution)/shard_map/ppermute | solution.py:351
  28.3 5.6 %collective-permute-start.6 = (f32[1,4096]{1,0:T(1,128)S(1)}, f32[1,4096]{1,0:T(1,128)S(1)}, u32[]{:S(2)}, u32[]{:S(2)}) collective-permute-start(f32[1,4096]{1,0:T(1,128)S(1)} %fusion.1), channel_id=1, source_target_pairs={{2,0},{3,1},{6,4},{7,5},{10,8},{11,9},{14,12},{15,13},{18,16},{19,... | collective-permute-start | bytes 49160 | tf_op jit(solution)/shard_map/ppermute | solution.py:353

commit v5 on v4

--- a/solution.py
+++ b/solution.py
@@ -132,7 +132,7 @@
 
 def backward_kernel(
     count, rho, ray_hbm, voxel_hbm, proj_hbm,
-    total, shared, vol, adjoint, edge, from_next, from_previous,
+    part, moved, vol, adjoint, edge, from_next, from_previous,
     grad_out, base_out, limit_out,
     ray, voxel, tiles, table, acc0, acc1, acc2, acc3, sems, tile_sems,
 ):
@@ -153,10 +153,9 @@
         acc[...] = jnp.zeros_like(acc)
     row, lane = iotas((8, 128))
     low, top = lane < TV, row < 4
-    holder = lax.axis_index("rep") == lax.axis_size("rep") - 1
     for q in range(rays // 4):
         at = slice(16 * q, 16 * q + 16)
-        both = jnp.where(holder, total[at, :].astype(jnp.float32), shared[at, :].astype(jnp.float32))
+        both = part[at, :].astype(jnp.float32) + moved[at, :].astype(jnp.float32)
         for k in range(2):
             x = both[8 * k:8 * k + 8]
             turned = pltpu.roll(x, 4, axis=0)
@@ -303,27 +302,26 @@
     )
 
     down = [(i, i - 1) for i in range(1, slabs)]
+    swap = [(0, 1), (1, 0)]
     if slabs == 2:
         halo = jnp.where(lax.axis_index("slab") == 0, edge, first)
-        from_next = from_previous = lax.ppermute(halo, "slab", [(0, 1), (1, 0)])
+        from_next = from_previous = lax.ppermute(halo, "slab", swap)
     else:
         from_next = lax.ppermute(first, "slab", down)
         from_previous = lax.ppermute(edge, "slab", [(i - 1, i) for i in range(1, slabs)])
 
     both = ("tile", "rep")
-    holders = range(reps - 1, group, reps)
-    moved = lax.ppermute(partial, "rep", [(0, 1)])
-    total = (partial.astype(f32) + moved.astype(f32)).astype(bf16)
-    step = reps
-    while step < group:
-        moved = lax.ppermute(total, both, [(i, i ^ step) for i in holders])
+    step = 1
+    while True:
+        moved = lax.ppermute(partial, both, [(i, i ^ step) for i in range(group)])
         if step == reps:
             moved, from_next, from_previous = lax.optimization_barrier(
                 (moved, from_next, from_previous)
             )
-        total = (total.astype(f32) + moved.astype(f32)).astype(bf16)
         step *= 2
-    shared = lax.ppermute(total, "rep", [(1, 0)])
+        if step == group:
+            break
+        partial = (partial.astype(f32) + moved.astype(f32)).astype(bf16)
 
     grad, base, limits = pl.pallas_call(
         backward_kernel,
@@ -346,11 +344,11 @@
         name="backward",
     )(
         tile_count, rho, ray_index, voxel_index, proj_tiles,
-        total, shared, volume_here, adjoint, edge, from_next, from_previous,
+        partial, moved, volume_here, adjoint, edge, from_next, from_previous,
     )
     grad_other = lax.ppermute(grad, "rep", [(i, i ^ 1) for i in range(reps)])
     new_first = base[0:1] - TAU * (grad[0:1] + grad_other[0:1])
-    first_next = lax.ppermute(new_first, "slab", down)
+    first_next = lax.ppermute(new_first, "slab", swap if slabs == 2 else down)
 
     return pl.pallas_call(
         update_kernel,

time: 35 us -> 28.2 us (0.81)
  waiting for transfers between devices: 15.4 us -> 7.97 us
  starting transfers between devices: 8.89 us -> 9.55 us
    ppermute x6 -> x5, waiting for transfers between devices: 14.3 us -> 6.73 us  [the longest x3 2.46 us: shards(): moved = lax.ppermute(partial, both, [(i, i ^ step) for i in range(group)])]
    ppermute x6 -> x5, starting transfers between devices: 8.66 us -> 9.48 us  [the longest x3 6.15 us: shards(): moved = lax.ppermute(partial, both, [(i, i ^ step) for i in range(group)])]
  transfers between devices with their start and end apart: 7 -> 6, of which waited for: 5 -> 5; matrix products, arithmetic and copies ran while one was open for 0% -> 0% of each run, Pallas kernels for 0% -> 0%
where the time goes in v5:
time: 28.2 us; the launch traced here: 28 us
  starting transfers between devices  9.55 us (34%)
  Pallas kernels  8.39 us (30%)
  waiting for transfers between devices  7.97 us (28%)
  between operations  2.02 us (7%)
    ppermute x3, starting transfers between devices, shards(): moved = lax.ppermute(partial, both, [(i, i ^ step) for i in range(group)])  6.15 us
    pallas_call x1, Pallas kernels, shards(): pl.pallas_call(forward_kernel, out_shape=(jax.ShapeDtypeStruct((rays * sl...  4.16 us
    pallas_call x1, Pallas kernels, shards(): pl.pallas_call(backward_kernel, out_shape=(jax.ShapeDtypeStruct((slices,...  3.34 us
    ppermute x3, waiting for transfers between devices, shards(): moved = lax.ppermute(partial, both, [(i, i ^ step) for i in range(group)])  2.46 us
    ppermute x1, waiting for transfers between devices, shards(): from_next = from_previous = lax.ppermute(halo, 'slab', swap)  2.25 us
    ppermute x1, waiting for transfers between devices, shards(): first_next = lax.ppermute(new_first, 'slab', swap if slabs == 2 else down)  2.02 us
    ppermute x1, starting transfers between devices, shards(): first_next = lax.ppermute(new_first, 'slab', swap if slabs == 2 else down)  1.78 us
    ppermute x1, starting transfers between devices, shards(): from_next = from_previous = lax.ppermute(halo, 'slab', swap)  1.56 us
  transfers between devices with their start and end apart: 6, of which 5 were waited for; matrix products, arithmetic and copies ran while one was open for 0% of the time, Pallas kernels for 0%

profile of v5, /device:TPU:0, one launch (start us, length us, event | category | flops | bytes accessed | tf_op | source)
XLA Modules:
  0.0 28.0 jit_solution(1720254680920359705)
XLA Ops:
  0.6 0.0 copy-start.1
  1.3 0.0 copy-start
  1.3 4.2 %forward.1 = (bf16[128,128]{1,0:T(8,128)(2,1)S(1)}, f32[4,4096]{1,0:T(4,128)S(1)}, f32[1,4096]{1,0:T(1,128)S(1)}, f32[1,4096]{1,0:T(1,128)S(1)}) custom-call(s32[1]{0:T(128)S(6)} %copy.12.count, s32[256]{0:T(256)} %ray_hbm.3, s32[256]{0:T(256)} %voxel_hbm.3, f32[4,4096]{1,0:T(4,128)} %vol.1, f32[3,4,4096]{2,1,0:T(4,128)} %split_hbm.1, f32[3,4,4096]{2,1,0:T(4,128)} %dual.1, ...), custom_call_target="tpu_custom_call" | custom-call | tf_op jit(solution)/shard_map/forward/pallas_call | solution.py:275
  5.5 0.5 %collective-permute-start = (bf16[128,128]{1,0:T(8,128)(2,1)S(1)}, bf16[128,128]{1,0:T(8,128)(2,1)S(1)}, u32[]{:S(2)}, u32[]{:S(2)}) collective-permute-start(bf16[128,128]{1,0:T(8,128)(2,1)S(1)} %get-tuple-element.13), channel_id=1, source_target_pairs={{0,1},{1,0},{4,5},{5,4},{8,9},{9,8},{12,13},{13,12},{2,3},{3,2},{6... | collective-permute-start | bytes 98312 | tf_op jit(solution)/shard_map/ppermute | solution.py:316
  6.0 0.9 %collective-permute-done = bf16[128,128]{1,0:T(8,128)(2,1)S(1)} collective-permute-done((bf16[128,128]{1,0:T(8,128)(2,1)S(1)}, bf16[128,128]{1,0:T(8,128)(2,1)S(1)}, u32[]{:S(2)}, u32[]{:S(2)}) %collective-permute-start) | collective-permute-done | bytes 32800 | tf_op jit(solution)/shard_map/ppermute | solution.py:316
  6.9 3.0 %collective-permute-start.1 = (bf16[128,128]{1,0:T(8,128)(2,1)S(1)}, bf16[128,128]{1,0:T(8,128)(2,1)S(1)}, u32[]{:S(2)}, u32[]{:S(2)}) collective-permute-start(bf16[128,128]{1,0:T(8,128)(2,1)S(1)} %add_convert_fusion.1), channel_id=1, source_target_pairs={{0,4},{1,5},{4,0},{5,1},{8,12},{9,13},{12,8},{13,9},{2,6},{3,7},{6... | collective-permute-start | bytes 98312 | tf_op jit(solution)/shard_map/ppermute | solution.py:316
  9.9 1.6 %collective-permute-start.2 = (f32[1,4096]{1,0:T(1,128)S(1)}, f32[1,4096]{1,0:T(1,128)S(1)}, u32[]{:S(2)}, u32[]{:S(2)}) collective-permute-start(f32[1,4096]{1,0:T(1,128)S(1)} %broadcast_select_fusion), channel_id=1, source_target_pairs={{0,2},{2,0},{1,3},{3,1},{4,6},{6,4},{5,7},{7,5},{8,10},{10,8},{9,1... | collective-permute-start | bytes 49160 | tf_op jit(solution)/shard_map/ppermute | solution.py:308
  11.5 2.2 %collective-permute-done.2.from_next.from_previous = f32[1,4096]{1,0:T(1,128)S(1)} collective-permute-done((f32[1,4096]{1,0:T(1,128)S(1)}, f32[1,4096]{1,0:T(1,128)S(1)}, u32[]{:S(2)}, u32[]{:S(2)}) %collective-permute-start.2) | collective-permute-done | bytes 16416 | tf_op jit(solution)/shard_map/ppermute | solution.py:308
  13.7 0.0 collective-permute-done.1
  13.7 2.6 %collective-permute-start.3 = (bf16[128,128]{1,0:T(8,128)(2,1)S(1)}, bf16[128,128]{1,0:T(8,128)(2,1)S(1)}, u32[]{:S(2)}, u32[]{:S(2)}) collective-permute-start(bf16[128,128]{1,0:T(8,128)(2,1)S(1)} %add_convert_fusion.part), channel_id=1, source_target_pairs={{0,8},{1,9},{4,12},{5,13},{8,0},{9,1},{12,4},{13,5},{2,10},{3,11},... | collective-permute-start | bytes 98312 | tf_op jit(solution)/shard_map/ppermute | solution.py:316
  17.0 1.6 %collective-permute-done.3.moved = bf16[128,128]{1,0:T(8,128)(2,1)S(1)} collective-permute-done((bf16[128,128]{1,0:T(8,128)(2,1)S(1)}, bf16[128,128]{1,0:T(8,128)(2,1)S(1)}, u32[]{:S(2)}, u32[]{:S(2)}) %collective-permute-start.3) | collective-permute-done | bytes 32800 | tf_op jit(solution)/shard_map/ppermute | solution.py:316
  18.6 0.0 copy-done.1
  18.6 3.3 %backward.1 = (f32[4,4096]{1,0:T(4,128)S(1)}, f32[4,4096]{1,0:T(4,128)S(1)}, f32[1,4096]{1,0:T(1,128)S(1)}) custom-call(s32[1]{0:T(128)S(6)} %copy.12.count, f32[1]{0:T(128)S(6)} %copy.13.rho, s32[256]{0:T(256)} %ray_hbm.3, s32[256]{0:T(256)} %voxel_hbm.3, bf16[256,64,128]{2,1,0:T(8,128)(2,1)} %proj_hbm.3, bf16[128,128]{1,0:T(8,128)(2,1)S(1)} %add_convert_fusion.part, ...), custom_call_target="tpu_custom_call" | custom-call | tf_op jit(solution)/shard_map/backward/pallas_call | solution.py:326
  22.0 0.1 collective-permute-start.4
  22.0 1.2 %collective-permute-done.4.grad_other = f32[4,4096]{1,0:T(4,128)S(1)} collective-permute-done((f32[4,4096]{1,0:T(4,128)S(1)}, f32[4,4096]{1,0:T(4,128)S(1)}, u32[]{:S(2)}, u32[]{:S(2)}) %collective-permute-start.4) | collective-permute-done | bytes 65568 | tf_op jit(solution)/shard_map/ppermute | solution.py:349
  23.3 1.8 %collective-permute-start.5 = (f32[1,4096]{1,0:T(1,128)S(1)}, f32[1,4096]{1,0:T(1,128)S(1)}, u32[]{:S(2)}, u32[]{:S(2)}) collective-permute-start(f32[1,4096]{1,0:T(1,128)S(1)} %fusion.1), channel_id=1, source_target_pairs={{0,2},{2,0},{1,3},{3,1},{4,6},{6,4},{5,7},{7,5},{8,10},{10,8},{9,1... | collective-permute-start | bytes 49160 | tf_op jit(solution)/shard_map/ppermute | solution.py:351
  25.1 2.0 %collective-permute-done.5.first_next = f32[1,4096]{1,0:T(1,128)S(1)} collective-permute-done((f32[1,4096]{1,0:T(1,128)S(1)}, f32[1,4096]{1,0:T(1,128)S(1)}, u32[]{:S(2)}, u32[]{:S(2)}) %collective-permute-start.5) | collective-permute-done | bytes 16416 | tf_op jit(solution)/shard_map/ppermute | solution.py:351
  27.1 0.0 copy-done
  27.1 0.9 %update.1 = (f32[4,4096]{1,0:T(4,128)}, f32[3,4,4096]{2,1,0:T(4,128)}, f32[3,4,4096]{2,1,0:T(4,128)}) custom-call(f32[4,4096]{1,0:T(4,128)S(1)} %get-tuple-element.20.grad, f32[4,4096]{1,0:T(4,128)S(1)} %collective-permute-done.4.grad_other, f32[1,4096]{1,0:T(1,128)S(1)} %collective-permute-done.5.first_next, f32[4,4096]{1,0:T(4,128)S(1)} %get-tuple-element.21.base, ...), custom_call_target="tpu_custom_call" | custom-call | tf_op jit(solution)/shard_map/update/pallas_call | solution.py:353
  (4 shorter events, 0.1 us)
Async XLA Ops:
  0.6 18.0 %copy-start.1 = (f32[4,4096]{1,0:T(4,128)S(1)}, f32[4,4096]{1,0:T(4,128)}, u32[]{:S(2)}) copy-start(f32[4,4096]{1,0:T(4,128)} %vol.1) | copy-start | bytes 196612
  1.3 25.8 %copy-start = (f32[3,4,4096]{2,1,0:T(4,128)S(1)}, f32[3,4,4096]{2,1,0:T(4,128)}, u32[]{:S(2)}) copy-start(f32[3,4,4096]{2,1,0:T(4,128)} %dual.1) | copy-start | bytes 589828
  5.5 1.4 %collective-permute-start = (bf16[128,128]{1,0:T(8,128)(2,1)S(1)}, bf16[128,128]{1,0:T(8,128)(2,1)S(1)}, u32[]{:S(2)}, u32[]{:S(2)}) collective-permute-start(bf16[128,128]{1,0:T(8,128)(2,1)S(1)} %get-tuple-element.13), channel_id=1, source_target_pairs={{0,1},{1,0},{4,5},{5,4},{8,9},{9,8},{12,13},{13,12},{2,3},{3,2},{6... | collective-permute-start | bytes 98312 | tf_op jit(solution)/shard_map/ppermute | solution.py:316
  6.9 6.8 %collective-permute-start.1 = (bf16[128,128]{1,0:T(8,128)(2,1)S(1)}, bf16[128,128]{1,0:T(8,128)(2,1)S(1)}, u32[]{:S(2)}, u32[]{:S(2)}) collective-permute-start(bf16[128,128]{1,0:T(8,128)(2,1)S(1)} %add_convert_fusion.1), channel_id=1, source_target_pairs={{0,4},{1,5},{4,0},{5,1},{8,12},{9,13},{12,8},{13,9},{2,6},{3,7},{6... | collective-permute-start | bytes 98312 | tf_op jit(solution)/shard_map/ppermute | solution.py:316
  9.9 3.8 %collective-permute-start.2 = (f32[1,4096]{1,0:T(1,128)S(1)}, f32[1,4096]{1,0:T(1,128)S(1)}, u32[]{:S(2)}, u32[]{:S(2)}) collective-permute-start(f32[1,4096]{1,0:T(1,128)S(1)} %broadcast_select_fusion), channel_id=1, source_target_pairs={{0,2},{2,0},{1,3},{3,1},{4,6},{6,4},{5,7},{7,5},{8,10},{10,8},{9,1... | collective-permute-start | bytes 49160 | tf_op jit(solution)/shard_map/ppermute | solution.py:308
  13.7 4.9 %collective-permute-start.3 = (bf16[128,128]{1,0:T(8,128)(2,1)S(1)}, bf16[128,128]{1,0:T(8,128)(2,1)S(1)}, u32[]{:S(2)}, u32[]{:S(2)}) collective-permute-start(bf16[128,128]{1,0:T(8,128)(2,1)S(1)} %add_convert_fusion.part), channel_id=1, source_target_pairs={{0,8},{1,9},{4,12},{5,13},{8,0},{9,1},{12,4},{13,5},{2,10},{3,11},... | collective-permute-start | bytes 98312 | tf_op jit(solution)/shard_map/ppermute | solution.py:316
  22.0 1.3 %collective-permute-start.4 = (f32[4,4096]{1,0:T(4,128)S(1)}, f32[4,4096]{1,0:T(4,128)S(1)}, u32[]{:S(2)}, u32[]{:S(2)}) collective-permute-start(f32[4,4096]{1,0:T(4,128)S(1)} %get-tuple-element.20.grad), channel_id=1, source_target_pairs={{0,1},{1,0},{2,3},{3,2},{4,5},{5,4},{6,7},{7,6},{8,9},{9,8},{10,11... | collective-permute-start | bytes 196616 | tf_op jit(solution)/shard_map/ppermute | solution.py:349
  23.3 3.8 %collective-permute-start.5 = (f32[1,4096]{1,0:T(1,128)S(1)}, f32[1,4096]{1,0:T(1,128)S(1)}, u32[]{:S(2)}, u32[]{:S(2)}) collective-permute-start(f32[1,4096]{1,0:T(1,128)S(1)} %fusion.1), channel_id=1, source_target_pairs={{0,2},{2,0},{1,3},{3,1},{4,6},{6,4},{5,7},{7,5},{8,10},{10,8},{9,1... | collective-permute-start | bytes 49160 | tf_op jit(solution)/shard_map/ppermute | solution.py:351

commit v6 on v5

--- a/solution.py
+++ b/solution.py
@@ -132,8 +132,8 @@
 
 def backward_kernel(
     count, rho, ray_hbm, voxel_hbm, proj_hbm,
-    part, moved, vol, adjoint, edge, from_next, from_previous,
-    grad_out, base_out, limit_out,
+    parts, vol, adjoint,
+    grad_out, base_out, scale_out,
     ray, voxel, tiles, table, acc0, acc1, acc2, acc3, sems, tile_sems,
 ):
     slots = proj_hbm.shape[0]
@@ -155,27 +155,24 @@
     low, top = lane < TV, row < 4
     for q in range(rays // 4):
         at = slice(16 * q, 16 * q + 16)
-        both = part[at, :].astype(jnp.float32) + moved[at, :].astype(jnp.float32)
+        total = parts[0, at, :].astype(jnp.float32)
+        for p in range(1, parts.shape[0]):
+            total += parts[p, at, :].astype(jnp.float32)
         for k in range(2):
-            x = both[8 * k:8 * k + 8]
+            x = total[8 * k:8 * k + 8]
             turned = pltpu.roll(x, 4, axis=0)
             table[4 * q + 2 * k] = jnp.where(top, x, turned)
             table[4 * q + 2 * k + 1] = jnp.where(top, turned, x)
 
     for load in loads:
         load.wait()
-    slab, slabs = lax.axis_index("slab"), lax.axis_size("slab")
     factor = TAU * rho[0]
     limit = 1.0 / rho[0]
-    short = lax.broadcasted_iota(jnp.int32, (4, 128), 0)
     for j in range(voxel_tiles // 2):
         at = slice(128 * j, 128 * j + 128)
-        field = vol[:, at]
-        above = jnp.where(slab == slabs - 1, 0.0, from_next[:, at] - edge[:, at])
-        below = jnp.where(slab == 0, 0.0, field[0:1] - from_previous[:, at])
-        turn = adjoint[:, at] + jnp.where(short == 0, below, jnp.where(short == 3, -above, 0.0))
-        base_out[:, at] = field - factor * turn
-        limit_out[:, at] = jnp.full((1, 128), limit, jnp.float32)
+        base_out[:, at] = vol[:, at] - factor * adjoint[:, at]
+        scale_out[0:1, at] = jnp.full((1, 128), limit, jnp.float32)
+        scale_out[1:2, at] = jnp.full((1, 128), factor, jnp.float32)
 
     used = count[0]
     per = slots // CHUNKS
@@ -211,18 +208,23 @@
 
 
 def update_kernel(
-    grad, grad_other, first_next, base, dual, limits,
+    grad, grad_other, from_next, from_previous, base, edge, first, dual, scales,
     new_volume, new_split, new_dual,
 ):
-    last = lax.axis_index("slab") == lax.axis_size("slab") - 1
+    slab, slabs = lax.axis_index("slab"), lax.axis_size("slab")
     row, lane = iotas((8, 128))
+    short = lax.broadcasted_iota(jnp.int32, (4, 128), 0)
     row_mask, col_mask = plane_masks(lane)
-    inner = jnp.logical_or(row < 3, jnp.logical_not(last))
+    inner = jnp.logical_or(row < 3, slab < slabs - 1)
     for j in range(dual.shape[2] // 128):
         at = slice(128 * j, 128 * j + 128)
-        limit = limits[:, at]
+        limit, factor = scales[0:1, at], scales[1:2, at]
+        above = jnp.where(slab == slabs - 1, 0.0, factor * (from_next[1:2, at] - edge[:, at]))
+        below = jnp.where(slab == 0, 0.0, factor * (first[:, at] - from_previous[0:1, at]))
         own = base[:, at] - TAU * (grad[:, at] + grad_other[:, at])
-        field = jnp.where(row < 4, jnp.concatenate([own] * 2, axis=0), first_next[:, at])
+        own += jnp.where(short == 0, -below, jnp.where(short == 3, above, 0.0))
+        ahead = from_next[0:1, at] - above
+        field = jnp.where(row < 4, jnp.concatenate([own] * 2, axis=0), ahead)
         new_volume[:, at] = own
         steps = (
             jnp.where(inner, pltpu.roll(field, 7, axis=0) - field, 0.0),
@@ -301,36 +303,21 @@
         tile_count, ray_index, voxel_index, volume, split_var, dual_var, sinogram, proj_tiles
     )
 
-    down = [(i, i - 1) for i in range(1, slabs)]
-    swap = [(0, 1), (1, 0)]
-    if slabs == 2:
-        halo = jnp.where(lax.axis_index("slab") == 0, edge, first)
-        from_next = from_previous = lax.ppermute(halo, "slab", swap)
-    else:
-        from_next = lax.ppermute(first, "slab", down)
-        from_previous = lax.ppermute(edge, "slab", [(i - 1, i) for i in range(1, slabs)])
-
-    both = ("tile", "rep")
-    step = 1
-    while True:
-        moved = lax.ppermute(partial, both, [(i, i ^ step) for i in range(group)])
-        if step == reps:
-            moved, from_next, from_previous = lax.optimization_barrier(
-                (moved, from_next, from_previous)
-            )
-        step *= 2
-        if step == group:
-            break
-        partial = (partial.astype(f32) + moved.astype(f32)).astype(bf16)
-
-    grad, base, limits = pl.pallas_call(
+    swap = [(i, i ^ 1) for i in range(reps)]
+    moved = lax.ppermute(partial, "rep", swap)
+    chip = (partial.astype(f32) + moved.astype(f32)).astype(bf16)
+    parts = lax.all_to_all(
+        jnp.broadcast_to(chip, (group // reps, *chip.shape)), "tile", 0, 0, tiled=True
+    )
+
+    grad, base, scales = pl.pallas_call(
         backward_kernel,
         out_shape=(
             jax.ShapeDtypeStruct((slices, width), f32),
             jax.ShapeDtypeStruct((slices, width), f32),
-            jax.ShapeDtypeStruct((1, width), f32),
-        ),
-        in_specs=[smem()] * 2 + [hbm()] * 3 + [vmem()] * 7,
+            jax.ShapeDtypeStruct((2, width), f32),
+        ),
+        in_specs=[smem()] * 2 + [hbm()] * 3 + [vmem()] * 3,
         out_specs=(vmem(), vmem(), vmem()),
         scratch_shapes=[
             pltpu.SMEM((slots,), jnp.int32),
@@ -344,11 +331,17 @@
         name="backward",
     )(
         tile_count, rho, ray_index, voxel_index, proj_tiles,
-        partial, moved, volume_here, adjoint, edge, from_next, from_previous,
-    )
-    grad_other = lax.ppermute(grad, "rep", [(i, i ^ 1) for i in range(reps)])
-    new_first = base[0:1] - TAU * (grad[0:1] + grad_other[0:1])
-    first_next = lax.ppermute(new_first, "slab", swap if slabs == 2 else down)
+        parts, volume_here, adjoint,
+    )
+    grad_other = lax.ppermute(grad, "rep", swap)
+    ahead = jnp.concatenate([base[0:1] - TAU * (grad[0:1] + grad_other[0:1]), first], axis=0)
+    behind = jnp.concatenate([edge, edge], axis=0)
+    if slabs == 2:
+        halo = jnp.where(lax.axis_index("slab") == 0, behind, ahead)
+        from_next = from_previous = lax.ppermute(halo, "slab", [(0, 1), (1, 0)])
+    else:
+        from_next = lax.ppermute(ahead, "slab", [(i, i - 1) for i in range(1, slabs)])
+        from_previous = lax.ppermute(behind, "slab", [(i - 1, i) for i in range(1, slabs)])
 
     return pl.pallas_call(
         update_kernel,
@@ -357,11 +350,11 @@
             jax.ShapeDtypeStruct((3, slices, width), f32),
             jax.ShapeDtypeStruct((3, slices, width), f32),
         ),
-        in_specs=[vmem()] * 6,
+        in_specs=[vmem()] * 9,
         out_specs=(vmem(), vmem(), vmem()),
         compiler_params=params(),
         name="update",
-    )(grad, grad_other, first_next, base, dual_here, limits)
+    )(grad, grad_other, from_next, from_previous, base, edge, first, dual_here, scales)
 
 
 def solution(mesh):

time: 28.2 us -> 30 us (1.064)
  waiting for transfers between devices: 7.97 us -> 10.1 us
  starting transfers between devices: 9.55 us -> 8.38 us
  local copies, waits for them, and re-layouts: 0.01 us -> 0.68 us
    ppermute x6 -> x3, starting transfers between devices: 9.55 us -> 2.14 us  [the longest x1 1.56 us: shards(): from_next = from_previous = lax.ppermute(halo, 'slab', [(0, 1), (1, 0)])]
    all_to_all x0 -> x1, starting transfers between devices: none -> 6.23 us  [shards(): lax.all_to_all(jnp.broadcast_to(chip, (group // reps, *chip.shape)), 'til...]
    all_to_all x0 -> x1, waiting for transfers between devices: none -> 5.59 us  [shards(): lax.all_to_all(jnp.broadcast_to(chip, (group // reps, *chip.shape)), 'til...]
    ppermute x6 -> x3, waiting for transfers between devices: 7.97 us -> 4.52 us  [the longest x1 2.42 us: shards(): from_next = from_previous = lax.ppermute(halo, 'slab', [(0, 1), (1, 0)])]
    broadcast_in_dim x0 -> x1, local copies, waits for them, and re-layouts: none -> 0.67 us  [shards(): jnp.broadcast_to(chip, (group // reps, *chip.shape))]
  transfers between devices with their start and end apart: 6 -> 4, of which waited for: 5 -> 4; matrix products, arithmetic and copies ran while one was open for 0% -> 0% of each run, Pallas kernels for 0% -> 0%
where the time goes in v6:
time: 30 us; the launch traced here: 29.7 us
  waiting for transfers between devices  10.1 us (34%)
  Pallas kernels  8.41 us (28%)
  starting transfers between devices  8.38 us (28%)
  between operations  2.02 us (7%)
  local copies, waits for them, and re-layouts  0.68 us (2%)
    all_to_all x1, starting transfers between devices, shards(): lax.all_to_all(jnp.broadcast_to(chip, (group // reps, *chip.shape)), 'til...  6.23 us
    all_to_all x1, waiting for transfers between devices, shards(): lax.all_to_all(jnp.broadcast_to(chip, (group // reps, *chip.shape)), 'til...  5.59 us
    pallas_call x1, Pallas kernels, shards(): pl.pallas_call(forward_kernel, out_shape=(jax.ShapeDtypeStruct((rays * sl...  4.15 us
    pallas_call x1, Pallas kernels, shards(): pl.pallas_call(backward_kernel, out_shape=(jax.ShapeDtypeStruct((slices,...  3.33 us
    ppermute x1, waiting for transfers between devices, shards(): from_next = from_previous = lax.ppermute(halo, 'slab', [(0, 1), (1, 0)])  2.42 us
    ppermute x1, starting transfers between devices, shards(): from_next = from_previous = lax.ppermute(halo, 'slab', [(0, 1), (1, 0)])  1.56 us
    ppermute x1, waiting for transfers between devices, shards(): grad_other = lax.ppermute(grad, 'rep', swap)  1.23 us
    pallas_call x1, Pallas kernels, shards(): pl.pallas_call(update_kernel, out_shape=(jax.ShapeDtypeStruct((slices, wi...  0.93 us
  transfers between devices with their start and end apart: 4, of which 4 were waited for; matrix products, arithmetic and copies ran while one was open for 0% of the time, Pallas kernels for 0%

profile of v6, /device:TPU:0, one launch (start us, length us, event | category | flops | bytes accessed | tf_op | source)
XLA Modules:
  0.0 29.7 jit_solution(7716098131479688519)
XLA Ops:
  0.6 0.0 copy-start.1
  1.3 0.0 copy-start
  1.3 4.1 %forward.1 = (bf16[128,128]{1,0:T(8,128)(2,1)S(1)}, f32[4,4096]{1,0:T(4,128)S(1)}, f32[1,4096]{1,0:T(1,128)S(1)}, f32[1,4096]{1,0:T(1,128)S(1)}) custom-call(s32[1]{0:T(128)S(6)} %copy.12.count, s32[256]{0:T(256)} %ray_hbm.3, s32[256]{0:T(256)} %voxel_hbm.3, f32[4,4096]{1,0:T(4,128)} %vol.1, f32[3,4,4096]{2,1,0:T(4,128)} %split_hbm.1, f32[3,4,4096]{2,1,0:T(4,128)} %dual.1, ...), custom_call_target="tpu_custom_call" | custom-call | tf_op jit(solution)/shard_map/forward/pallas_call | solution.py:277
  5.5 0.5 %collective-permute-start = (bf16[128,128]{1,0:T(8,128)(2,1)S(1)}, bf16[128,128]{1,0:T(8,128)(2,1)S(1)}, u32[]{:S(2)}, u32[]{:S(2)}) collective-permute-start(bf16[128,128]{1,0:T(8,128)(2,1)S(1)} %get-tuple-element.10), channel_id=1, source_target_pairs={{0,1},{1,0},{2,3},{3,2},{4,5},{5,4},{6,7},{7,6},{8,9},{9,8},{10,11... | collective-permute-start | bytes 98312 | tf_op jit(solution)/shard_map/ppermute | solution.py:307
  6.0 0.9 %collective-permute-done = bf16[128,128]{1,0:T(8,128)(2,1)S(1)} collective-permute-done((bf16[128,128]{1,0:T(8,128)(2,1)S(1)}, bf16[128,128]{1,0:T(8,128)(2,1)S(1)}, u32[]{:S(2)}, u32[]{:S(2)}) %collective-permute-start) | collective-permute-done | bytes 32800 | tf_op jit(solution)/shard_map/ppermute | solution.py:307
  6.9 0.7 %broadcast_in_dim.3 = bf16[4,128,128]{2,1,0:T(8,128)(2,1)} broadcast(bf16[128,128]{1,0:T(8,128)(2,1)S(1)} %add_convert_fusion), dimensions={1,2} | broadcast | bytes 163840 | tf_op jit(solution)/shard_map/broadcast_in_dim | solution.py:310
  7.6 6.2 %all-to-all-start = ((bf16[4,128,128]{2,1,0:T(8,128)(2,1)}), bf16[4,128,128]{2,1,0:T(8,128)(2,1)S(1)}, u32[]{:S(2)}, u32[]{:S(2)}) async-start(bf16[4,128,128]{2,1,0:T(8,128)(2,1)} %broadcast_in_dim.3), calls=%async_computation | async-start | bytes 262144 | tf_op jit(solution)/shard_map/all_to_all | solution.py:309
  14.4 5.6 %all-to-all-done.parts = bf16[4,128,128]{2,1,0:T(8,128)(2,1)S(1)} async-done(((bf16[4,128,128]{2,1,0:T(8,128)(2,1)}), bf16[4,128,128]{2,1,0:T(8,128)(2,1)S(1)}, u32[]{:S(2)}, u32[]{:S(2)}) %all-to-all-start) | async-done | bytes 131104 | tf_op jit(solution)/shard_map/all_to_all | solution.py:309
  20.0 0.0 copy-done.1
  20.0 3.3 %backward.1 = (f32[4,4096]{1,0:T(4,128)S(1)}, f32[4,4096]{1,0:T(4,128)S(1)}, f32[2,4096]{1,0:T(2,128)S(1)}) custom-call(s32[1]{0:T(128)S(6)} %copy.12.count, f32[1]{0:T(128)S(6)} %copy.13.rho, s32[256]{0:T(256)} %ray_hbm.3, s32[256]{0:T(256)} %voxel_hbm.3, bf16[256,64,128]{2,1,0:T(8,128)(2,1)} %proj_hbm.3, bf16[4,128,128]{2,1,0:T(8,128)(2,1)S(1)} %all-to-all-done.parts, ...), custom_call_target="tpu_custom_call" | custom-call | tf_op jit(solution)/shard_map/backward/pallas_call | solution.py:313
  23.4 0.1 collective-permute-start.1
  23.4 1.2 %collective-permute-done.1.grad_other = f32[4,4096]{1,0:T(4,128)S(1)} collective-permute-done((f32[4,4096]{1,0:T(4,128)S(1)}, f32[4,4096]{1,0:T(4,128)S(1)}, u32[]{:S(2)}, u32[]{:S(2)}) %collective-permute-start.1) | collective-permute-done | bytes 65568 | tf_op jit(solution)/shard_map/ppermute | solution.py:336
  24.7 0.1 maximum_select_fusion
  24.8 1.6 %collective-permute-start.2 = (f32[2,4096]{1,0:T(2,128)S(1)}, f32[2,4096]{1,0:T(2,128)S(1)}, u32[]{:S(2)}, u32[]{:S(2)}) collective-permute-start(f32[2,4096]{1,0:T(2,128)S(1)} %maximum_select_fusion), channel_id=1, source_target_pairs={{0,2},{2,0},{1,3},{3,1},{4,6},{6,4},{5,7},{7,5},{8,10},{10,8},{9,1... | collective-permute-start | bytes 98312 | tf_op jit(solution)/shard_map/ppermute | solution.py:341
  26.3 2.4 %collective-permute-done.2.from_next.from_previous = f32[2,4096]{1,0:T(2,128)S(1)} collective-permute-done((f32[2,4096]{1,0:T(2,128)S(1)}, f32[2,4096]{1,0:T(2,128)S(1)}, u32[]{:S(2)}, u32[]{:S(2)}) %collective-permute-start.2) | collective-permute-done | bytes 32800 | tf_op jit(solution)/shard_map/ppermute | solution.py:341
  28.8 0.0 copy-done
  28.8 0.9 %update.1 = (f32[4,4096]{1,0:T(4,128)}, f32[3,4,4096]{2,1,0:T(4,128)}, f32[3,4,4096]{2,1,0:T(4,128)}) custom-call(f32[4,4096]{1,0:T(4,128)S(1)} %get-tuple-element.12.grad, f32[4,4096]{1,0:T(4,128)S(1)} %collective-permute-done.1.grad_other, f32[2,4096]{1,0:T(2,128)S(1)} %collective-permute-done.2.from_next.from_previous, ...), custom_call_target="tpu_custom_call" | custom-call | tf_op jit(solution)/shard_map/update/pallas_call | solution.py:346
  (2 shorter events, 0.0 us)
Async XLA Ops:
  0.6 19.4 %copy-start.1 = (f32[4,4096]{1,0:T(4,128)S(1)}, f32[4,4096]{1,0:T(4,128)}, u32[]{:S(2)}) copy-start(f32[4,4096]{1,0:T(4,128)} %vol.1) | copy-start | bytes 196612
  1.3 27.4 %copy-start = (f32[3,4,4096]{2,1,0:T(4,128)S(1)}, f32[3,4,4096]{2,1,0:T(4,128)}, u32[]{:S(2)}) copy-start(f32[3,4,4096]{2,1,0:T(4,128)} %dual.1) | copy-start | bytes 589828
  5.5 1.4 %collective-permute-start = (bf16[128,128]{1,0:T(8,128)(2,1)S(1)}, bf16[128,128]{1,0:T(8,128)(2,1)S(1)}, u32[]{:S(2)}, u32[]{:S(2)}) collective-permute-start(bf16[128,128]{1,0:T(8,128)(2,1)S(1)} %get-tuple-element.10), channel_id=1, source_target_pairs={{0,1},{1,0},{2,3},{3,2},{4,5},{5,4},{6,7},{7,6},{8,9},{9,8},{10,11... | collective-permute-start | bytes 98312 | tf_op jit(solution)/shard_map/ppermute | solution.py:307
  7.6 12.5 %all-to-all-start = ((bf16[4,128,128]{2,1,0:T(8,128)(2,1)}), bf16[4,128,128]{2,1,0:T(8,128)(2,1)S(1)}, u32[]{:S(2)}, u32[]{:S(2)}) async-start(bf16[4,128,128]{2,1,0:T(8,128)(2,1)} %broadcast_in_dim.3), calls=%async_computation | async-start | bytes 262144 | tf_op jit(solution)/shard_map/all_to_all | solution.py:309
  23.4 1.3 %collective-permute-start.1 = (f32[4,4096]{1,0:T(4,128)S(1)}, f32[4,4096]{1,0:T(4,128)S(1)}, u32[]{:S(2)}, u32[]{:S(2)}) collective-permute-start(f32[4,4096]{1,0:T(4,128)S(1)} %get-tuple-element.12.grad), channel_id=1, source_target_pairs={{0,1},{1,0},{2,3},{3,2},{4,5},{5,4},{6,7},{7,6},{8,9},{9,8},{10,11... | collective-permute-start | bytes 196616 | tf_op jit(solution)/shard_map/ppermute | solution.py:336
  24.8 4.0 %collective-permute-start.2 = (f32[2,4096]{1,0:T(2,128)S(1)}, f32[2,4096]{1,0:T(2,128)S(1)}, u32[]{:S(2)}, u32[]{:S(2)}) collective-permute-start(f32[2,4096]{1,0:T(2,128)S(1)} %maximum_select_fusion), channel_id=1, source_target_pairs={{0,2},{2,0},{1,3},{3,1},{4,6},{6,4},{5,7},{7,5},{8,10},{10,8},{9,1... | collective-permute-start | bytes 98312 | tf_op jit(solution)/shard_map/ppermute | solution.py:341

commit v7 on v6

--- a/solution.py
+++ b/solution.py
@@ -132,7 +132,7 @@
 
 def backward_kernel(
     count, rho, ray_hbm, voxel_hbm, proj_hbm,
-    parts, vol, adjoint,
+    part, moved, vol, adjoint,
     grad_out, base_out, scale_out,
     ray, voxel, tiles, table, acc0, acc1, acc2, acc3, sems, tile_sems,
 ):
@@ -155,9 +155,7 @@
     low, top = lane < TV, row < 4
     for q in range(rays // 4):
         at = slice(16 * q, 16 * q + 16)
-        total = parts[0, at, :].astype(jnp.float32)
-        for p in range(1, parts.shape[0]):
-            total += parts[p, at, :].astype(jnp.float32)
+        total = part[at, :].astype(jnp.float32) + moved[at, :].astype(jnp.float32)
         for k in range(2):
             x = total[8 * k:8 * k + 8]
             turned = pltpu.roll(x, 4, axis=0)
@@ -304,11 +302,15 @@
     )
 
     swap = [(i, i ^ 1) for i in range(reps)]
-    moved = lax.ppermute(partial, "rep", swap)
-    chip = (partial.astype(f32) + moved.astype(f32)).astype(bf16)
-    parts = lax.all_to_all(
-        jnp.broadcast_to(chip, (group // reps, *chip.shape)), "tile", 0, 0, tiled=True
-    )
+    step = 1
+    while True:
+        moved = lax.ppermute(
+            partial, ("tile", "rep"), [(i, i ^ step) for i in range(group)]
+        )
+        step *= 2
+        if step == group:
+            break
+        partial = (partial.astype(f32) + moved.astype(f32)).astype(bf16)
 
     grad, base, scales = pl.pallas_call(
         backward_kernel,
@@ -317,7 +319,7 @@
             jax.ShapeDtypeStruct((slices, width), f32),
             jax.ShapeDtypeStruct((2, width), f32),
         ),
-        in_specs=[smem()] * 2 + [hbm()] * 3 + [vmem()] * 3,
+        in_specs=[smem()] * 2 + [hbm()] * 3 + [vmem()] * 4,
         out_specs=(vmem(), vmem(), vmem()),
         scratch_shapes=[
             pltpu.SMEM((slots,), jnp.int32),
@@ -331,7 +333,7 @@
         name="backward",
     )(
         tile_count, rho, ray_index, voxel_index, proj_tiles,
-        parts, volume_here, adjoint,
+        partial, moved, volume_here, adjoint,
     )
     grad_other = lax.ppermute(grad, "rep", swap)
     ahead = jnp.concatenate([base[0:1] - TAU * (grad[0:1] + grad_other[0:1]), first], axis=0)

time: 30 us -> 26.6 us (0.89)
  waiting for transfers between devices: 10.1 us -> 7.3 us
  local copies, waits for them, and re-layouts: 0.68 us -> 0.01 us
    all_to_all x1 -> x0, starting transfers between devices: 6.23 us -> none  [shards(): lax.all_to_all(jnp.broadcast_to(chip, (group // reps, *chip.shape)), 'til...]
    ppermute x1 -> x3, starting transfers between devices: 0.52 us -> 6.58 us  [shards(): lax.ppermute(partial, ('tile', 'rep'), [(i, i ^ step) for i in range(grou...]
    all_to_all x1 -> x0, waiting for transfers between devices: 5.59 us -> none  [shards(): lax.all_to_all(jnp.broadcast_to(chip, (group // reps, *chip.shape)), 'til...]
    ppermute x1 -> x3, waiting for transfers between devices: 0.86 us -> 4 us  [shards(): lax.ppermute(partial, ('tile', 'rep'), [(i, i ^ step) for i in range(grou...]
    broadcast_in_dim x1 -> x0, local copies, waits for them, and re-layouts: 0.67 us -> none  [shards(): jnp.broadcast_to(chip, (group // reps, *chip.shape))]
    ppermute x1, starting transfers between devices: 1.56 us -> 1.91 us  [shards(): from_next = from_previous = lax.ppermute(halo, 'slab', [(0, 1), (1, 0)])]
    ppermute x1, waiting for transfers between devices: 2.42 us -> 2.07 us  [shards(): from_next = from_previous = lax.ppermute(halo, 'slab', [(0, 1), (1, 0)])]
  transfers between devices with their start and end apart: 4 -> 5, of which waited for: 4 -> 5; matrix products, arithmetic and copies ran while one was open for 0% -> 0% of each run, Pallas kernels for 0% -> 0%
where the time goes in v7:
time: 26.6 us; the launch traced here: 26.5 us
  starting transfers between devices  8.56 us (32%)
  Pallas kernels  8.44 us (32%)
  waiting for transfers between devices  7.3 us (27%)
  between operations  2.03 us (8%)
    ppermute x3, starting transfers between devices, shards(): lax.ppermute(partial, ('tile', 'rep'), [(i, i ^ step) for i in range(grou...  6.58 us
    pallas_call x1, Pallas kernels, shards(): pl.pallas_call(forward_kernel, out_shape=(jax.ShapeDtypeStruct((rays * sl...  4.17 us
    ppermute x3, waiting for transfers between devices, shards(): lax.ppermute(partial, ('tile', 'rep'), [(i, i ^ step) for i in range(grou...  4 us
    pallas_call x1, Pallas kernels, shards(): pl.pallas_call(backward_kernel, out_shape=(jax.ShapeDtypeStruct((slices,...  3.34 us
    ppermute x1, waiting for transfers between devices, shards(): from_next = from_previous = lax.ppermute(halo, 'slab', [(0, 1), (1, 0)])  2.07 us
    ppermute x1, starting transfers between devices, shards(): from_next = from_previous = lax.ppermute(halo, 'slab', [(0, 1), (1, 0)])  1.91 us
    ppermute x1, waiting for transfers between devices, shards(): grad_other = lax.ppermute(grad, 'rep', swap)  1.23 us
    pallas_call x1, Pallas kernels, shards(): pl.pallas_call(update_kernel, out_shape=(jax.ShapeDtypeStruct((slices, wi...  0.93 us
  transfers between devices with their start and end apart: 5, of which 5 were waited for; matrix products, arithmetic and copies ran while one was open for 0% of the time, Pallas kernels for 0%

profile of v7, /device:TPU:0, one launch (start us, length us, event | category | flops | bytes accessed | tf_op | source)
XLA Modules:
  0.0 26.5 jit_solution(5368648014139211521)
XLA Ops:
  0.6 0.0 copy-start.1
  1.3 0.0 copy-start
  1.3 4.2 %forward.1 = (bf16[128,128]{1,0:T(8,128)(2,1)S(1)}, f32[4,4096]{1,0:T(4,128)S(1)}, f32[1,4096]{1,0:T(1,128)S(1)}, f32[1,4096]{1,0:T(1,128)S(1)}) custom-call(s32[1]{0:T(128)S(6)} %copy.12.count, s32[256]{0:T(256)} %ray_hbm.3, s32[256]{0:T(256)} %voxel_hbm.3, f32[4,4096]{1,0:T(4,128)} %vol.1, f32[3,4,4096]{2,1,0:T(4,128)} %split_hbm.1, f32[3,4,4096]{2,1,0:T(4,128)} %dual.1, ...), custom_call_target="tpu_custom_call" | custom-call | tf_op jit(solution)/shard_map/forward/pallas_call | solution.py:275
  5.5 0.5 %collective-permute-start = (bf16[128,128]{1,0:T(8,128)(2,1)S(1)}, bf16[128,128]{1,0:T(8,128)(2,1)S(1)}, u32[]{:S(2)}, u32[]{:S(2)}) collective-permute-start(bf16[128,128]{1,0:T(8,128)(2,1)S(1)} %get-tuple-element.10), channel_id=1, source_target_pairs={{0,1},{1,0},{4,5},{5,4},{8,9},{9,8},{12,13},{13,12},{2,3},{3,2},{6... | collective-permute-start | bytes 98312 | tf_op jit(solution)/shard_map/ppermute | solution.py:307
  6.0 0.9 %collective-permute-done = bf16[128,128]{1,0:T(8,128)(2,1)S(1)} collective-permute-done((bf16[128,128]{1,0:T(8,128)(2,1)S(1)}, bf16[128,128]{1,0:T(8,128)(2,1)S(1)}, u32[]{:S(2)}, u32[]{:S(2)}) %collective-permute-start) | collective-permute-done | bytes 32800 | tf_op jit(solution)/shard_map/ppermute | solution.py:307
  6.9 3.0 %collective-permute-start.1 = (bf16[128,128]{1,0:T(8,128)(2,1)S(1)}, bf16[128,128]{1,0:T(8,128)(2,1)S(1)}, u32[]{:S(2)}, u32[]{:S(2)}) collective-permute-start(bf16[128,128]{1,0:T(8,128)(2,1)S(1)} %add_convert_fusion.1), channel_id=1, source_target_pairs={{0,4},{1,5},{4,0},{5,1},{8,12},{9,13},{12,8},{13,9},{2,6},{3,7},{6... | collective-permute-start | bytes 98312 | tf_op jit(solution)/shard_map/ppermute | solution.py:307
  9.9 1.9 %collective-permute-done.1 = bf16[128,128]{1,0:T(8,128)(2,1)S(1)} collective-permute-done((bf16[128,128]{1,0:T(8,128)(2,1)S(1)}, bf16[128,128]{1,0:T(8,128)(2,1)S(1)}, u32[]{:S(2)}, u32[]{:S(2)}) %collective-permute-start.1) | collective-permute-done | bytes 32800 | tf_op jit(solution)/shard_map/ppermute | solution.py:307
  11.8 3.1 %collective-permute-start.2 = (bf16[128,128]{1,0:T(8,128)(2,1)S(1)}, bf16[128,128]{1,0:T(8,128)(2,1)S(1)}, u32[]{:S(2)}, u32[]{:S(2)}) collective-permute-start(bf16[128,128]{1,0:T(8,128)(2,1)S(1)} %add_convert_fusion.part), channel_id=1, source_target_pairs={{0,8},{1,9},{4,12},{5,13},{8,0},{9,1},{12,4},{13,5},{2,10},{3,11},... | collective-permute-start | bytes 98312 | tf_op jit(solution)/shard_map/ppermute | solution.py:307
  15.5 1.2 %collective-permute-done.2.moved = bf16[128,128]{1,0:T(8,128)(2,1)S(1)} collective-permute-done((bf16[128,128]{1,0:T(8,128)(2,1)S(1)}, bf16[128,128]{1,0:T(8,128)(2,1)S(1)}, u32[]{:S(2)}, u32[]{:S(2)}) %collective-permute-start.2) | collective-permute-done | bytes 32800 | tf_op jit(solution)/shard_map/ppermute | solution.py:307
  16.8 0.0 copy-done.1
  16.8 3.3 %backward.1 = (f32[4,4096]{1,0:T(4,128)S(1)}, f32[4,4096]{1,0:T(4,128)S(1)}, f32[2,4096]{1,0:T(2,128)S(1)}) custom-call(s32[1]{0:T(128)S(6)} %copy.12.count, f32[1]{0:T(128)S(6)} %copy.13.rho, s32[256]{0:T(256)} %ray_hbm.3, s32[256]{0:T(256)} %voxel_hbm.3, bf16[256,64,128]{2,1,0:T(8,128)(2,1)} %proj_hbm.3, bf16[128,128]{1,0:T(8,128)(2,1)S(1)} %add_convert_fusion.part, ...), custom_call_target="tpu_custom_call" | custom-call | tf_op jit(solution)/shard_map/backward/pallas_call | solution.py:315
  20.1 0.1 collective-permute-start.3
  20.2 1.2 %collective-permute-done.3.grad_other = f32[4,4096]{1,0:T(4,128)S(1)} collective-permute-done((f32[4,4096]{1,0:T(4,128)S(1)}, f32[4,4096]{1,0:T(4,128)S(1)}, u32[]{:S(2)}, u32[]{:S(2)}) %collective-permute-start.3) | collective-permute-done | bytes 65568 | tf_op jit(solution)/shard_map/ppermute | solution.py:338
  21.5 0.1 maximum_select_fusion
  21.5 1.9 %collective-permute-start.4 = (f32[2,4096]{1,0:T(2,128)S(1)}, f32[2,4096]{1,0:T(2,128)S(1)}, u32[]{:S(2)}, u32[]{:S(2)}) collective-permute-start(f32[2,4096]{1,0:T(2,128)S(1)} %maximum_select_fusion), channel_id=1, source_target_pairs={{0,2},{2,0},{1,3},{3,1},{4,6},{6,4},{5,7},{7,5},{8,10},{10,8},{9,1... | collective-permute-start | bytes 98312 | tf_op jit(solution)/shard_map/ppermute | solution.py:343
  23.4 2.1 %collective-permute-done.4.from_next.from_previous = f32[2,4096]{1,0:T(2,128)S(1)} collective-permute-done((f32[2,4096]{1,0:T(2,128)S(1)}, f32[2,4096]{1,0:T(2,128)S(1)}, u32[]{:S(2)}, u32[]{:S(2)}) %collective-permute-start.4) | collective-permute-done | bytes 32800 | tf_op jit(solution)/shard_map/ppermute | solution.py:343
  25.5 0.0 copy-done
  25.5 0.9 %update.1 = (f32[4,4096]{1,0:T(4,128)}, f32[3,4,4096]{2,1,0:T(4,128)}, f32[3,4,4096]{2,1,0:T(4,128)}) custom-call(f32[4,4096]{1,0:T(4,128)S(1)} %get-tuple-element.12.grad, f32[4,4096]{1,0:T(4,128)S(1)} %collective-permute-done.3.grad_other, f32[2,4096]{1,0:T(2,128)S(1)} %collective-permute-done.4.from_next.from_previous, ...), custom_call_target="tpu_custom_call" | custom-call | tf_op jit(solution)/shard_map/update/pallas_call | solution.py:348
  (3 shorter events, 0.1 us)
Async XLA Ops:
  0.6 16.1 %copy-start.1 = (f32[4,4096]{1,0:T(4,128)S(1)}, f32[4,4096]{1,0:T(4,128)}, u32[]{:S(2)}) copy-start(f32[4,4096]{1,0:T(4,128)} %vol.1) | copy-start | bytes 196612
  1.3 24.2 %copy-start = (f32[3,4,4096]{2,1,0:T(4,128)S(1)}, f32[3,4,4096]{2,1,0:T(4,128)}, u32[]{:S(2)}) copy-start(f32[3,4,4096]{2,1,0:T(4,128)} %dual.1) | copy-start | bytes 589828
  5.5 1.4 %collective-permute-start = (bf16[128,128]{1,0:T(8,128)(2,1)S(1)}, bf16[128,128]{1,0:T(8,128)(2,1)S(1)}, u32[]{:S(2)}, u32[]{:S(2)}) collective-permute-start(bf16[128,128]{1,0:T(8,128)(2,1)S(1)} %get-tuple-element.10), channel_id=1, source_target_pairs={{0,1},{1,0},{4,5},{5,4},{8,9},{9,8},{12,13},{13,12},{2,3},{3,2},{6... | collective-permute-start | bytes 98312 | tf_op jit(solution)/shard_map/ppermute | solution.py:307
  6.9 4.9 %collective-permute-start.1 = (bf16[128,128]{1,0:T(8,128)(2,1)S(1)}, bf16[128,128]{1,0:T(8,128)(2,1)S(1)}, u32[]{:S(2)}, u32[]{:S(2)}) collective-permute-start(bf16[128,128]{1,0:T(8,128)(2,1)S(1)} %add_convert_fusion.1), channel_id=1, source_target_pairs={{0,4},{1,5},{4,0},{5,1},{8,12},{9,13},{12,8},{13,9},{2,6},{3,7},{6... | collective-permute-start | bytes 98312 | tf_op jit(solution)/shard_map/ppermute | solution.py:307
  11.8 5.0 %collective-permute-start.2 = (bf16[128,128]{1,0:T(8,128)(2,1)S(1)}, bf16[128,128]{1,0:T(8,128)(2,1)S(1)}, u32[]{:S(2)}, u32[]{:S(2)}) collective-permute-start(bf16[128,128]{1,0:T(8,128)(2,1)S(1)} %add_convert_fusion.part), channel_id=1, source_target_pairs={{0,8},{1,9},{4,12},{5,13},{8,0},{9,1},{12,4},{13,5},{2,10},{3,11},... | collective-permute-start | bytes 98312 | tf_op jit(solution)/shard_map/ppermute | solution.py:307
  20.1 1.3 %collective-permute-start.3 = (f32[4,4096]{1,0:T(4,128)S(1)}, f32[4,4096]{1,0:T(4,128)S(1)}, u32[]{:S(2)}, u32[]{:S(2)}) collective-permute-start(f32[4,4096]{1,0:T(4,128)S(1)} %get-tuple-element.12.grad), channel_id=1, source_target_pairs={{0,1},{1,0},{2,3},{3,2},{4,5},{5,4},{6,7},{7,6},{8,9},{9,8},{10,11... | collective-permute-start | bytes 196616 | tf_op jit(solution)/shard_map/ppermute | solution.py:338
  21.5 4.0 %collective-permute-start.4 = (f32[2,4096]{1,0:T(2,128)S(1)}, f32[2,4096]{1,0:T(2,128)S(1)}, u32[]{:S(2)}, u32[]{:S(2)}) collective-permute-start(f32[2,4096]{1,0:T(2,128)S(1)} %maximum_select_fusion), channel_id=1, source_target_pairs={{0,2},{2,0},{1,3},{3,1},{4,6},{6,4},{5,7},{7,5},{8,10},{10,8},{9,1... | collective-permute-start | bytes 98312 | tf_op jit(solution)/shard_map/ppermute | solution.py:343

commit v8 on v7

--- a/solution.py
+++ b/solution.py
@@ -132,7 +132,7 @@
 
 def backward_kernel(
     count, rho, ray_hbm, voxel_hbm, proj_hbm,
-    part, moved, vol, adjoint,
+    held, shared, vol, adjoint,
     grad_out, base_out, scale_out,
     ray, voxel, tiles, table, acc0, acc1, acc2, acc3, sems, tile_sems,
 ):
@@ -153,9 +153,12 @@
         acc[...] = jnp.zeros_like(acc)
     row, lane = iotas((8, 128))
     low, top = lane < TV, row < 4
+    holder = lax.axis_index("rep") == lax.axis_size("rep") - 1
     for q in range(rays // 4):
         at = slice(16 * q, 16 * q + 16)
-        total = part[at, :].astype(jnp.float32) + moved[at, :].astype(jnp.float32)
+        total = jnp.where(
+            holder, held[at, :].astype(jnp.float32), shared[at, :].astype(jnp.float32)
+        )
         for k in range(2):
             x = total[8 * k:8 * k + 8]
             turned = pltpu.roll(x, 4, axis=0)
@@ -302,15 +305,15 @@
     )
 
     swap = [(i, i ^ 1) for i in range(reps)]
-    step = 1
-    while True:
-        moved = lax.ppermute(
-            partial, ("tile", "rep"), [(i, i ^ step) for i in range(group)]
-        )
+    moved = lax.ppermute(partial, "rep", swap)
+    total = (partial.astype(f32) + moved.astype(f32)).astype(bf16)
+    step = reps
+    while step < group:
+        pairs = [(i, i ^ step if i % reps == reps - 1 else i) for i in range(group)]
+        moved = lax.ppermute(total, ("tile", "rep"), pairs)
+        total = (total.astype(f32) + moved.astype(f32)).astype(bf16)
         step *= 2
-        if step == group:
-            break
-        partial = (partial.astype(f32) + moved.astype(f32)).astype(bf16)
+    shared = lax.ppermute(total, "rep", swap)
 
     grad, base, scales = pl.pallas_call(
         backward_kernel,
@@ -333,7 +336,7 @@
         name="backward",
     )(
         tile_count, rho, ray_index, voxel_index, proj_tiles,
-        partial, moved, volume_here, adjoint,
+        total, shared, volume_here, adjoint,
     )
     grad_other = lax.ppermute(grad, "rep", swap)
     ahead = jnp.concatenate([base[0:1] - TAU * (grad[0:1] + grad_other[0:1]), first], axis=0)

time: 26.6 us -> 29.4 us (1.11)
  starting transfers between devices: 8.56 us -> 14.2 us
  waiting for transfers between devices: 7.3 us -> 4.36 us
    ppermute x3 -> x4, starting transfers between devices: 6.58 us -> 12.2 us  [the longest x1 10.3 us: shards(): shared = lax.ppermute(total, 'rep', swap)]
    ppermute x3 -> x4, waiting for transfers between devices: 4 us -> 1.07 us  [the longest x1 0.86 us: shards(): moved = lax.ppermute(partial, 'rep', swap)]
    ppermute x1, starting transfers between devices: 0.07 us -> 0.43 us  [shards(): grad_other = lax.ppermute(grad, 'rep', swap)]
    ppermute x1, waiting for transfers between devices: 1.23 us -> 0.9 us  [shards(): grad_other = lax.ppermute(grad, 'rep', swap)]
    ppermute x1, starting transfers between devices: 1.91 us -> 1.6 us  [shards(): from_next = from_previous = lax.ppermute(halo, 'slab', [(0, 1), (1, 0)])]
    ppermute x1, waiting for transfers between devices: 2.07 us -> 2.38 us  [shards(): from_next = from_previous = lax.ppermute(halo, 'slab', [(0, 1), (1, 0)])]
  transfers between devices with their start and end apart: 5 -> 6, of which waited for: 5 -> 4; matrix products, arithmetic and copies ran while one was open for 0% -> 0% of each run, Pallas kernels for 0% -> 0%
where the time goes in v8:
time: 29.4 us; the launch traced here: 29.2 us
  starting transfers between devices  14.2 us (48%)
  Pallas kernels  8.39 us (29%)
  waiting for transfers between devices  4.36 us (15%)
  between operations  2.06 us (7%)
    ppermute x1, starting transfers between devices, shards(): shared = lax.ppermute(total, 'rep', swap)  10.3 us
    pallas_call x1, Pallas kernels, shards(): pl.pallas_call(forward_kernel, out_shape=(jax.ShapeDtypeStruct((rays * sl...  4.13 us
    pallas_call x1, Pallas kernels, shards(): pl.pallas_call(backward_kernel, out_shape=(jax.ShapeDtypeStruct((slices,...  3.32 us
    ppermute x1, waiting for transfers between devices, shards(): from_next = from_previous = lax.ppermute(halo, 'slab', [(0, 1), (1, 0)])  2.38 us
    ppermute x1, starting transfers between devices, shards(): from_next = from_previous = lax.ppermute(halo, 'slab', [(0, 1), (1, 0)])  1.6 us
    ppermute x2, starting transfers between devices, shards(): moved = lax.ppermute(total, ('tile', 'rep'), pairs)  1.33 us
    pallas_call x1, Pallas kernels, shards(): pl.pallas_call(update_kernel, out_shape=(jax.ShapeDtypeStruct((slices, wi...  0.93 us
    ppermute x1, waiting for transfers between devices, shards(): grad_other = lax.ppermute(grad, 'rep', swap)  0.9 us
  transfers between devices with their start and end apart: 6, of which 4 were waited for; matrix products, arithmetic and copies ran while one was open for 0% of the time, Pallas kernels for 0%

profile of v8, /device:TPU:0, one launch (start us, length us, event | category | flops | bytes accessed | tf_op | source)
XLA Modules:
  0.0 29.2 jit_solution(12861400964022086498)
XLA Ops:
  0.6 0.0 copy-start.1
  1.3 0.0 copy-start
  1.3 4.1 %forward.1 = (bf16[128,128]{1,0:T(8,128)(2,1)S(1)}, f32[4,4096]{1,0:T(4,128)S(1)}, f32[1,4096]{1,0:T(1,128)S(1)}, f32[1,4096]{1,0:T(1,128)S(1)}) custom-call(s32[1]{0:T(128)S(6)} %copy.12.count, s32[256]{0:T(256)} %ray_hbm.3, s32[256]{0:T(256)} %voxel_hbm.3, f32[4,4096]{1,0:T(4,128)} %vol.1, f32[3,4,4096]{2,1,0:T(4,128)} %split_hbm.1, f32[3,4,4096]{2,1,0:T(4,128)} %dual.1, ...), custom_call_target="tpu_custom_call" | custom-call | tf_op jit(solution)/shard_map/forward/pallas_call | solution.py:278
  5.5 0.6 %collective-permute-start = (bf16[128,128]{1,0:T(8,128)(2,1)S(1)}, bf16[128,128]{1,0:T(8,128)(2,1)S(1)}, u32[]{:S(2)}, u32[]{:S(2)}) collective-permute-start(bf16[128,128]{1,0:T(8,128)(2,1)S(1)} %get-tuple-element.10), channel_id=1, source_target_pairs={{0,1},{1,0},{2,3},{3,2},{4,5},{5,4},{6,7},{7,6},{8,9},{9,8},{10,11... | collective-permute-start | bytes 98312 | tf_op jit(solution)/shard_map/ppermute | solution.py:308
  6.0 0.9 %collective-permute-done = bf16[128,128]{1,0:T(8,128)(2,1)S(1)} collective-permute-done((bf16[128,128]{1,0:T(8,128)(2,1)S(1)}, bf16[128,128]{1,0:T(8,128)(2,1)S(1)}, u32[]{:S(2)}, u32[]{:S(2)}) %collective-permute-start) | collective-permute-done | bytes 32800 | tf_op jit(solution)/shard_map/ppermute | solution.py:308
  6.9 0.7 %collective-permute-start.1 = (bf16[128,128]{1,0:T(8,128)(2,1)S(1)}, bf16[128,128]{1,0:T(8,128)(2,1)S(1)}, u32[]{:S(2)}, u32[]{:S(2)}) collective-permute-start(bf16[128,128]{1,0:T(8,128)(2,1)S(1)} %add_convert_fusion.2), channel_id=1, source_target_pairs={{0,0},{1,5},{4,4},{5,1},{8,8},{9,13},{12,12},{13,9},{2,2},{3,7},{6... | collective-permute-start | bytes 98312 | tf_op jit(solution)/shard_map/ppermute | solution.py:313
  7.6 0.0 collective-permute-done.1
  7.6 0.7 %collective-permute-start.2 = (bf16[128,128]{1,0:T(8,128)(2,1)S(1)}, bf16[128,128]{1,0:T(8,128)(2,1)S(1)}, u32[]{:S(2)}, u32[]{:S(2)}) collective-permute-start(bf16[128,128]{1,0:T(8,128)(2,1)S(1)} %add_convert_fusion.1), channel_id=1, source_target_pairs={{0,0},{1,9},{4,4},{5,13},{8,8},{9,1},{12,12},{13,5},{2,2},{3,11},{... | collective-permute-start | bytes 98312 | tf_op jit(solution)/shard_map/ppermute | solution.py:313
  8.3 0.0 collective-permute-done.2
  8.3 10.3 %collective-permute-start.3 = (bf16[128,128]{1,0:T(8,128)(2,1)S(1)}, bf16[128,128]{1,0:T(8,128)(2,1)S(1)}, u32[]{:S(2)}, u32[]{:S(2)}) collective-permute-start(bf16[128,128]{1,0:T(8,128)(2,1)S(1)} %add_convert_fusion.held), channel_id=1, source_target_pairs={{0,1},{1,0},{2,3},{3,2},{4,5},{5,4},{6,7},{7,6},{8,9},{9,8},{10,11... | collective-permute-start | bytes 98312 | tf_op jit(solution)/shard_map/ppermute | solution.py:316
  19.3 0.2 collective-permute-done.3.shared
  19.5 0.0 copy-done.1
  19.5 3.3 %backward.1 = (f32[4,4096]{1,0:T(4,128)S(1)}, f32[4,4096]{1,0:T(4,128)S(1)}, f32[2,4096]{1,0:T(2,128)S(1)}) custom-call(s32[1]{0:T(128)S(6)} %copy.12.count, f32[1]{0:T(128)S(6)} %copy.13.rho, s32[256]{0:T(256)} %ray_hbm.3, s32[256]{0:T(256)} %voxel_hbm.3, bf16[256,64,128]{2,1,0:T(8,128)(2,1)} %proj_hbm.3, bf16[128,128]{1,0:T(8,128)(2,1)S(1)} %add_convert_fusion.held, ...), custom_call_target="tpu_custom_call" | custom-call | tf_op jit(solution)/shard_map/backward/pallas_call | solution.py:318
  22.8 0.4 %collective-permute-start.4 = (f32[4,4096]{1,0:T(4,128)S(1)}, f32[4,4096]{1,0:T(4,128)S(1)}, u32[]{:S(2)}, u32[]{:S(2)}) collective-permute-start(f32[4,4096]{1,0:T(4,128)S(1)} %get-tuple-element.12.grad), channel_id=1, source_target_pairs={{0,1},{1,0},{2,3},{3,2},{4,5},{5,4},{6,7},{7,6},{8,9},{9,8},{10,11... | collective-permute-start | bytes 196616 | tf_op jit(solution)/shard_map/ppermute | solution.py:341
  23.3 0.9 %collective-permute-done.4.grad_other = f32[4,4096]{1,0:T(4,128)S(1)} collective-permute-done((f32[4,4096]{1,0:T(4,128)S(1)}, f32[4,4096]{1,0:T(4,128)S(1)}, u32[]{:S(2)}, u32[]{:S(2)}) %collective-permute-start.4) | collective-permute-done | bytes 65568 | tf_op jit(solution)/shard_map/ppermute | solution.py:341
  24.2 0.1 maximum_select_fusion
  24.3 1.6 %collective-permute-start.5 = (f32[2,4096]{1,0:T(2,128)S(1)}, f32[2,4096]{1,0:T(2,128)S(1)}, u32[]{:S(2)}, u32[]{:S(2)}) collective-permute-start(f32[2,4096]{1,0:T(2,128)S(1)} %maximum_select_fusion), channel_id=1, source_target_pairs={{0,2},{2,0},{1,3},{3,1},{4,6},{6,4},{5,7},{7,5},{8,10},{10,8},{9,1... | collective-permute-start | bytes 98312 | tf_op jit(solution)/shard_map/ppermute | solution.py:346
  25.9 2.4 %collective-permute-done.5.from_next.from_previous = f32[2,4096]{1,0:T(2,128)S(1)} collective-permute-done((f32[2,4096]{1,0:T(2,128)S(1)}, f32[2,4096]{1,0:T(2,128)S(1)}, u32[]{:S(2)}, u32[]{:S(2)}) %collective-permute-start.5) | collective-permute-done | bytes 32800 | tf_op jit(solution)/shard_map/ppermute | solution.py:346
  28.2 0.0 copy-done
  28.3 0.9 %update.1 = (f32[4,4096]{1,0:T(4,128)}, f32[3,4,4096]{2,1,0:T(4,128)}, f32[3,4,4096]{2,1,0:T(4,128)}) custom-call(f32[4,4096]{1,0:T(4,128)S(1)} %get-tuple-element.12.grad, f32[4,4096]{1,0:T(4,128)S(1)} %collective-permute-done.4.grad_other, f32[2,4096]{1,0:T(2,128)S(1)} %collective-permute-done.5.from_next.from_previous, ...), custom_call_target="tpu_custom_call" | custom-call | tf_op jit(solution)/shard_map/update/pallas_call | solution.py:351
  (4 shorter events, 0.1 us)
Async XLA Ops:
  0.6 18.9 %copy-start.1 = (f32[4,4096]{1,0:T(4,128)S(1)}, f32[4,4096]{1,0:T(4,128)}, u32[]{:S(2)}) copy-start(f32[4,4096]{1,0:T(4,128)} %vol.1) | copy-start | bytes 196612
  1.3 26.9 %copy-start = (f32[3,4,4096]{2,1,0:T(4,128)S(1)}, f32[3,4,4096]{2,1,0:T(4,128)}, u32[]{:S(2)}) copy-start(f32[3,4,4096]{2,1,0:T(4,128)} %dual.1) | copy-start | bytes 589828
  5.5 1.4 %collective-permute-start = (bf16[128,128]{1,0:T(8,128)(2,1)S(1)}, bf16[128,128]{1,0:T(8,128)(2,1)S(1)}, u32[]{:S(2)}, u32[]{:S(2)}) collective-permute-start(bf16[128,128]{1,0:T(8,128)(2,1)S(1)} %get-tuple-element.10), channel_id=1, source_target_pairs={{0,1},{1,0},{2,3},{3,2},{4,5},{5,4},{6,7},{7,6},{8,9},{9,8},{10,11... | collective-permute-start | bytes 98312 | tf_op jit(solution)/shard_map/ppermute | solution.py:308
  6.9 0.7 %collective-permute-start.1 = (bf16[128,128]{1,0:T(8,128)(2,1)S(1)}, bf16[128,128]{1,0:T(8,128)(2,1)S(1)}, u32[]{:S(2)}, u32[]{:S(2)}) collective-permute-start(bf16[128,128]{1,0:T(8,128)(2,1)S(1)} %add_convert_fusion.2), channel_id=1, source_target_pairs={{0,0},{1,5},{4,4},{5,1},{8,8},{9,13},{12,12},{13,9},{2,2},{3,7},{6... | collective-permute-start | bytes 98312 | tf_op jit(solution)/shard_map/ppermute | solution.py:313
  7.6 0.7 %collective-permute-start.2 = (bf16[128,128]{1,0:T(8,128)(2,1)S(1)}, bf16[128,128]{1,0:T(8,128)(2,1)S(1)}, u32[]{:S(2)}, u32[]{:S(2)}) collective-permute-start(bf16[128,128]{1,0:T(8,128)(2,1)S(1)} %add_convert_fusion.1), channel_id=1, source_target_pairs={{0,0},{1,9},{4,4},{5,13},{8,8},{9,1},{12,12},{13,5},{2,2},{3,11},{... | collective-permute-start | bytes 98312 | tf_op jit(solution)/shard_map/ppermute | solution.py:313
  8.3 11.2 %collective-permute-start.3 = (bf16[128,128]{1,0:T(8,128)(2,1)S(1)}, bf16[128,128]{1,0:T(8,128)(2,1)S(1)}, u32[]{:S(2)}, u32[]{:S(2)}) collective-permute-start(bf16[128,128]{1,0:T(8,128)(2,1)S(1)} %add_convert_fusion.held), channel_id=1, source_target_pairs={{0,1},{1,0},{2,3},{3,2},{4,5},{5,4},{6,7},{7,6},{8,9},{9,8},{10,11... | collective-permute-start | bytes 98312 | tf_op jit(solution)/shard_map/ppermute | solution.py:316
  22.8 1.3 %collective-permute-start.4 = (f32[4,4096]{1,0:T(4,128)S(1)}, f32[4,4096]{1,0:T(4,128)S(1)}, u32[]{:S(2)}, u32[]{:S(2)}) collective-permute-start(f32[4,4096]{1,0:T(4,128)S(1)} %get-tuple-element.12.grad), channel_id=1, source_target_pairs={{0,1},{1,0},{2,3},{3,2},{4,5},{5,4},{6,7},{7,6},{8,9},{9,8},{10,11... | collective-permute-start | bytes 196616 | tf_op jit(solution)/shard_map/ppermute | solution.py:341
  24.3 4.0 %collective-permute-start.5 = (f32[2,4096]{1,0:T(2,128)S(1)}, f32[2,4096]{1,0:T(2,128)S(1)}, u32[]{:S(2)}, u32[]{:S(2)}) collective-permute-start(f32[2,4096]{1,0:T(2,128)S(1)} %maximum_select_fusion), channel_id=1, source_target_pairs={{0,2},{2,0},{1,3},{3,1},{4,6},{6,4},{5,7},{7,5},{8,10},{10,8},{9,1... | collective-permute-start | bytes 98312 | tf_op jit(solution)/shard_map/ppermute | solution.py:346

commit v9 on v7

--- a/solution.py
+++ b/solution.py
@@ -34,14 +34,26 @@
     return (lane % TV) // 8 < 7, lane % 8 < 7
 
 
+def rows8(start):
+    return pl.ds(pl.multiple_of(start, 8), 8)
+
+
+def add_rows(accs, starts, values):
+    held = [acc[rows8(start), :] for acc, start in zip(accs, starts)]
+    for acc, start, old, value in zip(accs, starts, held, values):
+        acc[rows8(start), :] = old + value
+
+
 def forward_kernel(
     count, ray_hbm, voxel_hbm, vol_hbm, split_hbm, dual_hbm, sino_hbm, proj_hbm,
-    partial_out, adjoint_out, edge_out, first_out,
-    ray, voxel, vol, split, dual, sino, tiles, double, table, acc0, acc1, acc2, acc3,
+    partial_out, adjoint_out, edge_out, first_out, index_out, tiles,
+    ray, voxel, index, vol, split, dual, sino, double, table, acc0, acc1, acc2, acc3,
     sems, tile_sems,
 ):
     slots = proj_hbm.shape[0]
-    rays = acc0.shape[0] - 1
+    lines = ray.shape[0]
+    rays = acc0.shape[0] // 8 - 1
+    voxel_tiles = table.shape[0] // 8
     owned = sino.shape[0]
     width = vol.shape[1]
     loads = [
@@ -73,14 +85,26 @@
         first = jnp.where(jnp.logical_and(top, low), x, zero)
         second = jnp.where(jnp.logical_and(top, low), turned, zero)
         other = jnp.logical_not(jnp.logical_or(top, low))
-        table[2 * j] = jnp.where(other, turned, first)
-        table[2 * j + 1] = jnp.where(other, x, second)
-
-    for load in loads[1:]:
+        table[16 * j:16 * j + 8, :] = jnp.where(other, turned, first)
+        table[16 * j + 8:16 * j + 16, :] = jnp.where(other, x, second)
+
+    loads[1].wait()
+    loads[2].wait()
+    line, place = iotas((lines, 128))
+    live = 128 * line + place < count[0]
+    rays8, voxels8 = ray[...] * 8, voxel[...] * 8
+    index_out[0:lines, :] = voxels8
+    index_out[lines:2 * lines, :] = jnp.where(live, rays8, rays * 8)
+    index_out[2 * lines:3 * lines, :] = rays8
+    index_out[3 * lines:4 * lines, :] = jnp.where(live, voxels8, voxel_tiles * 8)
+    to_scalar = pltpu.make_async_copy(index_out, index, sems.at[6])
+    to_scalar.start()
+
+    for load in loads[3:]:
         load.wait()
     mine = (lax.axis_index("tile") * lax.axis_size("rep") + lax.axis_index("rep")) * owned
     for r in range(owned):
-        acc0[mine + r, 0:4, :] = -sino[r]
+        acc0[pl.ds(pl.multiple_of((mine + r) * 8, 8), 4), :] = -sino[r]
     row_mask, col_mask = plane_masks(lane)
     for j in range(width // 128):
         at = slice(128 * j, 128 * j + 128)
@@ -98,15 +122,15 @@
         edge_out[:, at] = (x - gap[0])[3:4]
         first_out[:, at] = x[0:1]
 
-    used = count[0]
+    to_scalar.wait()
     per = slots // CHUNKS
     for g in range(slots // GROUP):
         if GROUP * g % per == 0:
             copies[GROUP * g // per].wait()
         n = GROUP * g
-        pairs = [
-            jnp.where(top, table[voxel[n + 2 * i]], table[voxel[n + 2 * i + 1]]) for i in range(2)
-        ]
+        at = [divmod(n + i, 128) for i in range(GROUP)]
+        picked = [table[rows8(index[line, place]), :] for line, place in at]
+        pairs = [jnp.where(top, picked[2 * i], picked[2 * i + 1]) for i in range(2)]
         zero = jnp.zeros_like(pairs[0])
         left = jnp.concatenate([pairs[0], zero], axis=0).astype(jnp.bfloat16)
         right = jnp.concatenate([zero, pairs[1]], axis=0).astype(jnp.bfloat16)
@@ -115,14 +139,17 @@
             tiles[n:n + GROUP].reshape(GROUP * TV, TR),
             preferred_element_type=jnp.float32,
         )
-        for i in range(GROUP):
-            at = jnp.where(n + i < used, ray[n + i], rays)
-            accs[i][at] += sums[8 * (i // 2):8 * (i // 2) + 8]
+        add_rows(
+            accs,
+            [index[lines + line, place] for line, place in at],
+            [sums[0:8], sums[0:8], sums[8:16], sums[8:16]],
+        )
     for q in range(rays // 4):
         halves = []
         for r in (4 * q, 4 * q + 2):
-            even = [acc0[r + k] + acc2[r + k] for k in range(2)]
-            odd = [acc1[r + k] + acc3[r + k] for k in range(2)]
+            at = [slice(8 * (r + k), 8 * (r + k) + 8) for k in range(2)]
+            even = [acc0[at[k], :] + acc2[at[k], :] for k in range(2)]
+            odd = [acc1[at[k], :] + acc3[at[k], :] for k in range(2)]
             halves.append(
                 jnp.where(top, even[0], odd[1])
                 + pltpu.roll(jnp.where(top, even[1], odd[0]), 4, axis=0)
@@ -131,23 +158,16 @@
 
 
 def backward_kernel(
-    count, rho, ray_hbm, voxel_hbm, proj_hbm,
-    part, moved, vol, adjoint,
+    rho, indices, tiles, part, moved, vol, adjoint,
     grad_out, base_out, scale_out,
-    ray, voxel, tiles, table, acc0, acc1, acc2, acc3, sems, tile_sems,
+    index, table, acc0, acc1, acc2, acc3, sem,
 ):
-    slots = proj_hbm.shape[0]
-    rays = table.shape[0]
-    voxel_tiles = acc0.shape[0] - 1
-    loads = [
-        pltpu.make_async_copy(source, target, sems.at[i])
-        for i, (source, target) in enumerate(
-            [(voxel_hbm, voxel), (ray_hbm, ray)]
-        )
-    ]
-    for load in loads:
-        load.start()
-    copies = start_tiles(proj_hbm, tiles, tile_sems)
+    slots = tiles.shape[0]
+    lines = indices.shape[0] // 4
+    rays = table.shape[0] // 8
+    voxel_tiles = acc0.shape[0] // 8 - 1
+    to_scalar = pltpu.make_async_copy(indices, index, sem)
+    to_scalar.start()
     accs = (acc0, acc1, acc2, acc3)
     for acc in accs:
         acc[...] = jnp.zeros_like(acc)
@@ -159,11 +179,10 @@
         for k in range(2):
             x = total[8 * k:8 * k + 8]
             turned = pltpu.roll(x, 4, axis=0)
-            table[4 * q + 2 * k] = jnp.where(top, x, turned)
-            table[4 * q + 2 * k + 1] = jnp.where(top, turned, x)
-
-    for load in loads:
-        load.wait()
+            r = 8 * (4 * q + 2 * k)
+            table[r:r + 8, :] = jnp.where(top, x, turned)
+            table[r + 8:r + 16, :] = jnp.where(top, turned, x)
+
     factor = TAU * rho[0]
     limit = 1.0 / rho[0]
     for j in range(voxel_tiles // 2):
@@ -172,18 +191,13 @@
         scale_out[0:1, at] = jnp.full((1, 128), limit, jnp.float32)
         scale_out[1:2, at] = jnp.full((1, 128), factor, jnp.float32)
 
-    used = count[0]
-    per = slots // CHUNKS
+    to_scalar.wait()
     for g in range(slots // GROUP):
-        if GROUP * g % per == 0:
-            copies[GROUP * g // per].wait()
         n = GROUP * g
+        at = [divmod(n + i, 128) for i in range(GROUP)]
+        picked = [table[rows8(index[2 * lines + line, place]), :] for line, place in at]
         rows = jnp.concatenate(
-            [
-                jnp.where(top, table[ray[n + 2 * i]], table[ray[n + 2 * i + 1]])
-                for i in range(GROUP // 2)
-            ],
-            axis=0,
+            [jnp.where(top, picked[2 * i], picked[2 * i + 1]) for i in range(2)], axis=0
         )
         back = lax.dot_general(
             rows.astype(jnp.bfloat16),
@@ -191,18 +205,18 @@
             (((1,), (1,)), ((), ())),
             preferred_element_type=jnp.float32,
         )
-        for i in range(GROUP):
-            at = jnp.where(n + i < used, voxel[n + i], voxel_tiles)
-            k = i // 2
-            accs[i][at] += back[8 * k:8 * k + 8, 128 * k:128 * k + 128]
+        add_rows(
+            accs,
+            [index[3 * lines + line, place] for line, place in at],
+            [back[8 * k:8 * k + 8, 128 * k:128 * k + 128] for k in (0, 0, 1, 1)],
+        )
     for j in range(voxel_tiles // 2):
-        at = slice(128 * j, 128 * j + 128)
-        even = [acc0[2 * j + k] + acc2[2 * j + k] for k in range(2)]
-        odd = [acc1[2 * j + k] + acc3[2 * j + k] for k in range(2)]
+        at = [slice(16 * j + 8 * k, 16 * j + 8 * k + 8) for k in range(2)]
+        even = [acc0[at[k], :] + acc2[at[k], :] for k in range(2)]
+        odd = [acc1[at[k], :] + acc3[at[k], :] for k in range(2)]
         turned = pltpu.roll(jnp.where(top, even[1], odd[0]), TV, axis=1)
         both = jnp.where(top == low, jnp.where(top, even[0], odd[1]), turned)
-        grad = (both + pltpu.roll(both, 4, axis=0))[0:4]
-        grad_out[:, at] = grad
+        grad_out[:, 128 * j:128 * j + 128] = (both + pltpu.roll(both, 4, axis=0))[0:4]
 
 
 def update_kernel(
@@ -265,6 +279,8 @@
     rays = owned * group
     voxel_tiles = width // TV
     volume_here, dual_here = volume, dual_var
+    lines = slots // 128
+    ray_index, voxel_index = ray_index.reshape(lines, 128), voxel_index.reshape(lines, 128)
     volume, split_var, dual_var, sinogram, proj_tiles, ray_index, voxel_index = (
         pltpu.with_memory_space_constraint(x, pltpu.HBM)
         for x in (
@@ -272,34 +288,34 @@
         )
     )
 
-    partial, adjoint, edge, first = pl.pallas_call(
+    partial, adjoint, edge, first, indices, tiles = pl.pallas_call(
         forward_kernel,
         out_shape=(
             jax.ShapeDtypeStruct((rays * slices, TR), bf16),
             jax.ShapeDtypeStruct((slices, width), f32),
             jax.ShapeDtypeStruct((1, width), f32),
             jax.ShapeDtypeStruct((1, width), f32),
+            jax.ShapeDtypeStruct((4 * lines, 128), jnp.int32),
+            jax.ShapeDtypeStruct(proj_tiles.shape, bf16),
         ),
         in_specs=[smem()] + [hbm()] * 7,
-        out_specs=(vmem(),) * 4,
+        out_specs=(vmem(),) * 6,
         scratch_shapes=[
-            pltpu.SMEM((slots,), jnp.int32),
-            pltpu.SMEM((slots,), jnp.int32),
+            pltpu.VMEM((lines, 128), jnp.int32),
+            pltpu.VMEM((lines, 128), jnp.int32),
+            pltpu.SMEM((4 * lines, 128), jnp.int32),
             pltpu.VMEM((slices, width), f32),
             pltpu.VMEM((3, slices, width), f32),
             pltpu.VMEM((3, slices, width), f32),
             pltpu.VMEM(sinogram.shape, f32),
-            pltpu.VMEM(proj_tiles.shape, bf16),
             pltpu.VMEM((8, width), f32),
-            pltpu.VMEM((voxel_tiles, 8, 128), f32),
+            pltpu.VMEM((voxel_tiles * 8, 128), f32),
         ]
-        + [pltpu.VMEM((rays + 1, 8, 128), f32)] * 4
-        + [pltpu.SemaphoreType.DMA((6,)), pltpu.SemaphoreType.DMA((CHUNKS,))],
+        + [pltpu.VMEM((rays * 8 + 8, 128), f32)] * 4
+        + [pltpu.SemaphoreType.DMA((7,)), pltpu.SemaphoreType.DMA((CHUNKS,))],
         compiler_params=params(),
         name="forward",
-    )(
-        tile_count, ray_index, voxel_index, volume, split_var, dual_var, sinogram, proj_tiles
-    )
+    )(tile_count, ray_index, voxel_index, volume, split_var, dual_var, sinogram, proj_tiles)
 
     swap = [(i, i ^ 1) for i in range(reps)]
     step = 1
@@ -319,22 +335,17 @@
             jax.ShapeDtypeStruct((slices, width), f32),
             jax.ShapeDtypeStruct((2, width), f32),
         ),
-        in_specs=[smem()] * 2 + [hbm()] * 3 + [vmem()] * 4,
+        in_specs=[smem()] + [vmem()] * 6,
         out_specs=(vmem(), vmem(), vmem()),
         scratch_shapes=[
-            pltpu.SMEM((slots,), jnp.int32),
-            pltpu.SMEM((slots,), jnp.int32),
-            pltpu.VMEM(proj_tiles.shape, bf16),
-            pltpu.VMEM((rays, 8, 128), f32),
+            pltpu.SMEM((4 * lines, 128), jnp.int32),
+            pltpu.VMEM((rays * 8, 128), f32),
         ]
-        + [pltpu.VMEM((voxel_tiles + 1, 8, 128), f32)] * 4
-        + [pltpu.SemaphoreType.DMA((2,)), pltpu.SemaphoreType.DMA((CHUNKS,))],
+        + [pltpu.VMEM((voxel_tiles * 8 + 8, 128), f32)] * 4
+        + [pltpu.SemaphoreType.DMA],
         compiler_params=params(),
         name="backward",
-    )(
-        tile_count, rho, ray_index, voxel_index, proj_tiles,
-        partial, moved, volume_here, adjoint,
-    )
+    )(rho, indices, tiles, partial, moved, volume_here, adjoint)
     grad_other = lax.ppermute(grad, "rep", swap)
     ahead = jnp.concatenate([base[0:1] - TAU * (grad[0:1] + grad_other[0:1]), first], axis=0)
     behind = jnp.concatenate([edge, edge], axis=0)

time: 26.6 us -> 25.3 us (0.951)
  Pallas kernels: 8.44 us -> 7.08 us
    pallas_call x1, Pallas kernels: 3.34 us -> 1.95 us  [shards(): pl.pallas_call(backward_kernel, out_shape=(jax.ShapeDtypeStruct((slices,...]
where the time goes in v9:
time: 25.3 us; the launch traced here: 25.1 us
  starting transfers between devices  8.56 us (34%)
  waiting for transfers between devices  7.35 us (29%)
  Pallas kernels  7.08 us (28%)
  between operations  2.03 us (8%)
    ppermute x3, starting transfers between devices, shards(): lax.ppermute(partial, ('tile', 'rep'), [(i, i ^ step) for i in range(grou...  6.63 us
    pallas_call x1, Pallas kernels, shards(): pl.pallas_call(forward_kernel, out_shape=(jax.ShapeDtypeStruct((rays * sl...  4.2 us
    ppermute x3, waiting for transfers between devices, shards(): lax.ppermute(partial, ('tile', 'rep'), [(i, i ^ step) for i in range(grou...  4 us
    ppermute x1, waiting for transfers between devices, shards(): from_next = from_previous = lax.ppermute(halo, 'slab', [(0, 1), (1, 0)])  2.12 us
    pallas_call x1, Pallas kernels, shards(): pl.pallas_call(backward_kernel, out_shape=(jax.ShapeDtypeStruct((slices,...  1.95 us
    ppermute x1, starting transfers between devices, shards(): from_next = from_previous = lax.ppermute(halo, 'slab', [(0, 1), (1, 0)])  1.86 us
    ppermute x1, waiting for transfers between devices, shards(): grad_other = lax.ppermute(grad, 'rep', swap)  1.23 us
    pallas_call x1, Pallas kernels, shards(): pl.pallas_call(update_kernel, out_shape=(jax.ShapeDtypeStruct((slices, wi...  0.93 us
  transfers between devices with their start and end apart: 5, of which 5 were waited for; matrix products, arithmetic and copies ran while one was open for 0% of the time, Pallas kernels for 0%

profile of v9, /device:TPU:0, one launch (start us, length us, event | category | flops | bytes accessed | tf_op | source)
XLA Modules:
  0.0 25.1 jit_solution(16359299671290411494)
XLA Ops:
  0.6 0.0 copy-start.1
  1.3 0.0 copy-start
  1.3 4.2 %forward.1 = (bf16[128,128]{1,0:T(8,128)(2,1)S(1)}, f32[4,4096]{1,0:T(4,128)S(1)}, f32[1,4096]{1,0:T(1,128)S(1)}, f32[1,4096]{1,0:T(1,128)S(1)}, s32[8,128]{1,0:...) custom-call(s32[1]{0:T(128)S(6)} %copy.12.count, s32[2,128]{1,0:T(2,128)} %bitcast.2, s32[2,128]{1,0:T(2,128)} %bitcast.3, ...), custom_call_target="tpu_custom_call" | custom-call | tf_op jit(solution)/shard_map/forward/pallas_call | solution.py:291
  5.5 0.5 %collective-permute-start = (bf16[128,128]{1,0:T(8,128)(2,1)S(1)}, bf16[128,128]{1,0:T(8,128)(2,1)S(1)}, u32[]{:S(2)}, u32[]{:S(2)}) collective-permute-start(bf16[128,128]{1,0:T(8,128)(2,1)S(1)} %get-tuple-element.14), channel_id=1, source_target_pairs={{0,1},{1,0},{4,5},{5,4},{8,9},{9,8},{12,13},{13,12},{2,3},{3,2},{6... | collective-permute-start | bytes 98312 | tf_op jit(solution)/shard_map/ppermute | solution.py:323
  6.1 0.9 %collective-permute-done = bf16[128,128]{1,0:T(8,128)(2,1)S(1)} collective-permute-done((bf16[128,128]{1,0:T(8,128)(2,1)S(1)}, bf16[128,128]{1,0:T(8,128)(2,1)S(1)}, u32[]{:S(2)}, u32[]{:S(2)}) %collective-permute-start) | collective-permute-done | bytes 32800 | tf_op jit(solution)/shard_map/ppermute | solution.py:323
  6.9 3.0 %collective-permute-start.1 = (bf16[128,128]{1,0:T(8,128)(2,1)S(1)}, bf16[128,128]{1,0:T(8,128)(2,1)S(1)}, u32[]{:S(2)}, u32[]{:S(2)}) collective-permute-start(bf16[128,128]{1,0:T(8,128)(2,1)S(1)} %add_convert_fusion.1), channel_id=1, source_target_pairs={{0,4},{1,5},{4,0},{5,1},{8,12},{9,13},{12,8},{13,9},{2,6},{3,7},{6... | collective-permute-start | bytes 98312 | tf_op jit(solution)/shard_map/ppermute | solution.py:323
  9.9 1.9 %collective-permute-done.1 = bf16[128,128]{1,0:T(8,128)(2,1)S(1)} collective-permute-done((bf16[128,128]{1,0:T(8,128)(2,1)S(1)}, bf16[128,128]{1,0:T(8,128)(2,1)S(1)}, u32[]{:S(2)}, u32[]{:S(2)}) %collective-permute-start.1) | collective-permute-done | bytes 32800 | tf_op jit(solution)/shard_map/ppermute | solution.py:323
  11.8 3.1 %collective-permute-start.2 = (bf16[128,128]{1,0:T(8,128)(2,1)S(1)}, bf16[128,128]{1,0:T(8,128)(2,1)S(1)}, u32[]{:S(2)}, u32[]{:S(2)}) collective-permute-start(bf16[128,128]{1,0:T(8,128)(2,1)S(1)} %add_convert_fusion.part), channel_id=1, source_target_pairs={{0,8},{1,9},{4,12},{5,13},{8,0},{9,1},{12,4},{13,5},{2,10},{3,11},... | collective-permute-start | bytes 98312 | tf_op jit(solution)/shard_map/ppermute | solution.py:323
  15.6 1.2 %collective-permute-done.2.moved = bf16[128,128]{1,0:T(8,128)(2,1)S(1)} collective-permute-done((bf16[128,128]{1,0:T(8,128)(2,1)S(1)}, bf16[128,128]{1,0:T(8,128)(2,1)S(1)}, u32[]{:S(2)}, u32[]{:S(2)}) %collective-permute-start.2) | collective-permute-done | bytes 32800 | tf_op jit(solution)/shard_map/ppermute | solution.py:323
  16.8 0.0 copy-done.1
  16.8 1.9 %backward.1 = (f32[4,4096]{1,0:T(4,128)S(1)}, f32[4,4096]{1,0:T(4,128)S(1)}, f32[2,4096]{1,0:T(2,128)S(1)}) custom-call(f32[1]{0:T(128)S(6)} %copy.13.rho, s32[8,128]{1,0:T(8,128)S(1)} %get-tuple-element.12.indices, bf16[256,64,128]{2,1,0:T(8,128)(2,1)S(1)} %get-tuple-element.13.tiles, bf16[128,128]{1,0:T(8,128)(2,1)S(1)} %add_convert_fusion.part, ...), custom_call_target="tpu_custom_call" | custom-call | tf_op jit(solution)/shard_map/backward/pallas_call | solution.py:331
  18.8 0.1 collective-permute-start.3
  18.9 1.2 %collective-permute-done.3.grad_other = f32[4,4096]{1,0:T(4,128)S(1)} collective-permute-done((f32[4,4096]{1,0:T(4,128)S(1)}, f32[4,4096]{1,0:T(4,128)S(1)}, u32[]{:S(2)}, u32[]{:S(2)}) %collective-permute-start.3) | collective-permute-done | bytes 65568 | tf_op jit(solution)/shard_map/ppermute | solution.py:349
  20.2 0.1 maximum_select_fusion
  20.2 1.9 %collective-permute-start.4 = (f32[2,4096]{1,0:T(2,128)S(1)}, f32[2,4096]{1,0:T(2,128)S(1)}, u32[]{:S(2)}, u32[]{:S(2)}) collective-permute-start(f32[2,4096]{1,0:T(2,128)S(1)} %maximum_select_fusion), channel_id=1, source_target_pairs={{0,2},{2,0},{1,3},{3,1},{4,6},{6,4},{5,7},{7,5},{8,10},{10,8},{9,1... | collective-permute-start | bytes 98312 | tf_op jit(solution)/shard_map/ppermute | solution.py:354
  22.1 2.1 %collective-permute-done.4.from_next.from_previous = f32[2,4096]{1,0:T(2,128)S(1)} collective-permute-done((f32[2,4096]{1,0:T(2,128)S(1)}, f32[2,4096]{1,0:T(2,128)S(1)}, u32[]{:S(2)}, u32[]{:S(2)}) %collective-permute-start.4) | collective-permute-done | bytes 32800 | tf_op jit(solution)/shard_map/ppermute | solution.py:354
  24.2 0.0 copy-done
  24.2 0.9 %update.1 = (f32[4,4096]{1,0:T(4,128)}, f32[3,4,4096]{2,1,0:T(4,128)}, f32[3,4,4096]{2,1,0:T(4,128)}) custom-call(f32[4,4096]{1,0:T(4,128)S(1)} %get-tuple-element.16.grad, f32[4,4096]{1,0:T(4,128)S(1)} %collective-permute-done.3.grad_other, f32[2,4096]{1,0:T(2,128)S(1)} %collective-permute-done.4.from_next.from_previous, ...), custom_call_target="tpu_custom_call" | custom-call | tf_op jit(solution)/shard_map/update/pallas_call | solution.py:359
  (3 shorter events, 0.1 us)
Async XLA Ops:
  0.6 16.2 %copy-start.1 = (f32[4,4096]{1,0:T(4,128)S(1)}, f32[4,4096]{1,0:T(4,128)}, u32[]{:S(2)}) copy-start(f32[4,4096]{1,0:T(4,128)} %vol.1) | copy-start | bytes 196612
  1.3 22.9 %copy-start = (f32[3,4,4096]{2,1,0:T(4,128)S(1)}, f32[3,4,4096]{2,1,0:T(4,128)}, u32[]{:S(2)}) copy-start(f32[3,4,4096]{2,1,0:T(4,128)} %dual.1) | copy-start | bytes 589828
  5.5 1.4 %collective-permute-start = (bf16[128,128]{1,0:T(8,128)(2,1)S(1)}, bf16[128,128]{1,0:T(8,128)(2,1)S(1)}, u32[]{:S(2)}, u32[]{:S(2)}) collective-permute-start(bf16[128,128]{1,0:T(8,128)(2,1)S(1)} %get-tuple-element.14), channel_id=1, source_target_pairs={{0,1},{1,0},{4,5},{5,4},{8,9},{9,8},{12,13},{13,12},{2,3},{3,2},{6... | collective-permute-start | bytes 98312 | tf_op jit(solution)/shard_map/ppermute | solution.py:323
  6.9 4.9 %collective-permute-start.1 = (bf16[128,128]{1,0:T(8,128)(2,1)S(1)}, bf16[128,128]{1,0:T(8,128)(2,1)S(1)}, u32[]{:S(2)}, u32[]{:S(2)}) collective-permute-start(bf16[128,128]{1,0:T(8,128)(2,1)S(1)} %add_convert_fusion.1), channel_id=1, source_target_pairs={{0,4},{1,5},{4,0},{5,1},{8,12},{9,13},{12,8},{13,9},{2,6},{3,7},{6... | collective-permute-start | bytes 98312 | tf_op jit(solution)/shard_map/ppermute | solution.py:323
  11.8 5.0 %collective-permute-start.2 = (bf16[128,128]{1,0:T(8,128)(2,1)S(1)}, bf16[128,128]{1,0:T(8,128)(2,1)S(1)}, u32[]{:S(2)}, u32[]{:S(2)}) collective-permute-start(bf16[128,128]{1,0:T(8,128)(2,1)S(1)} %add_convert_fusion.part), channel_id=1, source_target_pairs={{0,8},{1,9},{4,12},{5,13},{8,0},{9,1},{12,4},{13,5},{2,10},{3,11},... | collective-permute-start | bytes 98312 | tf_op jit(solution)/shard_map/ppermute | solution.py:323
  18.8 1.3 %collective-permute-start.3 = (f32[4,4096]{1,0:T(4,128)S(1)}, f32[4,4096]{1,0:T(4,128)S(1)}, u32[]{:S(2)}, u32[]{:S(2)}) collective-permute-start(f32[4,4096]{1,0:T(4,128)S(1)} %get-tuple-element.16.grad), channel_id=1, source_target_pairs={{0,1},{1,0},{2,3},{3,2},{4,5},{5,4},{6,7},{7,6},{8,9},{9,8},{10,11... | collective-permute-start | bytes 196616 | tf_op jit(solution)/shard_map/ppermute | solution.py:349
  20.2 4.0 %collective-permute-start.4 = (f32[2,4096]{1,0:T(2,128)S(1)}, f32[2,4096]{1,0:T(2,128)S(1)}, u32[]{:S(2)}, u32[]{:S(2)}) collective-permute-start(f32[2,4096]{1,0:T(2,128)S(1)} %maximum_select_fusion), channel_id=1, source_target_pairs={{0,2},{2,0},{1,3},{3,1},{4,6},{6,4},{5,7},{7,5},{8,10},{10,8},{9,1... | collective-permute-start | bytes 98312 | tf_op jit(solution)/shard_map/ppermute | solution.py:354

commit v10 on v9

--- a/solution.py
+++ b/solution.py
@@ -45,9 +45,9 @@
 
 
 def forward_kernel(
-    count, ray_hbm, voxel_hbm, vol_hbm, split_hbm, dual_hbm, sino_hbm, proj_hbm,
-    partial_out, adjoint_out, edge_out, first_out, index_out, tiles,
-    ray, voxel, index, vol, split, dual, sino, double, table, acc0, acc1, acc2, acc3,
+    count, ray_hbm, voxel_hbm, vol_hbm, sino_hbm, proj_hbm,
+    partial_out, index_out, tiles,
+    ray, voxel, index, vol, sino, double, table, acc0, acc1, acc2, acc3,
     sems, tile_sems,
 ):
     slots = proj_hbm.shape[0]
@@ -59,10 +59,7 @@
     loads = [
         pltpu.make_async_copy(source, target, sems.at[i])
         for i, (source, target) in enumerate(
-            [
-                (vol_hbm, vol), (voxel_hbm, voxel), (ray_hbm, ray), (sino_hbm, sino),
-                (split_hbm, split), (dual_hbm, dual),
-            ]
+            [(vol_hbm, vol), (voxel_hbm, voxel), (ray_hbm, ray), (sino_hbm, sino)]
         )
     ]
     for load in loads:
@@ -97,31 +94,13 @@
     index_out[lines:2 * lines, :] = jnp.where(live, rays8, rays * 8)
     index_out[2 * lines:3 * lines, :] = rays8
     index_out[3 * lines:4 * lines, :] = jnp.where(live, voxels8, voxel_tiles * 8)
-    to_scalar = pltpu.make_async_copy(index_out, index, sems.at[6])
+    to_scalar = pltpu.make_async_copy(index_out, index, sems.at[4])
     to_scalar.start()
 
-    for load in loads[3:]:
-        load.wait()
+    loads[3].wait()
     mine = (lax.axis_index("tile") * lax.axis_size("rep") + lax.axis_index("rep")) * owned
     for r in range(owned):
         acc0[pl.ds(pl.multiple_of((mine + r) * 8, 8), 4), :] = -sino[r]
-    row_mask, col_mask = plane_masks(lane)
-    for j in range(width // 128):
-        at = slice(128 * j, 128 * j + 128)
-        x = double[:, at]
-        gap = [
-            jnp.concatenate([dual[k, :, at] - split[k, :, at]] * 2, axis=0) for k in range(3)
-        ]
-        depth = jnp.where(row < 3, pltpu.roll(x, 7, axis=0) - x + gap[0], 0.0)
-        across = jnp.where(row_mask, pltpu.roll(x, 120, axis=1) - x + gap[1], 0.0)
-        along = jnp.where(col_mask, pltpu.roll(x, 127, axis=1) - x + gap[2], 0.0)
-        adjoint = pltpu.roll(depth, 1, axis=0) - depth
-        adjoint += jnp.where((lane % TV) >= 8, pltpu.roll(across, 8, axis=1), 0.0) - across
-        adjoint += jnp.where(lane % 8 >= 1, pltpu.roll(along, 1, axis=1), 0.0) - along
-        adjoint_out[:, at] = adjoint[0:4]
-        edge_out[:, at] = (x - gap[0])[3:4]
-        first_out[:, at] = x[0:1]
-
     to_scalar.wait()
     per = slots // CHUNKS
     for g in range(slots // GROUP):
@@ -157,9 +136,33 @@
         partial_out[16 * q:16 * q + 16, :] = jnp.concatenate(halves, axis=0).astype(jnp.bfloat16)
 
 
+def local_kernel(rho, vol, split, dual, base_out, edge_out, first_out, scale_out):
+    factor = TAU * rho[0]
+    limit = 1.0 / rho[0]
+    row, lane = iotas((8, 128))
+    row_mask, col_mask = plane_masks(lane)
+    for j in range(vol.shape[1] // 128):
+        at = slice(128 * j, 128 * j + 128)
+        field = vol[:, at]
+        x = jnp.concatenate([field] * 2, axis=0)
+        gap = [
+            jnp.concatenate([dual[k, :, at] - split[k, :, at]] * 2, axis=0) for k in range(3)
+        ]
+        depth = jnp.where(row < 3, pltpu.roll(x, 7, axis=0) - x + gap[0], 0.0)
+        across = jnp.where(row_mask, pltpu.roll(x, 120, axis=1) - x + gap[1], 0.0)
+        along = jnp.where(col_mask, pltpu.roll(x, 127, axis=1) - x + gap[2], 0.0)
+        adjoint = pltpu.roll(depth, 1, axis=0) - depth
+        adjoint += jnp.where((lane % TV) >= 8, pltpu.roll(across, 8, axis=1), 0.0) - across
+        adjoint += jnp.where(lane % 8 >= 1, pltpu.roll(along, 1, axis=1), 0.0) - along
+        base_out[:, at] = (x - factor * adjoint)[0:4]
+        edge_out[:, at] = (x - gap[0])[3:4]
+        first_out[:, at] = field[0:1]
+        scale_out[0:1, at] = jnp.full((1, 128), limit, jnp.float32)
+        scale_out[1:2, at] = jnp.full((1, 128), factor, jnp.float32)
+
+
 def backward_kernel(
-    rho, indices, tiles, part, moved, vol, adjoint,
-    grad_out, base_out, scale_out,
+    indices, tiles, part, moved, grad_out,
     index, table, acc0, acc1, acc2, acc3, sem,
 ):
     slots = tiles.shape[0]
@@ -182,14 +185,6 @@
             r = 8 * (4 * q + 2 * k)
             table[r:r + 8, :] = jnp.where(top, x, turned)
             table[r + 8:r + 16, :] = jnp.where(top, turned, x)
-
-    factor = TAU * rho[0]
-    limit = 1.0 / rho[0]
-    for j in range(voxel_tiles // 2):
-        at = slice(128 * j, 128 * j + 128)
-        base_out[:, at] = vol[:, at] - factor * adjoint[:, at]
-        scale_out[0:1, at] = jnp.full((1, 128), limit, jnp.float32)
-        scale_out[1:2, at] = jnp.full((1, 128), factor, jnp.float32)
 
     to_scalar.wait()
     for g in range(slots // GROUP):
@@ -278,65 +273,69 @@
     slabs = lax.axis_size("slab")
     rays = owned * group
     voxel_tiles = width // TV
-    volume_here, dual_here = volume, dual_var
     lines = slots // 128
     ray_index, voxel_index = ray_index.reshape(lines, 128), voxel_index.reshape(lines, 128)
-    volume, split_var, dual_var, sinogram, proj_tiles, ray_index, voxel_index = (
+    sources = [
         pltpu.with_memory_space_constraint(x, pltpu.HBM)
-        for x in (
-            volume, split_var, dual_var, sinogram, proj_tiles, ray_index, voxel_index
-        )
-    )
-
-    partial, adjoint, edge, first, indices, tiles = pl.pallas_call(
+        for x in (ray_index, voxel_index, volume, sinogram, proj_tiles)
+    ]
+
+    partial, indices, tiles = pl.pallas_call(
         forward_kernel,
         out_shape=(
             jax.ShapeDtypeStruct((rays * slices, TR), bf16),
-            jax.ShapeDtypeStruct((slices, width), f32),
-            jax.ShapeDtypeStruct((1, width), f32),
-            jax.ShapeDtypeStruct((1, width), f32),
             jax.ShapeDtypeStruct((4 * lines, 128), jnp.int32),
             jax.ShapeDtypeStruct(proj_tiles.shape, bf16),
         ),
-        in_specs=[smem()] + [hbm()] * 7,
-        out_specs=(vmem(),) * 6,
+        in_specs=[smem()] + [hbm()] * 5,
+        out_specs=(vmem(),) * 3,
         scratch_shapes=[
             pltpu.VMEM((lines, 128), jnp.int32),
             pltpu.VMEM((lines, 128), jnp.int32),
             pltpu.SMEM((4 * lines, 128), jnp.int32),
             pltpu.VMEM((slices, width), f32),
-            pltpu.VMEM((3, slices, width), f32),
-            pltpu.VMEM((3, slices, width), f32),
             pltpu.VMEM(sinogram.shape, f32),
             pltpu.VMEM((8, width), f32),
             pltpu.VMEM((voxel_tiles * 8, 128), f32),
         ]
         + [pltpu.VMEM((rays * 8 + 8, 128), f32)] * 4
-        + [pltpu.SemaphoreType.DMA((7,)), pltpu.SemaphoreType.DMA((CHUNKS,))],
+        + [pltpu.SemaphoreType.DMA((5,)), pltpu.SemaphoreType.DMA((CHUNKS,))],
         compiler_params=params(),
         name="forward",
-    )(tile_count, ray_index, voxel_index, volume, split_var, dual_var, sinogram, proj_tiles)
-
-    swap = [(i, i ^ 1) for i in range(reps)]
-    step = 1
-    while True:
-        moved = lax.ppermute(
-            partial, ("tile", "rep"), [(i, i ^ step) for i in range(group)]
-        )
-        step *= 2
-        if step == group:
-            break
-        partial = (partial.astype(f32) + moved.astype(f32)).astype(bf16)
-
-    grad, base, scales = pl.pallas_call(
-        backward_kernel,
+    )(tile_count, *sources)
+
+    base, edge, first, scales = pl.pallas_call(
+        local_kernel,
         out_shape=(
             jax.ShapeDtypeStruct((slices, width), f32),
-            jax.ShapeDtypeStruct((slices, width), f32),
+            jax.ShapeDtypeStruct((1, width), f32),
+            jax.ShapeDtypeStruct((1, width), f32),
             jax.ShapeDtypeStruct((2, width), f32),
         ),
-        in_specs=[smem()] + [vmem()] * 6,
-        out_specs=(vmem(), vmem(), vmem()),
+        in_specs=[smem()] + [vmem()] * 3,
+        out_specs=(vmem(),) * 4,
+        compiler_params=params(),
+        name="local",
+    )(rho, volume, split_var, dual_var)
+
+    swap = [(i, i ^ 1) for i in range(reps)]
+    moved = lax.ppermute(partial, "rep", swap)
+    step = reps
+    while step < group:
+        partial = (partial.astype(f32) + moved.astype(f32)).astype(bf16)
+        moved = lax.ppermute(
+            partial, ("tile", "rep"), [(i, i ^ (step + 1)) for i in range(group)]
+        )
+        step *= 2
+    moved, base, edge, first, scales = lax.optimization_barrier(
+        (moved, base, edge, first, scales)
+    )
+
+    grad = pl.pallas_call(
+        backward_kernel,
+        out_shape=jax.ShapeDtypeStruct((slices, width), f32),
+        in_specs=[vmem()] * 4,
+        out_specs=vmem(),
         scratch_shapes=[
             pltpu.SMEM((4 * lines, 128), jnp.int32),
             pltpu.VMEM((rays * 8, 128), f32),
@@ -345,13 +344,15 @@
         + [pltpu.SemaphoreType.DMA],
         compiler_params=params(),
         name="backward",
-    )(rho, indices, tiles, partial, moved, volume_here, adjoint)
+    )(indices, tiles, partial, moved)
     grad_other = lax.ppermute(grad, "rep", swap)
     ahead = jnp.concatenate([base[0:1] - TAU * (grad[0:1] + grad_other[0:1]), first], axis=0)
     behind = jnp.concatenate([edge, edge], axis=0)
     if slabs == 2:
         halo = jnp.where(lax.axis_index("slab") == 0, behind, ahead)
-        from_next = from_previous = lax.ppermute(halo, "slab", [(0, 1), (1, 0)])
+        from_next = from_previous = lax.ppermute(
+            halo, ("slab", "rep"), [(i, i ^ 3) for i in range(2 * reps)]
+        )
     else:
         from_next = lax.ppermute(ahead, "slab", [(i, i - 1) for i in range(1, slabs)])
         from_previous = lax.ppermute(behind, "slab", [(i - 1, i) for i in range(1, slabs)])
@@ -367,7 +368,7 @@
         out_specs=(vmem(), vmem(), vmem()),
         compiler_params=params(),
         name="update",
-    )(grad, grad_other, from_next, from_previous, base, edge, first, dual_here, scales)
+    )(grad, grad_other, from_next, from_previous, base, edge, first, dual_var, scales)
 
 
 def solution(mesh):

time: 25.3 us -> 23.5 us (0.929)
  waiting for transfers between devices: 7.35 us -> 5.81 us
  starting transfers between devices: 8.56 us -> 8.13 us
    ppermute x4, waiting for transfers between devices: 6.12 us -> 4.91 us  [the longest x2 2.24 us: shards(): lax.ppermute(partial, ('tile', 'rep'), [(i, i ^ step + 1) for i in range(...]
    ppermute x4, starting transfers between devices: 8.49 us -> 7.71 us  [the longest x2 5.6 us: shards(): lax.ppermute(partial, ('tile', 'rep'), [(i, i ^ step + 1) for i in range(...]
    ppermute x1, starting transfers between devices: 0.07 us -> 0.42 us  [shards(): grad_other = lax.ppermute(grad, 'rep', swap)]
    ppermute x1, waiting for transfers between devices: 1.23 us -> 0.9 us  [shards(): grad_other = lax.ppermute(grad, 'rep', swap)]
    pallas_call x1 -> x2, Pallas kernels: 1.95 us -> 2.23 us  [the longest x1 1.95 us: shards(): pl.pallas_call(backward_kernel, out_shape=jax.ShapeDtypeStruct((slices, w...]
  transfers between devices with their start and end apart: 5 -> 5, of which waited for: 5 -> 5; matrix products, arithmetic and copies ran while one was open for 0% -> 0% of each run, Pallas kernels for 0% -> 1%
where the time goes in v10:
time: 23.5 us; the launch traced here: 23.3 us
  starting transfers between devices  8.13 us (35%)
  Pallas kernels  7.15 us (30%)
  waiting for transfers between devices  5.81 us (25%)
  between operations  2.07 us (9%)
    ppermute x2, starting transfers between devices, shards(): lax.ppermute(partial, ('tile', 'rep'), [(i, i ^ step + 1) for i in range(...  5.6 us
    pallas_call x1, Pallas kernels, shards(): pl.pallas_call(forward_kernel, out_shape=(jax.ShapeDtypeStruct((rays * sl...  3.99 us
    ppermute x2, waiting for transfers between devices, shards(): lax.ppermute(partial, ('tile', 'rep'), [(i, i ^ step + 1) for i in range(...  2.24 us
    pallas_call x1, Pallas kernels, shards(): pl.pallas_call(backward_kernel, out_shape=jax.ShapeDtypeStruct((slices, w...  1.95 us
    ppermute x1, waiting for transfers between devices, shards(): lax.ppermute(halo, ('slab', 'rep'), [(i, i ^ 3) for i in range(2 * reps)])  1.81 us
    ppermute x1, starting transfers between devices, shards(): lax.ppermute(halo, ('slab', 'rep'), [(i, i ^ 3) for i in range(2 * reps)])  1.6 us
    pallas_call x1, Pallas kernels, shards(): pl.pallas_call(update_kernel, out_shape=(jax.ShapeDtypeStruct((slices, wi...  0.93 us
    ppermute x1, waiting for transfers between devices, shards(): grad_other = lax.ppermute(grad, 'rep', swap)  0.9 us
  transfers between devices with their start and end apart: 5, of which 5 were waited for; matrix products, arithmetic and copies ran while one was open for 0% of the time, Pallas kernels for 1%

profile of v10, /device:TPU:0, one launch (start us, length us, event | category | flops | bytes accessed | tf_op | source)
XLA Modules:
  0.0 23.3 jit_solution(1508882391045437171)
XLA Ops:
  0.6 0.0 copy-start.1
  0.6 0.0 copy-start.2
  0.7 0.0 copy-start
  1.4 4.0 %forward.1 = (bf16[128,128]{1,0:T(8,128)(2,1)S(1)}, s32[8,128]{1,0:T(8,128)S(1)}, bf16[256,64,128]{2,1,0:T(8,128)(2,1)S(1)}) custom-call(s32[1]{0:T(128)S(6)} %copy.12.count, s32[2,128]{1,0:T(2,128)} %bitcast.2, s32[2,128]{1,0:T(2,128)} %bitcast.3, f32[4,4096]{1,0:T(4,128)} %vol.1, f32[4,4,128]{2,1,0:T(4,128)} %sino_hbm.1, bf16[256,64,128]{2,1,0:T(8,128)(2,1)} %proj_hbm.1), custom_call_target="tpu_custom_call" | custom-call | tf_op jit(solution)/shard_map/forward/pallas_call | solution.py:283
  5.4 0.5 %collective-permute-start = (bf16[128,128]{1,0:T(8,128)(2,1)S(1)}, bf16[128,128]{1,0:T(8,128)(2,1)S(1)}, u32[]{:S(2)}, u32[]{:S(2)}) collective-permute-start(bf16[128,128]{1,0:T(8,128)(2,1)S(1)} %get-tuple-element.17), channel_id=1, source_target_pairs={{0,1},{1,0},{2,3},{3,2},{4,5},{5,4},{6,7},{7,6},{8,9},{9,8},{10,11... | collective-permute-start | bytes 98312 | tf_op jit(solution)/shard_map/ppermute | solution.py:322
  5.9 0.9 %collective-permute-done = bf16[128,128]{1,0:T(8,128)(2,1)S(1)} collective-permute-done((bf16[128,128]{1,0:T(8,128)(2,1)S(1)}, bf16[128,128]{1,0:T(8,128)(2,1)S(1)}, u32[]{:S(2)}, u32[]{:S(2)}) %collective-permute-start) | collective-permute-done | bytes 32800 | tf_op jit(solution)/shard_map/ppermute | solution.py:322
  6.8 2.8 %collective-permute-start.1 = (bf16[128,128]{1,0:T(8,128)(2,1)S(1)}, bf16[128,128]{1,0:T(8,128)(2,1)S(1)}, u32[]{:S(2)}, u32[]{:S(2)}) collective-permute-start(bf16[128,128]{1,0:T(8,128)(2,1)S(1)} %add_convert_fusion.1), channel_id=1, source_target_pairs={{0,5},{1,4},{4,1},{5,0},{8,13},{9,12},{12,9},{13,8},{2,7},{3,6},{6... | collective-permute-start | bytes 98312 | tf_op jit(solution)/shard_map/ppermute | solution.py:326
  9.5 1.6 %collective-permute-done.1 = bf16[128,128]{1,0:T(8,128)(2,1)S(1)} collective-permute-done((bf16[128,128]{1,0:T(8,128)(2,1)S(1)}, bf16[128,128]{1,0:T(8,128)(2,1)S(1)}, u32[]{:S(2)}, u32[]{:S(2)}) %collective-permute-start.1) | collective-permute-done | bytes 32800 | tf_op jit(solution)/shard_map/ppermute | solution.py:326
  11.1 2.8 %collective-permute-start.2 = (bf16[128,128]{1,0:T(8,128)(2,1)S(1)}, bf16[128,128]{1,0:T(8,128)(2,1)S(1)}, u32[]{:S(2)}, u32[]{:S(2)}) collective-permute-start(bf16[128,128]{1,0:T(8,128)(2,1)S(1)} %add_convert_fusion.part), channel_id=1, source_target_pairs={{0,9},{1,8},{4,13},{5,12},{8,1},{9,0},{12,5},{13,4},{2,11},{3,10},... | collective-permute-start | bytes 98312 | tf_op jit(solution)/shard_map/ppermute | solution.py:326
  14.6 0.0 copy-done.1
  14.6 0.0 copy-done.2
  14.6 0.0 copy-done
  14.7 0.3 %local.1 = (f32[4,4096]{1,0:T(4,128)S(1)}, f32[1,4096]{1,0:T(1,128)S(1)}, f32[1,4096]{1,0:T(1,128)S(1)}, f32[2,4096]{1,0:T(2,128)S(1)}) custom-call(f32[1]{0:T(128)S(6)} %copy.13.rho, f32[4,4096]{1,0:T(4,128)S(1)} %copy-done.1, f32[3,4,4096]{2,1,0:T(4,128)S(1)} %copy-done.2, f32[3,4,4096]{2,1,0:T(4,128)S(1)} %copy-done), custom_call_target="tpu_custom_call" | custom-call | tf_op jit(solution)/shard_map/local/pallas_call | solution.py:307
  14.9 0.6 %collective-permute-done.2.moved = bf16[128,128]{1,0:T(8,128)(2,1)S(1)} collective-permute-done((bf16[128,128]{1,0:T(8,128)(2,1)S(1)}, bf16[128,128]{1,0:T(8,128)(2,1)S(1)}, u32[]{:S(2)}, u32[]{:S(2)}) %collective-permute-start.2) | collective-permute-done | bytes 32800 | tf_op jit(solution)/shard_map/ppermute | solution.py:326
  15.6 1.9 %backward.1.grad = f32[4,4096]{1,0:T(4,128)S(1)} custom-call(s32[8,128]{1,0:T(8,128)S(1)} %get-tuple-element.15.indices, bf16[256,64,128]{2,1,0:T(8,128)(2,1)S(1)} %get-tuple-element.16.tiles, bf16[128,128]{1,0:T(8,128)(2,1)S(1)} %add_convert_fusion.part, bf16[128,128]{1,0:T(8,128)(2,1)S(1)} %collective-permute-done.2.moved), custom_call_target="tpu_custom_call" | custom-call | tf_op jit(solution)/shard_map/backward/pallas_call | solution.py:334
  17.5 0.4 %collective-permute-start.3 = (f32[4,4096]{1,0:T(4,128)S(1)}, f32[4,4096]{1,0:T(4,128)S(1)}, u32[]{:S(2)}, u32[]{:S(2)}) collective-permute-start(f32[4,4096]{1,0:T(4,128)S(1)} %backward.1.grad), channel_id=1, source_target_pairs={{0,1},{1,0},{2,3},{3,2},{4,5},{5,4},{6,7},{7,6},{8,9},{9,8},{10,11... | collective-permute-start | bytes 196616 | tf_op jit(solution)/shard_map/ppermute | solution.py:348
  17.9 0.9 %collective-permute-done.3.grad_other = f32[4,4096]{1,0:T(4,128)S(1)} collective-permute-done((f32[4,4096]{1,0:T(4,128)S(1)}, f32[4,4096]{1,0:T(4,128)S(1)}, u32[]{:S(2)}, u32[]{:S(2)}) %collective-permute-start.3) | collective-permute-done | bytes 65568 | tf_op jit(solution)/shard_map/ppermute | solution.py:348
  18.9 0.1 maximum_select_fusion
  18.9 1.6 %collective-permute-start.4 = (f32[2,4096]{1,0:T(2,128)S(1)}, f32[2,4096]{1,0:T(2,128)S(1)}, u32[]{:S(2)}, u32[]{:S(2)}) collective-permute-start(f32[2,4096]{1,0:T(2,128)S(1)} %maximum_select_fusion), channel_id=1, source_target_pairs={{0,3},{1,2},{2,1},{3,0},{4,7},{5,6},{6,5},{7,4},{8,11},{9,10},{10,... | collective-permute-start | bytes 98312 | tf_op jit(solution)/shard_map/ppermute | solution.py:353
  20.5 1.8 %collective-permute-done.4.from_next.from_previous = f32[2,4096]{1,0:T(2,128)S(1)} collective-permute-done((f32[2,4096]{1,0:T(2,128)S(1)}, f32[2,4096]{1,0:T(2,128)S(1)}, u32[]{:S(2)}, u32[]{:S(2)}) %collective-permute-start.4) | collective-permute-done | bytes 32800 | tf_op jit(solution)/shard_map/ppermute | solution.py:353
  22.4 0.9 %update.1 = (f32[4,4096]{1,0:T(4,128)}, f32[3,4,4096]{2,1,0:T(4,128)}, f32[3,4,4096]{2,1,0:T(4,128)}) custom-call(f32[4,4096]{1,0:T(4,128)S(1)} %backward.1.grad, f32[4,4096]{1,0:T(4,128)S(1)} %collective-permute-done.3.grad_other, f32[2,4096]{1,0:T(2,128)S(1)} %collective-permute-done.4.from_next.from_previous, ...), custom_call_target="tpu_custom_call" | custom-call | tf_op jit(solution)/shard_map/update/pallas_call | solution.py:360
  (3 shorter events, 0.1 us)
Async XLA Ops:
  0.6 14.0 %copy-start.1 = (f32[4,4096]{1,0:T(4,128)S(1)}, f32[4,4096]{1,0:T(4,128)}, u32[]{:S(2)}) copy-start(f32[4,4096]{1,0:T(4,128)} %vol.1) | copy-start | bytes 196612
  0.6 14.0 %copy-start.2 = (f32[3,4,4096]{2,1,0:T(4,128)S(1)}, f32[3,4,4096]{2,1,0:T(4,128)}, u32[]{:S(2)}) copy-start(f32[3,4,4096]{2,1,0:T(4,128)} %split.1) | copy-start | bytes 589828
  0.7 14.0 %copy-start = (f32[3,4,4096]{2,1,0:T(4,128)S(1)}, f32[3,4,4096]{2,1,0:T(4,128)}, u32[]{:S(2)}) copy-start(f32[3,4,4096]{2,1,0:T(4,128)} %dual.3) | copy-start | bytes 589828
  5.4 1.4 %collective-permute-start = (bf16[128,128]{1,0:T(8,128)(2,1)S(1)}, bf16[128,128]{1,0:T(8,128)(2,1)S(1)}, u32[]{:S(2)}, u32[]{:S(2)}) collective-permute-start(bf16[128,128]{1,0:T(8,128)(2,1)S(1)} %get-tuple-element.17), channel_id=1, source_target_pairs={{0,1},{1,0},{2,3},{3,2},{4,5},{5,4},{6,7},{7,6},{8,9},{9,8},{10,11... | collective-permute-start | bytes 98312 | tf_op jit(solution)/shard_map/ppermute | solution.py:322
  6.8 4.4 %collective-permute-start.1 = (bf16[128,128]{1,0:T(8,128)(2,1)S(1)}, bf16[128,128]{1,0:T(8,128)(2,1)S(1)}, u32[]{:S(2)}, u32[]{:S(2)}) collective-permute-start(bf16[128,128]{1,0:T(8,128)(2,1)S(1)} %add_convert_fusion.1), channel_id=1, source_target_pairs={{0,5},{1,4},{4,1},{5,0},{8,13},{9,12},{12,9},{13,8},{2,7},{3,6},{6... | collective-permute-start | bytes 98312 | tf_op jit(solution)/shard_map/ppermute | solution.py:326
  11.1 4.4 %collective-permute-start.2 = (bf16[128,128]{1,0:T(8,128)(2,1)S(1)}, bf16[128,128]{1,0:T(8,128)(2,1)S(1)}, u32[]{:S(2)}, u32[]{:S(2)}) collective-permute-start(bf16[128,128]{1,0:T(8,128)(2,1)S(1)} %add_convert_fusion.part), channel_id=1, source_target_pairs={{0,9},{1,8},{4,13},{5,12},{8,1},{9,0},{12,5},{13,4},{2,11},{3,10},... | collective-permute-start | bytes 98312 | tf_op jit(solution)/shard_map/ppermute | solution.py:326
  17.5 1.3 %collective-permute-start.3 = (f32[4,4096]{1,0:T(4,128)S(1)}, f32[4,4096]{1,0:T(4,128)S(1)}, u32[]{:S(2)}, u32[]{:S(2)}) collective-permute-start(f32[4,4096]{1,0:T(4,128)S(1)} %backward.1.grad), channel_id=1, source_target_pairs={{0,1},{1,0},{2,3},{3,2},{4,5},{5,4},{6,7},{7,6},{8,9},{9,8},{10,11... | collective-permute-start | bytes 196616 | tf_op jit(solution)/shard_map/ppermute | solution.py:348
  18.9 3.4 %collective-permute-start.4 = (f32[2,4096]{1,0:T(2,128)S(1)}, f32[2,4096]{1,0:T(2,128)S(1)}, u32[]{:S(2)}, u32[]{:S(2)}) collective-permute-start(f32[2,4096]{1,0:T(2,128)S(1)} %maximum_select_fusion), channel_id=1, source_target_pairs={{0,3},{1,2},{2,1},{3,0},{4,7},{5,6},{6,5},{7,4},{8,11},{9,10},{10,... | collective-permute-start | bytes 98312 | tf_op jit(solution)/shard_map/ppermute | solution.py:353

commit v11 on v10

--- a/solution.py
+++ b/solution.py
@@ -9,7 +9,7 @@
 TR = 128
 TAU = 0.5
 GROUP = 4
-CHUNKS = 8
+CHUNKS = 2
 VMEM_LIMIT = 16 * 1024 * 1024
 
 
@@ -59,7 +59,7 @@
     loads = [
         pltpu.make_async_copy(source, target, sems.at[i])
         for i, (source, target) in enumerate(
-            [(vol_hbm, vol), (voxel_hbm, voxel), (ray_hbm, ray), (sino_hbm, sino)]
+            [(voxel_hbm, voxel), (ray_hbm, ray), (vol_hbm, vol), (sino_hbm, sino)]
         )
     ]
     for load in loads:
@@ -72,6 +72,18 @@
     low, top = lane < TV, row < 4
 
     loads[0].wait()
+    loads[1].wait()
+    line, place = iotas((lines, 128))
+    live = 128 * line + place < count[0]
+    rays8, voxels8 = ray[...] * 8, voxel[...] * 8
+    index_out[0:lines, :] = voxels8
+    index_out[lines:2 * lines, :] = jnp.where(live, rays8, rays * 8)
+    index_out[2 * lines:3 * lines, :] = rays8
+    index_out[3 * lines:4 * lines, :] = jnp.where(live, voxels8, voxel_tiles * 8)
+    to_scalar = pltpu.make_async_copy(index_out, index, sems.at[4])
+    to_scalar.start()
+
+    loads[2].wait()
     field = vol[...]
     double[0:4, :] = field
     double[4:8, :] = field
@@ -84,18 +96,6 @@
         other = jnp.logical_not(jnp.logical_or(top, low))
         table[16 * j:16 * j + 8, :] = jnp.where(other, turned, first)
         table[16 * j + 8:16 * j + 16, :] = jnp.where(other, x, second)
-
-    loads[1].wait()
-    loads[2].wait()
-    line, place = iotas((lines, 128))
-    live = 128 * line + place < count[0]
-    rays8, voxels8 = ray[...] * 8, voxel[...] * 8
-    index_out[0:lines, :] = voxels8
-    index_out[lines:2 * lines, :] = jnp.where(live, rays8, rays * 8)
-    index_out[2 * lines:3 * lines, :] = rays8
-    index_out[3 * lines:4 * lines, :] = jnp.where(live, voxels8, voxel_tiles * 8)
-    to_scalar = pltpu.make_async_copy(index_out, index, sems.at[4])
-    to_scalar.start()
 
     loads[3].wait()
     mine = (lax.axis_index("tile") * lax.axis_size("rep") + lax.axis_index("rep")) * owned

time: 23.5 us -> 22.4 us (0.953)
  Pallas kernels: 7.15 us -> 6.02 us
    pallas_call x1, Pallas kernels: 3.99 us -> 2.86 us  [shards(): pl.pallas_call(forward_kernel, out_shape=(jax.ShapeDtypeStruct((rays * sl...]
where the time goes in v11:
time: 22.4 us; the launch traced here: 22.1 us
  starting transfers between devices  8.11 us (36%)
  Pallas kernels  6.02 us (27%)
  waiting for transfers between devices  5.79 us (26%)
  between operations  2.07 us (9%)
    ppermute x2, starting transfers between devices, shards(): lax.ppermute(partial, ('tile', 'rep'), [(i, i ^ step + 1) for i in range(...  5.57 us
    pallas_call x1, Pallas kernels, shards(): pl.pallas_call(forward_kernel, out_shape=(jax.ShapeDtypeStruct((rays * sl...  2.86 us
    ppermute x2, waiting for transfers between devices, shards(): lax.ppermute(partial, ('tile', 'rep'), [(i, i ^ step + 1) for i in range(...  2.24 us
    pallas_call x1, Pallas kernels, shards(): pl.pallas_call(backward_kernel, out_shape=jax.ShapeDtypeStruct((slices, w...  1.95 us
    ppermute x1, waiting for transfers between devices, shards(): lax.ppermute(halo, ('slab', 'rep'), [(i, i ^ 3) for i in range(2 * reps)])  1.78 us
    ppermute x1, starting transfers between devices, shards(): lax.ppermute(halo, ('slab', 'rep'), [(i, i ^ 3) for i in range(2 * reps)])  1.62 us
    pallas_call x1, Pallas kernels, shards(): pl.pallas_call(update_kernel, out_shape=(jax.ShapeDtypeStruct((slices, wi...  0.93 us
    ppermute x1, waiting for transfers between devices, shards(): grad_other = lax.ppermute(grad, 'rep', swap)  0.91 us
  transfers between devices with their start and end apart: 5, of which 5 were waited for; matrix products, arithmetic and copies ran while one was open for 0% of the time, Pallas kernels for 1%

profile of v11, /device:TPU:0, one launch (start us, length us, event | category | flops | bytes accessed | tf_op | source)
XLA Modules:
  0.0 22.1 jit_solution(14003749032867230675)
XLA Ops:
  0.6 0.0 copy-start.1
  0.6 0.0 copy-start.2
  0.7 0.0 copy-start
  1.4 2.9 %forward.1 = (bf16[128,128]{1,0:T(8,128)(2,1)S(1)}, s32[8,128]{1,0:T(8,128)S(1)}, bf16[256,64,128]{2,1,0:T(8,128)(2,1)S(1)}) custom-call(s32[1]{0:T(128)S(6)} %copy.12.count, s32[2,128]{1,0:T(2,128)} %bitcast.2, s32[2,128]{1,0:T(2,128)} %bitcast.3, f32[4,4096]{1,0:T(4,128)} %vol.1, f32[4,4,128]{2,1,0:T(4,128)} %sino_hbm.1, bf16[256,64,128]{2,1,0:T(8,128)(2,1)} %proj_hbm.1), custom_call_target="tpu_custom_call" | custom-call | tf_op jit(solution)/shard_map/forward/pallas_call | solution.py:283
  4.2 0.5 %collective-permute-start = (bf16[128,128]{1,0:T(8,128)(2,1)S(1)}, bf16[128,128]{1,0:T(8,128)(2,1)S(1)}, u32[]{:S(2)}, u32[]{:S(2)}) collective-permute-start(bf16[128,128]{1,0:T(8,128)(2,1)S(1)} %get-tuple-element.17), channel_id=1, source_target_pairs={{0,1},{1,0},{2,3},{3,2},{4,5},{5,4},{6,7},{7,6},{8,9},{9,8},{10,11... | collective-permute-start | bytes 98312 | tf_op jit(solution)/shard_map/ppermute | solution.py:322
  4.7 0.9 %collective-permute-done = bf16[128,128]{1,0:T(8,128)(2,1)S(1)} collective-permute-done((bf16[128,128]{1,0:T(8,128)(2,1)S(1)}, bf16[128,128]{1,0:T(8,128)(2,1)S(1)}, u32[]{:S(2)}, u32[]{:S(2)}) %collective-permute-start) | collective-permute-done | bytes 32800 | tf_op jit(solution)/shard_map/ppermute | solution.py:322
  5.6 2.7 %collective-permute-start.1 = (bf16[128,128]{1,0:T(8,128)(2,1)S(1)}, bf16[128,128]{1,0:T(8,128)(2,1)S(1)}, u32[]{:S(2)}, u32[]{:S(2)}) collective-permute-start(bf16[128,128]{1,0:T(8,128)(2,1)S(1)} %add_convert_fusion.1), channel_id=1, source_target_pairs={{0,5},{1,4},{4,1},{5,0},{8,13},{9,12},{12,9},{13,8},{2,7},{3,6},{6... | collective-permute-start | bytes 98312 | tf_op jit(solution)/shard_map/ppermute | solution.py:326
  8.4 1.6 %collective-permute-done.1 = bf16[128,128]{1,0:T(8,128)(2,1)S(1)} collective-permute-done((bf16[128,128]{1,0:T(8,128)(2,1)S(1)}, bf16[128,128]{1,0:T(8,128)(2,1)S(1)}, u32[]{:S(2)}, u32[]{:S(2)}) %collective-permute-start.1) | collective-permute-done | bytes 32800 | tf_op jit(solution)/shard_map/ppermute | solution.py:326
  10.0 2.8 %collective-permute-start.2 = (bf16[128,128]{1,0:T(8,128)(2,1)S(1)}, bf16[128,128]{1,0:T(8,128)(2,1)S(1)}, u32[]{:S(2)}, u32[]{:S(2)}) collective-permute-start(bf16[128,128]{1,0:T(8,128)(2,1)S(1)} %add_convert_fusion.part), channel_id=1, source_target_pairs={{0,9},{1,8},{4,13},{5,12},{8,1},{9,0},{12,5},{13,4},{2,11},{3,10},... | collective-permute-start | bytes 98312 | tf_op jit(solution)/shard_map/ppermute | solution.py:326
  13.5 0.0 copy-done.1
  13.5 0.0 copy-done.2
  13.5 0.0 copy-done
  13.5 0.3 %local.1 = (f32[4,4096]{1,0:T(4,128)S(1)}, f32[1,4096]{1,0:T(1,128)S(1)}, f32[1,4096]{1,0:T(1,128)S(1)}, f32[2,4096]{1,0:T(2,128)S(1)}) custom-call(f32[1]{0:T(128)S(6)} %copy.13.rho, f32[4,4096]{1,0:T(4,128)S(1)} %copy-done.1, f32[3,4,4096]{2,1,0:T(4,128)S(1)} %copy-done.2, f32[3,4,4096]{2,1,0:T(4,128)S(1)} %copy-done), custom_call_target="tpu_custom_call" | custom-call | tf_op jit(solution)/shard_map/local/pallas_call | solution.py:307
  13.8 0.6 %collective-permute-done.2.moved = bf16[128,128]{1,0:T(8,128)(2,1)S(1)} collective-permute-done((bf16[128,128]{1,0:T(8,128)(2,1)S(1)}, bf16[128,128]{1,0:T(8,128)(2,1)S(1)}, u32[]{:S(2)}, u32[]{:S(2)}) %collective-permute-start.2) | collective-permute-done | bytes 32800 | tf_op jit(solution)/shard_map/ppermute | solution.py:326
  14.4 2.0 %backward.1.grad = f32[4,4096]{1,0:T(4,128)S(1)} custom-call(s32[8,128]{1,0:T(8,128)S(1)} %get-tuple-element.15.indices, bf16[256,64,128]{2,1,0:T(8,128)(2,1)S(1)} %get-tuple-element.16.tiles, bf16[128,128]{1,0:T(8,128)(2,1)S(1)} %add_convert_fusion.part, bf16[128,128]{1,0:T(8,128)(2,1)S(1)} %collective-permute-done.2.moved), custom_call_target="tpu_custom_call" | custom-call | tf_op jit(solution)/shard_map/backward/pallas_call | solution.py:334
  16.4 0.4 %collective-permute-start.3 = (f32[4,4096]{1,0:T(4,128)S(1)}, f32[4,4096]{1,0:T(4,128)S(1)}, u32[]{:S(2)}, u32[]{:S(2)}) collective-permute-start(f32[4,4096]{1,0:T(4,128)S(1)} %backward.1.grad), channel_id=1, source_target_pairs={{0,1},{1,0},{2,3},{3,2},{4,5},{5,4},{6,7},{7,6},{8,9},{9,8},{10,11... | collective-permute-start | bytes 196616 | tf_op jit(solution)/shard_map/ppermute | solution.py:348
  16.8 0.9 %collective-permute-done.3.grad_other = f32[4,4096]{1,0:T(4,128)S(1)} collective-permute-done((f32[4,4096]{1,0:T(4,128)S(1)}, f32[4,4096]{1,0:T(4,128)S(1)}, u32[]{:S(2)}, u32[]{:S(2)}) %collective-permute-start.3) | collective-permute-done | bytes 65568 | tf_op jit(solution)/shard_map/ppermute | solution.py:348
  17.7 0.1 maximum_select_fusion
  17.8 1.6 %collective-permute-start.4 = (f32[2,4096]{1,0:T(2,128)S(1)}, f32[2,4096]{1,0:T(2,128)S(1)}, u32[]{:S(2)}, u32[]{:S(2)}) collective-permute-start(f32[2,4096]{1,0:T(2,128)S(1)} %maximum_select_fusion), channel_id=1, source_target_pairs={{0,3},{1,2},{2,1},{3,0},{4,7},{5,6},{6,5},{7,4},{8,11},{9,10},{10,... | collective-permute-start | bytes 98312 | tf_op jit(solution)/shard_map/ppermute | solution.py:353
  19.4 1.8 %collective-permute-done.4.from_next.from_previous = f32[2,4096]{1,0:T(2,128)S(1)} collective-permute-done((f32[2,4096]{1,0:T(2,128)S(1)}, f32[2,4096]{1,0:T(2,128)S(1)}, u32[]{:S(2)}, u32[]{:S(2)}) %collective-permute-start.4) | collective-permute-done | bytes 32800 | tf_op jit(solution)/shard_map/ppermute | solution.py:353
  21.2 0.9 %update.1 = (f32[4,4096]{1,0:T(4,128)}, f32[3,4,4096]{2,1,0:T(4,128)}, f32[3,4,4096]{2,1,0:T(4,128)}) custom-call(f32[4,4096]{1,0:T(4,128)S(1)} %backward.1.grad, f32[4,4096]{1,0:T(4,128)S(1)} %collective-permute-done.3.grad_other, f32[2,4096]{1,0:T(2,128)S(1)} %collective-permute-done.4.from_next.from_previous, ...), custom_call_target="tpu_custom_call" | custom-call | tf_op jit(solution)/shard_map/update/pallas_call | solution.py:360
  (3 shorter events, 0.1 us)
Async XLA Ops:
  0.6 12.8 %copy-start.1 = (f32[4,4096]{1,0:T(4,128)S(1)}, f32[4,4096]{1,0:T(4,128)}, u32[]{:S(2)}) copy-start(f32[4,4096]{1,0:T(4,128)} %vol.1) | copy-start | bytes 196612
  0.6 12.8 %copy-start.2 = (f32[3,4,4096]{2,1,0:T(4,128)S(1)}, f32[3,4,4096]{2,1,0:T(4,128)}, u32[]{:S(2)}) copy-start(f32[3,4,4096]{2,1,0:T(4,128)} %split.1) | copy-start | bytes 589828
  0.7 12.8 %copy-start = (f32[3,4,4096]{2,1,0:T(4,128)S(1)}, f32[3,4,4096]{2,1,0:T(4,128)}, u32[]{:S(2)}) copy-start(f32[3,4,4096]{2,1,0:T(4,128)} %dual.3) | copy-start | bytes 589828
  4.2 1.4 %collective-permute-start = (bf16[128,128]{1,0:T(8,128)(2,1)S(1)}, bf16[128,128]{1,0:T(8,128)(2,1)S(1)}, u32[]{:S(2)}, u32[]{:S(2)}) collective-permute-start(bf16[128,128]{1,0:T(8,128)(2,1)S(1)} %get-tuple-element.17), channel_id=1, source_target_pairs={{0,1},{1,0},{2,3},{3,2},{4,5},{5,4},{6,7},{7,6},{8,9},{9,8},{10,11... | collective-permute-start | bytes 98312 | tf_op jit(solution)/shard_map/ppermute | solution.py:322
  5.6 4.3 %collective-permute-start.1 = (bf16[128,128]{1,0:T(8,128)(2,1)S(1)}, bf16[128,128]{1,0:T(8,128)(2,1)S(1)}, u32[]{:S(2)}, u32[]{:S(2)}) collective-permute-start(bf16[128,128]{1,0:T(8,128)(2,1)S(1)} %add_convert_fusion.1), channel_id=1, source_target_pairs={{0,5},{1,4},{4,1},{5,0},{8,13},{9,12},{12,9},{13,8},{2,7},{3,6},{6... | collective-permute-start | bytes 98312 | tf_op jit(solution)/shard_map/ppermute | solution.py:326
  10.0 4.4 %collective-permute-start.2 = (bf16[128,128]{1,0:T(8,128)(2,1)S(1)}, bf16[128,128]{1,0:T(8,128)(2,1)S(1)}, u32[]{:S(2)}, u32[]{:S(2)}) collective-permute-start(bf16[128,128]{1,0:T(8,128)(2,1)S(1)} %add_convert_fusion.part), channel_id=1, source_target_pairs={{0,9},{1,8},{4,13},{5,12},{8,1},{9,0},{12,5},{13,4},{2,11},{3,10},... | collective-permute-start | bytes 98312 | tf_op jit(solution)/shard_map/ppermute | solution.py:326
  16.4 1.3 %collective-permute-start.3 = (f32[4,4096]{1,0:T(4,128)S(1)}, f32[4,4096]{1,0:T(4,128)S(1)}, u32[]{:S(2)}, u32[]{:S(2)}) collective-permute-start(f32[4,4096]{1,0:T(4,128)S(1)} %backward.1.grad), channel_id=1, source_target_pairs={{0,1},{1,0},{2,3},{3,2},{4,5},{5,4},{6,7},{7,6},{8,9},{9,8},{10,11... | collective-permute-start | bytes 196616 | tf_op jit(solution)/shard_map/ppermute | solution.py:348
  17.8 3.4 %collective-permute-start.4 = (f32[2,4096]{1,0:T(2,128)S(1)}, f32[2,4096]{1,0:T(2,128)S(1)}, u32[]{:S(2)}, u32[]{:S(2)}) collective-permute-start(f32[2,4096]{1,0:T(2,128)S(1)} %maximum_select_fusion), channel_id=1, source_target_pairs={{0,3},{1,2},{2,1},{3,0},{4,7},{5,6},{6,5},{7,4},{8,11},{9,10},{10,... | collective-permute-start | bytes 98312 | tf_op jit(solution)/shard_map/ppermute | solution.py:353

commit v12 on v11

--- a/solution.py
+++ b/solution.py
@@ -9,7 +9,8 @@
 TR = 128
 TAU = 0.5
 GROUP = 4
-CHUNKS = 2
+CHUNKS = 8
+WAITS = 2
 VMEM_LIMIT = 16 * 1024 * 1024
 
 
@@ -102,10 +103,12 @@
     for r in range(owned):
         acc0[pl.ds(pl.multiple_of((mine + r) * 8, 8), 4), :] = -sino[r]
     to_scalar.wait()
-    per = slots // CHUNKS
+    per = slots // WAITS
     for g in range(slots // GROUP):
         if GROUP * g % per == 0:
-            copies[GROUP * g // per].wait()
+            part = GROUP * g // per * CHUNKS // WAITS
+            for copy in copies[part:part + CHUNKS // WAITS]:
+                copy.wait()
         n = GROUP * g
         at = [divmod(n + i, 128) for i in range(GROUP)]
         picked = [table[rows8(index[line, place]), :] for line, place in at]
@@ -191,19 +194,22 @@
         n = GROUP * g
         at = [divmod(n + i, 128) for i in range(GROUP)]
         picked = [table[rows8(index[2 * lines + line, place]), :] for line, place in at]
-        rows = jnp.concatenate(
-            [jnp.where(top, picked[2 * i], picked[2 * i + 1]) for i in range(2)], axis=0
-        )
+        pairs = [jnp.where(top, picked[2 * i], picked[2 * i + 1]) for i in range(2)]
+        zero = jnp.zeros_like(pairs[0])
+        left = jnp.concatenate([pairs[0], zero], axis=0).astype(jnp.bfloat16)
+        right = jnp.concatenate([zero, pairs[1]], axis=0).astype(jnp.bfloat16)
         back = lax.dot_general(
-            rows.astype(jnp.bfloat16),
-            tiles[n:n + GROUP].reshape(GROUP * TV, TR),
+            jnp.concatenate([left, right], axis=1),
+            jnp.concatenate(
+                [tiles[n + 2 * i:n + 2 * i + 2].reshape(2 * TV, TR) for i in range(2)], axis=1
+            ),
             (((1,), (1,)), ((), ())),
             preferred_element_type=jnp.float32,
         )
         add_rows(
             accs,
             [index[3 * lines + line, place] for line, place in at],
-            [back[8 * k:8 * k + 8, 128 * k:128 * k + 128] for k in (0, 0, 1, 1)],
+            [back[0:8], back[0:8], back[8:16], back[8:16]],
         )
     for j in range(voxel_tiles // 2):
         at = [slice(16 * j + 8 * k, 16 * j + 8 * k + 8) for k in range(2)]

time: 22.4 us -> 22.7 us (1.013)
  Pallas kernels: 6.02 us -> 6.29 us
    pallas_call x1, Pallas kernels: 2.86 us -> 3.13 us  [shards(): pl.pallas_call(forward_kernel, out_shape=(jax.ShapeDtypeStruct((rays * sl...]
where the time goes in v12:
time: 22.7 us; the launch traced here: 22.5 us
  starting transfers between devices  8.16 us (36%)
  Pallas kernels  6.29 us (28%)
  waiting for transfers between devices  5.82 us (26%)
  between operations  2.07 us (9%)
    ppermute x2, starting transfers between devices, shards(): lax.ppermute(partial, ('tile', 'rep'), [(i, i ^ step + 1) for i in range(...  5.59 us
    pallas_call x1, Pallas kernels, shards(): pl.pallas_call(forward_kernel, out_shape=(jax.ShapeDtypeStruct((rays * sl...  3.13 us
    ppermute x2, waiting for transfers between devices, shards(): lax.ppermute(partial, ('tile', 'rep'), [(i, i ^ step + 1) for i in range(...  2.24 us
    pallas_call x1, Pallas kernels, shards(): pl.pallas_call(backward_kernel, out_shape=jax.ShapeDtypeStruct((slices, w...  1.95 us
    ppermute x1, waiting for transfers between devices, shards(): lax.ppermute(halo, ('slab', 'rep'), [(i, i ^ 3) for i in range(2 * reps)])  1.82 us
    ppermute x1, starting transfers between devices, shards(): lax.ppermute(halo, ('slab', 'rep'), [(i, i ^ 3) for i in range(2 * reps)])  1.59 us
    pallas_call x1, Pallas kernels, shards(): pl.pallas_call(update_kernel, out_shape=(jax.ShapeDtypeStruct((slices, wi...  0.93 us
    ppermute x1, waiting for transfers between devices, shards(): grad_other = lax.ppermute(grad, 'rep', swap)  0.9 us
  transfers between devices with their start and end apart: 5, of which 5 were waited for; matrix products, arithmetic and copies ran while one was open for 0% of the time, Pallas kernels for 1%

profile of v12, /device:TPU:0, one launch (start us, length us, event | category | flops | bytes accessed | tf_op | source)
XLA Modules:
  0.0 22.5 jit_solution(18126881996632363066)
XLA Ops:
  0.6 0.0 copy-start.1
  0.6 0.0 copy-start.2
  0.7 0.0 copy-start
  1.4 3.1 %forward.1 = (bf16[128,128]{1,0:T(8,128)(2,1)S(1)}, s32[8,128]{1,0:T(8,128)S(1)}, bf16[256,64,128]{2,1,0:T(8,128)(2,1)S(1)}) custom-call(s32[1]{0:T(128)S(6)} %copy.12.count, s32[2,128]{1,0:T(2,128)} %bitcast.2, s32[2,128]{1,0:T(2,128)} %bitcast.3, f32[4,4096]{1,0:T(4,128)} %vol.1, f32[4,4,128]{2,1,0:T(4,128)} %sino_hbm.1, bf16[256,64,128]{2,1,0:T(8,128)(2,1)} %proj_hbm.1), custom_call_target="tpu_custom_call" | custom-call | tf_op jit(solution)/shard_map/forward/pallas_call | solution.py:289
  4.5 0.5 %collective-permute-start = (bf16[128,128]{1,0:T(8,128)(2,1)S(1)}, bf16[128,128]{1,0:T(8,128)(2,1)S(1)}, u32[]{:S(2)}, u32[]{:S(2)}) collective-permute-start(bf16[128,128]{1,0:T(8,128)(2,1)S(1)} %get-tuple-element.17), channel_id=1, source_target_pairs={{0,1},{1,0},{2,3},{3,2},{4,5},{5,4},{6,7},{7,6},{8,9},{9,8},{10,11... | collective-permute-start | bytes 98312 | tf_op jit(solution)/shard_map/ppermute | solution.py:328
  5.0 0.9 %collective-permute-done = bf16[128,128]{1,0:T(8,128)(2,1)S(1)} collective-permute-done((bf16[128,128]{1,0:T(8,128)(2,1)S(1)}, bf16[128,128]{1,0:T(8,128)(2,1)S(1)}, u32[]{:S(2)}, u32[]{:S(2)}) %collective-permute-start) | collective-permute-done | bytes 32800 | tf_op jit(solution)/shard_map/ppermute | solution.py:328
  5.9 2.7 %collective-permute-start.1 = (bf16[128,128]{1,0:T(8,128)(2,1)S(1)}, bf16[128,128]{1,0:T(8,128)(2,1)S(1)}, u32[]{:S(2)}, u32[]{:S(2)}) collective-permute-start(bf16[128,128]{1,0:T(8,128)(2,1)S(1)} %add_convert_fusion.1), channel_id=1, source_target_pairs={{0,5},{1,4},{4,1},{5,0},{8,13},{9,12},{12,9},{13,8},{2,7},{3,6},{6... | collective-permute-start | bytes 98312 | tf_op jit(solution)/shard_map/ppermute | solution.py:332
  8.7 1.6 %collective-permute-done.1 = bf16[128,128]{1,0:T(8,128)(2,1)S(1)} collective-permute-done((bf16[128,128]{1,0:T(8,128)(2,1)S(1)}, bf16[128,128]{1,0:T(8,128)(2,1)S(1)}, u32[]{:S(2)}, u32[]{:S(2)}) %collective-permute-start.1) | collective-permute-done | bytes 32800 | tf_op jit(solution)/shard_map/ppermute | solution.py:332
  10.3 2.8 %collective-permute-start.2 = (bf16[128,128]{1,0:T(8,128)(2,1)S(1)}, bf16[128,128]{1,0:T(8,128)(2,1)S(1)}, u32[]{:S(2)}, u32[]{:S(2)}) collective-permute-start(bf16[128,128]{1,0:T(8,128)(2,1)S(1)} %add_convert_fusion.part), channel_id=1, source_target_pairs={{0,9},{1,8},{4,13},{5,12},{8,1},{9,0},{12,5},{13,4},{2,11},{3,10},... | collective-permute-start | bytes 98312 | tf_op jit(solution)/shard_map/ppermute | solution.py:332
  13.8 0.0 copy-done.1
  13.8 0.0 copy-done.2
  13.8 0.0 copy-done
  13.8 0.3 %local.1 = (f32[4,4096]{1,0:T(4,128)S(1)}, f32[1,4096]{1,0:T(1,128)S(1)}, f32[1,4096]{1,0:T(1,128)S(1)}, f32[2,4096]{1,0:T(2,128)S(1)}) custom-call(f32[1]{0:T(128)S(6)} %copy.13.rho, f32[4,4096]{1,0:T(4,128)S(1)} %copy-done.1, f32[3,4,4096]{2,1,0:T(4,128)S(1)} %copy-done.2, f32[3,4,4096]{2,1,0:T(4,128)S(1)} %copy-done), custom_call_target="tpu_custom_call" | custom-call | tf_op jit(solution)/shard_map/local/pallas_call | solution.py:313
  14.1 0.6 %collective-permute-done.2.moved = bf16[128,128]{1,0:T(8,128)(2,1)S(1)} collective-permute-done((bf16[128,128]{1,0:T(8,128)(2,1)S(1)}, bf16[128,128]{1,0:T(8,128)(2,1)S(1)}, u32[]{:S(2)}, u32[]{:S(2)}) %collective-permute-start.2) | collective-permute-done | bytes 32800 | tf_op jit(solution)/shard_map/ppermute | solution.py:332
  14.7 2.0 %backward.1.grad = f32[4,4096]{1,0:T(4,128)S(1)} custom-call(s32[8,128]{1,0:T(8,128)S(1)} %get-tuple-element.15.indices, bf16[256,64,128]{2,1,0:T(8,128)(2,1)S(1)} %get-tuple-element.16.tiles, bf16[128,128]{1,0:T(8,128)(2,1)S(1)} %add_convert_fusion.part, bf16[128,128]{1,0:T(8,128)(2,1)S(1)} %collective-permute-done.2.moved), custom_call_target="tpu_custom_call" | custom-call | tf_op jit(solution)/shard_map/backward/pallas_call | solution.py:340
  16.7 0.4 %collective-permute-start.3 = (f32[4,4096]{1,0:T(4,128)S(1)}, f32[4,4096]{1,0:T(4,128)S(1)}, u32[]{:S(2)}, u32[]{:S(2)}) collective-permute-start(f32[4,4096]{1,0:T(4,128)S(1)} %backward.1.grad), channel_id=1, source_target_pairs={{0,1},{1,0},{2,3},{3,2},{4,5},{5,4},{6,7},{7,6},{8,9},{9,8},{10,11... | collective-permute-start | bytes 196616 | tf_op jit(solution)/shard_map/ppermute | solution.py:354
  17.1 0.9 %collective-permute-done.3.grad_other = f32[4,4096]{1,0:T(4,128)S(1)} collective-permute-done((f32[4,4096]{1,0:T(4,128)S(1)}, f32[4,4096]{1,0:T(4,128)S(1)}, u32[]{:S(2)}, u32[]{:S(2)}) %collective-permute-start.3) | collective-permute-done | bytes 65568 | tf_op jit(solution)/shard_map/ppermute | solution.py:354
  18.1 0.1 maximum_select_fusion
  18.1 1.6 %collective-permute-start.4 = (f32[2,4096]{1,0:T(2,128)S(1)}, f32[2,4096]{1,0:T(2,128)S(1)}, u32[]{:S(2)}, u32[]{:S(2)}) collective-permute-start(f32[2,4096]{1,0:T(2,128)S(1)} %maximum_select_fusion), channel_id=1, source_target_pairs={{0,3},{1,2},{2,1},{3,0},{4,7},{5,6},{6,5},{7,4},{8,11},{9,10},{10,... | collective-permute-start | bytes 98312 | tf_op jit(solution)/shard_map/ppermute | solution.py:359
  19.7 1.8 %collective-permute-done.4.from_next.from_previous = f32[2,4096]{1,0:T(2,128)S(1)} collective-permute-done((f32[2,4096]{1,0:T(2,128)S(1)}, f32[2,4096]{1,0:T(2,128)S(1)}, u32[]{:S(2)}, u32[]{:S(2)}) %collective-permute-start.4) | collective-permute-done | bytes 32800 | tf_op jit(solution)/shard_map/ppermute | solution.py:359
  21.5 0.9 %update.1 = (f32[4,4096]{1,0:T(4,128)}, f32[3,4,4096]{2,1,0:T(4,128)}, f32[3,4,4096]{2,1,0:T(4,128)}) custom-call(f32[4,4096]{1,0:T(4,128)S(1)} %backward.1.grad, f32[4,4096]{1,0:T(4,128)S(1)} %collective-permute-done.3.grad_other, f32[2,4096]{1,0:T(2,128)S(1)} %collective-permute-done.4.from_next.from_previous, ...), custom_call_target="tpu_custom_call" | custom-call | tf_op jit(solution)/shard_map/update/pallas_call | solution.py:366
  (3 shorter events, 0.1 us)
Async XLA Ops:
  0.6 13.1 %copy-start.1 = (f32[4,4096]{1,0:T(4,128)S(1)}, f32[4,4096]{1,0:T(4,128)}, u32[]{:S(2)}) copy-start(f32[4,4096]{1,0:T(4,128)} %vol.1) | copy-start | bytes 196612
  0.6 13.1 %copy-start.2 = (f32[3,4,4096]{2,1,0:T(4,128)S(1)}, f32[3,4,4096]{2,1,0:T(4,128)}, u32[]{:S(2)}) copy-start(f32[3,4,4096]{2,1,0:T(4,128)} %split.1) | copy-start | bytes 589828
  0.7 13.1 %copy-start = (f32[3,4,4096]{2,1,0:T(4,128)S(1)}, f32[3,4,4096]{2,1,0:T(4,128)}, u32[]{:S(2)}) copy-start(f32[3,4,4096]{2,1,0:T(4,128)} %dual.3) | copy-start | bytes 589828
  4.5 1.4 %collective-permute-start = (bf16[128,128]{1,0:T(8,128)(2,1)S(1)}, bf16[128,128]{1,0:T(8,128)(2,1)S(1)}, u32[]{:S(2)}, u32[]{:S(2)}) collective-permute-start(bf16[128,128]{1,0:T(8,128)(2,1)S(1)} %get-tuple-element.17), channel_id=1, source_target_pairs={{0,1},{1,0},{2,3},{3,2},{4,5},{5,4},{6,7},{7,6},{8,9},{9,8},{10,11... | collective-permute-start | bytes 98312 | tf_op jit(solution)/shard_map/ppermute | solution.py:328
  5.9 4.3 %collective-permute-start.1 = (bf16[128,128]{1,0:T(8,128)(2,1)S(1)}, bf16[128,128]{1,0:T(8,128)(2,1)S(1)}, u32[]{:S(2)}, u32[]{:S(2)}) collective-permute-start(bf16[128,128]{1,0:T(8,128)(2,1)S(1)} %add_convert_fusion.1), channel_id=1, source_target_pairs={{0,5},{1,4},{4,1},{5,0},{8,13},{9,12},{12,9},{13,8},{2,7},{3,6},{6... | collective-permute-start | bytes 98312 | tf_op jit(solution)/shard_map/ppermute | solution.py:332
  10.3 4.4 %collective-permute-start.2 = (bf16[128,128]{1,0:T(8,128)(2,1)S(1)}, bf16[128,128]{1,0:T(8,128)(2,1)S(1)}, u32[]{:S(2)}, u32[]{:S(2)}) collective-permute-start(bf16[128,128]{1,0:T(8,128)(2,1)S(1)} %add_convert_fusion.part), channel_id=1, source_target_pairs={{0,9},{1,8},{4,13},{5,12},{8,1},{9,0},{12,5},{13,4},{2,11},{3,10},... | collective-permute-start | bytes 98312 | tf_op jit(solution)/shard_map/ppermute | solution.py:332
  16.7 1.3 %collective-permute-start.3 = (f32[4,4096]{1,0:T(4,128)S(1)}, f32[4,4096]{1,0:T(4,128)S(1)}, u32[]{:S(2)}, u32[]{:S(2)}) collective-permute-start(f32[4,4096]{1,0:T(4,128)S(1)} %backward.1.grad), channel_id=1, source_target_pairs={{0,1},{1,0},{2,3},{3,2},{4,5},{5,4},{6,7},{7,6},{8,9},{9,8},{10,11... | collective-permute-start | bytes 196616 | tf_op jit(solution)/shard_map/ppermute | solution.py:354
  18.1 3.4 %collective-permute-start.4 = (f32[2,4096]{1,0:T(2,128)S(1)}, f32[2,4096]{1,0:T(2,128)S(1)}, u32[]{:S(2)}, u32[]{:S(2)}) collective-permute-start(f32[2,4096]{1,0:T(2,128)S(1)} %maximum_select_fusion), channel_id=1, source_target_pairs={{0,3},{1,2},{2,1},{3,0},{4,7},{5,6},{6,5},{7,4},{8,11},{9,10},{10,... | collective-permute-start | bytes 98312 | tf_op jit(solution)/shard_map/ppermute | solution.py:359

commit v13 on v11

--- a/solution.py
+++ b/solution.py
@@ -10,6 +10,7 @@
 TAU = 0.5
 GROUP = 4
 CHUNKS = 2
+BATCH = 2
 VMEM_LIMIT = 16 * 1024 * 1024
 
 
@@ -44,12 +45,20 @@
         acc[rows8(start), :] = old + value
 
 
+def sum_of(accs, at):
+    total = accs[0][at, :]
+    for acc in accs[1:]:
+        total += acc[at, :]
+    return total
+
+
 def forward_kernel(
     count, ray_hbm, voxel_hbm, vol_hbm, sino_hbm, proj_hbm,
     partial_out, index_out, tiles,
-    ray, voxel, index, vol, sino, double, table, acc0, acc1, acc2, acc3,
-    sems, tile_sems,
+    ray, voxel, index, vol, sino, double, table, *rest,
 ):
+    accs, (sems, tile_sems) = rest[:-2], rest[-2:]
+    acc0 = accs[0]
     slots = proj_hbm.shape[0]
     lines = ray.shape[0]
     rays = acc0.shape[0] // 8 - 1
@@ -65,7 +74,6 @@
     for load in loads:
         load.start()
     copies = start_tiles(proj_hbm, tiles, tile_sems)
-    accs = (acc0, acc1, acc2, acc3)
     for acc in accs:
         acc[...] = jnp.zeros_like(acc)
     row, lane = iotas((8, 128))
@@ -103,32 +111,31 @@
         acc0[pl.ds(pl.multiple_of((mine + r) * 8, 8), 4), :] = -sino[r]
     to_scalar.wait()
     per = slots // CHUNKS
-    for g in range(slots // GROUP):
-        if GROUP * g % per == 0:
-            copies[GROUP * g // per].wait()
-        n = GROUP * g
-        at = [divmod(n + i, 128) for i in range(GROUP)]
-        picked = [table[rows8(index[line, place]), :] for line, place in at]
-        pairs = [jnp.where(top, picked[2 * i], picked[2 * i + 1]) for i in range(2)]
-        zero = jnp.zeros_like(pairs[0])
-        left = jnp.concatenate([pairs[0], zero], axis=0).astype(jnp.bfloat16)
-        right = jnp.concatenate([zero, pairs[1]], axis=0).astype(jnp.bfloat16)
-        sums = jnp.dot(
-            jnp.concatenate([left, right], axis=1),
-            tiles[n:n + GROUP].reshape(GROUP * TV, TR),
-            preferred_element_type=jnp.float32,
-        )
-        add_rows(
-            accs,
-            [index[lines + line, place] for line, place in at],
-            [sums[0:8], sums[0:8], sums[8:16], sums[8:16]],
-        )
+    for first in range(0, slots, GROUP * BATCH):
+        if first % per == 0:
+            copies[first // per].wait()
+        starts, values = [], []
+        for n in range(first, first + GROUP * BATCH, GROUP):
+            at = [divmod(n + i, 128) for i in range(GROUP)]
+            picked = [table[rows8(index[line, place]), :] for line, place in at]
+            pairs = [jnp.where(top, picked[2 * i], picked[2 * i + 1]) for i in range(2)]
+            zero = jnp.zeros_like(pairs[0])
+            left = jnp.concatenate([pairs[0], zero], axis=0).astype(jnp.bfloat16)
+            right = jnp.concatenate([zero, pairs[1]], axis=0).astype(jnp.bfloat16)
+            sums = jnp.dot(
+                jnp.concatenate([left, right], axis=1),
+                tiles[n:n + GROUP].reshape(GROUP * TV, TR),
+                preferred_element_type=jnp.float32,
+            )
+            starts += [index[lines + line, place] for line, place in at]
+            values += [sums[0:8], sums[0:8], sums[8:16], sums[8:16]]
+        add_rows(accs, starts, values)
     for q in range(rays // 4):
         halves = []
         for r in (4 * q, 4 * q + 2):
             at = [slice(8 * (r + k), 8 * (r + k) + 8) for k in range(2)]
-            even = [acc0[at[k], :] + acc2[at[k], :] for k in range(2)]
-            odd = [acc1[at[k], :] + acc3[at[k], :] for k in range(2)]
+            even = [sum_of(accs[0::2], at[k]) for k in range(2)]
+            odd = [sum_of(accs[1::2], at[k]) for k in range(2)]
             halves.append(
                 jnp.where(top, even[0], odd[1])
                 + pltpu.roll(jnp.where(top, even[1], odd[0]), 4, axis=0)
@@ -163,15 +170,16 @@
 
 def backward_kernel(
     indices, tiles, part, moved, grad_out,
-    index, table, acc0, acc1, acc2, acc3, sem,
+    index, table, *rest,
 ):
+    accs, sem = rest[:-1], rest[-1]
+    acc0 = accs[0]
     slots = tiles.shape[0]
     lines = indices.shape[0] // 4
     rays = table.shape[0] // 8
     voxel_tiles = acc0.shape[0] // 8 - 1
     to_scalar = pltpu.make_async_copy(indices, index, sem)
     to_scalar.start()
-    accs = (acc0, acc1, acc2, acc3)
     for acc in accs:
         acc[...] = jnp.zeros_like(acc)
     row, lane = iotas((8, 128))
@@ -187,28 +195,27 @@
             table[r + 8:r + 16, :] = jnp.where(top, turned, x)
 
     to_scalar.wait()
-    for g in range(slots // GROUP):
-        n = GROUP * g
-        at = [divmod(n + i, 128) for i in range(GROUP)]
-        picked = [table[rows8(index[2 * lines + line, place]), :] for line, place in at]
-        rows = jnp.concatenate(
-            [jnp.where(top, picked[2 * i], picked[2 * i + 1]) for i in range(2)], axis=0
-        )
-        back = lax.dot_general(
-            rows.astype(jnp.bfloat16),
-            tiles[n:n + GROUP].reshape(GROUP * TV, TR),
-            (((1,), (1,)), ((), ())),
-            preferred_element_type=jnp.float32,
-        )
-        add_rows(
-            accs,
-            [index[3 * lines + line, place] for line, place in at],
-            [back[8 * k:8 * k + 8, 128 * k:128 * k + 128] for k in (0, 0, 1, 1)],
-        )
+    for first in range(0, slots, GROUP * BATCH):
+        starts, values = [], []
+        for n in range(first, first + GROUP * BATCH, GROUP):
+            at = [divmod(n + i, 128) for i in range(GROUP)]
+            picked = [table[rows8(index[2 * lines + line, place]), :] for line, place in at]
+            rows = jnp.concatenate(
+                [jnp.where(top, picked[2 * i], picked[2 * i + 1]) for i in range(2)], axis=0
+            )
+            back = lax.dot_general(
+                rows.astype(jnp.bfloat16),
+                tiles[n:n + GROUP].reshape(GROUP * TV, TR),
+                (((1,), (1,)), ((), ())),
+                preferred_element_type=jnp.float32,
+            )
+            starts += [index[3 * lines + line, place] for line, place in at]
+            values += [back[8 * k:8 * k + 8, 128 * k:128 * k + 128] for k in (0, 0, 1, 1)]
+        add_rows(accs, starts, values)
     for j in range(voxel_tiles // 2):
         at = [slice(16 * j + 8 * k, 16 * j + 8 * k + 8) for k in range(2)]
-        even = [acc0[at[k], :] + acc2[at[k], :] for k in range(2)]
-        odd = [acc1[at[k], :] + acc3[at[k], :] for k in range(2)]
+        even = [sum_of(accs[0::2], at[k]) for k in range(2)]
+        odd = [sum_of(accs[1::2], at[k]) for k in range(2)]
         turned = pltpu.roll(jnp.where(top, even[1], odd[0]), TV, axis=1)
         both = jnp.where(top == low, jnp.where(top, even[0], odd[1]), turned)
         grad_out[:, 128 * j:128 * j + 128] = (both + pltpu.roll(both, 4, axis=0))[0:4]
@@ -298,7 +305,7 @@
             pltpu.VMEM((8, width), f32),
             pltpu.VMEM((voxel_tiles * 8, 128), f32),
         ]
-        + [pltpu.VMEM((rays * 8 + 8, 128), f32)] * 4
+        + [pltpu.VMEM((rays * 8 + 8, 128), f32)] * (GROUP * BATCH)
         + [pltpu.SemaphoreType.DMA((5,)), pltpu.SemaphoreType.DMA((CHUNKS,))],
         compiler_params=params(),
         name="forward",
@@ -340,7 +347,7 @@
             pltpu.SMEM((4 * lines, 128), jnp.int32),
             pltpu.VMEM((rays * 8, 128), f32),
         ]
-        + [pltpu.VMEM((voxel_tiles * 8 + 8, 128), f32)] * 4
+        + [pltpu.VMEM((voxel_tiles * 8 + 8, 128), f32)] * (GROUP * BATCH)
         + [pltpu.SemaphoreType.DMA],
         compiler_params=params(),
         name="backward",

time: 22.4 us -> 22.4 us (level)
  no operation moved by 1% of the time
where the time goes in v13:
time: 22.4 us; the launch traced here: 22.2 us
  starting transfers between devices  8.1 us (36%)
  Pallas kernels  6.07 us (27%)
  waiting for transfers between devices  5.82 us (26%)
  between operations  2.07 us (9%)
    ppermute x2, starting transfers between devices, shards(): lax.ppermute(partial, ('tile', 'rep'), [(i, i ^ step + 1) for i in range(...  5.58 us
    pallas_call x1, Pallas kernels, shards(): pl.pallas_call(forward_kernel, out_shape=(jax.ShapeDtypeStruct((rays * sl...  2.86 us
    ppermute x2, waiting for transfers between devices, shards(): lax.ppermute(partial, ('tile', 'rep'), [(i, i ^ step + 1) for i in range(...  2.24 us
    pallas_call x1, Pallas kernels, shards(): pl.pallas_call(backward_kernel, out_shape=jax.ShapeDtypeStruct((slices, w...  2 us
    ppermute x1, waiting for transfers between devices, shards(): lax.ppermute(halo, ('slab', 'rep'), [(i, i ^ 3) for i in range(2 * reps)])  1.8 us
    ppermute x1, starting transfers between devices, shards(): lax.ppermute(halo, ('slab', 'rep'), [(i, i ^ 3) for i in range(2 * reps)])  1.6 us
    pallas_call x1, Pallas kernels, shards(): pl.pallas_call(update_kernel, out_shape=(jax.ShapeDtypeStruct((slices, wi...  0.93 us
    ppermute x1, waiting for transfers between devices, shards(): grad_other = lax.ppermute(grad, 'rep', swap)  0.92 us
  transfers between devices with their start and end apart: 5, of which 5 were waited for; matrix products, arithmetic and copies ran while one was open for 0% of the time, Pallas kernels for 1%

profile of v13, /device:TPU:0, one launch (start us, length us, event | category | flops | bytes accessed | tf_op | source)
XLA Modules:
  0.0 22.2 jit_solution(6111999142373898233)
XLA Ops:
  0.6 0.0 copy-start.1
  0.6 0.0 copy-start.2
  0.7 0.0 copy-start
  1.4 2.9 %forward.1 = (bf16[128,128]{1,0:T(8,128)(2,1)S(1)}, s32[8,128]{1,0:T(8,128)S(1)}, bf16[256,64,128]{2,1,0:T(8,128)(2,1)S(1)}) custom-call(s32[1]{0:T(128)S(6)} %copy.12.count, s32[2,128]{1,0:T(2,128)} %bitcast.2, s32[2,128]{1,0:T(2,128)} %bitcast.3, f32[4,4096]{1,0:T(4,128)} %vol.1, f32[4,4,128]{2,1,0:T(4,128)} %sino_hbm.1, bf16[256,64,128]{2,1,0:T(8,128)(2,1)} %proj_hbm.1), custom_call_target="tpu_custom_call" | custom-call | tf_op jit(solution)/shard_map/forward/pallas_call | solution.py:290
  4.2 0.5 %collective-permute-start = (bf16[128,128]{1,0:T(8,128)(2,1)S(1)}, bf16[128,128]{1,0:T(8,128)(2,1)S(1)}, u32[]{:S(2)}, u32[]{:S(2)}) collective-permute-start(bf16[128,128]{1,0:T(8,128)(2,1)S(1)} %get-tuple-element.17), channel_id=1, source_target_pairs={{0,1},{1,0},{2,3},{3,2},{4,5},{5,4},{6,7},{7,6},{8,9},{9,8},{10,11... | collective-permute-start | bytes 98312 | tf_op jit(solution)/shard_map/ppermute | solution.py:329
  4.7 0.9 %collective-permute-done = bf16[128,128]{1,0:T(8,128)(2,1)S(1)} collective-permute-done((bf16[128,128]{1,0:T(8,128)(2,1)S(1)}, bf16[128,128]{1,0:T(8,128)(2,1)S(1)}, u32[]{:S(2)}, u32[]{:S(2)}) %collective-permute-start) | collective-permute-done | bytes 32800 | tf_op jit(solution)/shard_map/ppermute | solution.py:329
  5.6 2.7 %collective-permute-start.1 = (bf16[128,128]{1,0:T(8,128)(2,1)S(1)}, bf16[128,128]{1,0:T(8,128)(2,1)S(1)}, u32[]{:S(2)}, u32[]{:S(2)}) collective-permute-start(bf16[128,128]{1,0:T(8,128)(2,1)S(1)} %add_convert_fusion.1), channel_id=1, source_target_pairs={{0,5},{1,4},{4,1},{5,0},{8,13},{9,12},{12,9},{13,8},{2,7},{3,6},{6... | collective-permute-start | bytes 98312 | tf_op jit(solution)/shard_map/ppermute | solution.py:333
  8.4 1.6 %collective-permute-done.1 = bf16[128,128]{1,0:T(8,128)(2,1)S(1)} collective-permute-done((bf16[128,128]{1,0:T(8,128)(2,1)S(1)}, bf16[128,128]{1,0:T(8,128)(2,1)S(1)}, u32[]{:S(2)}, u32[]{:S(2)}) %collective-permute-start.1) | collective-permute-done | bytes 32800 | tf_op jit(solution)/shard_map/ppermute | solution.py:333
  10.0 2.8 %collective-permute-start.2 = (bf16[128,128]{1,0:T(8,128)(2,1)S(1)}, bf16[128,128]{1,0:T(8,128)(2,1)S(1)}, u32[]{:S(2)}, u32[]{:S(2)}) collective-permute-start(bf16[128,128]{1,0:T(8,128)(2,1)S(1)} %add_convert_fusion.part), channel_id=1, source_target_pairs={{0,9},{1,8},{4,13},{5,12},{8,1},{9,0},{12,5},{13,4},{2,11},{3,10},... | collective-permute-start | bytes 98312 | tf_op jit(solution)/shard_map/ppermute | solution.py:333
  13.5 0.0 copy-done.1
  13.5 0.0 copy-done.2
  13.5 0.0 copy-done
  13.5 0.3 %local.1 = (f32[4,4096]{1,0:T(4,128)S(1)}, f32[1,4096]{1,0:T(1,128)S(1)}, f32[1,4096]{1,0:T(1,128)S(1)}, f32[2,4096]{1,0:T(2,128)S(1)}) custom-call(f32[1]{0:T(128)S(6)} %copy.13.rho, f32[4,4096]{1,0:T(4,128)S(1)} %copy-done.1, f32[3,4,4096]{2,1,0:T(4,128)S(1)} %copy-done.2, f32[3,4,4096]{2,1,0:T(4,128)S(1)} %copy-done), custom_call_target="tpu_custom_call" | custom-call | tf_op jit(solution)/shard_map/local/pallas_call | solution.py:314
  13.8 0.6 %collective-permute-done.2.moved = bf16[128,128]{1,0:T(8,128)(2,1)S(1)} collective-permute-done((bf16[128,128]{1,0:T(8,128)(2,1)S(1)}, bf16[128,128]{1,0:T(8,128)(2,1)S(1)}, u32[]{:S(2)}, u32[]{:S(2)}) %collective-permute-start.2) | collective-permute-done | bytes 32800 | tf_op jit(solution)/shard_map/ppermute | solution.py:333
  14.4 2.0 %backward.1.grad = f32[4,4096]{1,0:T(4,128)S(1)} custom-call(s32[8,128]{1,0:T(8,128)S(1)} %get-tuple-element.15.indices, bf16[256,64,128]{2,1,0:T(8,128)(2,1)S(1)} %get-tuple-element.16.tiles, bf16[128,128]{1,0:T(8,128)(2,1)S(1)} %add_convert_fusion.part, bf16[128,128]{1,0:T(8,128)(2,1)S(1)} %collective-permute-done.2.moved), custom_call_target="tpu_custom_call" | custom-call | tf_op jit(solution)/shard_map/backward/pallas_call | solution.py:341
  16.4 0.4 %collective-permute-start.3 = (f32[4,4096]{1,0:T(4,128)S(1)}, f32[4,4096]{1,0:T(4,128)S(1)}, u32[]{:S(2)}, u32[]{:S(2)}) collective-permute-start(f32[4,4096]{1,0:T(4,128)S(1)} %backward.1.grad), channel_id=1, source_target_pairs={{0,1},{1,0},{2,3},{3,2},{4,5},{5,4},{6,7},{7,6},{8,9},{9,8},{10,11... | collective-permute-start | bytes 196616 | tf_op jit(solution)/shard_map/ppermute | solution.py:355
  16.8 0.9 %collective-permute-done.3.grad_other = f32[4,4096]{1,0:T(4,128)S(1)} collective-permute-done((f32[4,4096]{1,0:T(4,128)S(1)}, f32[4,4096]{1,0:T(4,128)S(1)}, u32[]{:S(2)}, u32[]{:S(2)}) %collective-permute-start.3) | collective-permute-done | bytes 65568 | tf_op jit(solution)/shard_map/ppermute | solution.py:355
  17.8 0.1 maximum_select_fusion
  17.8 1.6 %collective-permute-start.4 = (f32[2,4096]{1,0:T(2,128)S(1)}, f32[2,4096]{1,0:T(2,128)S(1)}, u32[]{:S(2)}, u32[]{:S(2)}) collective-permute-start(f32[2,4096]{1,0:T(2,128)S(1)} %maximum_select_fusion), channel_id=1, source_target_pairs={{0,3},{1,2},{2,1},{3,0},{4,7},{5,6},{6,5},{7,4},{8,11},{9,10},{10,... | collective-permute-start | bytes 98312 | tf_op jit(solution)/shard_map/ppermute | solution.py:360
  19.5 1.8 %collective-permute-done.4.from_next.from_previous = f32[2,4096]{1,0:T(2,128)S(1)} collective-permute-done((f32[2,4096]{1,0:T(2,128)S(1)}, f32[2,4096]{1,0:T(2,128)S(1)}, u32[]{:S(2)}, u32[]{:S(2)}) %collective-permute-start.4) | collective-permute-done | bytes 32800 | tf_op jit(solution)/shard_map/ppermute | solution.py:360
  21.3 0.9 %update.1 = (f32[4,4096]{1,0:T(4,128)}, f32[3,4,4096]{2,1,0:T(4,128)}, f32[3,4,4096]{2,1,0:T(4,128)}) custom-call(f32[4,4096]{1,0:T(4,128)S(1)} %backward.1.grad, f32[4,4096]{1,0:T(4,128)S(1)} %collective-permute-done.3.grad_other, f32[2,4096]{1,0:T(2,128)S(1)} %collective-permute-done.4.from_next.from_previous, ...), custom_call_target="tpu_custom_call" | custom-call | tf_op jit(solution)/shard_map/update/pallas_call | solution.py:367
  (3 shorter events, 0.1 us)
Async XLA Ops:
  0.6 12.8 %copy-start.1 = (f32[4,4096]{1,0:T(4,128)S(1)}, f32[4,4096]{1,0:T(4,128)}, u32[]{:S(2)}) copy-start(f32[4,4096]{1,0:T(4,128)} %vol.1) | copy-start | bytes 196612
  0.6 12.8 %copy-start.2 = (f32[3,4,4096]{2,1,0:T(4,128)S(1)}, f32[3,4,4096]{2,1,0:T(4,128)}, u32[]{:S(2)}) copy-start(f32[3,4,4096]{2,1,0:T(4,128)} %split.1) | copy-start | bytes 589828
  0.7 12.8 %copy-start = (f32[3,4,4096]{2,1,0:T(4,128)S(1)}, f32[3,4,4096]{2,1,0:T(4,128)}, u32[]{:S(2)}) copy-start(f32[3,4,4096]{2,1,0:T(4,128)} %dual.3) | copy-start | bytes 589828
  4.2 1.4 %collective-permute-start = (bf16[128,128]{1,0:T(8,128)(2,1)S(1)}, bf16[128,128]{1,0:T(8,128)(2,1)S(1)}, u32[]{:S(2)}, u32[]{:S(2)}) collective-permute-start(bf16[128,128]{1,0:T(8,128)(2,1)S(1)} %get-tuple-element.17), channel_id=1, source_target_pairs={{0,1},{1,0},{2,3},{3,2},{4,5},{5,4},{6,7},{7,6},{8,9},{9,8},{10,11... | collective-permute-start | bytes 98312 | tf_op jit(solution)/shard_map/ppermute | solution.py:329
  5.6 4.3 %collective-permute-start.1 = (bf16[128,128]{1,0:T(8,128)(2,1)S(1)}, bf16[128,128]{1,0:T(8,128)(2,1)S(1)}, u32[]{:S(2)}, u32[]{:S(2)}) collective-permute-start(bf16[128,128]{1,0:T(8,128)(2,1)S(1)} %add_convert_fusion.1), channel_id=1, source_target_pairs={{0,5},{1,4},{4,1},{5,0},{8,13},{9,12},{12,9},{13,8},{2,7},{3,6},{6... | collective-permute-start | bytes 98312 | tf_op jit(solution)/shard_map/ppermute | solution.py:333
  10.0 4.4 %collective-permute-start.2 = (bf16[128,128]{1,0:T(8,128)(2,1)S(1)}, bf16[128,128]{1,0:T(8,128)(2,1)S(1)}, u32[]{:S(2)}, u32[]{:S(2)}) collective-permute-start(bf16[128,128]{1,0:T(8,128)(2,1)S(1)} %add_convert_fusion.part), channel_id=1, source_target_pairs={{0,9},{1,8},{4,13},{5,12},{8,1},{9,0},{12,5},{13,4},{2,11},{3,10},... | collective-permute-start | bytes 98312 | tf_op jit(solution)/shard_map/ppermute | solution.py:333
  16.4 1.3 %collective-permute-start.3 = (f32[4,4096]{1,0:T(4,128)S(1)}, f32[4,4096]{1,0:T(4,128)S(1)}, u32[]{:S(2)}, u32[]{:S(2)}) collective-permute-start(f32[4,4096]{1,0:T(4,128)S(1)} %backward.1.grad), channel_id=1, source_target_pairs={{0,1},{1,0},{2,3},{3,2},{4,5},{5,4},{6,7},{7,6},{8,9},{9,8},{10,11... | collective-permute-start | bytes 196616 | tf_op jit(solution)/shard_map/ppermute | solution.py:355
  17.8 3.4 %collective-permute-start.4 = (f32[2,4096]{1,0:T(2,128)S(1)}, f32[2,4096]{1,0:T(2,128)S(1)}, u32[]{:S(2)}, u32[]{:S(2)}) collective-permute-start(f32[2,4096]{1,0:T(2,128)S(1)} %maximum_select_fusion), channel_id=1, source_target_pairs={{0,3},{1,2},{2,1},{3,0},{4,7},{5,6},{6,5},{7,4},{8,11},{9,10},{10,... | collective-permute-start | bytes 98312 | tf_op jit(solution)/shard_map/ppermute | solution.py:360

commit v14 on v11

--- a/solution.py
+++ b/solution.py
@@ -136,29 +136,37 @@
         partial_out[16 * q:16 * q + 16, :] = jnp.concatenate(halves, axis=0).astype(jnp.bfloat16)
 
 
-def local_kernel(rho, vol, split, dual, base_out, edge_out, first_out, scale_out):
+def edges_kernel(vol, split, dual, edge_out, first_out, halo_out):
+    start = lax.axis_index("slab") == 0
+    for j in range(vol.shape[1] // 128):
+        at = slice(128 * j, 128 * j + 128)
+        edge = vol[3:4, at] - dual[0, 3:4, at] + split[0, 3:4, at]
+        first = vol[0:1, at]
+        edge_out[:, at] = edge
+        first_out[:, at] = first
+        halo_out[:, at] = jnp.broadcast_to(jnp.where(start, edge, first), (4, 128))
+
+
+def local_kernel(rho, vol, split, dual, edge, from_next, from_previous, base_out):
+    slab, slabs = lax.axis_index("slab"), lax.axis_size("slab")
     factor = TAU * rho[0]
-    limit = 1.0 / rho[0]
     row, lane = iotas((8, 128))
     row_mask, col_mask = plane_masks(lane)
     for j in range(vol.shape[1] // 128):
         at = slice(128 * j, 128 * j + 128)
-        field = vol[:, at]
-        x = jnp.concatenate([field] * 2, axis=0)
+        x = jnp.concatenate([vol[:, at]] * 2, axis=0)
         gap = [
             jnp.concatenate([dual[k, :, at] - split[k, :, at]] * 2, axis=0) for k in range(3)
         ]
-        depth = jnp.where(row < 3, pltpu.roll(x, 7, axis=0) - x + gap[0], 0.0)
+        above = jnp.where(slab == slabs - 1, 0.0, from_next[0:1, at] - edge[:, at])
+        below = jnp.where(slab == 0, 0.0, x[0:1] - from_previous[0:1, at])
+        depth = jnp.where(row < 3, pltpu.roll(x, 7, axis=0) - x + gap[0], above)
         across = jnp.where(row_mask, pltpu.roll(x, 120, axis=1) - x + gap[1], 0.0)
         along = jnp.where(col_mask, pltpu.roll(x, 127, axis=1) - x + gap[2], 0.0)
-        adjoint = pltpu.roll(depth, 1, axis=0) - depth
+        adjoint = jnp.where(row == 0, below, pltpu.roll(depth, 1, axis=0)) - depth
         adjoint += jnp.where((lane % TV) >= 8, pltpu.roll(across, 8, axis=1), 0.0) - across
         adjoint += jnp.where(lane % 8 >= 1, pltpu.roll(along, 1, axis=1), 0.0) - along
         base_out[:, at] = (x - factor * adjoint)[0:4]
-        edge_out[:, at] = (x - gap[0])[3:4]
-        first_out[:, at] = field[0:1]
-        scale_out[0:1, at] = jnp.full((1, 128), limit, jnp.float32)
-        scale_out[1:2, at] = jnp.full((1, 128), factor, jnp.float32)
 
 
 def backward_kernel(
@@ -214,35 +222,65 @@
         grad_out[:, 128 * j:128 * j + 128] = (both + pltpu.roll(both, 4, axis=0))[0:4]
 
 
-def update_kernel(
-    grad, grad_other, from_next, from_previous, base, edge, first, dual, scales,
-    new_volume, new_split, new_dual,
+def plane_kernel(
+    grad, grad_other, base, dual, limits,
+    new_volume, field_out, split_hbm, dual_hbm,
+    split, clipped, sems,
 ):
-    slab, slabs = lax.axis_index("slab"), lax.axis_size("slab")
-    row, lane = iotas((8, 128))
-    short = lax.broadcasted_iota(jnp.int32, (4, 128), 0)
+    row, lane = iotas((4, 128))
     row_mask, col_mask = plane_masks(lane)
-    inner = jnp.logical_or(row < 3, slab < slabs - 1)
     for j in range(dual.shape[2] // 128):
         at = slice(128 * j, 128 * j + 128)
-        limit, factor = scales[0:1, at], scales[1:2, at]
-        above = jnp.where(slab == slabs - 1, 0.0, factor * (from_next[1:2, at] - edge[:, at]))
-        below = jnp.where(slab == 0, 0.0, factor * (first[:, at] - from_previous[0:1, at]))
-        own = base[:, at] - TAU * (grad[:, at] + grad_other[:, at])
-        own += jnp.where(short == 0, -below, jnp.where(short == 3, above, 0.0))
-        ahead = from_next[0:1, at] - above
-        field = jnp.where(row < 4, jnp.concatenate([own] * 2, axis=0), ahead)
-        new_volume[:, at] = own
+        limit = limits[:, at]
+        field = base[:, at] - TAU * (grad[:, at] + grad_other[:, at])
+        new_volume[:, at] = field
+        field_out[:, at] = field
+        x = jnp.concatenate([field] * 2, axis=0)
         steps = (
-            jnp.where(inner, pltpu.roll(field, 7, axis=0) - field, 0.0),
-            jnp.where(row_mask, pltpu.roll(field, 120, axis=1) - field, 0.0),
-            jnp.where(col_mask, pltpu.roll(field, 127, axis=1) - field, 0.0),
-        )
-        for k in range(3):
-            mixed = steps[k][0:4] + dual[k, :, at]
-            clipped = jnp.clip(mixed, -limit, limit)
-            new_dual[k, :, at] = clipped
-            new_split[k, :, at] = mixed - clipped
+            jnp.where(row_mask, pltpu.roll(x, 120, axis=1)[0:4] - field, 0.0),
+            jnp.where(col_mask, pltpu.roll(x, 127, axis=1)[0:4] - field, 0.0),
+        )
+        for k in range(2):
+            mixed = steps[k] + dual[k + 1, :, at]
+            bounded = jnp.clip(mixed, -limit, limit)
+            clipped[k, :, at] = bounded
+            split[k, :, at] = mixed - bounded
+    copies = [
+        pltpu.make_async_copy(split, split_hbm.at[pl.ds(1, 2)], sems.at[0]),
+        pltpu.make_async_copy(clipped, dual_hbm.at[pl.ds(1, 2)], sems.at[1]),
+    ]
+    for copy in copies:
+        copy.start()
+    for copy in copies:
+        copy.wait()
+
+
+def depth_kernel(
+    field_in, ahead, dual, limits, split_in, dual_in,
+    split_hbm, dual_hbm,
+    split, clipped, sems,
+):
+    del split_in, dual_in
+    last = lax.axis_index("slab") == lax.axis_size("slab") - 1
+    row, lane = iotas((8, 128))
+    inner = jnp.logical_or(row < 3, jnp.logical_not(last))
+    for j in range(dual.shape[2] // 128):
+        at = slice(128 * j, 128 * j + 128)
+        limit = limits[:, at]
+        x = jnp.concatenate([field_in[:, at]] * 2, axis=0)
+        following = jnp.where(row < 3, pltpu.roll(x, 7, axis=0), ahead[:, at])
+        mixed = jnp.where(inner, following - x, 0.0)[0:4] + dual[0, :, at]
+        bounded = jnp.clip(mixed, -limit, limit)
+        clipped[:, at] = bounded
+        split[:, at] = mixed - bounded
+    copies = [
+        pltpu.make_async_copy(split, split_hbm.at[0], sems.at[0]),
+        pltpu.make_async_copy(clipped, dual_hbm.at[0], sems.at[1]),
+    ]
+    for copy in copies:
+        copy.start()
+    for copy in copies:
+        copy.wait()
 
 
 def vmem():
@@ -304,20 +342,22 @@
         name="forward",
     )(tile_count, *sources)
 
-    base, edge, first, scales = pl.pallas_call(
-        local_kernel,
-        out_shape=(
-            jax.ShapeDtypeStruct((slices, width), f32),
-            jax.ShapeDtypeStruct((1, width), f32),
-            jax.ShapeDtypeStruct((1, width), f32),
-            jax.ShapeDtypeStruct((2, width), f32),
-        ),
-        in_specs=[smem()] + [vmem()] * 3,
-        out_specs=(vmem(),) * 4,
-        compiler_params=params(),
-        name="local",
-    )(rho, volume, split_var, dual_var)
-
+    row = jax.ShapeDtypeStruct((1, width), f32)
+    edge, first, halo = pl.pallas_call(
+        edges_kernel,
+        out_shape=(row, row, jax.ShapeDtypeStruct((4, width), f32)),
+        in_specs=[vmem()] * 3,
+        out_specs=(vmem(),) * 3,
+        compiler_params=params(),
+        name="edges",
+    )(volume, split_var, dual_var)
+    across = [(i, i ^ 3) for i in range(2 * reps)]
+    down = [(i, i - 1) for i in range(1, slabs)]
+    if slabs == 2:
+        from_next = from_previous = lax.ppermute(halo, ("slab", "rep"), across)
+    else:
+        from_next = lax.ppermute(first, "slab", down)
+        from_previous = lax.ppermute(edge, "slab", [(i - 1, i) for i in range(1, slabs)])
     swap = [(i, i ^ 1) for i in range(reps)]
     moved = lax.ppermute(partial, "rep", swap)
     step = reps
@@ -327,9 +367,19 @@
             partial, ("tile", "rep"), [(i, i ^ (step + 1)) for i in range(group)]
         )
         step *= 2
-    moved, base, edge, first, scales = lax.optimization_barrier(
-        (moved, base, edge, first, scales)
+    limits = jnp.broadcast_to((1.0 / rho)[:, None], (1, width))
+    moved, from_next, from_previous, limits = lax.optimization_barrier(
+        (moved, from_next, from_previous, limits)
     )
+
+    base = pl.pallas_call(
+        local_kernel,
+        out_shape=jax.ShapeDtypeStruct((slices, width), f32),
+        in_specs=[smem()] + [vmem()] * 6,
+        out_specs=vmem(),
+        compiler_params=params(),
+        name="local",
+    )(rho, volume, split_var, dual_var, edge, from_next, from_previous)
 
     grad = pl.pallas_call(
         backward_kernel,
@@ -346,29 +396,36 @@
         name="backward",
     )(indices, tiles, partial, moved)
     grad_other = lax.ppermute(grad, "rep", swap)
-    ahead = jnp.concatenate([base[0:1] - TAU * (grad[0:1] + grad_other[0:1]), first], axis=0)
-    behind = jnp.concatenate([edge, edge], axis=0)
+    ahead = base[0:1] - TAU * (grad[0:1] + grad_other[0:1])
     if slabs == 2:
-        halo = jnp.where(lax.axis_index("slab") == 0, behind, ahead)
-        from_next = from_previous = lax.ppermute(
-            halo, ("slab", "rep"), [(i, i ^ 3) for i in range(2 * reps)]
-        )
+        ahead = lax.ppermute(ahead, ("slab", "rep"), across)
     else:
-        from_next = lax.ppermute(ahead, "slab", [(i, i - 1) for i in range(1, slabs)])
-        from_previous = lax.ppermute(behind, "slab", [(i - 1, i) for i in range(1, slabs)])
-
-    return pl.pallas_call(
-        update_kernel,
-        out_shape=(
-            jax.ShapeDtypeStruct((slices, width), f32),
-            jax.ShapeDtypeStruct((3, slices, width), f32),
-            jax.ShapeDtypeStruct((3, slices, width), f32),
-        ),
-        in_specs=[vmem()] * 9,
-        out_specs=(vmem(), vmem(), vmem()),
-        compiler_params=params(),
-        name="update",
-    )(grad, grad_other, from_next, from_previous, base, edge, first, dual_var, scales)
+        ahead = lax.ppermute(ahead, "slab", down)
+
+    whole = jax.ShapeDtypeStruct((slices, width), f32)
+    triple = jax.ShapeDtypeStruct((3, slices, width), f32)
+    new_volume, field, new_split, new_dual = pl.pallas_call(
+        plane_kernel,
+        out_shape=(whole, whole, triple, triple),
+        in_specs=[vmem()] * 5,
+        out_specs=(vmem(), vmem(), hbm(), hbm()),
+        scratch_shapes=[pltpu.VMEM((2, slices, width), f32)] * 2
+        + [pltpu.SemaphoreType.DMA((2,))],
+        compiler_params=params(),
+        name="plane",
+    )(grad, grad_other, base, dual_var, limits)
+    new_split, new_dual = pl.pallas_call(
+        depth_kernel,
+        out_shape=(triple, triple),
+        in_specs=[vmem()] * 4 + [hbm()] * 2,
+        out_specs=(hbm(), hbm()),
+        scratch_shapes=[pltpu.VMEM((slices, width), f32)] * 2
+        + [pltpu.SemaphoreType.DMA((2,))],
+        input_output_aliases={4: 0, 5: 1},
+        compiler_params=params(),
+        name="depth",
+    )(field, ahead, dual_var, limits, new_split, new_dual)
+    return new_volume, new_split, new_dual
 
 
 def solution(mesh):

time: 22.4 us -> 22.3 us (level)
  waiting for transfers between devices: 5.79 us -> 3.31 us
  Pallas kernels: 6.02 us -> 7.96 us
  starting transfers between devices: 8.11 us -> 8.63 us
    pallas_call x2 -> x4, Pallas kernels: 1.21 us -> 3.14 us  [the longest x1 1.49 us: shards(): pl.pallas_call(plane_kernel, out_shape=(whole, whole, triple, triple), in...]
    ppermute x1 -> x2, waiting for transfers between devices: 1.78 us -> 0.48 us  [the longest x1 0.47 us: shards(): ahead = lax.ppermute(ahead, ('slab', 'rep'), across)]
    ppermute x1 -> x2, starting transfers between devices: 1.62 us -> 2.7 us  [the longest x1 1.44 us: shards(): from_next = from_previous = lax.ppermute(halo, ('slab', 'rep'), across)]
    ppermute x2, waiting for transfers between devices: 2.24 us -> 1.16 us  [shards(): lax.ppermute(partial, ('tile', 'rep'), [(i, i ^ step + 1) for i in range(...]
    ppermute x2, starting transfers between devices: 5.57 us -> 5.17 us  [shards(): lax.ppermute(partial, ('tile', 'rep'), [(i, i ^ step + 1) for i in range(...]
  transfers between devices with their start and end apart: 5 -> 6, of which waited for: 5 -> 4; matrix products, arithmetic and copies ran while one was open for 0% -> 0% of each run, Pallas kernels for 1% -> 11%
where the time goes in v14:
time: 22.3 us; the launch traced here: 22.1 us
  starting transfers between devices  8.63 us (39%)
  Pallas kernels  7.96 us (36%)
  waiting for transfers between devices  3.31 us (15%)
  between operations  2.1 us (9%)
    ppermute x2, starting transfers between devices, shards(): lax.ppermute(partial, ('tile', 'rep'), [(i, i ^ step + 1) for i in range(...  5.17 us
    pallas_call x1, Pallas kernels, shards(): pl.pallas_call(forward_kernel, out_shape=(jax.ShapeDtypeStruct((rays * sl...  2.86 us
    pallas_call x1, Pallas kernels, shards(): pl.pallas_call(backward_kernel, out_shape=jax.ShapeDtypeStruct((slices, w...  1.96 us
    pallas_call x1, Pallas kernels, shards(): pl.pallas_call(plane_kernel, out_shape=(whole, whole, triple, triple), in...  1.49 us
    ppermute x1, starting transfers between devices, shards(): from_next = from_previous = lax.ppermute(halo, ('slab', 'rep'), across)  1.44 us
    ppermute x1, starting transfers between devices, shards(): ahead = lax.ppermute(ahead, ('slab', 'rep'), across)  1.26 us
    ppermute x2, waiting for transfers between devices, shards(): lax.ppermute(partial, ('tile', 'rep'), [(i, i ^ step + 1) for i in range(...  1.16 us
    ppermute x1, waiting for transfers between devices, shards(): moved = lax.ppermute(partial, 'rep', swap)  0.86 us
  transfers between devices with their start and end apart: 6, of which 4 were waited for; matrix products, arithmetic and copies ran while one was open for 0% of the time, Pallas kernels for 11%

profile of v14, /device:TPU:0, one launch (start us, length us, event | category | flops | bytes accessed | tf_op | source)
XLA Modules:
  0.0 22.1 jit_solution(11254177274305296018)
XLA Ops:
  0.6 0.0 copy-start.2
  0.6 0.0 copy-start
  0.7 0.0 copy-start.1
  1.4 2.9 %forward.1 = (bf16[128,128]{1,0:T(8,128)(2,1)S(1)}, s32[8,128]{1,0:T(8,128)S(1)}, bf16[256,64,128]{2,1,0:T(8,128)(2,1)S(1)}) custom-call(s32[1]{0:T(128)S(6)} %copy.16.count, s32[2,128]{1,0:T(2,128)} %bitcast.3, s32[2,128]{1,0:T(2,128)} %bitcast.4, f32[4,4096]{1,0:T(4,128)} %vol.3, f32[4,4,128]{2,1,0:T(4,128)} %sino_hbm.1, bf16[256,64,128]{2,1,0:T(8,128)(2,1)} %proj_hbm.1), custom_call_target="tpu_custom_call" | custom-call | tf_op jit(solution)/shard_map/forward/pallas_call | solution.py:321
  4.2 0.5 %collective-permute-start = (bf16[128,128]{1,0:T(8,128)(2,1)S(1)}, bf16[128,128]{1,0:T(8,128)(2,1)S(1)}, u32[]{:S(2)}, u32[]{:S(2)}) collective-permute-start(bf16[128,128]{1,0:T(8,128)(2,1)S(1)} %get-tuple-element.20), channel_id=1, source_target_pairs={{0,1},{1,0},{2,3},{3,2},{4,5},{5,4},{6,7},{7,6},{8,9},{9,8},{10,11... | collective-permute-start | bytes 98312 | tf_op jit(solution)/shard_map/ppermute | solution.py:362
  4.7 0.9 %collective-permute-done = bf16[128,128]{1,0:T(8,128)(2,1)S(1)} collective-permute-done((bf16[128,128]{1,0:T(8,128)(2,1)S(1)}, bf16[128,128]{1,0:T(8,128)(2,1)S(1)}, u32[]{:S(2)}, u32[]{:S(2)}) %collective-permute-start) | collective-permute-done | bytes 32800 | tf_op jit(solution)/shard_map/ppermute | solution.py:362
  5.6 2.7 %collective-permute-start.1 = (bf16[128,128]{1,0:T(8,128)(2,1)S(1)}, bf16[128,128]{1,0:T(8,128)(2,1)S(1)}, u32[]{:S(2)}, u32[]{:S(2)}) collective-permute-start(bf16[128,128]{1,0:T(8,128)(2,1)S(1)} %add_convert_fusion.1), channel_id=1, source_target_pairs={{0,5},{1,4},{4,1},{5,0},{8,13},{9,12},{12,9},{13,8},{2,7},{3,6},{6... | collective-permute-start | bytes 98312 | tf_op jit(solution)/shard_map/ppermute | solution.py:366
  8.3 0.0 copy-done.2
  8.4 0.0 copy-done
  8.4 0.0 copy-done.1
  8.4 0.7 %edges.1 = (f32[1,4096]{1,0:T(1,128)S(1)}, f32[1,4096]{1,0:T(1,128)}, f32[4,4096]{1,0:T(4,128)S(1)}) custom-call(f32[4,4096]{1,0:T(4,128)S(1)} %copy-done.2, f32[3,4,4096]{2,1,0:T(4,128)S(1)} %copy-done.1, f32[3,4,4096]{2,1,0:T(4,128)S(1)} %copy-done), custom_call_target="tpu_custom_call" | custom-call | tf_op jit(solution)/shard_map/edges/pallas_call | solution.py:346
  9.0 1.4 %collective-permute-start.3 = (f32[4,4096]{1,0:T(4,128)S(1)}, f32[4,4096]{1,0:T(4,128)S(1)}, u32[]{:S(2)}, u32[]{:S(2)}) collective-permute-start(f32[4,4096]{1,0:T(4,128)S(1)} %get-tuple-element.21), channel_id=1, source_target_pairs={{0,3},{1,2},{2,1},{3,0},{4,7},{5,6},{6,5},{7,4},{8,11},{9,10},{10,... | collective-permute-start | bytes 196616 | tf_op jit(solution)/shard_map/ppermute | solution.py:357
  10.5 0.0 collective-permute-done.1
  10.5 2.4 %collective-permute-start.2 = (bf16[128,128]{1,0:T(8,128)(2,1)S(1)}, bf16[128,128]{1,0:T(8,128)(2,1)S(1)}, u32[]{:S(2)}, u32[]{:S(2)}) collective-permute-start(bf16[128,128]{1,0:T(8,128)(2,1)S(1)} %add_convert_fusion.part), channel_id=1, source_target_pairs={{0,9},{1,8},{4,13},{5,12},{8,1},{9,0},{12,5},{13,4},{2,11},{3,10},... | collective-permute-start | bytes 98312 | tf_op jit(solution)/shard_map/ppermute | solution.py:366
  13.6 0.0 collective-permute-done.3.from_next.from_previous
  13.6 1.2 %collective-permute-done.2.moved = bf16[128,128]{1,0:T(8,128)(2,1)S(1)} collective-permute-done((bf16[128,128]{1,0:T(8,128)(2,1)S(1)}, bf16[128,128]{1,0:T(8,128)(2,1)S(1)}, u32[]{:S(2)}, u32[]{:S(2)}) %collective-permute-start.2) | collective-permute-done | bytes 32800 | tf_op jit(solution)/shard_map/ppermute | solution.py:366
  14.8 2.0 %backward.1.grad = f32[4,4096]{1,0:T(4,128)S(1)} custom-call(s32[8,128]{1,0:T(8,128)S(1)} %get-tuple-element.18.indices, bf16[256,64,128]{2,1,0:T(8,128)(2,1)S(1)} %get-tuple-element.19.tiles, bf16[128,128]{1,0:T(8,128)(2,1)S(1)} %add_convert_fusion.part, bf16[128,128]{1,0:T(8,128)(2,1)S(1)} %collective-permute-done.2.moved), custom_call_target="tpu_custom_call" | custom-call | tf_op jit(solution)/shard_map/backward/pallas_call | solution.py:384
  16.8 0.2 %collective-permute-start.4 = (f32[4,4096]{1,0:T(4,128)S(1)}, f32[4,4096]{1,0:T(4,128)S(1)}, u32[]{:S(2)}, u32[]{:S(2)}) collective-permute-start(f32[4,4096]{1,0:T(4,128)S(1)} %backward.1.grad), channel_id=1, source_target_pairs={{0,1},{1,0},{2,3},{3,2},{4,5},{5,4},{6,7},{7,6},{8,9},{9,8},{10,11... | collective-permute-start | bytes 196616 | tf_op jit(solution)/shard_map/ppermute | solution.py:398
  17.0 0.3 %local.1.base = f32[4,4096]{1,0:T(4,128)S(1)} custom-call(f32[1]{0:T(128)S(6)} %copy.17.rho, f32[4,4096]{1,0:T(4,128)S(1)} %copy-done.2, f32[3,4,4096]{2,1,0:T(4,128)S(1)} %copy-done.1, f32[3,4,4096]{2,1,0:T(4,128)S(1)} %copy-done, f32[1,4096]{1,0:T(1,128)S(1)} %get-tuple-element.23.edge, f32[4,4096]{1,0:T(4,128)S(1)} %collective-permute-done.3.from_next.from_previous, ...), custom_call_target="tpu_custom_call" | custom-call | tf_op jit(solution)/shard_map/local/pallas_call | solution.py:375
  17.3 0.8 %collective-permute-done.4.grad_other = f32[4,4096]{1,0:T(4,128)S(1)} collective-permute-done((f32[4,4096]{1,0:T(4,128)S(1)}, f32[4,4096]{1,0:T(4,128)S(1)}, u32[]{:S(2)}, u32[]{:S(2)}) %collective-permute-start.4) | collective-permute-done | bytes 65568 | tf_op jit(solution)/shard_map/ppermute | solution.py:398
  18.1 1.3 %collective-permute-start.5 = (f32[1,4096]{1,0:T(1,128)S(1)}, f32[1,4096]{1,0:T(1,128)S(1)}, u32[]{:S(2)}, u32[]{:S(2)}) collective-permute-start(f32[1,4096]{1,0:T(1,128)S(1)} %fusion.1), channel_id=1, source_target_pairs={{0,3},{1,2},{2,1},{3,0},{4,7},{5,6},{6,5},{7,4},{8,11},{9,10},{10,... | collective-permute-start | bytes 49160 | tf_op jit(solution)/shard_map/ppermute | solution.py:401
  19.4 1.5 %plane.1 = (f32[4,4096]{1,0:T(4,128)}, f32[4,4096]{1,0:T(4,128)S(1)}, f32[3,4,4096]{2,1,0:T(4,128)}, f32[3,4,4096]{2,1,0:T(4,128)}) custom-call(f32[4,4096]{1,0:T(4,128)S(1)} %backward.1.grad, f32[4,4096]{1,0:T(4,128)S(1)} %collective-permute-done.4.grad_other, f32[4,4096]{1,0:T(4,128)S(1)} %local.1.base, f32[3,4,4096]{2,1,0:T(4,128)S(1)} %copy-done, ...), custom_call_target="tpu_custom_call" | custom-call | tf_op jit(solution)/shard_map/plane/pallas_call | solution.py:407
  20.9 0.5 %collective-permute-done.5.ahead = f32[1,4096]{1,0:T(1,128)S(1)} collective-permute-done((f32[1,4096]{1,0:T(1,128)S(1)}, f32[1,4096]{1,0:T(1,128)S(1)}, u32[]{:S(2)}, u32[]{:S(2)}) %collective-permute-start.5) | collective-permute-done | bytes 16416 | tf_op jit(solution)/shard_map/ppermute | solution.py:401
  21.4 0.7 %depth.1 = (f32[3,4,4096]{2,1,0:T(4,128)}, f32[3,4,4096]{2,1,0:T(4,128)}) custom-call(f32[4,4096]{1,0:T(4,128)S(1)} %get-tuple-element.28.field_in, f32[1,4096]{1,0:T(1,128)S(1)} %collective-permute-done.5.ahead, f32[3,4,4096]{2,1,0:T(4,128)S(1)} %copy-done, f32[1,4096]{1,0:T(1,128)S(1)} %broadcast_in_dim.9.limits, ...), custom_call_target="tpu_custom_call", output_to_operand_aliasing={{0}: (4, {}), {1}: (5, {})} | custom-call | tf_op jit(solution)/shard_map/depth/pallas_call | solution.py:417
  (4 shorter events, 0.1 us)
Async XLA Ops:
  0.6 7.7 %copy-start.2 = (f32[4,4096]{1,0:T(4,128)S(1)}, f32[4,4096]{1,0:T(4,128)}, u32[]{:S(2)}) copy-start(f32[4,4096]{1,0:T(4,128)} %vol.3) | copy-start | bytes 196612
  0.6 7.7 %copy-start = (f32[3,4,4096]{2,1,0:T(4,128)S(1)}, f32[3,4,4096]{2,1,0:T(4,128)}, u32[]{:S(2)}) copy-start(f32[3,4,4096]{2,1,0:T(4,128)} %dual.7) | copy-start | bytes 589828
  0.7 7.7 %copy-start.1 = (f32[3,4,4096]{2,1,0:T(4,128)S(1)}, f32[3,4,4096]{2,1,0:T(4,128)}, u32[]{:S(2)}) copy-start(f32[3,4,4096]{2,1,0:T(4,128)} %split.3) | copy-start | bytes 589828
  4.2 1.4 %collective-permute-start = (bf16[128,128]{1,0:T(8,128)(2,1)S(1)}, bf16[128,128]{1,0:T(8,128)(2,1)S(1)}, u32[]{:S(2)}, u32[]{:S(2)}) collective-permute-start(bf16[128,128]{1,0:T(8,128)(2,1)S(1)} %get-tuple-element.20), channel_id=1, source_target_pairs={{0,1},{1,0},{2,3},{3,2},{4,5},{5,4},{6,7},{7,6},{8,9},{9,8},{10,11... | collective-permute-start | bytes 98312 | tf_op jit(solution)/shard_map/ppermute | solution.py:362
  5.6 4.8 %collective-permute-start.1 = (bf16[128,128]{1,0:T(8,128)(2,1)S(1)}, bf16[128,128]{1,0:T(8,128)(2,1)S(1)}, u32[]{:S(2)}, u32[]{:S(2)}) collective-permute-start(bf16[128,128]{1,0:T(8,128)(2,1)S(1)} %add_convert_fusion.1), channel_id=1, source_target_pairs={{0,5},{1,4},{4,1},{5,0},{8,13},{9,12},{12,9},{13,8},{2,7},{3,6},{6... | collective-permute-start | bytes 98312 | tf_op jit(solution)/shard_map/ppermute | solution.py:366
  9.0 4.6 %collective-permute-start.3 = (f32[4,4096]{1,0:T(4,128)S(1)}, f32[4,4096]{1,0:T(4,128)S(1)}, u32[]{:S(2)}, u32[]{:S(2)}) collective-permute-start(f32[4,4096]{1,0:T(4,128)S(1)} %get-tuple-element.21), channel_id=1, source_target_pairs={{0,3},{1,2},{2,1},{3,0},{4,7},{5,6},{6,5},{7,4},{8,11},{9,10},{10,... | collective-permute-start | bytes 196616 | tf_op jit(solution)/shard_map/ppermute | solution.py:357
  10.5 4.3 %collective-permute-start.2 = (bf16[128,128]{1,0:T(8,128)(2,1)S(1)}, bf16[128,128]{1,0:T(8,128)(2,1)S(1)}, u32[]{:S(2)}, u32[]{:S(2)}) collective-permute-start(bf16[128,128]{1,0:T(8,128)(2,1)S(1)} %add_convert_fusion.part), channel_id=1, source_target_pairs={{0,9},{1,8},{4,13},{5,12},{8,1},{9,0},{12,5},{13,4},{2,11},{3,10},... | collective-permute-start | bytes 98312 | tf_op jit(solution)/shard_map/ppermute | solution.py:366
  16.8 1.3 %collective-permute-start.4 = (f32[4,4096]{1,0:T(4,128)S(1)}, f32[4,4096]{1,0:T(4,128)S(1)}, u32[]{:S(2)}, u32[]{:S(2)}) collective-permute-start(f32[4,4096]{1,0:T(4,128)S(1)} %backward.1.grad), channel_id=1, source_target_pairs={{0,1},{1,0},{2,3},{3,2},{4,5},{5,4},{6,7},{7,6},{8,9},{9,8},{10,11... | collective-permute-start | bytes 196616 | tf_op jit(solution)/shard_map/ppermute | solution.py:398
  18.1 3.2 %collective-permute-start.5 = (f32[1,4096]{1,0:T(1,128)S(1)}, f32[1,4096]{1,0:T(1,128)S(1)}, u32[]{:S(2)}, u32[]{:S(2)}) collective-permute-start(f32[1,4096]{1,0:T(1,128)S(1)} %fusion.1), channel_id=1, source_target_pairs={{0,3},{1,2},{2,1},{3,0},{4,7},{5,6},{6,5},{7,4},{8,11},{9,10},{10,... | collective-permute-start | bytes 49160 | tf_op jit(solution)/shard_map/ppermute | solution.py:401

commit v15 on v11

--- a/solution.py
+++ b/solution.py
@@ -136,29 +136,35 @@
         partial_out[16 * q:16 * q + 16, :] = jnp.concatenate(halves, axis=0).astype(jnp.bfloat16)
 
 
-def local_kernel(rho, vol, split, dual, base_out, edge_out, first_out, scale_out):
+def edges_kernel(vol, split, dual, edge_out, halo_out):
+    start = lax.axis_index("slab") == 0
+    for j in range(vol.shape[1] // 128):
+        at = slice(128 * j, 128 * j + 128)
+        edge = vol[3:4, at] - dual[0, 3:4, at] + split[0, 3:4, at]
+        edge_out[:, at] = edge
+        halo_out[:, at] = jnp.broadcast_to(jnp.where(start, edge, vol[0:1, at]), (4, 128))
+
+
+def local_kernel(rho, vol, split, dual, edge, from_next, from_previous, base_out):
+    slab, slabs = lax.axis_index("slab"), lax.axis_size("slab")
     factor = TAU * rho[0]
-    limit = 1.0 / rho[0]
     row, lane = iotas((8, 128))
     row_mask, col_mask = plane_masks(lane)
     for j in range(vol.shape[1] // 128):
         at = slice(128 * j, 128 * j + 128)
-        field = vol[:, at]
-        x = jnp.concatenate([field] * 2, axis=0)
+        x = jnp.concatenate([vol[:, at]] * 2, axis=0)
         gap = [
             jnp.concatenate([dual[k, :, at] - split[k, :, at]] * 2, axis=0) for k in range(3)
         ]
-        depth = jnp.where(row < 3, pltpu.roll(x, 7, axis=0) - x + gap[0], 0.0)
+        above = jnp.where(slab == slabs - 1, 0.0, from_next[0:1, at] - edge[:, at])
+        below = jnp.where(slab == 0, 0.0, x[0:1] - from_previous[0:1, at])
+        depth = jnp.where(row < 3, pltpu.roll(x, 7, axis=0) - x + gap[0], above)
         across = jnp.where(row_mask, pltpu.roll(x, 120, axis=1) - x + gap[1], 0.0)
         along = jnp.where(col_mask, pltpu.roll(x, 127, axis=1) - x + gap[2], 0.0)
-        adjoint = pltpu.roll(depth, 1, axis=0) - depth
+        adjoint = jnp.where(row == 0, below, pltpu.roll(depth, 1, axis=0)) - depth
         adjoint += jnp.where((lane % TV) >= 8, pltpu.roll(across, 8, axis=1), 0.0) - across
         adjoint += jnp.where(lane % 8 >= 1, pltpu.roll(along, 1, axis=1), 0.0) - along
         base_out[:, at] = (x - factor * adjoint)[0:4]
-        edge_out[:, at] = (x - gap[0])[3:4]
-        first_out[:, at] = field[0:1]
-        scale_out[0:1, at] = jnp.full((1, 128), limit, jnp.float32)
-        scale_out[1:2, at] = jnp.full((1, 128), factor, jnp.float32)
 
 
 def backward_kernel(
@@ -215,23 +221,18 @@
 
 
 def update_kernel(
-    grad, grad_other, from_next, from_previous, base, edge, first, dual, scales,
+    grad, grad_other, ahead, base, dual, limits,
     new_volume, new_split, new_dual,
 ):
-    slab, slabs = lax.axis_index("slab"), lax.axis_size("slab")
+    last = lax.axis_index("slab") == lax.axis_size("slab") - 1
     row, lane = iotas((8, 128))
-    short = lax.broadcasted_iota(jnp.int32, (4, 128), 0)
     row_mask, col_mask = plane_masks(lane)
-    inner = jnp.logical_or(row < 3, slab < slabs - 1)
+    inner = jnp.logical_or(row < 3, jnp.logical_not(last))
     for j in range(dual.shape[2] // 128):
         at = slice(128 * j, 128 * j + 128)
-        limit, factor = scales[0:1, at], scales[1:2, at]
-        above = jnp.where(slab == slabs - 1, 0.0, factor * (from_next[1:2, at] - edge[:, at]))
-        below = jnp.where(slab == 0, 0.0, factor * (first[:, at] - from_previous[0:1, at]))
+        limit = limits[:, at]
         own = base[:, at] - TAU * (grad[:, at] + grad_other[:, at])
-        own += jnp.where(short == 0, -below, jnp.where(short == 3, above, 0.0))
-        ahead = from_next[0:1, at] - above
-        field = jnp.where(row < 4, jnp.concatenate([own] * 2, axis=0), ahead)
+        field = jnp.where(row < 4, jnp.concatenate([own] * 2, axis=0), ahead[:, at])
         new_volume[:, at] = own
         steps = (
             jnp.where(inner, pltpu.roll(field, 7, axis=0) - field, 0.0),
@@ -304,20 +305,22 @@
         name="forward",
     )(tile_count, *sources)
 
-    base, edge, first, scales = pl.pallas_call(
-        local_kernel,
-        out_shape=(
-            jax.ShapeDtypeStruct((slices, width), f32),
-            jax.ShapeDtypeStruct((1, width), f32),
-            jax.ShapeDtypeStruct((1, width), f32),
-            jax.ShapeDtypeStruct((2, width), f32),
-        ),
-        in_specs=[smem()] + [vmem()] * 3,
-        out_specs=(vmem(),) * 4,
+    row = jax.ShapeDtypeStruct((1, width), f32)
+    edge, halo = pl.pallas_call(
+        edges_kernel,
+        out_shape=(row, jax.ShapeDtypeStruct((4, width), f32)),
+        in_specs=[vmem()] * 3,
+        out_specs=(vmem(),) * 2,
         compiler_params=params(),
-        name="local",
-    )(rho, volume, split_var, dual_var)
-
+        name="edges",
+    )(volume, split_var, dual_var)
+    across = [(i, i ^ 3) for i in range(2 * reps)]
+    down = [(i, i - 1) for i in range(1, slabs)]
+    if slabs == 2:
+        from_next = from_previous = lax.ppermute(halo, ("slab", "rep"), across)
+    else:
+        from_next = lax.ppermute(volume[0:1], "slab", down)
+        from_previous = lax.ppermute(edge, "slab", [(i - 1, i) for i in range(1, slabs)])
     swap = [(i, i ^ 1) for i in range(reps)]
     moved = lax.ppermute(partial, "rep", swap)
     step = reps
@@ -327,9 +330,19 @@
             partial, ("tile", "rep"), [(i, i ^ (step + 1)) for i in range(group)]
         )
         step *= 2
-    moved, base, edge, first, scales = lax.optimization_barrier(
-        (moved, base, edge, first, scales)
+    limits = jnp.broadcast_to((1.0 / rho)[:, None], (1, width))
+    moved, from_next, from_previous, limits = lax.optimization_barrier(
+        (moved, from_next, from_previous, limits)
     )
+
+    base = pl.pallas_call(
+        local_kernel,
+        out_shape=jax.ShapeDtypeStruct((slices, width), f32),
+        in_specs=[smem()] + [vmem()] * 6,
+        out_specs=vmem(),
+        compiler_params=params(),
+        name="local",
+    )(rho, volume, split_var, dual_var, edge, from_next, from_previous)
 
     grad = pl.pallas_call(
         backward_kernel,
@@ -346,29 +359,21 @@
         name="backward",
     )(indices, tiles, partial, moved)
     grad_other = lax.ppermute(grad, "rep", swap)
-    ahead = jnp.concatenate([base[0:1] - TAU * (grad[0:1] + grad_other[0:1]), first], axis=0)
-    behind = jnp.concatenate([edge, edge], axis=0)
+    ahead = base[0:1] - TAU * (grad[0:1] + grad_other[0:1])
     if slabs == 2:
-        halo = jnp.where(lax.axis_index("slab") == 0, behind, ahead)
-        from_next = from_previous = lax.ppermute(
-            halo, ("slab", "rep"), [(i, i ^ 3) for i in range(2 * reps)]
-        )
+        ahead = lax.ppermute(ahead, ("slab", "rep"), across)
     else:
-        from_next = lax.ppermute(ahead, "slab", [(i, i - 1) for i in range(1, slabs)])
-        from_previous = lax.ppermute(behind, "slab", [(i - 1, i) for i in range(1, slabs)])
-
+        ahead = lax.ppermute(ahead, "slab", down)
+
+    triple = jax.ShapeDtypeStruct((3, slices, width), f32)
     return pl.pallas_call(
         update_kernel,
-        out_shape=(
-            jax.ShapeDtypeStruct((slices, width), f32),
-            jax.ShapeDtypeStruct((3, slices, width), f32),
-            jax.ShapeDtypeStruct((3, slices, width), f32),
-        ),
-        in_specs=[vmem()] * 9,
-        out_specs=(vmem(), vmem(), vmem()),
+        out_shape=(jax.ShapeDtypeStruct((slices, width), f32), triple, triple),
+        in_specs=[vmem()] * 6,
+        out_specs=(vmem(),) * 3,
         compiler_params=params(),
         name="update",
-    )(grad, grad_other, from_next, from_previous, base, edge, first, dual_var, scales)
+    )(grad, grad_other, ahead, base, dual_var, limits)
 
 
 def solution(mesh):

time: 22.4 us -> 22.1 us (0.987)
  waiting for transfers between devices: 5.79 us -> 4.04 us
  starting transfers between devices: 8.11 us -> 9.64 us
    ppermute x1 -> x2, starting transfers between devices: 1.62 us -> 3.13 us  [the longest x1 1.62 us: shards(): ahead = lax.ppermute(ahead, ('slab', 'rep'), across)]
    ppermute x2, waiting for transfers between devices: 2.24 us -> 0.93 us  [shards(): lax.ppermute(partial, ('tile', 'rep'), [(i, i ^ step + 1) for i in range(...]
    ppermute x1, waiting for transfers between devices: 0.91 us -> 0.63 us  [shards(): grad_other = lax.ppermute(grad, 'rep', swap)]
    ppermute x1 -> x2, waiting for transfers between devices: 1.78 us -> 1.61 us  [the longest x1 1.61 us: shards(): ahead = lax.ppermute(ahead, ('slab', 'rep'), across)]
  transfers between devices with their start and end apart: 5 -> 6, of which waited for: 5 -> 4; matrix products, arithmetic and copies ran while one was open for 0% -> 0% of each run, Pallas kernels for 1% -> 1%
where the time goes in v15:
time: 22.1 us; the launch traced here: 21.9 us
  starting transfers between devices  9.64 us (44%)
  Pallas kernels  6.04 us (27%)
  waiting for transfers between devices  4.04 us (18%)
  between operations  2.1 us (10%)
    ppermute x2, starting transfers between devices, shards(): lax.ppermute(partial, ('tile', 'rep'), [(i, i ^ step + 1) for i in range(...  5.58 us
    pallas_call x1, Pallas kernels, shards(): pl.pallas_call(forward_kernel, out_shape=(jax.ShapeDtypeStruct((rays * sl...  2.86 us
    pallas_call x1, Pallas kernels, shards(): pl.pallas_call(backward_kernel, out_shape=jax.ShapeDtypeStruct((slices, w...  1.97 us
    ppermute x1, starting transfers between devices, shards(): ahead = lax.ppermute(ahead, ('slab', 'rep'), across)  1.62 us
    ppermute x1, waiting for transfers between devices, shards(): ahead = lax.ppermute(ahead, ('slab', 'rep'), across)  1.61 us
    ppermute x1, starting transfers between devices, shards(): from_next = from_previous = lax.ppermute(halo, ('slab', 'rep'), across)  1.51 us
    ppermute x2, waiting for transfers between devices, shards(): lax.ppermute(partial, ('tile', 'rep'), [(i, i ^ step + 1) for i in range(...  0.93 us
    pallas_call x1, Pallas kernels, shards(): pl.pallas_call(update_kernel, out_shape=(jax.ShapeDtypeStruct((slices, wi...  0.89 us
  transfers between devices with their start and end apart: 6, of which 4 were waited for; matrix products, arithmetic and copies ran while one was open for 0% of the time, Pallas kernels for 1%

profile of v15, /device:TPU:0, one launch (start us, length us, event | category | flops | bytes accessed | tf_op | source)
XLA Modules:
  0.0 21.9 jit_solution(2616368074018739713)
XLA Ops:
  0.6 0.0 copy-start.2
  0.6 0.0 copy-start
  0.7 0.0 copy-start.1
  1.4 2.9 %forward.1 = (bf16[128,128]{1,0:T(8,128)(2,1)S(1)}, s32[8,128]{1,0:T(8,128)S(1)}, bf16[256,64,128]{2,1,0:T(8,128)(2,1)S(1)}) custom-call(s32[1]{0:T(128)S(6)} %copy.12.count, s32[2,128]{1,0:T(2,128)} %bitcast.3, s32[2,128]{1,0:T(2,128)} %bitcast.4, f32[4,4096]{1,0:T(4,128)} %vol.3, f32[4,4,128]{2,1,0:T(4,128)} %sino_hbm.1, bf16[256,64,128]{2,1,0:T(8,128)(2,1)} %proj_hbm.1), custom_call_target="tpu_custom_call" | custom-call | tf_op jit(solution)/shard_map/forward/pallas_call | solution.py:284
  4.2 0.5 %collective-permute-start = (bf16[128,128]{1,0:T(8,128)(2,1)S(1)}, bf16[128,128]{1,0:T(8,128)(2,1)S(1)}, u32[]{:S(2)}, u32[]{:S(2)}) collective-permute-start(bf16[128,128]{1,0:T(8,128)(2,1)S(1)} %get-tuple-element.14), channel_id=1, source_target_pairs={{0,1},{1,0},{2,3},{3,2},{4,5},{5,4},{6,7},{7,6},{8,9},{9,8},{10,11... | collective-permute-start | bytes 98312 | tf_op jit(solution)/shard_map/ppermute | solution.py:325
  4.7 0.9 %collective-permute-done = bf16[128,128]{1,0:T(8,128)(2,1)S(1)} collective-permute-done((bf16[128,128]{1,0:T(8,128)(2,1)S(1)}, bf16[128,128]{1,0:T(8,128)(2,1)S(1)}, u32[]{:S(2)}, u32[]{:S(2)}) %collective-permute-start) | collective-permute-done | bytes 32800 | tf_op jit(solution)/shard_map/ppermute | solution.py:325
  5.6 2.8 %collective-permute-start.1 = (bf16[128,128]{1,0:T(8,128)(2,1)S(1)}, bf16[128,128]{1,0:T(8,128)(2,1)S(1)}, u32[]{:S(2)}, u32[]{:S(2)}) collective-permute-start(bf16[128,128]{1,0:T(8,128)(2,1)S(1)} %add_convert_fusion.1), channel_id=1, source_target_pairs={{0,5},{1,4},{4,1},{5,0},{8,13},{9,12},{12,9},{13,8},{2,7},{3,6},{6... | collective-permute-start | bytes 98312 | tf_op jit(solution)/shard_map/ppermute | solution.py:329
  8.4 0.0 copy-done.2
  8.4 0.0 copy-done
  8.4 0.0 copy-done.1
  8.4 1.5 %collective-permute-start.3 = (f32[4,4096]{1,0:T(4,128)S(1)}, f32[4,4096]{1,0:T(4,128)S(1)}, u32[]{:S(2)}, u32[]{:S(2)}) collective-permute-start(f32[4,4096]{1,0:T(4,128)S(1)} %get-tuple-element.15), channel_id=1, source_target_pairs={{0,3},{1,2},{2,1},{3,0},{4,7},{5,6},{6,5},{7,4},{8,11},{9,10},{10,... | collective-permute-start | bytes 196616 | tf_op jit(solution)/shard_map/ppermute | solution.py:320
  9.9 0.0 collective-permute-done.1
  10.0 2.8 %collective-permute-start.2 = (bf16[128,128]{1,0:T(8,128)(2,1)S(1)}, bf16[128,128]{1,0:T(8,128)(2,1)S(1)}, u32[]{:S(2)}, u32[]{:S(2)}) collective-permute-start(bf16[128,128]{1,0:T(8,128)(2,1)S(1)} %add_convert_fusion.part), channel_id=1, source_target_pairs={{0,9},{1,8},{4,13},{5,12},{8,1},{9,0},{12,5},{13,4},{2,11},{3,10},... | collective-permute-start | bytes 98312 | tf_op jit(solution)/shard_map/ppermute | solution.py:329
  13.5 0.0 collective-permute-done.3.from_next.from_previous
  13.5 0.9 %collective-permute-done.2.moved = bf16[128,128]{1,0:T(8,128)(2,1)S(1)} collective-permute-done((bf16[128,128]{1,0:T(8,128)(2,1)S(1)}, bf16[128,128]{1,0:T(8,128)(2,1)S(1)}, u32[]{:S(2)}, u32[]{:S(2)}) %collective-permute-start.2) | collective-permute-done | bytes 32800 | tf_op jit(solution)/shard_map/ppermute | solution.py:329
  14.4 2.0 %backward.1.grad = f32[4,4096]{1,0:T(4,128)S(1)} custom-call(s32[8,128]{1,0:T(8,128)S(1)} %get-tuple-element.12.indices, bf16[256,64,128]{2,1,0:T(8,128)(2,1)S(1)} %get-tuple-element.13.tiles, bf16[128,128]{1,0:T(8,128)(2,1)S(1)} %add_convert_fusion.part, bf16[128,128]{1,0:T(8,128)(2,1)S(1)} %collective-permute-done.2.moved), custom_call_target="tpu_custom_call" | custom-call | tf_op jit(solution)/shard_map/backward/pallas_call | solution.py:347
  16.4 0.4 %collective-permute-start.4 = (f32[4,4096]{1,0:T(4,128)S(1)}, f32[4,4096]{1,0:T(4,128)S(1)}, u32[]{:S(2)}, u32[]{:S(2)}) collective-permute-start(f32[4,4096]{1,0:T(4,128)S(1)} %backward.1.grad), channel_id=1, source_target_pairs={{0,1},{1,0},{2,3},{3,2},{4,5},{5,4},{6,7},{7,6},{8,9},{9,8},{10,11... | collective-permute-start | bytes 196616 | tf_op jit(solution)/shard_map/ppermute | solution.py:361
  16.8 0.3 %local.1.base = f32[4,4096]{1,0:T(4,128)S(1)} custom-call(f32[1]{0:T(128)S(6)} %copy.13.rho, f32[4,4096]{1,0:T(4,128)S(1)} %copy-done.2, f32[3,4,4096]{2,1,0:T(4,128)S(1)} %copy-done.1, f32[3,4,4096]{2,1,0:T(4,128)S(1)} %copy-done, f32[1,4096]{1,0:T(1,128)S(1)} %get-tuple-element.17.edge, f32[4,4096]{1,0:T(4,128)S(1)} %collective-permute-done.3.from_next.from_previous, ...), custom_call_target="tpu_custom_call" | custom-call | tf_op jit(solution)/shard_map/local/pallas_call | solution.py:338
  17.1 0.6 %collective-permute-done.4.grad_other = f32[4,4096]{1,0:T(4,128)S(1)} collective-permute-done((f32[4,4096]{1,0:T(4,128)S(1)}, f32[4,4096]{1,0:T(4,128)S(1)}, u32[]{:S(2)}, u32[]{:S(2)}) %collective-permute-start.4) | collective-permute-done | bytes 65568 | tf_op jit(solution)/shard_map/ppermute | solution.py:361
  17.8 1.6 %collective-permute-start.5 = (f32[1,4096]{1,0:T(1,128)S(1)}, f32[1,4096]{1,0:T(1,128)S(1)}, u32[]{:S(2)}, u32[]{:S(2)}) collective-permute-start(f32[1,4096]{1,0:T(1,128)S(1)} %fusion.1), channel_id=1, source_target_pairs={{0,3},{1,2},{2,1},{3,0},{4,7},{5,6},{6,5},{7,4},{8,11},{9,10},{10,... | collective-permute-start | bytes 49160 | tf_op jit(solution)/shard_map/ppermute | solution.py:364
  19.4 1.6 %collective-permute-done.5.ahead = f32[1,4096]{1,0:T(1,128)S(1)} collective-permute-done((f32[1,4096]{1,0:T(1,128)S(1)}, f32[1,4096]{1,0:T(1,128)S(1)}, u32[]{:S(2)}, u32[]{:S(2)}) %collective-permute-start.5) | collective-permute-done | bytes 16416 | tf_op jit(solution)/shard_map/ppermute | solution.py:364
  21.0 0.9 %update.1 = (f32[4,4096]{1,0:T(4,128)}, f32[3,4,4096]{2,1,0:T(4,128)}, f32[3,4,4096]{2,1,0:T(4,128)}) custom-call(f32[4,4096]{1,0:T(4,128)S(1)} %backward.1.grad, f32[4,4096]{1,0:T(4,128)S(1)} %collective-permute-done.4.grad_other, f32[1,4096]{1,0:T(1,128)S(1)} %collective-permute-done.5.ahead, f32[4,4096]{1,0:T(4,128)S(1)} %local.1.base, ...), custom_call_target="tpu_custom_call" | custom-call | tf_op jit(solution)/shard_map/update/pallas_call | solution.py:369
  (5 shorter events, 0.1 us)
Async XLA Ops:
  0.6 7.7 %copy-start.2 = (f32[4,4096]{1,0:T(4,128)S(1)}, f32[4,4096]{1,0:T(4,128)}, u32[]{:S(2)}) copy-start(f32[4,4096]{1,0:T(4,128)} %vol.3) | copy-start | bytes 196612
  0.6 7.7 %copy-start = (f32[3,4,4096]{2,1,0:T(4,128)S(1)}, f32[3,4,4096]{2,1,0:T(4,128)}, u32[]{:S(2)}) copy-start(f32[3,4,4096]{2,1,0:T(4,128)} %dual.5) | copy-start | bytes 589828
  0.7 7.7 %copy-start.1 = (f32[3,4,4096]{2,1,0:T(4,128)S(1)}, f32[3,4,4096]{2,1,0:T(4,128)}, u32[]{:S(2)}) copy-start(f32[3,4,4096]{2,1,0:T(4,128)} %split.3) | copy-start | bytes 589828
  4.2 1.4 %collective-permute-start = (bf16[128,128]{1,0:T(8,128)(2,1)S(1)}, bf16[128,128]{1,0:T(8,128)(2,1)S(1)}, u32[]{:S(2)}, u32[]{:S(2)}) collective-permute-start(bf16[128,128]{1,0:T(8,128)(2,1)S(1)} %get-tuple-element.14), channel_id=1, source_target_pairs={{0,1},{1,0},{2,3},{3,2},{4,5},{5,4},{6,7},{7,6},{8,9},{9,8},{10,11... | collective-permute-start | bytes 98312 | tf_op jit(solution)/shard_map/ppermute | solution.py:325
  5.6 4.4 %collective-permute-start.1 = (bf16[128,128]{1,0:T(8,128)(2,1)S(1)}, bf16[128,128]{1,0:T(8,128)(2,1)S(1)}, u32[]{:S(2)}, u32[]{:S(2)}) collective-permute-start(bf16[128,128]{1,0:T(8,128)(2,1)S(1)} %add_convert_fusion.1), channel_id=1, source_target_pairs={{0,5},{1,4},{4,1},{5,0},{8,13},{9,12},{12,9},{13,8},{2,7},{3,6},{6... | collective-permute-start | bytes 98312 | tf_op jit(solution)/shard_map/ppermute | solution.py:329
  8.4 5.1 %collective-permute-start.3 = (f32[4,4096]{1,0:T(4,128)S(1)}, f32[4,4096]{1,0:T(4,128)S(1)}, u32[]{:S(2)}, u32[]{:S(2)}) collective-permute-start(f32[4,4096]{1,0:T(4,128)S(1)} %get-tuple-element.15), channel_id=1, source_target_pairs={{0,3},{1,2},{2,1},{3,0},{4,7},{5,6},{6,5},{7,4},{8,11},{9,10},{10,... | collective-permute-start | bytes 196616 | tf_op jit(solution)/shard_map/ppermute | solution.py:320
  10.0 4.4 %collective-permute-start.2 = (bf16[128,128]{1,0:T(8,128)(2,1)S(1)}, bf16[128,128]{1,0:T(8,128)(2,1)S(1)}, u32[]{:S(2)}, u32[]{:S(2)}) collective-permute-start(bf16[128,128]{1,0:T(8,128)(2,1)S(1)} %add_convert_fusion.part), channel_id=1, source_target_pairs={{0,9},{1,8},{4,13},{5,12},{8,1},{9,0},{12,5},{13,4},{2,11},{3,10},... | collective-permute-start | bytes 98312 | tf_op jit(solution)/shard_map/ppermute | solution.py:329
  16.4 1.3 %collective-permute-start.4 = (f32[4,4096]{1,0:T(4,128)S(1)}, f32[4,4096]{1,0:T(4,128)S(1)}, u32[]{:S(2)}, u32[]{:S(2)}) collective-permute-start(f32[4,4096]{1,0:T(4,128)S(1)} %backward.1.grad), channel_id=1, source_target_pairs={{0,1},{1,0},{2,3},{3,2},{4,5},{5,4},{6,7},{7,6},{8,9},{9,8},{10,11... | collective-permute-start | bytes 196616 | tf_op jit(solution)/shard_map/ppermute | solution.py:361
  17.8 3.2 %collective-permute-start.5 = (f32[1,4096]{1,0:T(1,128)S(1)}, f32[1,4096]{1,0:T(1,128)S(1)}, u32[]{:S(2)}, u32[]{:S(2)}) collective-permute-start(f32[1,4096]{1,0:T(1,128)S(1)} %fusion.1), channel_id=1, source_target_pairs={{0,3},{1,2},{2,1},{3,0},{4,7},{5,6},{6,5},{7,4},{8,11},{9,10},{10,... | collective-permute-start | bytes 49160 | tf_op jit(solution)/shard_map/ppermute | solution.py:364

commit v16 on v15

--- a/solution.py
+++ b/solution.py
@@ -62,9 +62,9 @@
             [(voxel_hbm, voxel), (ray_hbm, ray), (vol_hbm, vol), (sino_hbm, sino)]
         )
     ]
+    copies = start_tiles(proj_hbm, tiles, tile_sems)
     for load in loads:
         load.start()
-    copies = start_tiles(proj_hbm, tiles, tile_sems)
     accs = (acc0, acc1, acc2, acc3)
     for acc in accs:
         acc[...] = jnp.zeros_like(acc)
@@ -169,7 +169,7 @@
 
 def backward_kernel(
     indices, tiles, part, moved, grad_out,
-    index, table, acc0, acc1, acc2, acc3, sem,
+    index, table, acc0, acc1, sem,
 ):
     slots = tiles.shape[0]
     lines = indices.shape[0] // 4
@@ -177,7 +177,7 @@
     voxel_tiles = acc0.shape[0] // 8 - 1
     to_scalar = pltpu.make_async_copy(indices, index, sem)
     to_scalar.start()
-    accs = (acc0, acc1, acc2, acc3)
+    accs = (acc0, acc1)
     for acc in accs:
         acc[...] = jnp.zeros_like(acc)
     row, lane = iotas((8, 128))
@@ -206,15 +206,14 @@
             (((1,), (1,)), ((), ())),
             preferred_element_type=jnp.float32,
         )
-        add_rows(
-            accs,
-            [index[3 * lines + line, place] for line, place in at],
-            [back[8 * k:8 * k + 8, 128 * k:128 * k + 128] for k in (0, 0, 1, 1)],
-        )
+        for k in range(2):
+            value = back[8 * k:8 * k + 8, 128 * k:128 * k + 128]
+            starts = [index[3 * lines + line, place] for line, place in at[2 * k:2 * k + 2]]
+            add_rows(accs, starts, [value, value])
     for j in range(voxel_tiles // 2):
         at = [slice(16 * j + 8 * k, 16 * j + 8 * k + 8) for k in range(2)]
-        even = [acc0[at[k], :] + acc2[at[k], :] for k in range(2)]
-        odd = [acc1[at[k], :] + acc3[at[k], :] for k in range(2)]
+        even = [acc0[at[k], :] for k in range(2)]
+        odd = [acc1[at[k], :] for k in range(2)]
         turned = pltpu.roll(jnp.where(top, even[1], odd[0]), TV, axis=1)
         both = jnp.where(top == low, jnp.where(top, even[0], odd[1]), turned)
         grad_out[:, 128 * j:128 * j + 128] = (both + pltpu.roll(both, 4, axis=0))[0:4]
@@ -353,7 +352,7 @@
             pltpu.SMEM((4 * lines, 128), jnp.int32),
             pltpu.VMEM((rays * 8, 128), f32),
         ]
-        + [pltpu.VMEM((voxel_tiles * 8 + 8, 128), f32)] * 4
+        + [pltpu.VMEM((voxel_tiles * 8 + 8, 128), f32)] * 2
         + [pltpu.SemaphoreType.DMA],
         compiler_params=params(),
         name="backward",

time: 22.1 us -> 22.4 us (1.014)
  no operation moved by 1% of the time
where the time goes in v16:
time: 22.4 us; the launch traced here: 22.2 us
  starting transfers between devices  9.7 us (43%)
  Pallas kernels  6.25 us (28%)
  waiting for transfers between devices  4.04 us (18%)
  between operations  2.1 us (9%)
    ppermute x2, starting transfers between devices, shards(): lax.ppermute(partial, ('tile', 'rep'), [(i, i ^ step + 1) for i in range(...  5.56 us
    pallas_call x1, Pallas kernels, shards(): pl.pallas_call(forward_kernel, out_shape=(jax.ShapeDtypeStruct((rays * sl...  3.01 us
    pallas_call x1, Pallas kernels, shards(): pl.pallas_call(backward_kernel, out_shape=jax.ShapeDtypeStruct((slices, w...  2.03 us
    ppermute x1, starting transfers between devices, shards(): ahead = lax.ppermute(ahead, ('slab', 'rep'), across)  1.62 us
    ppermute x1, waiting for transfers between devices, shards(): ahead = lax.ppermute(ahead, ('slab', 'rep'), across)  1.61 us
    ppermute x1, starting transfers between devices, shards(): from_next = from_previous = lax.ppermute(halo, ('slab', 'rep'), across)  1.51 us
    ppermute x2, waiting for transfers between devices, shards(): lax.ppermute(partial, ('tile', 'rep'), [(i, i ^ step + 1) for i in range(...  0.93 us
    pallas_call x1, Pallas kernels, shards(): pl.pallas_call(update_kernel, out_shape=(jax.ShapeDtypeStruct((slices, wi...  0.89 us
  transfers between devices with their start and end apart: 6, of which 4 were waited for; matrix products, arithmetic and copies ran while one was open for 0% of the time, Pallas kernels for 1%

profile of v16, /device:TPU:0, one launch (start us, length us, event | category | flops | bytes accessed | tf_op | source)
XLA Modules:
  0.0 22.2 jit_solution(10519369696560716046)
XLA Ops:
  0.6 0.0 copy-start.2
  0.6 0.0 copy-start
  0.7 0.0 copy-start.1
  1.4 3.0 %forward.1 = (bf16[128,128]{1,0:T(8,128)(2,1)S(1)}, s32[8,128]{1,0:T(8,128)S(1)}, bf16[256,64,128]{2,1,0:T(8,128)(2,1)S(1)}) custom-call(s32[1]{0:T(128)S(6)} %copy.12.count, s32[2,128]{1,0:T(2,128)} %bitcast.3, s32[2,128]{1,0:T(2,128)} %bitcast.4, f32[4,4096]{1,0:T(4,128)} %vol.3, f32[4,4,128]{2,1,0:T(4,128)} %sino_hbm.1, bf16[256,64,128]{2,1,0:T(8,128)(2,1)} %proj_hbm.1), custom_call_target="tpu_custom_call" | custom-call | tf_op jit(solution)/shard_map/forward/pallas_call | solution.py:283
  4.4 0.5 %collective-permute-start = (bf16[128,128]{1,0:T(8,128)(2,1)S(1)}, bf16[128,128]{1,0:T(8,128)(2,1)S(1)}, u32[]{:S(2)}, u32[]{:S(2)}) collective-permute-start(bf16[128,128]{1,0:T(8,128)(2,1)S(1)} %get-tuple-element.14), channel_id=1, source_target_pairs={{0,1},{1,0},{2,3},{3,2},{4,5},{5,4},{6,7},{7,6},{8,9},{9,8},{10,11... | collective-permute-start | bytes 98312 | tf_op jit(solution)/shard_map/ppermute | solution.py:324
  4.9 0.9 %collective-permute-done = bf16[128,128]{1,0:T(8,128)(2,1)S(1)} collective-permute-done((bf16[128,128]{1,0:T(8,128)(2,1)S(1)}, bf16[128,128]{1,0:T(8,128)(2,1)S(1)}, u32[]{:S(2)}, u32[]{:S(2)}) %collective-permute-start) | collective-permute-done | bytes 32800 | tf_op jit(solution)/shard_map/ppermute | solution.py:324
  5.8 2.7 %collective-permute-start.1 = (bf16[128,128]{1,0:T(8,128)(2,1)S(1)}, bf16[128,128]{1,0:T(8,128)(2,1)S(1)}, u32[]{:S(2)}, u32[]{:S(2)}) collective-permute-start(bf16[128,128]{1,0:T(8,128)(2,1)S(1)} %add_convert_fusion.1), channel_id=1, source_target_pairs={{0,5},{1,4},{4,1},{5,0},{8,13},{9,12},{12,9},{13,8},{2,7},{3,6},{6... | collective-permute-start | bytes 98312 | tf_op jit(solution)/shard_map/ppermute | solution.py:328
  8.5 0.0 copy-done.2
  8.5 0.0 copy-done
  8.5 0.0 copy-done.1
  8.6 1.5 %collective-permute-start.3 = (f32[4,4096]{1,0:T(4,128)S(1)}, f32[4,4096]{1,0:T(4,128)S(1)}, u32[]{:S(2)}, u32[]{:S(2)}) collective-permute-start(f32[4,4096]{1,0:T(4,128)S(1)} %get-tuple-element.15), channel_id=1, source_target_pairs={{0,3},{1,2},{2,1},{3,0},{4,7},{5,6},{6,5},{7,4},{8,11},{9,10},{10,... | collective-permute-start | bytes 196616 | tf_op jit(solution)/shard_map/ppermute | solution.py:319
  10.1 0.0 collective-permute-done.1
  10.1 2.8 %collective-permute-start.2 = (bf16[128,128]{1,0:T(8,128)(2,1)S(1)}, bf16[128,128]{1,0:T(8,128)(2,1)S(1)}, u32[]{:S(2)}, u32[]{:S(2)}) collective-permute-start(bf16[128,128]{1,0:T(8,128)(2,1)S(1)} %add_convert_fusion.part), channel_id=1, source_target_pairs={{0,9},{1,8},{4,13},{5,12},{8,1},{9,0},{12,5},{13,4},{2,11},{3,10},... | collective-permute-start | bytes 98312 | tf_op jit(solution)/shard_map/ppermute | solution.py:328
  13.7 0.0 collective-permute-done.3.from_next.from_previous
  13.7 0.9 %collective-permute-done.2.moved = bf16[128,128]{1,0:T(8,128)(2,1)S(1)} collective-permute-done((bf16[128,128]{1,0:T(8,128)(2,1)S(1)}, bf16[128,128]{1,0:T(8,128)(2,1)S(1)}, u32[]{:S(2)}, u32[]{:S(2)}) %collective-permute-start.2) | collective-permute-done | bytes 32800 | tf_op jit(solution)/shard_map/ppermute | solution.py:328
  14.6 2.0 %backward.1.grad = f32[4,4096]{1,0:T(4,128)S(1)} custom-call(s32[8,128]{1,0:T(8,128)S(1)} %get-tuple-element.12.indices, bf16[256,64,128]{2,1,0:T(8,128)(2,1)S(1)} %get-tuple-element.13.tiles, bf16[128,128]{1,0:T(8,128)(2,1)S(1)} %add_convert_fusion.part, bf16[128,128]{1,0:T(8,128)(2,1)S(1)} %collective-permute-done.2.moved), custom_call_target="tpu_custom_call" | custom-call | tf_op jit(solution)/shard_map/backward/pallas_call | solution.py:346
  16.6 0.5 %collective-permute-start.4 = (f32[4,4096]{1,0:T(4,128)S(1)}, f32[4,4096]{1,0:T(4,128)S(1)}, u32[]{:S(2)}, u32[]{:S(2)}) collective-permute-start(f32[4,4096]{1,0:T(4,128)S(1)} %backward.1.grad), channel_id=1, source_target_pairs={{0,1},{1,0},{2,3},{3,2},{4,5},{5,4},{6,7},{7,6},{8,9},{9,8},{10,11... | collective-permute-start | bytes 196616 | tf_op jit(solution)/shard_map/ppermute | solution.py:360
  17.1 0.3 %local.1.base = f32[4,4096]{1,0:T(4,128)S(1)} custom-call(f32[1]{0:T(128)S(6)} %copy.13.rho, f32[4,4096]{1,0:T(4,128)S(1)} %copy-done.2, f32[3,4,4096]{2,1,0:T(4,128)S(1)} %copy-done.1, f32[3,4,4096]{2,1,0:T(4,128)S(1)} %copy-done, f32[1,4096]{1,0:T(1,128)S(1)} %get-tuple-element.17.edge, f32[4,4096]{1,0:T(4,128)S(1)} %collective-permute-done.3.from_next.from_previous, ...), custom_call_target="tpu_custom_call" | custom-call | tf_op jit(solution)/shard_map/local/pallas_call | solution.py:337
  17.4 0.6 %collective-permute-done.4.grad_other = f32[4,4096]{1,0:T(4,128)S(1)} collective-permute-done((f32[4,4096]{1,0:T(4,128)S(1)}, f32[4,4096]{1,0:T(4,128)S(1)}, u32[]{:S(2)}, u32[]{:S(2)}) %collective-permute-start.4) | collective-permute-done | bytes 65568 | tf_op jit(solution)/shard_map/ppermute | solution.py:360
  18.0 1.6 %collective-permute-start.5 = (f32[1,4096]{1,0:T(1,128)S(1)}, f32[1,4096]{1,0:T(1,128)S(1)}, u32[]{:S(2)}, u32[]{:S(2)}) collective-permute-start(f32[1,4096]{1,0:T(1,128)S(1)} %fusion.1), channel_id=1, source_target_pairs={{0,3},{1,2},{2,1},{3,0},{4,7},{5,6},{6,5},{7,4},{8,11},{9,10},{10,... | collective-permute-start | bytes 49160 | tf_op jit(solution)/shard_map/ppermute | solution.py:363
  19.7 1.6 %collective-permute-done.5.ahead = f32[1,4096]{1,0:T(1,128)S(1)} collective-permute-done((f32[1,4096]{1,0:T(1,128)S(1)}, f32[1,4096]{1,0:T(1,128)S(1)}, u32[]{:S(2)}, u32[]{:S(2)}) %collective-permute-start.5) | collective-permute-done | bytes 16416 | tf_op jit(solution)/shard_map/ppermute | solution.py:363
  21.3 0.9 %update.1 = (f32[4,4096]{1,0:T(4,128)}, f32[3,4,4096]{2,1,0:T(4,128)}, f32[3,4,4096]{2,1,0:T(4,128)}) custom-call(f32[4,4096]{1,0:T(4,128)S(1)} %backward.1.grad, f32[4,4096]{1,0:T(4,128)S(1)} %collective-permute-done.4.grad_other, f32[1,4096]{1,0:T(1,128)S(1)} %collective-permute-done.5.ahead, f32[4,4096]{1,0:T(4,128)S(1)} %local.1.base, ...), custom_call_target="tpu_custom_call" | custom-call | tf_op jit(solution)/shard_map/update/pallas_call | solution.py:368
  (5 shorter events, 0.1 us)
Async XLA Ops:
  0.6 7.9 %copy-start.2 = (f32[4,4096]{1,0:T(4,128)S(1)}, f32[4,4096]{1,0:T(4,128)}, u32[]{:S(2)}) copy-start(f32[4,4096]{1,0:T(4,128)} %vol.3) | copy-start | bytes 196612
  0.6 7.9 %copy-start = (f32[3,4,4096]{2,1,0:T(4,128)S(1)}, f32[3,4,4096]{2,1,0:T(4,128)}, u32[]{:S(2)}) copy-start(f32[3,4,4096]{2,1,0:T(4,128)} %dual.5) | copy-start | bytes 589828
  0.7 7.9 %copy-start.1 = (f32[3,4,4096]{2,1,0:T(4,128)S(1)}, f32[3,4,4096]{2,1,0:T(4,128)}, u32[]{:S(2)}) copy-start(f32[3,4,4096]{2,1,0:T(4,128)} %split.3) | copy-start | bytes 589828
  4.4 1.4 %collective-permute-start = (bf16[128,128]{1,0:T(8,128)(2,1)S(1)}, bf16[128,128]{1,0:T(8,128)(2,1)S(1)}, u32[]{:S(2)}, u32[]{:S(2)}) collective-permute-start(bf16[128,128]{1,0:T(8,128)(2,1)S(1)} %get-tuple-element.14), channel_id=1, source_target_pairs={{0,1},{1,0},{2,3},{3,2},{4,5},{5,4},{6,7},{7,6},{8,9},{9,8},{10,11... | collective-permute-start | bytes 98312 | tf_op jit(solution)/shard_map/ppermute | solution.py:324
  5.8 4.3 %collective-permute-start.1 = (bf16[128,128]{1,0:T(8,128)(2,1)S(1)}, bf16[128,128]{1,0:T(8,128)(2,1)S(1)}, u32[]{:S(2)}, u32[]{:S(2)}) collective-permute-start(bf16[128,128]{1,0:T(8,128)(2,1)S(1)} %add_convert_fusion.1), channel_id=1, source_target_pairs={{0,5},{1,4},{4,1},{5,0},{8,13},{9,12},{12,9},{13,8},{2,7},{3,6},{6... | collective-permute-start | bytes 98312 | tf_op jit(solution)/shard_map/ppermute | solution.py:328
  8.6 5.1 %collective-permute-start.3 = (f32[4,4096]{1,0:T(4,128)S(1)}, f32[4,4096]{1,0:T(4,128)S(1)}, u32[]{:S(2)}, u32[]{:S(2)}) collective-permute-start(f32[4,4096]{1,0:T(4,128)S(1)} %get-tuple-element.15), channel_id=1, source_target_pairs={{0,3},{1,2},{2,1},{3,0},{4,7},{5,6},{6,5},{7,4},{8,11},{9,10},{10,... | collective-permute-start | bytes 196616 | tf_op jit(solution)/shard_map/ppermute | solution.py:319
  10.1 4.4 %collective-permute-start.2 = (bf16[128,128]{1,0:T(8,128)(2,1)S(1)}, bf16[128,128]{1,0:T(8,128)(2,1)S(1)}, u32[]{:S(2)}, u32[]{:S(2)}) collective-permute-start(bf16[128,128]{1,0:T(8,128)(2,1)S(1)} %add_convert_fusion.part), channel_id=1, source_target_pairs={{0,9},{1,8},{4,13},{5,12},{8,1},{9,0},{12,5},{13,4},{2,11},{3,10},... | collective-permute-start | bytes 98312 | tf_op jit(solution)/shard_map/ppermute | solution.py:328
  16.6 1.4 %collective-permute-start.4 = (f32[4,4096]{1,0:T(4,128)S(1)}, f32[4,4096]{1,0:T(4,128)S(1)}, u32[]{:S(2)}, u32[]{:S(2)}) collective-permute-start(f32[4,4096]{1,0:T(4,128)S(1)} %backward.1.grad), channel_id=1, source_target_pairs={{0,1},{1,0},{2,3},{3,2},{4,5},{5,4},{6,7},{7,6},{8,9},{9,8},{10,11... | collective-permute-start | bytes 196616 | tf_op jit(solution)/shard_map/ppermute | solution.py:360
  18.0 3.2 %collective-permute-start.5 = (f32[1,4096]{1,0:T(1,128)S(1)}, f32[1,4096]{1,0:T(1,128)S(1)}, u32[]{:S(2)}, u32[]{:S(2)}) collective-permute-start(f32[1,4096]{1,0:T(1,128)S(1)} %fusion.1), channel_id=1, source_target_pairs={{0,3},{1,2},{2,1},{3,0},{4,7},{5,6},{6,5},{7,4},{8,11},{9,10},{10,... | collective-permute-start | bytes 49160 | tf_op jit(solution)/shard_map/ppermute | solution.py:363

commit v17 on v15

--- a/solution.py
+++ b/solution.py
@@ -168,7 +168,7 @@
 
 
 def backward_kernel(
-    indices, tiles, part, moved, grad_out,
+    indices, tiles, part, moved, base, grad_out, row_out,
     index, table, acc0, acc1, acc2, acc3, sem,
 ):
     slots = tiles.shape[0]
@@ -217,11 +217,14 @@
         odd = [acc1[at[k], :] + acc3[at[k], :] for k in range(2)]
         turned = pltpu.roll(jnp.where(top, even[1], odd[0]), TV, axis=1)
         both = jnp.where(top == low, jnp.where(top, even[0], odd[1]), turned)
-        grad_out[:, 128 * j:128 * j + 128] = (both + pltpu.roll(both, 4, axis=0))[0:4]
+        grad = (both + pltpu.roll(both, 4, axis=0))[0:4]
+        lanes = slice(128 * j, 128 * j + 128)
+        grad_out[:, lanes] = grad
+        row_out[:, lanes] = 0.5 * base[0:1, lanes] - TAU * grad[0:1]
 
 
 def update_kernel(
-    grad, grad_other, ahead, base, dual, limits,
+    grad, grad_other, piece, piece_other, base, dual, limits,
     new_volume, new_split, new_dual,
 ):
     last = lax.axis_index("slab") == lax.axis_size("slab") - 1
@@ -232,7 +235,8 @@
         at = slice(128 * j, 128 * j + 128)
         limit = limits[:, at]
         own = base[:, at] - TAU * (grad[:, at] + grad_other[:, at])
-        field = jnp.where(row < 4, jnp.concatenate([own] * 2, axis=0), ahead[:, at])
+        ahead = piece[:, at] + piece_other[:, at]
+        field = jnp.where(row < 4, jnp.concatenate([own] * 2, axis=0), ahead)
         new_volume[:, at] = own
         steps = (
             jnp.where(inner, pltpu.roll(field, 7, axis=0) - field, 0.0),
@@ -330,11 +334,6 @@
             partial, ("tile", "rep"), [(i, i ^ (step + 1)) for i in range(group)]
         )
         step *= 2
-    limits = jnp.broadcast_to((1.0 / rho)[:, None], (1, width))
-    moved, from_next, from_previous, limits = lax.optimization_barrier(
-        (moved, from_next, from_previous, limits)
-    )
-
     base = pl.pallas_call(
         local_kernel,
         out_shape=jax.ShapeDtypeStruct((slices, width), f32),
@@ -344,11 +343,14 @@
         name="local",
     )(rho, volume, split_var, dual_var, edge, from_next, from_previous)
 
-    grad = pl.pallas_call(
+    limits = jnp.broadcast_to((1.0 / rho)[:, None], (1, width))
+    moved, base, limits = lax.optimization_barrier((moved, base, limits))
+
+    grad, piece = pl.pallas_call(
         backward_kernel,
-        out_shape=jax.ShapeDtypeStruct((slices, width), f32),
-        in_specs=[vmem()] * 4,
-        out_specs=vmem(),
+        out_shape=(jax.ShapeDtypeStruct((slices, width), f32), row),
+        in_specs=[vmem()] * 5,
+        out_specs=(vmem(), vmem()),
         scratch_shapes=[
             pltpu.SMEM((4 * lines, 128), jnp.int32),
             pltpu.VMEM((rays * 8, 128), f32),
@@ -357,23 +359,23 @@
         + [pltpu.SemaphoreType.DMA],
         compiler_params=params(),
         name="backward",
-    )(indices, tiles, partial, moved)
+    )(indices, tiles, partial, moved, base)
+    if slabs == 2:
+        piece = lax.ppermute(piece, ("slab", "rep"), across)
+    else:
+        piece = lax.ppermute(piece, "slab", down)
     grad_other = lax.ppermute(grad, "rep", swap)
-    ahead = base[0:1] - TAU * (grad[0:1] + grad_other[0:1])
-    if slabs == 2:
-        ahead = lax.ppermute(ahead, ("slab", "rep"), across)
-    else:
-        ahead = lax.ppermute(ahead, "slab", down)
+    piece_other = lax.ppermute(piece, "rep", swap)
 
     triple = jax.ShapeDtypeStruct((3, slices, width), f32)
     return pl.pallas_call(
         update_kernel,
         out_shape=(jax.ShapeDtypeStruct((slices, width), f32), triple, triple),
-        in_specs=[vmem()] * 6,
+        in_specs=[vmem()] * 7,
         out_specs=(vmem(),) * 3,
         compiler_params=params(),
         name="update",
-    )(grad, grad_other, ahead, base, dual_var, limits)
+    )(grad, grad_other, piece, piece_other, base, dual_var, limits)
 
 
 def solution(mesh):

time: 22.1 us -> 22.3 us (level)
    ppermute x1 -> x2, waiting for transfers between devices: 1.61 us -> 2.48 us  [the longest x1 1.53 us: shards(): piece = lax.ppermute(piece, ('slab', 'rep'), across)]
    ppermute x1, waiting for transfers between devices: 0.63 us -> 0.01 us  [shards(): grad_other = lax.ppermute(grad, 'rep', swap)]
    ppermute x2, waiting for transfers between devices: 0.93 us -> 0.66 us  [shards(): lax.ppermute(partial, ('tile', 'rep'), [(i, i ^ step + 1) for i in range(...]
    ppermute x1 -> x2, starting transfers between devices: 1.62 us -> 1.87 us  [the longest x1 1.63 us: shards(): piece = lax.ppermute(piece, ('slab', 'rep'), across)]
  transfers between devices with their start and end apart: 6 -> 7, of which waited for: 4 -> 4; matrix products, arithmetic and copies ran while one was open for 0% -> 0% of each run, Pallas kernels for 1% -> 1%
where the time goes in v17:
time: 22.3 us; the launch traced here: 22.1 us
  starting transfers between devices  9.81 us (44%)
  Pallas kernels  6.1 us (27%)
  waiting for transfers between devices  4 us (18%)
  between operations  2.1 us (9%)
    ppermute x2, starting transfers between devices, shards(): lax.ppermute(partial, ('tile', 'rep'), [(i, i ^ step + 1) for i in range(...  5.61 us
    pallas_call x1, Pallas kernels, shards(): pl.pallas_call(forward_kernel, out_shape=(jax.ShapeDtypeStruct((rays * sl...  2.86 us
    pallas_call x1, Pallas kernels, shards(): pl.pallas_call(backward_kernel, out_shape=(jax.ShapeDtypeStruct((slices,...  2.03 us
    ppermute x1, starting transfers between devices, shards(): piece = lax.ppermute(piece, ('slab', 'rep'), across)  1.63 us
    ppermute x1, waiting for transfers between devices, shards(): piece = lax.ppermute(piece, ('slab', 'rep'), across)  1.53 us
    ppermute x1, starting transfers between devices, shards(): from_next = from_previous = lax.ppermute(halo, ('slab', 'rep'), across)  1.51 us
    ppermute x1, waiting for transfers between devices, shards(): piece_other = lax.ppermute(piece, 'rep', swap)  0.94 us
    pallas_call x1, Pallas kernels, shards(): pl.pallas_call(update_kernel, out_shape=(jax.ShapeDtypeStruct((slices, wi...  0.9 us
  transfers between devices with their start and end apart: 7, of which 4 were waited for; matrix products, arithmetic and copies ran while one was open for 0% of the time, Pallas kernels for 1%

profile of v17, /device:TPU:0, one launch (start us, length us, event | category | flops | bytes accessed | tf_op | source)
XLA Modules:
  0.0 22.1 jit_solution(13528996196329377424)
XLA Ops:
  0.6 0.0 copy-start.2
  0.6 0.0 copy-start
  0.7 0.0 copy-start.1
  1.4 2.9 %forward.1 = (bf16[128,128]{1,0:T(8,128)(2,1)S(1)}, s32[8,128]{1,0:T(8,128)S(1)}, bf16[256,64,128]{2,1,0:T(8,128)(2,1)S(1)}) custom-call(s32[1]{0:T(128)S(6)} %copy.12.count, s32[2,128]{1,0:T(2,128)} %bitcast.3, s32[2,128]{1,0:T(2,128)} %bitcast.4, f32[4,4096]{1,0:T(4,128)} %vol.3, f32[4,4,128]{2,1,0:T(4,128)} %sino_hbm.1, bf16[256,64,128]{2,1,0:T(8,128)(2,1)} %proj_hbm.1), custom_call_target="tpu_custom_call" | custom-call | tf_op jit(solution)/shard_map/forward/pallas_call | solution.py:288
  4.2 0.5 %collective-permute-start = (bf16[128,128]{1,0:T(8,128)(2,1)S(1)}, bf16[128,128]{1,0:T(8,128)(2,1)S(1)}, u32[]{:S(2)}, u32[]{:S(2)}) collective-permute-start(bf16[128,128]{1,0:T(8,128)(2,1)S(1)} %get-tuple-element.15), channel_id=1, source_target_pairs={{0,1},{1,0},{2,3},{3,2},{4,5},{5,4},{6,7},{7,6},{8,9},{9,8},{10,11... | collective-permute-start | bytes 98312 | tf_op jit(solution)/shard_map/ppermute | solution.py:329
  4.7 0.9 %collective-permute-done = bf16[128,128]{1,0:T(8,128)(2,1)S(1)} collective-permute-done((bf16[128,128]{1,0:T(8,128)(2,1)S(1)}, bf16[128,128]{1,0:T(8,128)(2,1)S(1)}, u32[]{:S(2)}, u32[]{:S(2)}) %collective-permute-start) | collective-permute-done | bytes 32800 | tf_op jit(solution)/shard_map/ppermute | solution.py:329
  5.6 2.8 %collective-permute-start.1 = (bf16[128,128]{1,0:T(8,128)(2,1)S(1)}, bf16[128,128]{1,0:T(8,128)(2,1)S(1)}, u32[]{:S(2)}, u32[]{:S(2)}) collective-permute-start(bf16[128,128]{1,0:T(8,128)(2,1)S(1)} %add_convert_fusion.1), channel_id=1, source_target_pairs={{0,5},{1,4},{4,1},{5,0},{8,13},{9,12},{12,9},{13,8},{2,7},{3,6},{6... | collective-permute-start | bytes 98312 | tf_op jit(solution)/shard_map/ppermute | solution.py:333
  8.4 0.0 copy-done.2
  8.4 0.0 copy-done
  8.4 0.0 copy-done.1
  8.4 1.5 %collective-permute-start.3 = (f32[4,4096]{1,0:T(4,128)S(1)}, f32[4,4096]{1,0:T(4,128)S(1)}, u32[]{:S(2)}, u32[]{:S(2)}) collective-permute-start(f32[4,4096]{1,0:T(4,128)S(1)} %get-tuple-element.17), channel_id=1, source_target_pairs={{0,3},{1,2},{2,1},{3,0},{4,7},{5,6},{6,5},{7,4},{8,11},{9,10},{10,... | collective-permute-start | bytes 196616 | tf_op jit(solution)/shard_map/ppermute | solution.py:324
  9.9 0.0 collective-permute-done.1
  10.0 2.8 %collective-permute-start.2 = (bf16[128,128]{1,0:T(8,128)(2,1)S(1)}, bf16[128,128]{1,0:T(8,128)(2,1)S(1)}, u32[]{:S(2)}, u32[]{:S(2)}) collective-permute-start(bf16[128,128]{1,0:T(8,128)(2,1)S(1)} %add_convert_fusion.part), channel_id=1, source_target_pairs={{0,9},{1,8},{4,13},{5,12},{8,1},{9,0},{12,5},{13,4},{2,11},{3,10},... | collective-permute-start | bytes 98312 | tf_op jit(solution)/shard_map/ppermute | solution.py:333
  13.5 0.0 collective-permute-done.3.from_next.from_previous
  13.5 0.3 %local.1.base = f32[4,4096]{1,0:T(4,128)S(1)} custom-call(f32[1]{0:T(128)S(6)} %copy.13.rho, f32[4,4096]{1,0:T(4,128)S(1)} %copy-done.2, f32[3,4,4096]{2,1,0:T(4,128)S(1)} %copy-done.1, f32[3,4,4096]{2,1,0:T(4,128)S(1)} %copy-done, f32[1,4096]{1,0:T(1,128)S(1)} %get-tuple-element.16.edge, f32[4,4096]{1,0:T(4,128)S(1)} %collective-permute-done.3.from_next.from_previous, ...), custom_call_target="tpu_custom_call" | custom-call | tf_op jit(solution)/shard_map/local/pallas_call | solution.py:337
  13.8 0.6 %collective-permute-done.2.moved = bf16[128,128]{1,0:T(8,128)(2,1)S(1)} collective-permute-done((bf16[128,128]{1,0:T(8,128)(2,1)S(1)}, bf16[128,128]{1,0:T(8,128)(2,1)S(1)}, u32[]{:S(2)}, u32[]{:S(2)}) %collective-permute-start.2) | collective-permute-done | bytes 32800 | tf_op jit(solution)/shard_map/ppermute | solution.py:333
  14.4 2.0 %backward.1 = (f32[4,4096]{1,0:T(4,128)S(1)}, f32[1,4096]{1,0:T(1,128)S(1)}) custom-call(s32[8,128]{1,0:T(8,128)S(1)} %get-tuple-element.13.indices, bf16[256,64,128]{2,1,0:T(8,128)(2,1)S(1)} %get-tuple-element.14.tiles, bf16[128,128]{1,0:T(8,128)(2,1)S(1)} %add_convert_fusion.part, bf16[128,128]{1,0:T(8,128)(2,1)S(1)} %collective-permute-done.2.moved, ...), custom_call_target="tpu_custom_call" | custom-call | tf_op jit(solution)/shard_map/backward/pallas_call | solution.py:349
  16.5 0.3 %collective-permute-start.4 = (f32[4,4096]{1,0:T(4,128)S(1)}, f32[4,4096]{1,0:T(4,128)S(1)}, u32[]{:S(2)}, u32[]{:S(2)}) collective-permute-start(f32[4,4096]{1,0:T(4,128)S(1)} %get-tuple-element.20.grad), channel_id=1, source_target_pairs={{0,1},{1,0},{2,3},{3,2},{4,5},{5,4},{6,7},{7,6},{8,9},{9,8},{10,11... | collective-permute-start | bytes 196616 | tf_op jit(solution)/shard_map/ppermute | solution.py:367
  16.8 1.6 %collective-permute-start.5 = (f32[1,4096]{1,0:T(1,128)S(1)}, f32[1,4096]{1,0:T(1,128)S(1)}, u32[]{:S(2)}, u32[]{:S(2)}) collective-permute-start(f32[1,4096]{1,0:T(1,128)S(1)} %get-tuple-element.21), channel_id=1, source_target_pairs={{0,3},{1,2},{2,1},{3,0},{4,7},{5,6},{6,5},{7,4},{8,11},{9,10},{10,... | collective-permute-start | bytes 49160 | tf_op jit(solution)/shard_map/ppermute | solution.py:364
  18.4 1.5 %collective-permute-done.5.piece = f32[1,4096]{1,0:T(1,128)S(1)} collective-permute-done((f32[1,4096]{1,0:T(1,128)S(1)}, f32[1,4096]{1,0:T(1,128)S(1)}, u32[]{:S(2)}, u32[]{:S(2)}) %collective-permute-start.5) | collective-permute-done | bytes 16416 | tf_op jit(solution)/shard_map/ppermute | solution.py:364
  20.0 0.2 %collective-permute-start.6 = (f32[1,4096]{1,0:T(1,128)S(1)}, f32[1,4096]{1,0:T(1,128)S(1)}, u32[]{:S(2)}, u32[]{:S(2)}) collective-permute-start(f32[1,4096]{1,0:T(1,128)S(1)} %collective-permute-done.5.piece), channel_id=1, source_target_pairs={{0,1},{1,0},{2,3},{3,2},{4,5},{5,4},{6,7},{7,6},{8,9},{9,8},{10,11... | collective-permute-start | bytes 49160 | tf_op jit(solution)/shard_map/ppermute | solution.py:368
  20.2 0.9 %collective-permute-done.6.piece_other = f32[1,4096]{1,0:T(1,128)S(1)} collective-permute-done((f32[1,4096]{1,0:T(1,128)S(1)}, f32[1,4096]{1,0:T(1,128)S(1)}, u32[]{:S(2)}, u32[]{:S(2)}) %collective-permute-start.6) | collective-permute-done | bytes 16416 | tf_op jit(solution)/shard_map/ppermute | solution.py:368
  21.2 0.0 collective-permute-done.4.grad_other
  21.2 0.9 %update.1 = (f32[4,4096]{1,0:T(4,128)}, f32[3,4,4096]{2,1,0:T(4,128)}, f32[3,4,4096]{2,1,0:T(4,128)}) custom-call(f32[4,4096]{1,0:T(4,128)S(1)} %get-tuple-element.20.grad, f32[4,4096]{1,0:T(4,128)S(1)} %collective-permute-done.4.grad_other, f32[1,4096]{1,0:T(1,128)S(1)} %collective-permute-done.5.piece, f32[1,4096]{1,0:T(1,128)S(1)} %collective-permute-done.6.piece_other, ...), custom_call_target="tpu_custom_call" | custom-call | tf_op jit(solution)/shard_map/update/pallas_call | solution.py:371
  (4 shorter events, 0.1 us)
Async XLA Ops:
  0.6 7.7 %copy-start.2 = (f32[4,4096]{1,0:T(4,128)S(1)}, f32[4,4096]{1,0:T(4,128)}, u32[]{:S(2)}) copy-start(f32[4,4096]{1,0:T(4,128)} %vol.3) | copy-start | bytes 196612
  0.6 7.7 %copy-start = (f32[3,4,4096]{2,1,0:T(4,128)S(1)}, f32[3,4,4096]{2,1,0:T(4,128)}, u32[]{:S(2)}) copy-start(f32[3,4,4096]{2,1,0:T(4,128)} %dual.5) | copy-start | bytes 589828
  0.7 7.7 %copy-start.1 = (f32[3,4,4096]{2,1,0:T(4,128)S(1)}, f32[3,4,4096]{2,1,0:T(4,128)}, u32[]{:S(2)}) copy-start(f32[3,4,4096]{2,1,0:T(4,128)} %split.3) | copy-start | bytes 589828
  4.2 1.4 %collective-permute-start = (bf16[128,128]{1,0:T(8,128)(2,1)S(1)}, bf16[128,128]{1,0:T(8,128)(2,1)S(1)}, u32[]{:S(2)}, u32[]{:S(2)}) collective-permute-start(bf16[128,128]{1,0:T(8,128)(2,1)S(1)} %get-tuple-element.15), channel_id=1, source_target_pairs={{0,1},{1,0},{2,3},{3,2},{4,5},{5,4},{6,7},{7,6},{8,9},{9,8},{10,11... | collective-permute-start | bytes 98312 | tf_op jit(solution)/shard_map/ppermute | solution.py:329
  5.6 4.4 %collective-permute-start.1 = (bf16[128,128]{1,0:T(8,128)(2,1)S(1)}, bf16[128,128]{1,0:T(8,128)(2,1)S(1)}, u32[]{:S(2)}, u32[]{:S(2)}) collective-permute-start(bf16[128,128]{1,0:T(8,128)(2,1)S(1)} %add_convert_fusion.1), channel_id=1, source_target_pairs={{0,5},{1,4},{4,1},{5,0},{8,13},{9,12},{12,9},{13,8},{2,7},{3,6},{6... | collective-permute-start | bytes 98312 | tf_op jit(solution)/shard_map/ppermute | solution.py:333
  8.4 5.1 %collective-permute-start.3 = (f32[4,4096]{1,0:T(4,128)S(1)}, f32[4,4096]{1,0:T(4,128)S(1)}, u32[]{:S(2)}, u32[]{:S(2)}) collective-permute-start(f32[4,4096]{1,0:T(4,128)S(1)} %get-tuple-element.17), channel_id=1, source_target_pairs={{0,3},{1,2},{2,1},{3,0},{4,7},{5,6},{6,5},{7,4},{8,11},{9,10},{10,... | collective-permute-start | bytes 196616 | tf_op jit(solution)/shard_map/ppermute | solution.py:324
  10.0 4.4 %collective-permute-start.2 = (bf16[128,128]{1,0:T(8,128)(2,1)S(1)}, bf16[128,128]{1,0:T(8,128)(2,1)S(1)}, u32[]{:S(2)}, u32[]{:S(2)}) collective-permute-start(bf16[128,128]{1,0:T(8,128)(2,1)S(1)} %add_convert_fusion.part), channel_id=1, source_target_pairs={{0,9},{1,8},{4,13},{5,12},{8,1},{9,0},{12,5},{13,4},{2,11},{3,10},... | collective-permute-start | bytes 98312 | tf_op jit(solution)/shard_map/ppermute | solution.py:333
  16.5 4.7 %collective-permute-start.4 = (f32[4,4096]{1,0:T(4,128)S(1)}, f32[4,4096]{1,0:T(4,128)S(1)}, u32[]{:S(2)}, u32[]{:S(2)}) collective-permute-start(f32[4,4096]{1,0:T(4,128)S(1)} %get-tuple-element.20.grad), channel_id=1, source_target_pairs={{0,1},{1,0},{2,3},{3,2},{4,5},{5,4},{6,7},{7,6},{8,9},{9,8},{10,11... | collective-permute-start | bytes 196616 | tf_op jit(solution)/shard_map/ppermute | solution.py:367
  16.8 3.2 %collective-permute-start.5 = (f32[1,4096]{1,0:T(1,128)S(1)}, f32[1,4096]{1,0:T(1,128)S(1)}, u32[]{:S(2)}, u32[]{:S(2)}) collective-permute-start(f32[1,4096]{1,0:T(1,128)S(1)} %get-tuple-element.21), channel_id=1, source_target_pairs={{0,3},{1,2},{2,1},{3,0},{4,7},{5,6},{6,5},{7,4},{8,11},{9,10},{10,... | collective-permute-start | bytes 49160 | tf_op jit(solution)/shard_map/ppermute | solution.py:364
  20.0 1.2 %collective-permute-start.6 = (f32[1,4096]{1,0:T(1,128)S(1)}, f32[1,4096]{1,0:T(1,128)S(1)}, u32[]{:S(2)}, u32[]{:S(2)}) collective-permute-start(f32[1,4096]{1,0:T(1,128)S(1)} %collective-permute-done.5.piece), channel_id=1, source_target_pairs={{0,1},{1,0},{2,3},{3,2},{4,5},{5,4},{6,7},{7,6},{8,9},{9,8},{10,11... | collective-permute-start | bytes 49160 | tf_op jit(solution)/shard_map/ppermute | solution.py:368

commit v18 on v15

--- a/solution.py
+++ b/solution.py
@@ -103,26 +103,37 @@
         acc0[pl.ds(pl.multiple_of((mine + r) * 8, 8), 4), :] = -sino[r]
     to_scalar.wait()
     per = slots // CHUNKS
-    for g in range(slots // GROUP):
-        if GROUP * g % per == 0:
-            copies[GROUP * g // per].wait()
-        n = GROUP * g
-        at = [divmod(n + i, 128) for i in range(GROUP)]
-        picked = [table[rows8(index[line, place]), :] for line, place in at]
-        pairs = [jnp.where(top, picked[2 * i], picked[2 * i + 1]) for i in range(2)]
-        zero = jnp.zeros_like(pairs[0])
-        left = jnp.concatenate([pairs[0], zero], axis=0).astype(jnp.bfloat16)
-        right = jnp.concatenate([zero, pairs[1]], axis=0).astype(jnp.bfloat16)
+    for first in range(0, slots, 2 * GROUP):
+        if first % per == 0:
+            copies[first // per].wait()
+        rows = []
+        for n in (first, first + GROUP):
+            picked = [
+                table[rows8(index[(n + i) // 128, (n + i) % 128]), :] for i in range(GROUP)
+            ]
+            pairs = [jnp.where(top, picked[2 * i], picked[2 * i + 1]) for i in range(2)]
+            zero = jnp.zeros_like(pairs[0])
+            left = jnp.concatenate([pairs[0], zero], axis=0).astype(jnp.bfloat16)
+            right = jnp.concatenate([zero, pairs[1]], axis=0).astype(jnp.bfloat16)
+            rows.append(jnp.concatenate([left, right], axis=1))
         sums = jnp.dot(
-            jnp.concatenate([left, right], axis=1),
-            tiles[n:n + GROUP].reshape(GROUP * TV, TR),
+            jnp.concatenate(rows, axis=0),
+            jnp.concatenate(
+                [
+                    tiles[n:n + GROUP].reshape(GROUP * TV, TR)
+                    for n in (first, first + GROUP)
+                ],
+                axis=1,
+            ),
             preferred_element_type=jnp.float32,
         )
-        add_rows(
-            accs,
-            [index[lines + line, place] for line, place in at],
-            [sums[0:8], sums[0:8], sums[8:16], sums[8:16]],
-        )
+        for part, n in enumerate((first, first + GROUP)):
+            mine = sums[16 * part:16 * part + 16, TR * part:TR * part + TR]
+            add_rows(
+                accs,
+                [index[lines + (n + i) // 128, (n + i) % 128] for i in range(GROUP)],
+                [mine[0:8], mine[0:8], mine[8:16], mine[8:16]],
+            )
     for q in range(rays // 4):
         halves = []
         for r in (4 * q, 4 * q + 2):
@@ -193,24 +204,41 @@
             table[r + 8:r + 16, :] = jnp.where(top, turned, x)
 
     to_scalar.wait()
-    for g in range(slots // GROUP):
-        n = GROUP * g
-        at = [divmod(n + i, 128) for i in range(GROUP)]
-        picked = [table[rows8(index[2 * lines + line, place]), :] for line, place in at]
-        rows = jnp.concatenate(
-            [jnp.where(top, picked[2 * i], picked[2 * i + 1]) for i in range(2)], axis=0
-        )
+    for first in range(0, slots, 2 * GROUP):
+        rows = []
+        for n in (first, first + GROUP):
+            picked = [
+                table[rows8(index[2 * lines + (n + i) // 128, (n + i) % 128]), :]
+                for i in range(GROUP)
+            ]
+            pairs = [jnp.where(top, picked[2 * i], picked[2 * i + 1]) for i in range(2)]
+            rows.append(jnp.concatenate(pairs, axis=0).astype(jnp.bfloat16))
+        zero = jnp.zeros_like(rows[0])
         back = lax.dot_general(
-            rows.astype(jnp.bfloat16),
-            tiles[n:n + GROUP].reshape(GROUP * TV, TR),
+            jnp.concatenate(
+                [
+                    jnp.concatenate([rows[0], zero], axis=1),
+                    jnp.concatenate([zero, rows[1]], axis=1),
+                ],
+                axis=0,
+            ),
+            jnp.concatenate(
+                [
+                    tiles[n:n + GROUP].reshape(GROUP * TV, TR)
+                    for n in (first, first + GROUP)
+                ],
+                axis=1,
+            ),
             (((1,), (1,)), ((), ())),
             preferred_element_type=jnp.float32,
         )
-        add_rows(
-            accs,
-            [index[3 * lines + line, place] for line, place in at],
-            [back[8 * k:8 * k + 8, 128 * k:128 * k + 128] for k in (0, 0, 1, 1)],
-        )
+        for part, n in enumerate((first, first + GROUP)):
+            mine = back[16 * part:16 * part + 16]
+            add_rows(
+                accs,
+                [index[3 * lines + (n + i) // 128, (n + i) % 128] for i in range(GROUP)],
+                [mine[8 * k:8 * k + 8, 128 * k:128 * k + 128] for k in (0, 0, 1, 1)],
+            )
     for j in range(voxel_tiles // 2):
         at = [slice(16 * j + 8 * k, 16 * j + 8 * k + 8) for k in range(2)]
         even = [acc0[at[k], :] + acc2[at[k], :] for k in range(2)]

time: 22.1 us -> 22.3 us (level)
  no operation moved by 1% of the time
where the time goes in v18:
time: 22.3 us; the launch traced here: 22.1 us
  starting transfers between devices  9.63 us (43%)
  Pallas kernels  6.26 us (28%)
  waiting for transfers between devices  4.05 us (18%)
  between operations  2.1 us (9%)
    ppermute x2, starting transfers between devices, shards(): lax.ppermute(partial, ('tile', 'rep'), [(i, i ^ step + 1) for i in range(...  5.58 us
    pallas_call x1, Pallas kernels, shards(): pl.pallas_call(forward_kernel, out_shape=(jax.ShapeDtypeStruct((rays * sl...  2.89 us
    pallas_call x1, Pallas kernels, shards(): pl.pallas_call(backward_kernel, out_shape=jax.ShapeDtypeStruct((slices, w...  2.17 us
    ppermute x1, waiting for transfers between devices, shards(): ahead = lax.ppermute(ahead, ('slab', 'rep'), across)  1.62 us
    ppermute x1, starting transfers between devices, shards(): ahead = lax.ppermute(ahead, ('slab', 'rep'), across)  1.61 us
    ppermute x1, starting transfers between devices, shards(): from_next = from_previous = lax.ppermute(halo, ('slab', 'rep'), across)  1.51 us
    ppermute x2, waiting for transfers between devices, shards(): lax.ppermute(partial, ('tile', 'rep'), [(i, i ^ step + 1) for i in range(...  0.93 us
    pallas_call x1, Pallas kernels, shards(): pl.pallas_call(update_kernel, out_shape=(jax.ShapeDtypeStruct((slices, wi...  0.89 us
  transfers between devices with their start and end apart: 6, of which 4 were waited for; matrix products, arithmetic and copies ran while one was open for 0% of the time, Pallas kernels for 1%

profile of v18, /device:TPU:0, one launch (start us, length us, event | category | flops | bytes accessed | tf_op | source)
XLA Modules:
  0.0 22.1 jit_solution(956050872258654487)
XLA Ops:
  0.6 0.0 copy-start.2
  0.6 0.0 copy-start
  0.7 0.0 copy-start.1
  1.4 2.9 %forward.1 = (bf16[128,128]{1,0:T(8,128)(2,1)S(1)}, s32[8,128]{1,0:T(8,128)S(1)}, bf16[256,64,128]{2,1,0:T(8,128)(2,1)S(1)}) custom-call(s32[1]{0:T(128)S(6)} %copy.12.count, s32[2,128]{1,0:T(2,128)} %bitcast.3, s32[2,128]{1,0:T(2,128)} %bitcast.4, f32[4,4096]{1,0:T(4,128)} %vol.3, f32[4,4,128]{2,1,0:T(4,128)} %sino_hbm.1, bf16[256,64,128]{2,1,0:T(8,128)(2,1)} %proj_hbm.1), custom_call_target="tpu_custom_call" | custom-call | tf_op jit(solution)/shard_map/forward/pallas_call | solution.py:312
  4.3 0.5 %collective-permute-start = (bf16[128,128]{1,0:T(8,128)(2,1)S(1)}, bf16[128,128]{1,0:T(8,128)(2,1)S(1)}, u32[]{:S(2)}, u32[]{:S(2)}) collective-permute-start(bf16[128,128]{1,0:T(8,128)(2,1)S(1)} %get-tuple-element.14), channel_id=1, source_target_pairs={{0,1},{1,0},{2,3},{3,2},{4,5},{5,4},{6,7},{7,6},{8,9},{9,8},{10,11... | collective-permute-start | bytes 98312 | tf_op jit(solution)/shard_map/ppermute | solution.py:353
  4.8 0.9 %collective-permute-done = bf16[128,128]{1,0:T(8,128)(2,1)S(1)} collective-permute-done((bf16[128,128]{1,0:T(8,128)(2,1)S(1)}, bf16[128,128]{1,0:T(8,128)(2,1)S(1)}, u32[]{:S(2)}, u32[]{:S(2)}) %collective-permute-start) | collective-permute-done | bytes 32800 | tf_op jit(solution)/shard_map/ppermute | solution.py:353
  5.7 2.8 %collective-permute-start.1 = (bf16[128,128]{1,0:T(8,128)(2,1)S(1)}, bf16[128,128]{1,0:T(8,128)(2,1)S(1)}, u32[]{:S(2)}, u32[]{:S(2)}) collective-permute-start(bf16[128,128]{1,0:T(8,128)(2,1)S(1)} %add_convert_fusion.1), channel_id=1, source_target_pairs={{0,5},{1,4},{4,1},{5,0},{8,13},{9,12},{12,9},{13,8},{2,7},{3,6},{6... | collective-permute-start | bytes 98312 | tf_op jit(solution)/shard_map/ppermute | solution.py:357
  8.4 0.0 copy-done.2
  8.4 0.0 copy-done
  8.4 0.0 copy-done.1
  8.5 1.5 %collective-permute-start.3 = (f32[4,4096]{1,0:T(4,128)S(1)}, f32[4,4096]{1,0:T(4,128)S(1)}, u32[]{:S(2)}, u32[]{:S(2)}) collective-permute-start(f32[4,4096]{1,0:T(4,128)S(1)} %get-tuple-element.15), channel_id=1, source_target_pairs={{0,3},{1,2},{2,1},{3,0},{4,7},{5,6},{6,5},{7,4},{8,11},{9,10},{10,... | collective-permute-start | bytes 196616 | tf_op jit(solution)/shard_map/ppermute | solution.py:348
  10.0 0.0 collective-permute-done.1
  10.0 2.8 %collective-permute-start.2 = (bf16[128,128]{1,0:T(8,128)(2,1)S(1)}, bf16[128,128]{1,0:T(8,128)(2,1)S(1)}, u32[]{:S(2)}, u32[]{:S(2)}) collective-permute-start(bf16[128,128]{1,0:T(8,128)(2,1)S(1)} %add_convert_fusion.part), channel_id=1, source_target_pairs={{0,9},{1,8},{4,13},{5,12},{8,1},{9,0},{12,5},{13,4},{2,11},{3,10},... | collective-permute-start | bytes 98312 | tf_op jit(solution)/shard_map/ppermute | solution.py:357
  13.5 0.0 collective-permute-done.3.from_next.from_previous
  13.6 0.9 %collective-permute-done.2.moved = bf16[128,128]{1,0:T(8,128)(2,1)S(1)} collective-permute-done((bf16[128,128]{1,0:T(8,128)(2,1)S(1)}, bf16[128,128]{1,0:T(8,128)(2,1)S(1)}, u32[]{:S(2)}, u32[]{:S(2)}) %collective-permute-start.2) | collective-permute-done | bytes 32800 | tf_op jit(solution)/shard_map/ppermute | solution.py:357
  14.5 2.2 %backward.1.grad = f32[4,4096]{1,0:T(4,128)S(1)} custom-call(s32[8,128]{1,0:T(8,128)S(1)} %get-tuple-element.12.indices, bf16[256,64,128]{2,1,0:T(8,128)(2,1)S(1)} %get-tuple-element.13.tiles, bf16[128,128]{1,0:T(8,128)(2,1)S(1)} %add_convert_fusion.part, bf16[128,128]{1,0:T(8,128)(2,1)S(1)} %collective-permute-done.2.moved), custom_call_target="tpu_custom_call" | custom-call | tf_op jit(solution)/shard_map/backward/pallas_call | solution.py:375
  16.6 0.4 %collective-permute-start.4 = (f32[4,4096]{1,0:T(4,128)S(1)}, f32[4,4096]{1,0:T(4,128)S(1)}, u32[]{:S(2)}, u32[]{:S(2)}) collective-permute-start(f32[4,4096]{1,0:T(4,128)S(1)} %backward.1.grad), channel_id=1, source_target_pairs={{0,1},{1,0},{2,3},{3,2},{4,5},{5,4},{6,7},{7,6},{8,9},{9,8},{10,11... | collective-permute-start | bytes 196616 | tf_op jit(solution)/shard_map/ppermute | solution.py:389
  17.1 0.3 %local.1.base = f32[4,4096]{1,0:T(4,128)S(1)} custom-call(f32[1]{0:T(128)S(6)} %copy.13.rho, f32[4,4096]{1,0:T(4,128)S(1)} %copy-done.2, f32[3,4,4096]{2,1,0:T(4,128)S(1)} %copy-done.1, f32[3,4,4096]{2,1,0:T(4,128)S(1)} %copy-done, f32[1,4096]{1,0:T(1,128)S(1)} %get-tuple-element.17.edge, f32[4,4096]{1,0:T(4,128)S(1)} %collective-permute-done.3.from_next.from_previous, ...), custom_call_target="tpu_custom_call" | custom-call | tf_op jit(solution)/shard_map/local/pallas_call | solution.py:366
  17.3 0.6 %collective-permute-done.4.grad_other = f32[4,4096]{1,0:T(4,128)S(1)} collective-permute-done((f32[4,4096]{1,0:T(4,128)S(1)}, f32[4,4096]{1,0:T(4,128)S(1)}, u32[]{:S(2)}, u32[]{:S(2)}) %collective-permute-start.4) | collective-permute-done | bytes 65568 | tf_op jit(solution)/shard_map/ppermute | solution.py:389
  18.0 1.6 %collective-permute-start.5 = (f32[1,4096]{1,0:T(1,128)S(1)}, f32[1,4096]{1,0:T(1,128)S(1)}, u32[]{:S(2)}, u32[]{:S(2)}) collective-permute-start(f32[1,4096]{1,0:T(1,128)S(1)} %fusion.1), channel_id=1, source_target_pairs={{0,3},{1,2},{2,1},{3,0},{4,7},{5,6},{6,5},{7,4},{8,11},{9,10},{10,... | collective-permute-start | bytes 49160 | tf_op jit(solution)/shard_map/ppermute | solution.py:392
  19.6 1.6 %collective-permute-done.5.ahead = f32[1,4096]{1,0:T(1,128)S(1)} collective-permute-done((f32[1,4096]{1,0:T(1,128)S(1)}, f32[1,4096]{1,0:T(1,128)S(1)}, u32[]{:S(2)}, u32[]{:S(2)}) %collective-permute-start.5) | collective-permute-done | bytes 16416 | tf_op jit(solution)/shard_map/ppermute | solution.py:392
  21.2 0.9 %update.1 = (f32[4,4096]{1,0:T(4,128)}, f32[3,4,4096]{2,1,0:T(4,128)}, f32[3,4,4096]{2,1,0:T(4,128)}) custom-call(f32[4,4096]{1,0:T(4,128)S(1)} %backward.1.grad, f32[4,4096]{1,0:T(4,128)S(1)} %collective-permute-done.4.grad_other, f32[1,4096]{1,0:T(1,128)S(1)} %collective-permute-done.5.ahead, f32[4,4096]{1,0:T(4,128)S(1)} %local.1.base, ...), custom_call_target="tpu_custom_call" | custom-call | tf_op jit(solution)/shard_map/update/pallas_call | solution.py:397
  (5 shorter events, 0.1 us)
Async XLA Ops:
  0.6 7.8 %copy-start.2 = (f32[4,4096]{1,0:T(4,128)S(1)}, f32[4,4096]{1,0:T(4,128)}, u32[]{:S(2)}) copy-start(f32[4,4096]{1,0:T(4,128)} %vol.3) | copy-start | bytes 196612
  0.6 7.8 %copy-start = (f32[3,4,4096]{2,1,0:T(4,128)S(1)}, f32[3,4,4096]{2,1,0:T(4,128)}, u32[]{:S(2)}) copy-start(f32[3,4,4096]{2,1,0:T(4,128)} %dual.5) | copy-start | bytes 589828
  0.7 7.8 %copy-start.1 = (f32[3,4,4096]{2,1,0:T(4,128)S(1)}, f32[3,4,4096]{2,1,0:T(4,128)}, u32[]{:S(2)}) copy-start(f32[3,4,4096]{2,1,0:T(4,128)} %split.3) | copy-start | bytes 589828
  4.3 1.4 %collective-permute-start = (bf16[128,128]{1,0:T(8,128)(2,1)S(1)}, bf16[128,128]{1,0:T(8,128)(2,1)S(1)}, u32[]{:S(2)}, u32[]{:S(2)}) collective-permute-start(bf16[128,128]{1,0:T(8,128)(2,1)S(1)} %get-tuple-element.14), channel_id=1, source_target_pairs={{0,1},{1,0},{2,3},{3,2},{4,5},{5,4},{6,7},{7,6},{8,9},{9,8},{10,11... | collective-permute-start | bytes 98312 | tf_op jit(solution)/shard_map/ppermute | solution.py:353
  5.7 4.4 %collective-permute-start.1 = (bf16[128,128]{1,0:T(8,128)(2,1)S(1)}, bf16[128,128]{1,0:T(8,128)(2,1)S(1)}, u32[]{:S(2)}, u32[]{:S(2)}) collective-permute-start(bf16[128,128]{1,0:T(8,128)(2,1)S(1)} %add_convert_fusion.1), channel_id=1, source_target_pairs={{0,5},{1,4},{4,1},{5,0},{8,13},{9,12},{12,9},{13,8},{2,7},{3,6},{6... | collective-permute-start | bytes 98312 | tf_op jit(solution)/shard_map/ppermute | solution.py:357
  8.5 5.1 %collective-permute-start.3 = (f32[4,4096]{1,0:T(4,128)S(1)}, f32[4,4096]{1,0:T(4,128)S(1)}, u32[]{:S(2)}, u32[]{:S(2)}) collective-permute-start(f32[4,4096]{1,0:T(4,128)S(1)} %get-tuple-element.15), channel_id=1, source_target_pairs={{0,3},{1,2},{2,1},{3,0},{4,7},{5,6},{6,5},{7,4},{8,11},{9,10},{10,... | collective-permute-start | bytes 196616 | tf_op jit(solution)/shard_map/ppermute | solution.py:348
  10.0 4.4 %collective-permute-start.2 = (bf16[128,128]{1,0:T(8,128)(2,1)S(1)}, bf16[128,128]{1,0:T(8,128)(2,1)S(1)}, u32[]{:S(2)}, u32[]{:S(2)}) collective-permute-start(bf16[128,128]{1,0:T(8,128)(2,1)S(1)} %add_convert_fusion.part), channel_id=1, source_target_pairs={{0,9},{1,8},{4,13},{5,12},{8,1},{9,0},{12,5},{13,4},{2,11},{3,10},... | collective-permute-start | bytes 98312 | tf_op jit(solution)/shard_map/ppermute | solution.py:357
  16.6 1.3 %collective-permute-start.4 = (f32[4,4096]{1,0:T(4,128)S(1)}, f32[4,4096]{1,0:T(4,128)S(1)}, u32[]{:S(2)}, u32[]{:S(2)}) collective-permute-start(f32[4,4096]{1,0:T(4,128)S(1)} %backward.1.grad), channel_id=1, source_target_pairs={{0,1},{1,0},{2,3},{3,2},{4,5},{5,4},{6,7},{7,6},{8,9},{9,8},{10,11... | collective-permute-start | bytes 196616 | tf_op jit(solution)/shard_map/ppermute | solution.py:389
  18.0 3.2 %collective-permute-start.5 = (f32[1,4096]{1,0:T(1,128)S(1)}, f32[1,4096]{1,0:T(1,128)S(1)}, u32[]{:S(2)}, u32[]{:S(2)}) collective-permute-start(f32[1,4096]{1,0:T(1,128)S(1)} %fusion.1), channel_id=1, source_target_pairs={{0,3},{1,2},{2,1},{3,0},{4,7},{5,6},{6,5},{7,4},{8,11},{9,10},{10,... | collective-permute-start | bytes 49160 | tf_op jit(solution)/shard_map/ppermute | solution.py:392

commit v19 on v11

--- a/solution.py
+++ b/solution.py
@@ -1,3 +1,5 @@
+import functools
+
 import jax
 import jax.numpy as jnp
 from jax import lax
@@ -9,7 +11,7 @@
 TR = 128
 TAU = 0.5
 GROUP = 4
-CHUNKS = 2
+CUTS = (0, 2, 5, 8)
 VMEM_LIMIT = 16 * 1024 * 1024
 
 
@@ -20,13 +22,13 @@
 
 
 def start_tiles(proj_hbm, tiles, sems):
-    per = proj_hbm.shape[0] // CHUNKS
-    copies = []
-    for c in range(CHUNKS):
-        part = pl.ds(c * per, per)
+    eighth = proj_hbm.shape[0] // CUTS[-1]
+    copies = {}
+    for c, (low, high) in enumerate(zip(CUTS, CUTS[1:])):
+        part = pl.ds(low * eighth, (high - low) * eighth)
         copy = pltpu.make_async_copy(proj_hbm.at[part], tiles.at[part], sems.at[c])
         copy.start()
-        copies.append(copy)
+        copies[low * eighth] = copy
     return copies
 
 
@@ -47,41 +49,31 @@
 def forward_kernel(
     count, ray_hbm, voxel_hbm, vol_hbm, sino_hbm, proj_hbm,
     partial_out, index_out, tiles,
-    ray, voxel, index, vol, sino, double, table, acc0, acc1, acc2, acc3,
+    ray, voxel, vol, sino, double, table, acc0, acc1, acc2, acc3,
     sems, tile_sems,
 ):
     slots = proj_hbm.shape[0]
     lines = ray.shape[0]
     rays = acc0.shape[0] // 8 - 1
-    voxel_tiles = table.shape[0] // 8
     owned = sino.shape[0]
     width = vol.shape[1]
+    pairs = [
+        (voxel_hbm, voxel), (ray_hbm, ray), (vol_hbm, vol), (sino_hbm, sino),
+        (voxel_hbm, index_out.at[pl.ds(0, lines)]), (ray_hbm, index_out.at[pl.ds(lines, lines)]),
+    ]
     loads = [
-        pltpu.make_async_copy(source, target, sems.at[i])
-        for i, (source, target) in enumerate(
-            [(voxel_hbm, voxel), (ray_hbm, ray), (vol_hbm, vol), (sino_hbm, sino)]
-        )
+        pltpu.make_async_copy(source, target, sems.at[i]) for i, (source, target) in enumerate(pairs)
     ]
-    for load in loads:
+    for load in loads[:3]:
         load.start()
     copies = start_tiles(proj_hbm, tiles, tile_sems)
+    for load in loads[3:]:
+        load.start()
     accs = (acc0, acc1, acc2, acc3)
     for acc in accs:
         acc[...] = jnp.zeros_like(acc)
     row, lane = iotas((8, 128))
     low, top = lane < TV, row < 4
-
-    loads[0].wait()
-    loads[1].wait()
-    line, place = iotas((lines, 128))
-    live = 128 * line + place < count[0]
-    rays8, voxels8 = ray[...] * 8, voxel[...] * 8
-    index_out[0:lines, :] = voxels8
-    index_out[lines:2 * lines, :] = jnp.where(live, rays8, rays * 8)
-    index_out[2 * lines:3 * lines, :] = rays8
-    index_out[3 * lines:4 * lines, :] = jnp.where(live, voxels8, voxel_tiles * 8)
-    to_scalar = pltpu.make_async_copy(index_out, index, sems.at[4])
-    to_scalar.start()
 
     loads[2].wait()
     field = vol[...]
@@ -101,14 +93,14 @@
     mine = (lax.axis_index("tile") * lax.axis_size("rep") + lax.axis_index("rep")) * owned
     for r in range(owned):
         acc0[pl.ds(pl.multiple_of((mine + r) * 8, 8), 4), :] = -sino[r]
-    to_scalar.wait()
-    per = slots // CHUNKS
-    for g in range(slots // GROUP):
-        if GROUP * g % per == 0:
-            copies[GROUP * g // per].wait()
-        n = GROUP * g
+    loads[0].wait()
+    loads[1].wait()
+    used = count[0]
+    for n in range(0, slots, GROUP):
+        if n in copies:
+            copies[n].wait()
         at = [divmod(n + i, 128) for i in range(GROUP)]
-        picked = [table[rows8(index[line, place]), :] for line, place in at]
+        picked = [table[rows8(voxel[line, place] * 8), :] for line, place in at]
         pairs = [jnp.where(top, picked[2 * i], picked[2 * i + 1]) for i in range(2)]
         zero = jnp.zeros_like(pairs[0])
         left = jnp.concatenate([pairs[0], zero], axis=0).astype(jnp.bfloat16)
@@ -120,9 +112,14 @@
         )
         add_rows(
             accs,
-            [index[lines + line, place] for line, place in at],
+            [
+                jnp.where(n + i < used, ray[line, place], rays) * 8
+                for i, (line, place) in enumerate(at)
+            ],
             [sums[0:8], sums[0:8], sums[8:16], sums[8:16]],
         )
+    loads[4].wait()
+    loads[5].wait()
     for q in range(rays // 4):
         halves = []
         for r in (4 * q, 4 * q + 2):
@@ -161,12 +158,10 @@
         scale_out[1:2, at] = jnp.full((1, 128), factor, jnp.float32)
 
 
-def backward_kernel(
-    indices, tiles, part, moved, grad_out,
-    index, table, acc0, acc1, acc2, acc3, sem,
-):
+def backward_kernel(columns, count, indices, tiles, *refs):
+    parts, (grad_out, index, table, acc0, acc1, acc2, acc3, sem) = refs[:columns], refs[columns:]
     slots = tiles.shape[0]
-    lines = indices.shape[0] // 4
+    lines = indices.shape[0] // 2
     rays = table.shape[0] // 8
     voxel_tiles = acc0.shape[0] // 8 - 1
     to_scalar = pltpu.make_async_copy(indices, index, sem)
@@ -178,7 +173,9 @@
     low, top = lane < TV, row < 4
     for q in range(rays // 4):
         at = slice(16 * q, 16 * q + 16)
-        total = part[at, :].astype(jnp.float32) + moved[at, :].astype(jnp.float32)
+        total = parts[0][at, :].astype(jnp.float32)
+        for part in parts[1:]:
+            total += part[at, :].astype(jnp.float32)
         for k in range(2):
             x = total[8 * k:8 * k + 8]
             turned = pltpu.roll(x, 4, axis=0)
@@ -187,10 +184,10 @@
             table[r + 8:r + 16, :] = jnp.where(top, turned, x)
 
     to_scalar.wait()
-    for g in range(slots // GROUP):
-        n = GROUP * g
+    used = count[0]
+    for n in range(0, slots, GROUP):
         at = [divmod(n + i, 128) for i in range(GROUP)]
-        picked = [table[rows8(index[2 * lines + line, place]), :] for line, place in at]
+        picked = [table[rows8(index[lines + line, place] * 8), :] for line, place in at]
         rows = jnp.concatenate(
             [jnp.where(top, picked[2 * i], picked[2 * i + 1]) for i in range(2)], axis=0
         )
@@ -202,7 +199,10 @@
         )
         add_rows(
             accs,
-            [index[3 * lines + line, place] for line, place in at],
+            [
+                jnp.where(n + i < used, index[line, place], voxel_tiles) * 8
+                for i, (line, place) in enumerate(at)
+            ],
             [back[8 * k:8 * k + 8, 128 * k:128 * k + 128] for k in (0, 0, 1, 1)],
         )
     for j in range(voxel_tiles // 2):
@@ -284,22 +284,21 @@
         forward_kernel,
         out_shape=(
             jax.ShapeDtypeStruct((rays * slices, TR), bf16),
-            jax.ShapeDtypeStruct((4 * lines, 128), jnp.int32),
+            jax.ShapeDtypeStruct((2 * lines, 128), jnp.int32),
             jax.ShapeDtypeStruct(proj_tiles.shape, bf16),
         ),
         in_specs=[smem()] + [hbm()] * 5,
         out_specs=(vmem(),) * 3,
         scratch_shapes=[
-            pltpu.VMEM((lines, 128), jnp.int32),
-            pltpu.VMEM((lines, 128), jnp.int32),
-            pltpu.SMEM((4 * lines, 128), jnp.int32),
+            pltpu.SMEM((lines, 128), jnp.int32),
+            pltpu.SMEM((lines, 128), jnp.int32),
             pltpu.VMEM((slices, width), f32),
             pltpu.VMEM(sinogram.shape, f32),
             pltpu.VMEM((8, width), f32),
             pltpu.VMEM((voxel_tiles * 8, 128), f32),
         ]
         + [pltpu.VMEM((rays * 8 + 8, 128), f32)] * 4
-        + [pltpu.SemaphoreType.DMA((5,)), pltpu.SemaphoreType.DMA((CHUNKS,))],
+        + [pltpu.SemaphoreType.DMA((6,)), pltpu.SemaphoreType.DMA((len(CUTS) - 1,))],
         compiler_params=params(),
         name="forward",
     )(tile_count, *sources)
@@ -320,31 +319,34 @@
 
     swap = [(i, i ^ 1) for i in range(reps)]
     moved = lax.ppermute(partial, "rep", swap)
-    step = reps
-    while step < group:
-        partial = (partial.astype(f32) + moved.astype(f32)).astype(bf16)
-        moved = lax.ppermute(
-            partial, ("tile", "rep"), [(i, i ^ (step + 1)) for i in range(group)]
-        )
-        step *= 2
-    moved, base, edge, first, scales = lax.optimization_barrier(
-        (moved, base, edge, first, scales)
+    chip = (partial.astype(f32) + moved.astype(f32)).astype(bf16)
+    columns = group // reps
+    steps = [*range(1, columns)]
+    steps[:2] = steps[1::-1]
+    parts = [chip] + [
+        lax.ppermute(
+            chip, ("tile", "rep"), [(i, i ^ (reps * step + 1)) for i in range(group)]
+        )
+        for step in steps
+    ]
+    parts[-1], base, edge, first, scales = lax.optimization_barrier(
+        (parts[-1], base, edge, first, scales)
     )
 
     grad = pl.pallas_call(
-        backward_kernel,
+        functools.partial(backward_kernel, columns),
         out_shape=jax.ShapeDtypeStruct((slices, width), f32),
-        in_specs=[vmem()] * 4,
+        in_specs=[smem()] + [vmem()] * (2 + columns),
         out_specs=vmem(),
         scratch_shapes=[
-            pltpu.SMEM((4 * lines, 128), jnp.int32),
+            pltpu.SMEM((2 * lines, 128), jnp.int32),
             pltpu.VMEM((rays * 8, 128), f32),
         ]
         + [pltpu.VMEM((voxel_tiles * 8 + 8, 128), f32)] * 4
         + [pltpu.SemaphoreType.DMA],
         compiler_params=params(),
         name="backward",
-    )(indices, tiles, partial, moved)
+    )(tile_count, indices, tiles, *parts)
     grad_other = lax.ppermute(grad, "rep", swap)
     ahead = jnp.concatenate([base[0:1] - TAU * (grad[0:1] + grad_other[0:1]), first], axis=0)
     behind = jnp.concatenate([edge, edge], axis=0)

time: 22.4 us -> 22.4 us (level)
  waiting for transfers between devices: 5.79 us -> 6.34 us
  starting transfers between devices: 8.11 us -> 7.85 us
    ppermute x2 -> x3, waiting for transfers between devices: 2.24 us -> 2.68 us  [shards(): lax.ppermute(chip, ('tile', 'rep'), [(i, i ^ reps * step + 1) for i in ra...]
    ppermute x2 -> x3, starting transfers between devices: 5.57 us -> 5.37 us  [shards(): lax.ppermute(chip, ('tile', 'rep'), [(i, i ^ reps * step + 1) for i in ra...]
  transfers between devices with their start and end apart: 5 -> 6, of which waited for: 5 -> 5; matrix products, arithmetic and copies ran while one was open for 0% -> 0% of each run, Pallas kernels for 1% -> 1%
where the time goes in v19:
time: 22.4 us; the launch traced here: 22.2 us
  starting transfers between devices  7.85 us (35%)
  waiting for transfers between devices  6.34 us (28%)
  Pallas kernels  5.86 us (26%)
  between operations  2.07 us (9%)
    ppermute x3, starting transfers between devices, shards(): lax.ppermute(chip, ('tile', 'rep'), [(i, i ^ reps * step + 1) for i in ra...  5.37 us
    pallas_call x1, Pallas kernels, shards(): pl.pallas_call(forward_kernel, out_shape=(jax.ShapeDtypeStruct((rays * sl...  2.73 us
    ppermute x3, waiting for transfers between devices, shards(): lax.ppermute(chip, ('tile', 'rep'), [(i, i ^ reps * step + 1) for i in ra...  2.68 us
    pallas_call x1, Pallas kernels, shards(): pl.pallas_call(functools.partial(backward_kernel, columns), out_shape=jax...  1.92 us
    ppermute x1, waiting for transfers between devices, shards(): lax.ppermute(halo, ('slab', 'rep'), [(i, i ^ 3) for i in range(2 * reps)])  1.89 us
    ppermute x1, starting transfers between devices, shards(): lax.ppermute(halo, ('slab', 'rep'), [(i, i ^ 3) for i in range(2 * reps)])  1.51 us
    pallas_call x1, Pallas kernels, shards(): pl.pallas_call(update_kernel, out_shape=(jax.ShapeDtypeStruct((slices, wi...  0.93 us
    ppermute x1, waiting for transfers between devices, shards(): grad_other = lax.ppermute(grad, 'rep', swap)  0.9 us
  transfers between devices with their start and end apart: 6, of which 5 were waited for; matrix products, arithmetic and copies ran while one was open for 0% of the time, Pallas kernels for 1%

profile of v19, /device:TPU:0, one launch (start us, length us, event | category | flops | bytes accessed | tf_op | source)
XLA Modules:
  0.0 22.2 jit_solution(4806355752631152934)
XLA Ops:
  0.6 0.0 copy-start.1
  0.6 0.0 copy-start.2
  0.7 0.0 copy-start
  1.4 2.7 %forward.1 = (bf16[128,128]{1,0:T(8,128)(2,1)S(1)}, s32[4,128]{1,0:T(4,128)S(1)}, bf16[256,64,128]{2,1,0:T(8,128)(2,1)S(1)}) custom-call(s32[1]{0:T(128)S(6)} %copy.12.count, s32[2,128]{1,0:T(2,128)} %bitcast.2, s32[2,128]{1,0:T(2,128)} %bitcast.3, f32[4,4096]{1,0:T(4,128)} %vol.1, f32[4,4,128]{2,1,0:T(4,128)} %sino_hbm.1, bf16[256,64,128]{2,1,0:T(8,128)(2,1)} %proj_hbm.1), custom_call_target="tpu_custom_call" | custom-call | tf_op jit(solution)/shard_map/forward/pallas_call | solution.py:283
  4.1 0.5 %collective-permute-start = (bf16[128,128]{1,0:T(8,128)(2,1)S(1)}, bf16[128,128]{1,0:T(8,128)(2,1)S(1)}, u32[]{:S(2)}, u32[]{:S(2)}) collective-permute-start(bf16[128,128]{1,0:T(8,128)(2,1)S(1)} %get-tuple-element.17), channel_id=1, source_target_pairs={{0,1},{1,0},{2,3},{3,2},{4,5},{5,4},{6,7},{7,6},{8,9},{9,8},{10,11... | collective-permute-start | bytes 98312 | tf_op jit(solution)/shard_map/ppermute | solution.py:321
  4.6 0.9 %collective-permute-done = bf16[128,128]{1,0:T(8,128)(2,1)S(1)} collective-permute-done((bf16[128,128]{1,0:T(8,128)(2,1)S(1)}, bf16[128,128]{1,0:T(8,128)(2,1)S(1)}, u32[]{:S(2)}, u32[]{:S(2)}) %collective-permute-start) | collective-permute-done | bytes 32800 | tf_op jit(solution)/shard_map/ppermute | solution.py:321
  5.5 4.8 %collective-permute-start.3 = (bf16[128,128]{1,0:T(8,128)(2,1)S(1)}, bf16[128,128]{1,0:T(8,128)(2,1)S(1)}, u32[]{:S(2)}, u32[]{:S(2)}) collective-permute-start(bf16[128,128]{1,0:T(8,128)(2,1)S(1)} %add_convert_fusion.refs_0_), channel_id=1, source_target_pairs={{0,13},{1,12},{4,9},{5,8},{8,5},{9,4},{12,1},{13,0},{2,15},{3,14},... | collective-permute-start | bytes 98312 | tf_op jit(solution)/shard_map/ppermute | solution.py:327
  10.3 0.0 collective-permute-start.1
  10.3 0.6 %collective-permute-start.2 = (bf16[128,128]{1,0:T(8,128)(2,1)S(1)}, bf16[128,128]{1,0:T(8,128)(2,1)S(1)}, u32[]{:S(2)}, u32[]{:S(2)}) collective-permute-start(bf16[128,128]{1,0:T(8,128)(2,1)S(1)} %add_convert_fusion.refs_0_), channel_id=1, source_target_pairs={{0,5},{1,4},{4,1},{5,0},{8,13},{9,12},{12,9},{13,8},{2,7},{3,6},{6... | collective-permute-start | bytes 98312 | tf_op jit(solution)/shard_map/ppermute | solution.py:327
  11.5 0.0 copy-done.1
  11.5 0.0 copy-done.2
  11.5 0.0 copy-done
  11.6 0.3 %local.1 = (f32[4,4096]{1,0:T(4,128)S(1)}, f32[1,4096]{1,0:T(1,128)S(1)}, f32[1,4096]{1,0:T(1,128)S(1)}, f32[2,4096]{1,0:T(2,128)S(1)}) custom-call(f32[1]{0:T(128)S(6)} %copy.13.rho, f32[4,4096]{1,0:T(4,128)S(1)} %copy-done.1, f32[3,4,4096]{2,1,0:T(4,128)S(1)} %copy-done.2, f32[3,4,4096]{2,1,0:T(4,128)S(1)} %copy-done), custom_call_target="tpu_custom_call" | custom-call | tf_op jit(solution)/shard_map/local/pallas_call | solution.py:306
  11.8 0.2 %collective-permute-done.3.refs_3_ = bf16[128,128]{1,0:T(8,128)(2,1)S(1)} collective-permute-done((bf16[128,128]{1,0:T(8,128)(2,1)S(1)}, bf16[128,128]{1,0:T(8,128)(2,1)S(1)}, u32[]{:S(2)}, u32[]{:S(2)}) %collective-permute-start.3) | collective-permute-done | bytes 32800 | tf_op jit(solution)/shard_map/ppermute | solution.py:327
  12.1 2.5 %collective-permute-done.1.refs_1_ = bf16[128,128]{1,0:T(8,128)(2,1)S(1)} collective-permute-done((bf16[128,128]{1,0:T(8,128)(2,1)S(1)}, bf16[128,128]{1,0:T(8,128)(2,1)S(1)}, u32[]{:S(2)}, u32[]{:S(2)}) %collective-permute-start.1) | collective-permute-done | bytes 32800 | tf_op jit(solution)/shard_map/ppermute | solution.py:327
  14.5 0.0 collective-permute-done.2.refs_2_
  14.5 1.9 %backward.1.grad = f32[4,4096]{1,0:T(4,128)S(1)} custom-call(s32[1]{0:T(128)S(6)} %copy.12.count, s32[4,128]{1,0:T(4,128)S(1)} %get-tuple-element.15.indices, bf16[256,64,128]{2,1,0:T(8,128)(2,1)S(1)} %get-tuple-element.16.tiles, bf16[128,128]{1,0:T(8,128)(2,1)S(1)} %add_convert_fusion.refs_0_, bf16[128,128]{1,0:T(8,128)(2,1)S(1)} %collective-permute-done.1.refs_1_, ...), custom_call_target="tpu_custom_call" | custom-call | tf_op jit(solution)/shard_map/backward/pallas_call | solution.py:336
  16.4 0.4 %collective-permute-start.4 = (f32[4,4096]{1,0:T(4,128)S(1)}, f32[4,4096]{1,0:T(4,128)S(1)}, u32[]{:S(2)}, u32[]{:S(2)}) collective-permute-start(f32[4,4096]{1,0:T(4,128)S(1)} %backward.1.grad), channel_id=1, source_target_pairs={{0,1},{1,0},{2,3},{3,2},{4,5},{5,4},{6,7},{7,6},{8,9},{9,8},{10,11... | collective-permute-start | bytes 196616 | tf_op jit(solution)/shard_map/ppermute | solution.py:350
  16.9 0.9 %collective-permute-done.4.grad_other = f32[4,4096]{1,0:T(4,128)S(1)} collective-permute-done((f32[4,4096]{1,0:T(4,128)S(1)}, f32[4,4096]{1,0:T(4,128)S(1)}, u32[]{:S(2)}, u32[]{:S(2)}) %collective-permute-start.4) | collective-permute-done | bytes 65568 | tf_op jit(solution)/shard_map/ppermute | solution.py:350
  17.8 0.1 maximum_select_fusion
  17.9 1.5 %collective-permute-start.5 = (f32[2,4096]{1,0:T(2,128)S(1)}, f32[2,4096]{1,0:T(2,128)S(1)}, u32[]{:S(2)}, u32[]{:S(2)}) collective-permute-start(f32[2,4096]{1,0:T(2,128)S(1)} %maximum_select_fusion), channel_id=1, source_target_pairs={{0,3},{1,2},{2,1},{3,0},{4,7},{5,6},{6,5},{7,4},{8,11},{9,10},{10,... | collective-permute-start | bytes 98312 | tf_op jit(solution)/shard_map/ppermute | solution.py:355
  19.4 1.9 %collective-permute-done.5.from_next.from_previous = f32[2,4096]{1,0:T(2,128)S(1)} collective-permute-done((f32[2,4096]{1,0:T(2,128)S(1)}, f32[2,4096]{1,0:T(2,128)S(1)}, u32[]{:S(2)}, u32[]{:S(2)}) %collective-permute-start.5) | collective-permute-done | bytes 32800 | tf_op jit(solution)/shard_map/ppermute | solution.py:355
  21.3 0.9 %update.1 = (f32[4,4096]{1,0:T(4,128)}, f32[3,4,4096]{2,1,0:T(4,128)}, f32[3,4,4096]{2,1,0:T(4,128)}) custom-call(f32[4,4096]{1,0:T(4,128)S(1)} %backward.1.grad, f32[4,4096]{1,0:T(4,128)S(1)} %collective-permute-done.4.grad_other, f32[2,4096]{1,0:T(2,128)S(1)} %collective-permute-done.5.from_next.from_previous, ...), custom_call_target="tpu_custom_call" | custom-call | tf_op jit(solution)/shard_map/update/pallas_call | solution.py:362
  (2 shorter events, 0.0 us)
Async XLA Ops:
  0.6 10.9 %copy-start.1 = (f32[4,4096]{1,0:T(4,128)S(1)}, f32[4,4096]{1,0:T(4,128)}, u32[]{:S(2)}) copy-start(f32[4,4096]{1,0:T(4,128)} %vol.1) | copy-start | bytes 196612
  0.6 10.9 %copy-start.2 = (f32[3,4,4096]{2,1,0:T(4,128)S(1)}, f32[3,4,4096]{2,1,0:T(4,128)}, u32[]{:S(2)}) copy-start(f32[3,4,4096]{2,1,0:T(4,128)} %split.1) | copy-start | bytes 589828
  0.7 10.9 %copy-start = (f32[3,4,4096]{2,1,0:T(4,128)S(1)}, f32[3,4,4096]{2,1,0:T(4,128)}, u32[]{:S(2)}) copy-start(f32[3,4,4096]{2,1,0:T(4,128)} %dual.3) | copy-start | bytes 589828
  4.1 1.4 %collective-permute-start = (bf16[128,128]{1,0:T(8,128)(2,1)S(1)}, bf16[128,128]{1,0:T(8,128)(2,1)S(1)}, u32[]{:S(2)}, u32[]{:S(2)}) collective-permute-start(bf16[128,128]{1,0:T(8,128)(2,1)S(1)} %get-tuple-element.17), channel_id=1, source_target_pairs={{0,1},{1,0},{2,3},{3,2},{4,5},{5,4},{6,7},{7,6},{8,9},{9,8},{10,11... | collective-permute-start | bytes 98312 | tf_op jit(solution)/shard_map/ppermute | solution.py:321
  5.5 6.6 %collective-permute-start.3 = (bf16[128,128]{1,0:T(8,128)(2,1)S(1)}, bf16[128,128]{1,0:T(8,128)(2,1)S(1)}, u32[]{:S(2)}, u32[]{:S(2)}) collective-permute-start(bf16[128,128]{1,0:T(8,128)(2,1)S(1)} %add_convert_fusion.refs_0_), channel_id=1, source_target_pairs={{0,13},{1,12},{4,9},{5,8},{8,5},{9,4},{12,1},{13,0},{2,15},{3,14},... | collective-permute-start | bytes 98312 | tf_op jit(solution)/shard_map/ppermute | solution.py:327
  10.3 4.2 %collective-permute-start.1 = (bf16[128,128]{1,0:T(8,128)(2,1)S(1)}, bf16[128,128]{1,0:T(8,128)(2,1)S(1)}, u32[]{:S(2)}, u32[]{:S(2)}) collective-permute-start(bf16[128,128]{1,0:T(8,128)(2,1)S(1)} %add_convert_fusion.refs_0_), channel_id=1, source_target_pairs={{0,9},{1,8},{4,13},{5,12},{8,1},{9,0},{12,5},{13,4},{2,11},{3,10},... | collective-permute-start | bytes 98312 | tf_op jit(solution)/shard_map/ppermute | solution.py:327
  10.3 4.2 %collective-permute-start.2 = (bf16[128,128]{1,0:T(8,128)(2,1)S(1)}, bf16[128,128]{1,0:T(8,128)(2,1)S(1)}, u32[]{:S(2)}, u32[]{:S(2)}) collective-permute-start(bf16[128,128]{1,0:T(8,128)(2,1)S(1)} %add_convert_fusion.refs_0_), channel_id=1, source_target_pairs={{0,5},{1,4},{4,1},{5,0},{8,13},{9,12},{12,9},{13,8},{2,7},{3,6},{6... | collective-permute-start | bytes 98312 | tf_op jit(solution)/shard_map/ppermute | solution.py:327
  16.4 1.3 %collective-permute-start.4 = (f32[4,4096]{1,0:T(4,128)S(1)}, f32[4,4096]{1,0:T(4,128)S(1)}, u32[]{:S(2)}, u32[]{:S(2)}) collective-permute-start(f32[4,4096]{1,0:T(4,128)S(1)} %backward.1.grad), channel_id=1, source_target_pairs={{0,1},{1,0},{2,3},{3,2},{4,5},{5,4},{6,7},{7,6},{8,9},{9,8},{10,11... | collective-permute-start | bytes 196616 | tf_op jit(solution)/shard_map/ppermute | solution.py:350
  17.9 3.4 %collective-permute-start.5 = (f32[2,4096]{1,0:T(2,128)S(1)}, f32[2,4096]{1,0:T(2,128)S(1)}, u32[]{:S(2)}, u32[]{:S(2)}) collective-permute-start(f32[2,4096]{1,0:T(2,128)S(1)} %maximum_select_fusion), channel_id=1, source_target_pairs={{0,3},{1,2},{2,1},{3,0},{4,7},{5,6},{6,5},{7,4},{8,11},{9,10},{10,... | collective-permute-start | bytes 98312 | tf_op jit(solution)/shard_map/ppermute | solution.py:355

commit v20 on v14

--- a/solution.py
+++ b/solution.py
@@ -9,7 +9,7 @@
 TR = 128
 TAU = 0.5
 GROUP = 4
-CHUNKS = 2
+CUTS = (0, 2, 5, 8)
 VMEM_LIMIT = 16 * 1024 * 1024
 
 
@@ -20,13 +20,13 @@
 
 
 def start_tiles(proj_hbm, tiles, sems):
-    per = proj_hbm.shape[0] // CHUNKS
-    copies = []
-    for c in range(CHUNKS):
-        part = pl.ds(c * per, per)
+    eighth = proj_hbm.shape[0] // CUTS[-1]
+    copies = {}
+    for c, (low, high) in enumerate(zip(CUTS, CUTS[1:])):
+        part = pl.ds(low * eighth, (high - low) * eighth)
         copy = pltpu.make_async_copy(proj_hbm.at[part], tiles.at[part], sems.at[c])
         copy.start()
-        copies.append(copy)
+        copies[low * eighth] = copy
     return copies
 
 
@@ -47,41 +47,31 @@
 def forward_kernel(
     count, ray_hbm, voxel_hbm, vol_hbm, sino_hbm, proj_hbm,
     partial_out, index_out, tiles,
-    ray, voxel, index, vol, sino, double, table, acc0, acc1, acc2, acc3,
+    ray, voxel, vol, sino, double, table, acc0, acc1, acc2, acc3,
     sems, tile_sems,
 ):
     slots = proj_hbm.shape[0]
     lines = ray.shape[0]
     rays = acc0.shape[0] // 8 - 1
-    voxel_tiles = table.shape[0] // 8
     owned = sino.shape[0]
     width = vol.shape[1]
+    pairs = [
+        (voxel_hbm, voxel), (ray_hbm, ray), (vol_hbm, vol), (sino_hbm, sino),
+        (voxel_hbm, index_out.at[pl.ds(0, lines)]), (ray_hbm, index_out.at[pl.ds(lines, lines)]),
+    ]
     loads = [
-        pltpu.make_async_copy(source, target, sems.at[i])
-        for i, (source, target) in enumerate(
-            [(voxel_hbm, voxel), (ray_hbm, ray), (vol_hbm, vol), (sino_hbm, sino)]
-        )
+        pltpu.make_async_copy(source, target, sems.at[i]) for i, (source, target) in enumerate(pairs)
     ]
-    for load in loads:
+    for load in loads[:3]:
         load.start()
     copies = start_tiles(proj_hbm, tiles, tile_sems)
+    for load in loads[3:]:
+        load.start()
     accs = (acc0, acc1, acc2, acc3)
     for acc in accs:
         acc[...] = jnp.zeros_like(acc)
     row, lane = iotas((8, 128))
     low, top = lane < TV, row < 4
-
-    loads[0].wait()
-    loads[1].wait()
-    line, place = iotas((lines, 128))
-    live = 128 * line + place < count[0]
-    rays8, voxels8 = ray[...] * 8, voxel[...] * 8
-    index_out[0:lines, :] = voxels8
-    index_out[lines:2 * lines, :] = jnp.where(live, rays8, rays * 8)
-    index_out[2 * lines:3 * lines, :] = rays8
-    index_out[3 * lines:4 * lines, :] = jnp.where(live, voxels8, voxel_tiles * 8)
-    to_scalar = pltpu.make_async_copy(index_out, index, sems.at[4])
-    to_scalar.start()
 
     loads[2].wait()
     field = vol[...]
@@ -101,14 +91,14 @@
     mine = (lax.axis_index("tile") * lax.axis_size("rep") + lax.axis_index("rep")) * owned
     for r in range(owned):
         acc0[pl.ds(pl.multiple_of((mine + r) * 8, 8), 4), :] = -sino[r]
-    to_scalar.wait()
-    per = slots // CHUNKS
-    for g in range(slots // GROUP):
-        if GROUP * g % per == 0:
-            copies[GROUP * g // per].wait()
-        n = GROUP * g
+    loads[0].wait()
+    loads[1].wait()
+    used = count[0]
+    for n in range(0, slots, GROUP):
+        if n in copies:
+            copies[n].wait()
         at = [divmod(n + i, 128) for i in range(GROUP)]
-        picked = [table[rows8(index[line, place]), :] for line, place in at]
+        picked = [table[rows8(voxel[line, place] * 8), :] for line, place in at]
         pairs = [jnp.where(top, picked[2 * i], picked[2 * i + 1]) for i in range(2)]
         zero = jnp.zeros_like(pairs[0])
         left = jnp.concatenate([pairs[0], zero], axis=0).astype(jnp.bfloat16)
@@ -120,9 +110,14 @@
         )
         add_rows(
             accs,
-            [index[lines + line, place] for line, place in at],
+            [
+                jnp.where(n + i < used, ray[line, place], rays) * 8
+                for i, (line, place) in enumerate(at)
+            ],
             [sums[0:8], sums[0:8], sums[8:16], sums[8:16]],
         )
+    loads[4].wait()
+    loads[5].wait()
     for q in range(rays // 4):
         halves = []
         for r in (4 * q, 4 * q + 2):
@@ -136,15 +131,13 @@
         partial_out[16 * q:16 * q + 16, :] = jnp.concatenate(halves, axis=0).astype(jnp.bfloat16)
 
 
-def edges_kernel(vol, split, dual, edge_out, first_out, halo_out):
+def edges_kernel(vol, split, dual, edge_out, halo_out):
     start = lax.axis_index("slab") == 0
     for j in range(vol.shape[1] // 128):
         at = slice(128 * j, 128 * j + 128)
         edge = vol[3:4, at] - dual[0, 3:4, at] + split[0, 3:4, at]
-        first = vol[0:1, at]
         edge_out[:, at] = edge
-        first_out[:, at] = first
-        halo_out[:, at] = jnp.broadcast_to(jnp.where(start, edge, first), (4, 128))
+        halo_out[:, at] = jnp.broadcast_to(jnp.where(start, edge, vol[0:1, at]), (4, 128))
 
 
 def local_kernel(rho, vol, split, dual, edge, from_next, from_previous, base_out):
@@ -170,11 +163,11 @@
 
 
 def backward_kernel(
-    indices, tiles, part, moved, grad_out,
+    count, indices, tiles, part, moved, grad_out,
     index, table, acc0, acc1, acc2, acc3, sem,
 ):
     slots = tiles.shape[0]
-    lines = indices.shape[0] // 4
+    lines = indices.shape[0] // 2
     rays = table.shape[0] // 8
     voxel_tiles = acc0.shape[0] // 8 - 1
     to_scalar = pltpu.make_async_copy(indices, index, sem)
@@ -195,10 +188,10 @@
             table[r + 8:r + 16, :] = jnp.where(top, turned, x)
 
     to_scalar.wait()
-    for g in range(slots // GROUP):
-        n = GROUP * g
+    used = count[0]
+    for n in range(0, slots, GROUP):
         at = [divmod(n + i, 128) for i in range(GROUP)]
-        picked = [table[rows8(index[2 * lines + line, place]), :] for line, place in at]
+        picked = [table[rows8(index[lines + line, place] * 8), :] for line, place in at]
         rows = jnp.concatenate(
             [jnp.where(top, picked[2 * i], picked[2 * i + 1]) for i in range(2)], axis=0
         )
@@ -210,7 +203,10 @@
         )
         add_rows(
             accs,
-            [index[3 * lines + line, place] for line, place in at],
+            [
+                jnp.where(n + i < used, index[line, place], voxel_tiles) * 8
+                for i, (line, place) in enumerate(at)
+            ],
             [back[8 * k:8 * k + 8, 128 * k:128 * k + 128] for k in (0, 0, 1, 1)],
         )
     for j in range(voxel_tiles // 2):
@@ -224,7 +220,7 @@
 
 def plane_kernel(
     grad, grad_other, base, dual, limits,
-    new_volume, field_out, split_hbm, dual_hbm,
+    field_out, volume_hbm, split_hbm, dual_hbm,
     split, clipped, sems,
 ):
     row, lane = iotas((4, 128))
@@ -233,7 +229,6 @@
         at = slice(128 * j, 128 * j + 128)
         limit = limits[:, at]
         field = base[:, at] - TAU * (grad[:, at] + grad_other[:, at])
-        new_volume[:, at] = field
         field_out[:, at] = field
         x = jnp.concatenate([field] * 2, axis=0)
         steps = (
@@ -248,6 +243,7 @@
     copies = [
         pltpu.make_async_copy(split, split_hbm.at[pl.ds(1, 2)], sems.at[0]),
         pltpu.make_async_copy(clipped, dual_hbm.at[pl.ds(1, 2)], sems.at[1]),
+        pltpu.make_async_copy(field_out, volume_hbm, sems.at[2]),
     ]
     for copy in copies:
         copy.start()
@@ -322,32 +318,31 @@
         forward_kernel,
         out_shape=(
             jax.ShapeDtypeStruct((rays * slices, TR), bf16),
-            jax.ShapeDtypeStruct((4 * lines, 128), jnp.int32),
+            jax.ShapeDtypeStruct((2 * lines, 128), jnp.int32),
             jax.ShapeDtypeStruct(proj_tiles.shape, bf16),
         ),
         in_specs=[smem()] + [hbm()] * 5,
         out_specs=(vmem(),) * 3,
         scratch_shapes=[
-            pltpu.VMEM((lines, 128), jnp.int32),
-            pltpu.VMEM((lines, 128), jnp.int32),
-            pltpu.SMEM((4 * lines, 128), jnp.int32),
+            pltpu.SMEM((lines, 128), jnp.int32),
+            pltpu.SMEM((lines, 128), jnp.int32),
             pltpu.VMEM((slices, width), f32),
             pltpu.VMEM(sinogram.shape, f32),
             pltpu.VMEM((8, width), f32),
             pltpu.VMEM((voxel_tiles * 8, 128), f32),
         ]
         + [pltpu.VMEM((rays * 8 + 8, 128), f32)] * 4
-        + [pltpu.SemaphoreType.DMA((5,)), pltpu.SemaphoreType.DMA((CHUNKS,))],
+        + [pltpu.SemaphoreType.DMA((6,)), pltpu.SemaphoreType.DMA((len(CUTS) - 1,))],
         compiler_params=params(),
         name="forward",
     )(tile_count, *sources)
 
     row = jax.ShapeDtypeStruct((1, width), f32)
-    edge, first, halo = pl.pallas_call(
+    edge, halo = pl.pallas_call(
         edges_kernel,
-        out_shape=(row, row, jax.ShapeDtypeStruct((4, width), f32)),
+        out_shape=(row, jax.ShapeDtypeStruct((4, width), f32)),
         in_specs=[vmem()] * 3,
-        out_specs=(vmem(),) * 3,
+        out_specs=(vmem(),) * 2,
         compiler_params=params(),
         name="edges",
     )(volume, split_var, dual_var)
@@ -356,7 +351,7 @@
     if slabs == 2:
         from_next = from_previous = lax.ppermute(halo, ("slab", "rep"), across)
     else:
-        from_next = lax.ppermute(first, "slab", down)
+        from_next = lax.ppermute(volume[0:1], "slab", down)
         from_previous = lax.ppermute(edge, "slab", [(i - 1, i) for i in range(1, slabs)])
     swap = [(i, i ^ 1) for i in range(reps)]
     moved = lax.ppermute(partial, "rep", swap)
@@ -384,17 +379,17 @@
     grad = pl.pallas_call(
         backward_kernel,
         out_shape=jax.ShapeDtypeStruct((slices, width), f32),
-        in_specs=[vmem()] * 4,
+        in_specs=[smem()] + [vmem()] * 4,
         out_specs=vmem(),
         scratch_shapes=[
-            pltpu.SMEM((4 * lines, 128), jnp.int32),
+            pltpu.SMEM((2 * lines, 128), jnp.int32),
             pltpu.VMEM((rays * 8, 128), f32),
         ]
         + [pltpu.VMEM((voxel_tiles * 8 + 8, 128), f32)] * 4
         + [pltpu.SemaphoreType.DMA],
         compiler_params=params(),
         name="backward",
-    )(indices, tiles, partial, moved)
+    )(tile_count, indices, tiles, partial, moved)
     grad_other = lax.ppermute(grad, "rep", swap)
     ahead = base[0:1] - TAU * (grad[0:1] + grad_other[0:1])
     if slabs == 2:
@@ -404,13 +399,13 @@
 
     whole = jax.ShapeDtypeStruct((slices, width), f32)
     triple = jax.ShapeDtypeStruct((3, slices, width), f32)
-    new_volume, field, new_split, new_dual = pl.pallas_call(
+    field, new_volume, new_split, new_dual = pl.pallas_call(
         plane_kernel,
         out_shape=(whole, whole, triple, triple),
         in_specs=[vmem()] * 5,
-        out_specs=(vmem(), vmem(), hbm(), hbm()),
+        out_specs=(vmem(), hbm(), hbm(), hbm()),
         scratch_shapes=[pltpu.VMEM((2, slices, width), f32)] * 2
-        + [pltpu.SemaphoreType.DMA((2,))],
+        + [pltpu.SemaphoreType.DMA((3,))],
         compiler_params=params(),
         name="plane",
     )(grad, grad_other, base, dual_var, limits)

time: 22.3 us -> 21.8 us (0.978)
  Pallas kernels: 7.96 us -> 6.57 us
  starting transfers between devices: 8.63 us -> 9.67 us
    pallas_call x1, Pallas kernels: 0.65 us -> 0.04 us  [shards(): pl.pallas_call(edges_kernel, out_shape=(row, jax.ShapeDtypeStruct((4, wid...]
    pallas_call x1, Pallas kernels: 1.49 us -> 0.89 us  [shards(): pl.pallas_call(plane_kernel, out_shape=(whole, whole, triple, triple), in...]
    ppermute x2, starting transfers between devices: 5.17 us -> 5.58 us  [shards(): lax.ppermute(partial, ('tile', 'rep'), [(i, i ^ step + 1) for i in range(...]
    ppermute x1, starting transfers between devices: 1.26 us -> 1.61 us  [shards(): ahead = lax.ppermute(ahead, ('slab', 'rep'), across)]
    ppermute x1, waiting for transfers between devices: 0.47 us -> 0.72 us  [shards(): ahead = lax.ppermute(ahead, ('slab', 'rep'), across)]
    ppermute x2, waiting for transfers between devices: 1.16 us -> 0.93 us  [shards(): lax.ppermute(partial, ('tile', 'rep'), [(i, i ^ step + 1) for i in range(...]
  transfers between devices with their start and end apart: 6 -> 6, of which waited for: 4 -> 4; matrix products, arithmetic and copies ran while one was open for 0% -> 0% of each run, Pallas kernels for 11% -> 6%
where the time goes in v20:
time: 21.8 us; the launch traced here: 21.6 us
  starting transfers between devices  9.67 us (44%)
  Pallas kernels  6.57 us (30%)
  waiting for transfers between devices  3.15 us (14%)
  between operations  2.11 us (10%)
    ppermute x2, starting transfers between devices, shards(): lax.ppermute(partial, ('tile', 'rep'), [(i, i ^ step + 1) for i in range(...  5.58 us
    pallas_call x1, Pallas kernels, shards(): pl.pallas_call(forward_kernel, out_shape=(jax.ShapeDtypeStruct((rays * sl...  2.73 us
    pallas_call x1, Pallas kernels, shards(): pl.pallas_call(backward_kernel, out_shape=jax.ShapeDtypeStruct((slices, w...  1.92 us
    ppermute x1, starting transfers between devices, shards(): ahead = lax.ppermute(ahead, ('slab', 'rep'), across)  1.61 us
    ppermute x1, starting transfers between devices, shards(): from_next = from_previous = lax.ppermute(halo, ('slab', 'rep'), across)  1.51 us
    ppermute x2, waiting for transfers between devices, shards(): lax.ppermute(partial, ('tile', 'rep'), [(i, i ^ step + 1) for i in range(...  0.93 us
    pallas_call x1, Pallas kernels, shards(): pl.pallas_call(plane_kernel, out_shape=(whole, whole, triple, triple), in...  0.89 us
    ppermute x1, waiting for transfers between devices, shards(): moved = lax.ppermute(partial, 'rep', swap)  0.86 us
  transfers between devices with their start and end apart: 6, of which 4 were waited for; matrix products, arithmetic and copies ran while one was open for 0% of the time, Pallas kernels for 6%

profile of v20, /device:TPU:0, one launch (start us, length us, event | category | flops | bytes accessed | tf_op | source)
XLA Modules:
  0.0 21.6 jit_solution(3330090696960222062)
XLA Ops:
  0.6 0.0 copy-start.2
  0.6 0.0 copy-start
  0.7 0.0 copy-start.1
  1.4 2.7 %forward.1 = (bf16[128,128]{1,0:T(8,128)(2,1)S(1)}, s32[4,128]{1,0:T(4,128)S(1)}, bf16[256,64,128]{2,1,0:T(8,128)(2,1)S(1)}) custom-call(s32[1]{0:T(128)S(6)} %copy.16.count, s32[2,128]{1,0:T(2,128)} %bitcast.3, s32[2,128]{1,0:T(2,128)} %bitcast.4, f32[4,4096]{1,0:T(4,128)} %vol.3, f32[4,4,128]{2,1,0:T(4,128)} %sino_hbm.1, bf16[256,64,128]{2,1,0:T(8,128)(2,1)} %proj_hbm.1), custom_call_target="tpu_custom_call" | custom-call | tf_op jit(solution)/shard_map/forward/pallas_call | solution.py:317
  4.1 0.5 %collective-permute-start = (bf16[128,128]{1,0:T(8,128)(2,1)S(1)}, bf16[128,128]{1,0:T(8,128)(2,1)S(1)}, u32[]{:S(2)}, u32[]{:S(2)}) collective-permute-start(bf16[128,128]{1,0:T(8,128)(2,1)S(1)} %get-tuple-element.20), channel_id=1, source_target_pairs={{0,1},{1,0},{2,3},{3,2},{4,5},{5,4},{6,7},{7,6},{8,9},{9,8},{10,11... | collective-permute-start | bytes 98312 | tf_op jit(solution)/shard_map/ppermute | solution.py:357
  4.6 0.9 %collective-permute-done = bf16[128,128]{1,0:T(8,128)(2,1)S(1)} collective-permute-done((bf16[128,128]{1,0:T(8,128)(2,1)S(1)}, bf16[128,128]{1,0:T(8,128)(2,1)S(1)}, u32[]{:S(2)}, u32[]{:S(2)}) %collective-permute-start) | collective-permute-done | bytes 32800 | tf_op jit(solution)/shard_map/ppermute | solution.py:357
  5.5 2.8 %collective-permute-start.1 = (bf16[128,128]{1,0:T(8,128)(2,1)S(1)}, bf16[128,128]{1,0:T(8,128)(2,1)S(1)}, u32[]{:S(2)}, u32[]{:S(2)}) collective-permute-start(bf16[128,128]{1,0:T(8,128)(2,1)S(1)} %add_convert_fusion.1), channel_id=1, source_target_pairs={{0,5},{1,4},{4,1},{5,0},{8,13},{9,12},{12,9},{13,8},{2,7},{3,6},{6... | collective-permute-start | bytes 98312 | tf_op jit(solution)/shard_map/ppermute | solution.py:361
  8.3 0.0 copy-done.2
  8.3 0.0 copy-done
  8.3 0.0 copy-done.1
  8.3 1.5 %collective-permute-start.3 = (f32[4,4096]{1,0:T(4,128)S(1)}, f32[4,4096]{1,0:T(4,128)S(1)}, u32[]{:S(2)}, u32[]{:S(2)}) collective-permute-start(f32[4,4096]{1,0:T(4,128)S(1)} %get-tuple-element.21), channel_id=1, source_target_pairs={{0,3},{1,2},{2,1},{3,0},{4,7},{5,6},{6,5},{7,4},{8,11},{9,10},{10,... | collective-permute-start | bytes 196616 | tf_op jit(solution)/shard_map/ppermute | solution.py:352
  9.8 0.0 collective-permute-done.1
  9.9 2.8 %collective-permute-start.2 = (bf16[128,128]{1,0:T(8,128)(2,1)S(1)}, bf16[128,128]{1,0:T(8,128)(2,1)S(1)}, u32[]{:S(2)}, u32[]{:S(2)}) collective-permute-start(bf16[128,128]{1,0:T(8,128)(2,1)S(1)} %add_convert_fusion.part), channel_id=1, source_target_pairs={{0,9},{1,8},{4,13},{5,12},{8,1},{9,0},{12,5},{13,4},{2,11},{3,10},... | collective-permute-start | bytes 98312 | tf_op jit(solution)/shard_map/ppermute | solution.py:361
  13.4 0.0 collective-permute-done.3.from_next.from_previous
  13.4 0.9 %collective-permute-done.2.moved = bf16[128,128]{1,0:T(8,128)(2,1)S(1)} collective-permute-done((bf16[128,128]{1,0:T(8,128)(2,1)S(1)}, bf16[128,128]{1,0:T(8,128)(2,1)S(1)}, u32[]{:S(2)}, u32[]{:S(2)}) %collective-permute-start.2) | collective-permute-done | bytes 32800 | tf_op jit(solution)/shard_map/ppermute | solution.py:361
  14.3 1.9 %backward.1.grad = f32[4,4096]{1,0:T(4,128)S(1)} custom-call(s32[1]{0:T(128)S(6)} %copy.16.count, s32[4,128]{1,0:T(4,128)S(1)} %get-tuple-element.18.indices, bf16[256,64,128]{2,1,0:T(8,128)(2,1)S(1)} %get-tuple-element.19.tiles, bf16[128,128]{1,0:T(8,128)(2,1)S(1)} %add_convert_fusion.part, bf16[128,128]{1,0:T(8,128)(2,1)S(1)} %collective-permute-done.2.moved), custom_call_target="tpu_custom_call" | custom-call | tf_op jit(solution)/shard_map/backward/pallas_call | solution.py:379
  16.2 0.4 %collective-permute-start.4 = (f32[4,4096]{1,0:T(4,128)S(1)}, f32[4,4096]{1,0:T(4,128)S(1)}, u32[]{:S(2)}, u32[]{:S(2)}) collective-permute-start(f32[4,4096]{1,0:T(4,128)S(1)} %backward.1.grad), channel_id=1, source_target_pairs={{0,1},{1,0},{2,3},{3,2},{4,5},{5,4},{6,7},{7,6},{8,9},{9,8},{10,11... | collective-permute-start | bytes 196616 | tf_op jit(solution)/shard_map/ppermute | solution.py:393
  16.7 0.3 %local.1.base = f32[4,4096]{1,0:T(4,128)S(1)} custom-call(f32[1]{0:T(128)S(6)} %copy.17.rho, f32[4,4096]{1,0:T(4,128)S(1)} %copy-done.2, f32[3,4,4096]{2,1,0:T(4,128)S(1)} %copy-done.1, f32[3,4,4096]{2,1,0:T(4,128)S(1)} %copy-done, f32[1,4096]{1,0:T(1,128)S(1)} %get-tuple-element.23.edge, f32[4,4096]{1,0:T(4,128)S(1)} %collective-permute-done.3.from_next.from_previous, ...), custom_call_target="tpu_custom_call" | custom-call | tf_op jit(solution)/shard_map/local/pallas_call | solution.py:370
  17.0 0.6 %collective-permute-done.4.grad_other = f32[4,4096]{1,0:T(4,128)S(1)} collective-permute-done((f32[4,4096]{1,0:T(4,128)S(1)}, f32[4,4096]{1,0:T(4,128)S(1)}, u32[]{:S(2)}, u32[]{:S(2)}) %collective-permute-start.4) | collective-permute-done | bytes 65568 | tf_op jit(solution)/shard_map/ppermute | solution.py:393
  17.6 1.6 %collective-permute-start.5 = (f32[1,4096]{1,0:T(1,128)S(1)}, f32[1,4096]{1,0:T(1,128)S(1)}, u32[]{:S(2)}, u32[]{:S(2)}) collective-permute-start(f32[1,4096]{1,0:T(1,128)S(1)} %fusion.1), channel_id=1, source_target_pairs={{0,3},{1,2},{2,1},{3,0},{4,7},{5,6},{6,5},{7,4},{8,11},{9,10},{10,... | collective-permute-start | bytes 49160 | tf_op jit(solution)/shard_map/ppermute | solution.py:396
  19.2 0.9 %plane.1 = (f32[4,4096]{1,0:T(4,128)S(1)}, f32[4,4096]{1,0:T(4,128)}, f32[3,4,4096]{2,1,0:T(4,128)}, f32[3,4,4096]{2,1,0:T(4,128)}) custom-call(f32[4,4096]{1,0:T(4,128)S(1)} %backward.1.grad, f32[4,4096]{1,0:T(4,128)S(1)} %collective-permute-done.4.grad_other, f32[4,4096]{1,0:T(4,128)S(1)} %local.1.base, f32[3,4,4096]{2,1,0:T(4,128)S(1)} %copy-done, ...), custom_call_target="tpu_custom_call" | custom-call | tf_op jit(solution)/shard_map/plane/pallas_call | solution.py:402
  20.1 0.7 %collective-permute-done.5.ahead = f32[1,4096]{1,0:T(1,128)S(1)} collective-permute-done((f32[1,4096]{1,0:T(1,128)S(1)}, f32[1,4096]{1,0:T(1,128)S(1)}, u32[]{:S(2)}, u32[]{:S(2)}) %collective-permute-start.5) | collective-permute-done | bytes 16416 | tf_op jit(solution)/shard_map/ppermute | solution.py:396
  20.8 0.7 %depth.1 = (f32[3,4,4096]{2,1,0:T(4,128)}, f32[3,4,4096]{2,1,0:T(4,128)}) custom-call(f32[4,4096]{1,0:T(4,128)S(1)} %get-tuple-element.28.field_in, f32[1,4096]{1,0:T(1,128)S(1)} %collective-permute-done.5.ahead, f32[3,4,4096]{2,1,0:T(4,128)S(1)} %copy-done, f32[1,4096]{1,0:T(1,128)S(1)} %broadcast_in_dim.9.limits, ...), custom_call_target="tpu_custom_call", output_to_operand_aliasing={{0}: (4, {}), {1}: (5, {})} | custom-call | tf_op jit(solution)/shard_map/depth/pallas_call | solution.py:412
  (5 shorter events, 0.1 us)
Async XLA Ops:
  0.6 7.6 %copy-start.2 = (f32[4,4096]{1,0:T(4,128)S(1)}, f32[4,4096]{1,0:T(4,128)}, u32[]{:S(2)}) copy-start(f32[4,4096]{1,0:T(4,128)} %vol.3) | copy-start | bytes 196612
  0.6 7.6 %copy-start = (f32[3,4,4096]{2,1,0:T(4,128)S(1)}, f32[3,4,4096]{2,1,0:T(4,128)}, u32[]{:S(2)}) copy-start(f32[3,4,4096]{2,1,0:T(4,128)} %dual.7) | copy-start | bytes 589828
  0.7 7.6 %copy-start.1 = (f32[3,4,4096]{2,1,0:T(4,128)S(1)}, f32[3,4,4096]{2,1,0:T(4,128)}, u32[]{:S(2)}) copy-start(f32[3,4,4096]{2,1,0:T(4,128)} %split.3) | copy-start | bytes 589828
  4.1 1.4 %collective-permute-start = (bf16[128,128]{1,0:T(8,128)(2,1)S(1)}, bf16[128,128]{1,0:T(8,128)(2,1)S(1)}, u32[]{:S(2)}, u32[]{:S(2)}) collective-permute-start(bf16[128,128]{1,0:T(8,128)(2,1)S(1)} %get-tuple-element.20), channel_id=1, source_target_pairs={{0,1},{1,0},{2,3},{3,2},{4,5},{5,4},{6,7},{7,6},{8,9},{9,8},{10,11... | collective-permute-start | bytes 98312 | tf_op jit(solution)/shard_map/ppermute | solution.py:357
  5.5 4.4 %collective-permute-start.1 = (bf16[128,128]{1,0:T(8,128)(2,1)S(1)}, bf16[128,128]{1,0:T(8,128)(2,1)S(1)}, u32[]{:S(2)}, u32[]{:S(2)}) collective-permute-start(bf16[128,128]{1,0:T(8,128)(2,1)S(1)} %add_convert_fusion.1), channel_id=1, source_target_pairs={{0,5},{1,4},{4,1},{5,0},{8,13},{9,12},{12,9},{13,8},{2,7},{3,6},{6... | collective-permute-start | bytes 98312 | tf_op jit(solution)/shard_map/ppermute | solution.py:361
  8.3 5.1 %collective-permute-start.3 = (f32[4,4096]{1,0:T(4,128)S(1)}, f32[4,4096]{1,0:T(4,128)S(1)}, u32[]{:S(2)}, u32[]{:S(2)}) collective-permute-start(f32[4,4096]{1,0:T(4,128)S(1)} %get-tuple-element.21), channel_id=1, source_target_pairs={{0,3},{1,2},{2,1},{3,0},{4,7},{5,6},{6,5},{7,4},{8,11},{9,10},{10,... | collective-permute-start | bytes 196616 | tf_op jit(solution)/shard_map/ppermute | solution.py:352
  9.9 4.4 %collective-permute-start.2 = (bf16[128,128]{1,0:T(8,128)(2,1)S(1)}, bf16[128,128]{1,0:T(8,128)(2,1)S(1)}, u32[]{:S(2)}, u32[]{:S(2)}) collective-permute-start(bf16[128,128]{1,0:T(8,128)(2,1)S(1)} %add_convert_fusion.part), channel_id=1, source_target_pairs={{0,9},{1,8},{4,13},{5,12},{8,1},{9,0},{12,5},{13,4},{2,11},{3,10},... | collective-permute-start | bytes 98312 | tf_op jit(solution)/shard_map/ppermute | solution.py:361
  16.2 1.3 %collective-permute-start.4 = (f32[4,4096]{1,0:T(4,128)S(1)}, f32[4,4096]{1,0:T(4,128)S(1)}, u32[]{:S(2)}, u32[]{:S(2)}) collective-permute-start(f32[4,4096]{1,0:T(4,128)S(1)} %backward.1.grad), channel_id=1, source_target_pairs={{0,1},{1,0},{2,3},{3,2},{4,5},{5,4},{6,7},{7,6},{8,9},{9,8},{10,11... | collective-permute-start | bytes 196616 | tf_op jit(solution)/shard_map/ppermute | solution.py:393
  17.6 3.2 %collective-permute-start.5 = (f32[1,4096]{1,0:T(1,128)S(1)}, f32[1,4096]{1,0:T(1,128)S(1)}, u32[]{:S(2)}, u32[]{:S(2)}) collective-permute-start(f32[1,4096]{1,0:T(1,128)S(1)} %fusion.1), channel_id=1, source_target_pairs={{0,3},{1,2},{2,1},{3,0},{4,7},{5,6},{6,5},{7,4},{8,11},{9,10},{10,... | collective-permute-start | bytes 49160 | tf_op jit(solution)/shard_map/ppermute | solution.py:396

commit v21 on v20

--- a/solution.py
+++ b/solution.py
@@ -46,19 +46,15 @@
 
 def forward_kernel(
     count, ray_hbm, voxel_hbm, vol_hbm, sino_hbm, proj_hbm,
-    partial_out, index_out, tiles,
+    partial_out, tiles,
     ray, voxel, vol, sino, double, table, acc0, acc1, acc2, acc3,
     sems, tile_sems,
 ):
     slots = proj_hbm.shape[0]
-    lines = ray.shape[0]
     rays = acc0.shape[0] // 8 - 1
     owned = sino.shape[0]
     width = vol.shape[1]
-    pairs = [
-        (voxel_hbm, voxel), (ray_hbm, ray), (vol_hbm, vol), (sino_hbm, sino),
-        (voxel_hbm, index_out.at[pl.ds(0, lines)]), (ray_hbm, index_out.at[pl.ds(lines, lines)]),
-    ]
+    pairs = [(voxel_hbm, voxel), (ray_hbm, ray), (vol_hbm, vol), (sino_hbm, sino)]
     loads = [
         pltpu.make_async_copy(source, target, sems.at[i]) for i, (source, target) in enumerate(pairs)
     ]
@@ -116,8 +112,6 @@
             ],
             [sums[0:8], sums[0:8], sums[8:16], sums[8:16]],
         )
-    loads[4].wait()
-    loads[5].wait()
     for q in range(rays // 4):
         halves = []
         for r in (4 * q, 4 * q + 2):
@@ -163,15 +157,18 @@
 
 
 def backward_kernel(
-    count, indices, tiles, part, moved, grad_out,
-    index, table, acc0, acc1, acc2, acc3, sem,
+    count, voxel_in, ray_in, tiles, part, moved, grad_out,
+    voxel, ray, table, acc0, acc1, acc2, acc3, sems,
 ):
     slots = tiles.shape[0]
-    lines = indices.shape[0] // 2
     rays = table.shape[0] // 8
     voxel_tiles = acc0.shape[0] // 8 - 1
-    to_scalar = pltpu.make_async_copy(indices, index, sem)
-    to_scalar.start()
+    loads = [
+        pltpu.make_async_copy(ray_in, ray, sems.at[0]),
+        pltpu.make_async_copy(voxel_in, voxel, sems.at[1]),
+    ]
+    for load in loads:
+        load.start()
     accs = (acc0, acc1, acc2, acc3)
     for acc in accs:
         acc[...] = jnp.zeros_like(acc)
@@ -187,11 +184,12 @@
             table[r:r + 8, :] = jnp.where(top, x, turned)
             table[r + 8:r + 16, :] = jnp.where(top, turned, x)
 
-    to_scalar.wait()
+    for load in loads:
+        load.wait()
     used = count[0]
     for n in range(0, slots, GROUP):
         at = [divmod(n + i, 128) for i in range(GROUP)]
-        picked = [table[rows8(index[lines + line, place] * 8), :] for line, place in at]
+        picked = [table[rows8(ray[line, place] * 8), :] for line, place in at]
         rows = jnp.concatenate(
             [jnp.where(top, picked[2 * i], picked[2 * i + 1]) for i in range(2)], axis=0
         )
@@ -204,7 +202,7 @@
         add_rows(
             accs,
             [
-                jnp.where(n + i < used, index[line, place], voxel_tiles) * 8
+                jnp.where(n + i < used, voxel[line, place], voxel_tiles) * 8
                 for i, (line, place) in enumerate(at)
             ],
             [back[8 * k:8 * k + 8, 128 * k:128 * k + 128] for k in (0, 0, 1, 1)],
@@ -314,15 +312,14 @@
         for x in (ray_index, voxel_index, volume, sinogram, proj_tiles)
     ]
 
-    partial, indices, tiles = pl.pallas_call(
+    partial, tiles = pl.pallas_call(
         forward_kernel,
         out_shape=(
             jax.ShapeDtypeStruct((rays * slices, TR), bf16),
-            jax.ShapeDtypeStruct((2 * lines, 128), jnp.int32),
             jax.ShapeDtypeStruct(proj_tiles.shape, bf16),
         ),
         in_specs=[smem()] + [hbm()] * 5,
-        out_specs=(vmem(),) * 3,
+        out_specs=(vmem(),) * 2,
         scratch_shapes=[
             pltpu.SMEM((lines, 128), jnp.int32),
             pltpu.SMEM((lines, 128), jnp.int32),
@@ -332,7 +329,7 @@
             pltpu.VMEM((voxel_tiles * 8, 128), f32),
         ]
         + [pltpu.VMEM((rays * 8 + 8, 128), f32)] * 4
-        + [pltpu.SemaphoreType.DMA((6,)), pltpu.SemaphoreType.DMA((len(CUTS) - 1,))],
+        + [pltpu.SemaphoreType.DMA((4,)), pltpu.SemaphoreType.DMA((len(CUTS) - 1,))],
         compiler_params=params(),
         name="forward",
     )(tile_count, *sources)
@@ -379,17 +376,18 @@
     grad = pl.pallas_call(
         backward_kernel,
         out_shape=jax.ShapeDtypeStruct((slices, width), f32),
-        in_specs=[smem()] + [vmem()] * 4,
+        in_specs=[smem()] + [vmem()] * 5,
         out_specs=vmem(),
         scratch_shapes=[
-            pltpu.SMEM((2 * lines, 128), jnp.int32),
+            pltpu.SMEM((lines, 128), jnp.int32),
+            pltpu.SMEM((lines, 128), jnp.int32),
             pltpu.VMEM((rays * 8, 128), f32),
         ]
         + [pltpu.VMEM((voxel_tiles * 8 + 8, 128), f32)] * 4
-        + [pltpu.SemaphoreType.DMA],
+        + [pltpu.SemaphoreType.DMA((2,))],
         compiler_params=params(),
         name="backward",
-    )(tile_count, indices, tiles, partial, moved)
+    )(tile_count, voxel_index, ray_index, tiles, partial, moved)
     grad_other = lax.ppermute(grad, "rep", swap)
     ahead = base[0:1] - TAU * (grad[0:1] + grad_other[0:1])
     if slabs == 2:

time: 21.8 us -> 22.2 us (1.018)
  Pallas kernels: 6.57 us -> 6.97 us
    pallas_call x1, Pallas kernels: 2.73 us -> 3.09 us  [shards(): pl.pallas_call(forward_kernel, out_shape=(jax.ShapeDtypeStruct((rays * sl...]
  transfers between devices with their start and end apart: 6 -> 6, of which waited for: 4 -> 4; matrix products, arithmetic and copies ran while one was open for 0% -> 0% of each run, Pallas kernels for 6% -> 5%
where the time goes in v21:
time: 22.2 us; the launch traced here: 22 us
  starting transfers between devices  9.57 us (43%)
  Pallas kernels  6.97 us (31%)
  waiting for transfers between devices  3.2 us (14%)
  between operations  2.14 us (10%)
    ppermute x2, starting transfers between devices, shards(): lax.ppermute(partial, ('tile', 'rep'), [(i, i ^ step + 1) for i in range(...  5.61 us
    pallas_call x1, Pallas kernels, shards(): pl.pallas_call(forward_kernel, out_shape=(jax.ShapeDtypeStruct((rays * sl...  3.09 us
    pallas_call x1, Pallas kernels, shards(): pl.pallas_call(backward_kernel, out_shape=jax.ShapeDtypeStruct((slices, w...  1.95 us
    ppermute x1, starting transfers between devices, shards(): ahead = lax.ppermute(ahead, ('slab', 'rep'), across)  1.6 us
    ppermute x1, starting transfers between devices, shards(): from_next = from_previous = lax.ppermute(halo, ('slab', 'rep'), across)  1.51 us
    ppermute x2, waiting for transfers between devices, shards(): lax.ppermute(partial, ('tile', 'rep'), [(i, i ^ step + 1) for i in range(...  0.93 us
    pallas_call x1, Pallas kernels, shards(): pl.pallas_call(plane_kernel, out_shape=(whole, whole, triple, triple), in...  0.89 us
    ppermute x1, waiting for transfers between devices, shards(): moved = lax.ppermute(partial, 'rep', swap)  0.86 us
  transfers between devices with their start and end apart: 6, of which 4 were waited for; matrix products, arithmetic and copies ran while one was open for 0% of the time, Pallas kernels for 5%

profile of v21, /device:TPU:0, one launch (start us, length us, event | category | flops | bytes accessed | tf_op | source)
XLA Modules:
  0.0 22.0 jit_solution(15673329848487326584)
XLA Ops:
  0.6 0.0 copy-start.2
  0.6 0.0 copy-start.3
  0.7 0.0 copy-start.4
  0.7 0.0 copy-start
  0.7 0.0 copy-start.1
  1.4 3.1 %forward.1 = (bf16[128,128]{1,0:T(8,128)(2,1)S(1)}, bf16[256,64,128]{2,1,0:T(8,128)(2,1)S(1)}) custom-call(s32[1]{0:T(128)S(6)} %copy.16.count, s32[2,128]{1,0:T(2,128)} %bitcast.5, s32[2,128]{1,0:T(2,128)} %bitcast.3, f32[4,4096]{1,0:T(4,128)} %vol.3, f32[4,4,128]{2,1,0:T(4,128)} %sino_hbm.1, bf16[256,64,128]{2,1,0:T(8,128)(2,1)} %proj_hbm.1), custom_call_target="tpu_custom_call" | custom-call | tf_op jit(solution)/shard_map/forward/pallas_call | solution.py:315
  4.5 0.5 %collective-permute-start = (bf16[128,128]{1,0:T(8,128)(2,1)S(1)}, bf16[128,128]{1,0:T(8,128)(2,1)S(1)}, u32[]{:S(2)}, u32[]{:S(2)}) collective-permute-start(bf16[128,128]{1,0:T(8,128)(2,1)S(1)} %get-tuple-element.18), channel_id=1, source_target_pairs={{0,1},{1,0},{2,3},{3,2},{4,5},{5,4},{6,7},{7,6},{8,9},{9,8},{10,11... | collective-permute-start | bytes 98312 | tf_op jit(solution)/shard_map/ppermute | solution.py:354
  5.0 0.9 %collective-permute-done = bf16[128,128]{1,0:T(8,128)(2,1)S(1)} collective-permute-done((bf16[128,128]{1,0:T(8,128)(2,1)S(1)}, bf16[128,128]{1,0:T(8,128)(2,1)S(1)}, u32[]{:S(2)}, u32[]{:S(2)}) %collective-permute-start) | collective-permute-done | bytes 32800 | tf_op jit(solution)/shard_map/ppermute | solution.py:354
  5.8 2.8 %collective-permute-start.1 = (bf16[128,128]{1,0:T(8,128)(2,1)S(1)}, bf16[128,128]{1,0:T(8,128)(2,1)S(1)}, u32[]{:S(2)}, u32[]{:S(2)}) collective-permute-start(bf16[128,128]{1,0:T(8,128)(2,1)S(1)} %add_convert_fusion.1), channel_id=1, source_target_pairs={{0,5},{1,4},{4,1},{5,0},{8,13},{9,12},{12,9},{13,8},{2,7},{3,6},{6... | collective-permute-start | bytes 98312 | tf_op jit(solution)/shard_map/ppermute | solution.py:358
  8.6 0.0 copy-done.2
  8.6 0.0 copy-done.1
  8.7 1.5 %collective-permute-start.3 = (f32[4,4096]{1,0:T(4,128)S(1)}, f32[4,4096]{1,0:T(4,128)S(1)}, u32[]{:S(2)}, u32[]{:S(2)}) collective-permute-start(f32[4,4096]{1,0:T(4,128)S(1)} %get-tuple-element.19), channel_id=1, source_target_pairs={{0,3},{1,2},{2,1},{3,0},{4,7},{5,6},{6,5},{7,4},{8,11},{9,10},{10,... | collective-permute-start | bytes 196616 | tf_op jit(solution)/shard_map/ppermute | solution.py:349
  10.2 0.0 collective-permute-done.1
  10.2 2.8 %collective-permute-start.2 = (bf16[128,128]{1,0:T(8,128)(2,1)S(1)}, bf16[128,128]{1,0:T(8,128)(2,1)S(1)}, u32[]{:S(2)}, u32[]{:S(2)}) collective-permute-start(bf16[128,128]{1,0:T(8,128)(2,1)S(1)} %add_convert_fusion.part), channel_id=1, source_target_pairs={{0,9},{1,8},{4,13},{5,12},{8,1},{9,0},{12,5},{13,4},{2,11},{3,10},... | collective-permute-start | bytes 98312 | tf_op jit(solution)/shard_map/ppermute | solution.py:358
  13.8 0.0 collective-permute-done.3.from_next.from_previous
  13.8 0.9 %collective-permute-done.2.moved = bf16[128,128]{1,0:T(8,128)(2,1)S(1)} collective-permute-done((bf16[128,128]{1,0:T(8,128)(2,1)S(1)}, bf16[128,128]{1,0:T(8,128)(2,1)S(1)}, u32[]{:S(2)}, u32[]{:S(2)}) %collective-permute-start.2) | collective-permute-done | bytes 32800 | tf_op jit(solution)/shard_map/ppermute | solution.py:358
  14.7 2.0 %backward.1.grad = f32[4,4096]{1,0:T(4,128)S(1)} custom-call(s32[1]{0:T(128)S(6)} %copy.16.count, s32[2,128]{1,0:T(2,128)S(1)} %bitcast.4, s32[2,128]{1,0:T(2,128)S(1)} %bitcast.6, bf16[256,64,128]{2,1,0:T(8,128)(2,1)S(1)} %get-tuple-element.17.tiles, bf16[128,128]{1,0:T(8,128)(2,1)S(1)} %add_convert_fusion.part, ...), custom_call_target="tpu_custom_call" | custom-call | tf_op jit(solution)/shard_map/backward/pallas_call | solution.py:376
  16.7 0.4 %collective-permute-start.4 = (f32[4,4096]{1,0:T(4,128)S(1)}, f32[4,4096]{1,0:T(4,128)S(1)}, u32[]{:S(2)}, u32[]{:S(2)}) collective-permute-start(f32[4,4096]{1,0:T(4,128)S(1)} %backward.1.grad), channel_id=1, source_target_pairs={{0,1},{1,0},{2,3},{3,2},{4,5},{5,4},{6,7},{7,6},{8,9},{9,8},{10,11... | collective-permute-start | bytes 196616 | tf_op jit(solution)/shard_map/ppermute | solution.py:391
  17.0 0.3 %local.1.base = f32[4,4096]{1,0:T(4,128)S(1)} custom-call(f32[1]{0:T(128)S(6)} %copy.17.rho, f32[4,4096]{1,0:T(4,128)S(1)} %copy-done.2, f32[3,4,4096]{2,1,0:T(4,128)S(1)} %copy-done.1, f32[3,4,4096]{2,1,0:T(4,128)S(1)} %copy-done, f32[1,4096]{1,0:T(1,128)S(1)} %get-tuple-element.21.edge, f32[4,4096]{1,0:T(4,128)S(1)} %collective-permute-done.3.from_next.from_previous, ...), custom_call_target="tpu_custom_call" | custom-call | tf_op jit(solution)/shard_map/local/pallas_call | solution.py:367
  17.3 0.7 %collective-permute-done.4.grad_other = f32[4,4096]{1,0:T(4,128)S(1)} collective-permute-done((f32[4,4096]{1,0:T(4,128)S(1)}, f32[4,4096]{1,0:T(4,128)S(1)}, u32[]{:S(2)}, u32[]{:S(2)}) %collective-permute-start.4) | collective-permute-done | bytes 65568 | tf_op jit(solution)/shard_map/ppermute | solution.py:391
  18.0 1.6 %collective-permute-start.5 = (f32[1,4096]{1,0:T(1,128)S(1)}, f32[1,4096]{1,0:T(1,128)S(1)}, u32[]{:S(2)}, u32[]{:S(2)}) collective-permute-start(f32[1,4096]{1,0:T(1,128)S(1)} %fusion.1), channel_id=1, source_target_pairs={{0,3},{1,2},{2,1},{3,0},{4,7},{5,6},{6,5},{7,4},{8,11},{9,10},{10,... | collective-permute-start | bytes 49160 | tf_op jit(solution)/shard_map/ppermute | solution.py:394
  19.6 0.9 %plane.1 = (f32[4,4096]{1,0:T(4,128)S(1)}, f32[4,4096]{1,0:T(4,128)}, f32[3,4,4096]{2,1,0:T(4,128)}, f32[3,4,4096]{2,1,0:T(4,128)}) custom-call(f32[4,4096]{1,0:T(4,128)S(1)} %backward.1.grad, f32[4,4096]{1,0:T(4,128)S(1)} %collective-permute-done.4.grad_other, f32[4,4096]{1,0:T(4,128)S(1)} %local.1.base, f32[3,4,4096]{2,1,0:T(4,128)S(1)} %copy-done, ...), custom_call_target="tpu_custom_call" | custom-call | tf_op jit(solution)/shard_map/plane/pallas_call | solution.py:400
  20.5 0.7 %collective-permute-done.5.ahead = f32[1,4096]{1,0:T(1,128)S(1)} collective-permute-done((f32[1,4096]{1,0:T(1,128)S(1)}, f32[1,4096]{1,0:T(1,128)S(1)}, u32[]{:S(2)}, u32[]{:S(2)}) %collective-permute-start.5) | collective-permute-done | bytes 16416 | tf_op jit(solution)/shard_map/ppermute | solution.py:394
  21.2 0.7 %depth.1 = (f32[3,4,4096]{2,1,0:T(4,128)}, f32[3,4,4096]{2,1,0:T(4,128)}) custom-call(f32[4,4096]{1,0:T(4,128)S(1)} %get-tuple-element.26.field_in, f32[1,4096]{1,0:T(1,128)S(1)} %collective-permute-done.5.ahead, f32[3,4,4096]{2,1,0:T(4,128)S(1)} %copy-done, f32[1,4096]{1,0:T(1,128)S(1)} %broadcast_in_dim.9.limits, ...), custom_call_target="tpu_custom_call", output_to_operand_aliasing={{0}: (4, {}), {1}: (5, {})} | custom-call | tf_op jit(solution)/shard_map/depth/pallas_call | solution.py:410
  (8 shorter events, 0.1 us)
Async XLA Ops:
  0.6 8.0 %copy-start.2 = (f32[4,4096]{1,0:T(4,128)S(1)}, f32[4,4096]{1,0:T(4,128)}, u32[]{:S(2)}) copy-start(f32[4,4096]{1,0:T(4,128)} %vol.3) | copy-start | bytes 196612
  0.6 14.0 %copy-start.3 = (s32[256]{0:T(256)S(1)}, s32[256]{0:T(256)}, u32[]{:S(2)}) copy-start(s32[256]{0:T(256)} %param.15) | copy-start | bytes 3076
  0.7 14.0 %copy-start.4 = (s32[256]{0:T(256)S(1)}, s32[256]{0:T(256)}, u32[]{:S(2)}) copy-start(s32[256]{0:T(256)} %param.14) | copy-start | bytes 3076
  0.7 7.9 %copy-start = (f32[3,4,4096]{2,1,0:T(4,128)S(1)}, f32[3,4,4096]{2,1,0:T(4,128)}, u32[]{:S(2)}) copy-start(f32[3,4,4096]{2,1,0:T(4,128)} %dual.7) | copy-start | bytes 589828
  0.7 7.9 %copy-start.1 = (f32[3,4,4096]{2,1,0:T(4,128)S(1)}, f32[3,4,4096]{2,1,0:T(4,128)}, u32[]{:S(2)}) copy-start(f32[3,4,4096]{2,1,0:T(4,128)} %split.3) | copy-start | bytes 589828
  4.5 1.3 %collective-permute-start = (bf16[128,128]{1,0:T(8,128)(2,1)S(1)}, bf16[128,128]{1,0:T(8,128)(2,1)S(1)}, u32[]{:S(2)}, u32[]{:S(2)}) collective-permute-start(bf16[128,128]{1,0:T(8,128)(2,1)S(1)} %get-tuple-element.18), channel_id=1, source_target_pairs={{0,1},{1,0},{2,3},{3,2},{4,5},{5,4},{6,7},{7,6},{8,9},{9,8},{10,11... | collective-permute-start | bytes 98312 | tf_op jit(solution)/shard_map/ppermute | solution.py:354
  5.8 4.4 %collective-permute-start.1 = (bf16[128,128]{1,0:T(8,128)(2,1)S(1)}, bf16[128,128]{1,0:T(8,128)(2,1)S(1)}, u32[]{:S(2)}, u32[]{:S(2)}) collective-permute-start(bf16[128,128]{1,0:T(8,128)(2,1)S(1)} %add_convert_fusion.1), channel_id=1, source_target_pairs={{0,5},{1,4},{4,1},{5,0},{8,13},{9,12},{12,9},{13,8},{2,7},{3,6},{6... | collective-permute-start | bytes 98312 | tf_op jit(solution)/shard_map/ppermute | solution.py:358
  8.7 5.1 %collective-permute-start.3 = (f32[4,4096]{1,0:T(4,128)S(1)}, f32[4,4096]{1,0:T(4,128)S(1)}, u32[]{:S(2)}, u32[]{:S(2)}) collective-permute-start(f32[4,4096]{1,0:T(4,128)S(1)} %get-tuple-element.19), channel_id=1, source_target_pairs={{0,3},{1,2},{2,1},{3,0},{4,7},{5,6},{6,5},{7,4},{8,11},{9,10},{10,... | collective-permute-start | bytes 196616 | tf_op jit(solution)/shard_map/ppermute | solution.py:349
  10.2 4.4 %collective-permute-start.2 = (bf16[128,128]{1,0:T(8,128)(2,1)S(1)}, bf16[128,128]{1,0:T(8,128)(2,1)S(1)}, u32[]{:S(2)}, u32[]{:S(2)}) collective-permute-start(bf16[128,128]{1,0:T(8,128)(2,1)S(1)} %add_convert_fusion.part), channel_id=1, source_target_pairs={{0,9},{1,8},{4,13},{5,12},{8,1},{9,0},{12,5},{13,4},{2,11},{3,10},... | collective-permute-start | bytes 98312 | tf_op jit(solution)/shard_map/ppermute | solution.py:358
  16.7 1.3 %collective-permute-start.4 = (f32[4,4096]{1,0:T(4,128)S(1)}, f32[4,4096]{1,0:T(4,128)S(1)}, u32[]{:S(2)}, u32[]{:S(2)}) collective-permute-start(f32[4,4096]{1,0:T(4,128)S(1)} %backward.1.grad), channel_id=1, source_target_pairs={{0,1},{1,0},{2,3},{3,2},{4,5},{5,4},{6,7},{7,6},{8,9},{9,8},{10,11... | collective-permute-start | bytes 196616 | tf_op jit(solution)/shard_map/ppermute | solution.py:391
  18.0 3.2 %collective-permute-start.5 = (f32[1,4096]{1,0:T(1,128)S(1)}, f32[1,4096]{1,0:T(1,128)S(1)}, u32[]{:S(2)}, u32[]{:S(2)}) collective-permute-start(f32[1,4096]{1,0:T(1,128)S(1)} %fusion.1), channel_id=1, source_target_pairs={{0,3},{1,2},{2,1},{3,0},{4,7},{5,6},{6,5},{7,4},{8,11},{9,10},{10,... | collective-permute-start | bytes 49160 | tf_op jit(solution)/shard_map/ppermute | solution.py:394

commit v22 on v20

--- a/solution.py
+++ b/solution.py
@@ -131,7 +131,17 @@
         partial_out[16 * q:16 * q + 16, :] = jnp.concatenate(halves, axis=0).astype(jnp.bfloat16)
 
 
-def edges_kernel(vol, split, dual, edge_out, halo_out):
+def edges_kernel(
+    vol_hbm, split_hbm, dual_hbm, edge_out, halo_out, vol, split, dual, sems
+):
+    loads = [
+        pltpu.make_async_copy(source, target, sems.at[i])
+        for i, (source, target) in enumerate([(vol_hbm, vol), (split_hbm, split), (dual_hbm, dual)])
+    ]
+    for load in loads:
+        load.start()
+    for load in loads:
+        load.wait()
     start = lax.axis_index("slab") == 0
     for j in range(vol.shape[1] // 128):
         at = slice(128 * j, 128 * j + 128)
@@ -338,14 +348,21 @@
     )(tile_count, *sources)
 
     row = jax.ShapeDtypeStruct((1, width), f32)
-    edge, halo = pl.pallas_call(
+    whole = jax.ShapeDtypeStruct((slices, width), f32)
+    triple = jax.ShapeDtypeStruct((3, slices, width), f32)
+    wide = [pltpu.with_memory_space_constraint(x, pltpu.HBM) for x in (split_var, dual_var)]
+    edge, halo, vol_near, split_near, dual_near = pl.pallas_call(
         edges_kernel,
-        out_shape=(row, jax.ShapeDtypeStruct((4, width), f32)),
-        in_specs=[vmem()] * 3,
-        out_specs=(vmem(),) * 2,
+        out_shape=(row, whole, whole, triple, triple),
+        in_specs=[hbm()] * 3,
+        out_specs=(vmem(),) * 5,
+        scratch_shapes=[pltpu.SemaphoreType.DMA((3,))],
         compiler_params=params(),
         name="edges",
-    )(volume, split_var, dual_var)
+    )(sources[2], *wide)
+    swap = [(i, i ^ 1) for i in range(reps)]
+    moved = lax.ppermute(partial, "rep", swap)
+    moved, halo = lax.optimization_barrier((moved, halo))
     across = [(i, i ^ 3) for i in range(2 * reps)]
     down = [(i, i - 1) for i in range(1, slabs)]
     if slabs == 2:
@@ -353,8 +370,6 @@
     else:
         from_next = lax.ppermute(volume[0:1], "slab", down)
         from_previous = lax.ppermute(edge, "slab", [(i - 1, i) for i in range(1, slabs)])
-    swap = [(i, i ^ 1) for i in range(reps)]
-    moved = lax.ppermute(partial, "rep", swap)
     step = reps
     while step < group:
         partial = (partial.astype(f32) + moved.astype(f32)).astype(bf16)
@@ -374,7 +389,7 @@
         out_specs=vmem(),
         compiler_params=params(),
         name="local",
-    )(rho, volume, split_var, dual_var, edge, from_next, from_previous)
+    )(rho, vol_near, split_near, dual_near, edge, from_next, from_previous)
 
     grad = pl.pallas_call(
         backward_kernel,
@@ -397,8 +412,6 @@
     else:
         ahead = lax.ppermute(ahead, "slab", down)
 
-    whole = jax.ShapeDtypeStruct((slices, width), f32)
-    triple = jax.ShapeDtypeStruct((3, slices, width), f32)
     field, new_volume, new_split, new_dual = pl.pallas_call(
         plane_kernel,
         out_shape=(whole, whole, triple, triple),
@@ -408,7 +421,7 @@
         + [pltpu.SemaphoreType.DMA((3,))],
         compiler_params=params(),
         name="plane",
-    )(grad, grad_other, base, dual_var, limits)
+    )(grad, grad_other, base, dual_near, limits)
     new_split, new_dual = pl.pallas_call(
         depth_kernel,
         out_shape=(triple, triple),
@@ -419,7 +432,7 @@
         input_output_aliases={4: 0, 5: 1},
         compiler_params=params(),
         name="depth",
-    )(field, ahead, dual_var, limits, new_split, new_dual)
+    )(field, ahead, dual_near, limits, new_split, new_dual)
     return new_volume, new_split, new_dual
 
 

time: 21.8 us -> 22 us (level)
  Pallas kernels: 6.57 us -> 7.69 us
  starting transfers between devices: 9.67 us -> 8.79 us
    pallas_call x1, Pallas kernels: 0.04 us -> 1.13 us  [shards(): pl.pallas_call(edges_kernel, out_shape=(row, whole, whole, triple, triple...]
    ppermute x1, waiting for transfers between devices: 0.86 us -> 0.01 us  [shards(): moved = lax.ppermute(partial, 'rep', swap)]
    ppermute x2, waiting for transfers between devices: 0.93 us -> 1.53 us  [shards(): lax.ppermute(partial, ('tile', 'rep'), [(i, i ^ step + 1) for i in range(...]
    ppermute x1, starting transfers between devices: 1.51 us -> 1.15 us  [shards(): from_next = from_previous = lax.ppermute(halo, ('slab', 'rep'), across)]
    ppermute x1, starting transfers between devices: 0.44 us -> 0.15 us  [shards(): grad_other = lax.ppermute(grad, 'rep', swap)]
    ppermute x1, waiting for transfers between devices: 0.63 us -> 0.89 us  [shards(): grad_other = lax.ppermute(grad, 'rep', swap)]
  transfers between devices with their start and end apart: 6 -> 6, of which waited for: 4 -> 4; matrix products, arithmetic and copies ran while one was open for 0% -> 0% of each run, Pallas kernels for 6% -> 10%
where the time goes in v22:
time: 22 us; the launch traced here: 21.8 us
  starting transfers between devices  8.79 us (40%)
  Pallas kernels  7.69 us (35%)
  waiting for transfers between devices  3.26 us (15%)
  between operations  2.04 us (9%)
    ppermute x2, starting transfers between devices, shards(): lax.ppermute(partial, ('tile', 'rep'), [(i, i ^ step + 1) for i in range(...  5.48 us
    pallas_call x1, Pallas kernels, shards(): pl.pallas_call(forward_kernel, out_shape=(jax.ShapeDtypeStruct((rays * sl...  2.74 us
    pallas_call x1, Pallas kernels, shards(): pl.pallas_call(backward_kernel, out_shape=jax.ShapeDtypeStruct((slices, w...  1.94 us
    ppermute x2, waiting for transfers between devices, shards(): lax.ppermute(partial, ('tile', 'rep'), [(i, i ^ step + 1) for i in range(...  1.53 us
    ppermute x1, starting transfers between devices, shards(): ahead = lax.ppermute(ahead, ('slab', 'rep'), across)  1.51 us
    ppermute x1, starting transfers between devices, shards(): from_next = from_previous = lax.ppermute(halo, ('slab', 'rep'), across)  1.15 us
    pallas_call x1, Pallas kernels, shards(): pl.pallas_call(edges_kernel, out_shape=(row, whole, whole, triple, triple...  1.13 us
    ppermute x1, waiting for transfers between devices, shards(): grad_other = lax.ppermute(grad, 'rep', swap)  0.89 us
  transfers between devices with their start and end apart: 6, of which 4 were waited for; matrix products, arithmetic and copies ran while one was open for 0% of the time, Pallas kernels for 10%

profile of v22, /device:TPU:0, one launch (start us, length us, event | category | flops | bytes accessed | tf_op | source)
XLA Modules:
  0.0 21.8 jit_solution(10178110674986489029)
XLA Ops:
  1.3 2.7 %forward.1 = (bf16[128,128]{1,0:T(8,128)(2,1)S(1)}, s32[4,128]{1,0:T(4,128)S(1)}, bf16[256,64,128]{2,1,0:T(8,128)(2,1)S(1)}) custom-call(s32[1]{0:T(128)S(6)} %copy.16.count, s32[2,128]{1,0:T(2,128)} %bitcast.3, s32[2,128]{1,0:T(2,128)} %bitcast.4, f32[4,4096]{1,0:T(4,128)} %vol_hbm.3, f32[4,4,128]{2,1,0:T(4,128)} %sino_hbm.1, bf16[256,64,128]{2,1,0:T(8,128)(2,1)} %proj_hbm.1), custom_call_target="tpu_custom_call" | custom-call | tf_op jit(solution)/shard_map/forward/pallas_call | solution.py:327
  4.0 0.5 %collective-permute-start = (bf16[128,128]{1,0:T(8,128)(2,1)S(1)}, bf16[128,128]{1,0:T(8,128)(2,1)S(1)}, u32[]{:S(2)}, u32[]{:S(2)}) collective-permute-start(bf16[128,128]{1,0:T(8,128)(2,1)S(1)} %get-tuple-element.25), channel_id=1, source_target_pairs={{0,1},{1,0},{2,3},{3,2},{4,5},{5,4},{6,7},{7,6},{8,9},{9,8},{10,11... | collective-permute-start | bytes 98312 | tf_op jit(solution)/shard_map/ppermute | solution.py:364
  4.5 1.1 %edges.1 = (f32[1,4096]{1,0:T(1,128)S(1)}, f32[4,4096]{1,0:T(4,128)S(1)}, f32[4,4096]{1,0:T(4,128)S(1)}, f32[3,4,4096]{2,1,0:T(4,128)S(1)}, f32[3,4,4096]{2,1,0:T(4,128)S(1)}) custom-call(f32[4,4096]{1,0:T(4,128)} %vol_hbm.3, f32[3,4,4096]{2,1,0:T(4,128)} %split_hbm.1, f32[3,4,4096]{2,1,0:T(4,128)} %dual_hbm.1), custom_call_target="tpu_custom_call" | custom-call | tf_op jit(solution)/shard_map/edges/pallas_call | solution.py:354
  5.7 0.0 collective-permute-done
  5.7 2.8 %collective-permute-start.1 = (bf16[128,128]{1,0:T(8,128)(2,1)S(1)}, bf16[128,128]{1,0:T(8,128)(2,1)S(1)}, u32[]{:S(2)}, u32[]{:S(2)}) collective-permute-start(bf16[128,128]{1,0:T(8,128)(2,1)S(1)} %add_convert_fusion.1), channel_id=1, source_target_pairs={{0,5},{1,4},{4,1},{5,0},{8,13},{9,12},{12,9},{13,8},{2,7},{3,6},{6... | collective-permute-start | bytes 98312 | tf_op jit(solution)/shard_map/ppermute | solution.py:376
  8.4 1.2 %collective-permute-start.3 = (f32[4,4096]{1,0:T(4,128)S(1)}, f32[4,4096]{1,0:T(4,128)S(1)}, u32[]{:S(2)}, u32[]{:S(2)}) collective-permute-start(f32[4,4096]{1,0:T(4,128)S(1)} %get-tuple-element.28), channel_id=1, source_target_pairs={{0,3},{1,2},{2,1},{3,0},{4,7},{5,6},{6,5},{7,4},{8,11},{9,10},{10,... | collective-permute-start | bytes 196616 | tf_op jit(solution)/shard_map/ppermute | solution.py:369
  9.6 0.6 %collective-permute-done.1 = bf16[128,128]{1,0:T(8,128)(2,1)S(1)} collective-permute-done((bf16[128,128]{1,0:T(8,128)(2,1)S(1)}, bf16[128,128]{1,0:T(8,128)(2,1)S(1)}, u32[]{:S(2)}, u32[]{:S(2)}) %collective-permute-start.1) | collective-permute-done | bytes 32800 | tf_op jit(solution)/shard_map/ppermute | solution.py:376
  10.2 2.7 %collective-permute-start.2 = (bf16[128,128]{1,0:T(8,128)(2,1)S(1)}, bf16[128,128]{1,0:T(8,128)(2,1)S(1)}, u32[]{:S(2)}, u32[]{:S(2)}) collective-permute-start(bf16[128,128]{1,0:T(8,128)(2,1)S(1)} %add_convert_fusion.part), channel_id=1, source_target_pairs={{0,9},{1,8},{4,13},{5,12},{8,1},{9,0},{12,5},{13,4},{2,11},{3,10},... | collective-permute-start | bytes 98312 | tf_op jit(solution)/shard_map/ppermute | solution.py:376
  13.6 1.0 %collective-permute-done.2.moved = bf16[128,128]{1,0:T(8,128)(2,1)S(1)} collective-permute-done((bf16[128,128]{1,0:T(8,128)(2,1)S(1)}, bf16[128,128]{1,0:T(8,128)(2,1)S(1)}, u32[]{:S(2)}, u32[]{:S(2)}) %collective-permute-start.2) | collective-permute-done | bytes 32800 | tf_op jit(solution)/shard_map/ppermute | solution.py:376
  14.6 0.0 collective-permute-done.3.from_next.from_previous
  14.6 1.9 %backward.1.grad = f32[4,4096]{1,0:T(4,128)S(1)} custom-call(s32[1]{0:T(128)S(6)} %copy.16.count, s32[4,128]{1,0:T(4,128)S(1)} %get-tuple-element.23.indices, bf16[256,64,128]{2,1,0:T(8,128)(2,1)S(1)} %get-tuple-element.24.tiles, bf16[128,128]{1,0:T(8,128)(2,1)S(1)} %add_convert_fusion.part, bf16[128,128]{1,0:T(8,128)(2,1)S(1)} %collective-permute-done.2.moved), custom_call_target="tpu_custom_call" | custom-call | tf_op jit(solution)/shard_map/backward/pallas_call | solution.py:394
  16.5 0.2 collective-permute-start.4
  16.7 0.3 %local.1.base = f32[4,4096]{1,0:T(4,128)S(1)} custom-call(f32[1]{0:T(128)S(6)} %copy.17.rho, f32[4,4096]{1,0:T(4,128)S(1)} %get-tuple-element.30.vol, f32[3,4,4096]{2,1,0:T(4,128)S(1)} %get-tuple-element.31.split, f32[3,4,4096]{2,1,0:T(4,128)S(1)} %get-tuple-element.32.dual, f32[1,4096]{1,0:T(1,128)S(1)} %get-tuple-element.33.edge, ...), custom_call_target="tpu_custom_call" | custom-call | tf_op jit(solution)/shard_map/local/pallas_call | solution.py:385
  17.0 0.9 %collective-permute-done.4.grad_other = f32[4,4096]{1,0:T(4,128)S(1)} collective-permute-done((f32[4,4096]{1,0:T(4,128)S(1)}, f32[4,4096]{1,0:T(4,128)S(1)}, u32[]{:S(2)}, u32[]{:S(2)}) %collective-permute-start.4) | collective-permute-done | bytes 65568 | tf_op jit(solution)/shard_map/ppermute | solution.py:408
  17.9 1.5 %collective-permute-start.5 = (f32[1,4096]{1,0:T(1,128)S(1)}, f32[1,4096]{1,0:T(1,128)S(1)}, u32[]{:S(2)}, u32[]{:S(2)}) collective-permute-start(f32[1,4096]{1,0:T(1,128)S(1)} %fusion.1), channel_id=1, source_target_pairs={{0,3},{1,2},{2,1},{3,0},{4,7},{5,6},{6,5},{7,4},{8,11},{9,10},{10,... | collective-permute-start | bytes 49160 | tf_op jit(solution)/shard_map/ppermute | solution.py:411
  19.4 0.9 %plane.1 = (f32[4,4096]{1,0:T(4,128)S(1)}, f32[4,4096]{1,0:T(4,128)}, f32[3,4,4096]{2,1,0:T(4,128)}, f32[3,4,4096]{2,1,0:T(4,128)}) custom-call(f32[4,4096]{1,0:T(4,128)S(1)} %backward.1.grad, f32[4,4096]{1,0:T(4,128)S(1)} %collective-permute-done.4.grad_other, f32[4,4096]{1,0:T(4,128)S(1)} %local.1.base, f32[3,4,4096]{2,1,0:T(4,128)S(1)} %get-tuple-element.32.dual, ...), custom_call_target="tpu_custom_call" | custom-call | tf_op jit(solution)/shard_map/plane/pallas_call | solution.py:415
  20.3 0.8 %collective-permute-done.5.ahead = f32[1,4096]{1,0:T(1,128)S(1)} collective-permute-done((f32[1,4096]{1,0:T(1,128)S(1)}, f32[1,4096]{1,0:T(1,128)S(1)}, u32[]{:S(2)}, u32[]{:S(2)}) %collective-permute-start.5) | collective-permute-done | bytes 16416 | tf_op jit(solution)/shard_map/ppermute | solution.py:411
  21.1 0.7 %depth.1 = (f32[3,4,4096]{2,1,0:T(4,128)}, f32[3,4,4096]{2,1,0:T(4,128)}) custom-call(f32[4,4096]{1,0:T(4,128)S(1)} %get-tuple-element.38.field_in, f32[1,4096]{1,0:T(1,128)S(1)} %collective-permute-done.5.ahead, f32[3,4,4096]{2,1,0:T(4,128)S(1)} %get-tuple-element.32.dual, ...), custom_call_target="tpu_custom_call", output_to_operand_aliasing={{0}: (4, {}), {1}: (5, {})} | custom-call | tf_op jit(solution)/shard_map/depth/pallas_call | solution.py:425
  (4 shorter events, 0.1 us)
Async XLA Ops:
  4.0 1.6 %collective-permute-start = (bf16[128,128]{1,0:T(8,128)(2,1)S(1)}, bf16[128,128]{1,0:T(8,128)(2,1)S(1)}, u32[]{:S(2)}, u32[]{:S(2)}) collective-permute-start(bf16[128,128]{1,0:T(8,128)(2,1)S(1)} %get-tuple-element.25), channel_id=1, source_target_pairs={{0,1},{1,0},{2,3},{3,2},{4,5},{5,4},{6,7},{7,6},{8,9},{9,8},{10,11... | collective-permute-start | bytes 98312 | tf_op jit(solution)/shard_map/ppermute | solution.py:364
  5.7 4.5 %collective-permute-start.1 = (bf16[128,128]{1,0:T(8,128)(2,1)S(1)}, bf16[128,128]{1,0:T(8,128)(2,1)S(1)}, u32[]{:S(2)}, u32[]{:S(2)}) collective-permute-start(bf16[128,128]{1,0:T(8,128)(2,1)S(1)} %add_convert_fusion.1), channel_id=1, source_target_pairs={{0,5},{1,4},{4,1},{5,0},{8,13},{9,12},{12,9},{13,8},{2,7},{3,6},{6... | collective-permute-start | bytes 98312 | tf_op jit(solution)/shard_map/ppermute | solution.py:376
  8.4 6.1 %collective-permute-start.3 = (f32[4,4096]{1,0:T(4,128)S(1)}, f32[4,4096]{1,0:T(4,128)S(1)}, u32[]{:S(2)}, u32[]{:S(2)}) collective-permute-start(f32[4,4096]{1,0:T(4,128)S(1)} %get-tuple-element.28), channel_id=1, source_target_pairs={{0,3},{1,2},{2,1},{3,0},{4,7},{5,6},{6,5},{7,4},{8,11},{9,10},{10,... | collective-permute-start | bytes 196616 | tf_op jit(solution)/shard_map/ppermute | solution.py:369
  10.2 4.4 %collective-permute-start.2 = (bf16[128,128]{1,0:T(8,128)(2,1)S(1)}, bf16[128,128]{1,0:T(8,128)(2,1)S(1)}, u32[]{:S(2)}, u32[]{:S(2)}) collective-permute-start(bf16[128,128]{1,0:T(8,128)(2,1)S(1)} %add_convert_fusion.part), channel_id=1, source_target_pairs={{0,9},{1,8},{4,13},{5,12},{8,1},{9,0},{12,5},{13,4},{2,11},{3,10},... | collective-permute-start | bytes 98312 | tf_op jit(solution)/shard_map/ppermute | solution.py:376
  16.5 1.3 %collective-permute-start.4 = (f32[4,4096]{1,0:T(4,128)S(1)}, f32[4,4096]{1,0:T(4,128)S(1)}, u32[]{:S(2)}, u32[]{:S(2)}) collective-permute-start(f32[4,4096]{1,0:T(4,128)S(1)} %backward.1.grad), channel_id=1, source_target_pairs={{0,1},{1,0},{2,3},{3,2},{4,5},{5,4},{6,7},{7,6},{8,9},{9,8},{10,11... | collective-permute-start | bytes 196616 | tf_op jit(solution)/shard_map/ppermute | solution.py:408
  17.9 3.2 %collective-permute-start.5 = (f32[1,4096]{1,0:T(1,128)S(1)}, f32[1,4096]{1,0:T(1,128)S(1)}, u32[]{:S(2)}, u32[]{:S(2)}) collective-permute-start(f32[1,4096]{1,0:T(1,128)S(1)} %fusion.1), channel_id=1, source_target_pairs={{0,3},{1,2},{2,1},{3,0},{4,7},{5,6},{6,5},{7,4},{8,11},{9,10},{10,... | collective-permute-start | bytes 49160 | tf_op jit(solution)/shard_map/ppermute | solution.py:411

commit v23 on v20

--- a/solution.py
+++ b/solution.py
@@ -19,14 +19,14 @@
     return row, lane
 
 
-def start_tiles(proj_hbm, tiles, sems):
+def tile_copies(proj_hbm, tiles, sems):
     eighth = proj_hbm.shape[0] // CUTS[-1]
     copies = {}
     for c, (low, high) in enumerate(zip(CUTS, CUTS[1:])):
         part = pl.ds(low * eighth, (high - low) * eighth)
-        copy = pltpu.make_async_copy(proj_hbm.at[part], tiles.at[part], sems.at[c])
-        copy.start()
-        copies[low * eighth] = copy
+        copies[low * eighth] = pltpu.make_async_copy(
+            proj_hbm.at[part], tiles.at[part], sems.at[c]
+        )
     return copies
 
 
@@ -62,9 +62,14 @@
     loads = [
         pltpu.make_async_copy(source, target, sems.at[i]) for i, (source, target) in enumerate(pairs)
     ]
-    for load in loads[:3]:
-        load.start()
-    copies = start_tiles(proj_hbm, tiles, tile_sems)
+    copies = tile_copies(proj_hbm, tiles, tile_sems)
+    loads[2].start()
+    loads[0].start()
+    copies[0].start()
+    loads[1].start()
+    for n in copies:
+        if n > 0:
+            copies[n].start()
     for load in loads[3:]:
         load.start()
     accs = (acc0, acc1, acc2, acc3)
@@ -87,10 +92,6 @@
         table[16 * j:16 * j + 8, :] = jnp.where(other, turned, first)
         table[16 * j + 8:16 * j + 16, :] = jnp.where(other, x, second)
 
-    loads[3].wait()
-    mine = (lax.axis_index("tile") * lax.axis_size("rep") + lax.axis_index("rep")) * owned
-    for r in range(owned):
-        acc0[pl.ds(pl.multiple_of((mine + r) * 8, 8), 4), :] = -sino[r]
     loads[0].wait()
     loads[1].wait()
     used = count[0]
@@ -116,6 +117,11 @@
             ],
             [sums[0:8], sums[0:8], sums[8:16], sums[8:16]],
         )
+    loads[3].wait()
+    mine = (lax.axis_index("tile") * lax.axis_size("rep") + lax.axis_index("rep")) * owned
+    for r in range(owned):
+        at = pl.ds(pl.multiple_of((mine + r) * 8, 8), 4)
+        acc0[at, :] = acc0[at, :] - sino[r]
     loads[4].wait()
     loads[5].wait()
     for q in range(rays // 4):

time: 21.8 us -> 21.8 us (level)
  no operation moved by 1% of the time
where the time goes in v23:
time: 21.8 us; the launch traced here: 21.6 us
  starting transfers between devices  9.64 us (44%)
  Pallas kernels  6.62 us (30%)
  waiting for transfers between devices  3.15 us (14%)
  between operations  2.11 us (10%)
    ppermute x2, starting transfers between devices, shards(): lax.ppermute(partial, ('tile', 'rep'), [(i, i ^ step + 1) for i in range(...  5.58 us
    pallas_call x1, Pallas kernels, shards(): pl.pallas_call(forward_kernel, out_shape=(jax.ShapeDtypeStruct((rays * sl...  2.74 us
    pallas_call x1, Pallas kernels, shards(): pl.pallas_call(backward_kernel, out_shape=jax.ShapeDtypeStruct((slices, w...  1.95 us
    ppermute x1, starting transfers between devices, shards(): ahead = lax.ppermute(ahead, ('slab', 'rep'), across)  1.62 us
    ppermute x1, starting transfers between devices, shards(): from_next = from_previous = lax.ppermute(halo, ('slab', 'rep'), across)  1.51 us
    ppermute x2, waiting for transfers between devices, shards(): lax.ppermute(partial, ('tile', 'rep'), [(i, i ^ step + 1) for i in range(...  0.93 us
    pallas_call x1, Pallas kernels, shards(): pl.pallas_call(plane_kernel, out_shape=(whole, whole, triple, triple), in...  0.89 us
    ppermute x1, waiting for transfers between devices, shards(): moved = lax.ppermute(partial, 'rep', swap)  0.86 us
  transfers between devices with their start and end apart: 6, of which 4 were waited for; matrix products, arithmetic and copies ran while one was open for 0% of the time, Pallas kernels for 6%

profile of v23, /device:TPU:0, one launch (start us, length us, event | category | flops | bytes accessed | tf_op | source)
XLA Modules:
  0.0 21.6 jit_solution(13611151703562218013)
XLA Ops:
  0.6 0.0 copy-start.2
  0.6 0.0 copy-start
  0.7 0.0 copy-start.1
  1.4 2.7 %forward.1 = (bf16[128,128]{1,0:T(8,128)(2,1)S(1)}, s32[4,128]{1,0:T(4,128)S(1)}, bf16[256,64,128]{2,1,0:T(8,128)(2,1)S(1)}) custom-call(s32[1]{0:T(128)S(6)} %copy.16.count, s32[2,128]{1,0:T(2,128)} %bitcast.3, s32[2,128]{1,0:T(2,128)} %bitcast.4, f32[4,4096]{1,0:T(4,128)} %vol.3, f32[4,4,128]{2,1,0:T(4,128)} %sino_hbm.1, bf16[256,64,128]{2,1,0:T(8,128)(2,1)} %proj_hbm.1), custom_call_target="tpu_custom_call" | custom-call | tf_op jit(solution)/shard_map/forward/pallas_call | solution.py:323
  4.1 0.5 %collective-permute-start = (bf16[128,128]{1,0:T(8,128)(2,1)S(1)}, bf16[128,128]{1,0:T(8,128)(2,1)S(1)}, u32[]{:S(2)}, u32[]{:S(2)}) collective-permute-start(bf16[128,128]{1,0:T(8,128)(2,1)S(1)} %get-tuple-element.20), channel_id=1, source_target_pairs={{0,1},{1,0},{2,3},{3,2},{4,5},{5,4},{6,7},{7,6},{8,9},{9,8},{10,11... | collective-permute-start | bytes 98312 | tf_op jit(solution)/shard_map/ppermute | solution.py:363
  4.6 0.9 %collective-permute-done = bf16[128,128]{1,0:T(8,128)(2,1)S(1)} collective-permute-done((bf16[128,128]{1,0:T(8,128)(2,1)S(1)}, bf16[128,128]{1,0:T(8,128)(2,1)S(1)}, u32[]{:S(2)}, u32[]{:S(2)}) %collective-permute-start) | collective-permute-done | bytes 32800 | tf_op jit(solution)/shard_map/ppermute | solution.py:363
  5.5 2.8 %collective-permute-start.1 = (bf16[128,128]{1,0:T(8,128)(2,1)S(1)}, bf16[128,128]{1,0:T(8,128)(2,1)S(1)}, u32[]{:S(2)}, u32[]{:S(2)}) collective-permute-start(bf16[128,128]{1,0:T(8,128)(2,1)S(1)} %add_convert_fusion.1), channel_id=1, source_target_pairs={{0,5},{1,4},{4,1},{5,0},{8,13},{9,12},{12,9},{13,8},{2,7},{3,6},{6... | collective-permute-start | bytes 98312 | tf_op jit(solution)/shard_map/ppermute | solution.py:367
  8.3 0.0 copy-done.2
  8.3 0.0 copy-done
  8.3 0.0 copy-done.1
  8.3 1.5 %collective-permute-start.3 = (f32[4,4096]{1,0:T(4,128)S(1)}, f32[4,4096]{1,0:T(4,128)S(1)}, u32[]{:S(2)}, u32[]{:S(2)}) collective-permute-start(f32[4,4096]{1,0:T(4,128)S(1)} %get-tuple-element.21), channel_id=1, source_target_pairs={{0,3},{1,2},{2,1},{3,0},{4,7},{5,6},{6,5},{7,4},{8,11},{9,10},{10,... | collective-permute-start | bytes 196616 | tf_op jit(solution)/shard_map/ppermute | solution.py:358
  9.8 0.0 collective-permute-done.1
  9.9 2.8 %collective-permute-start.2 = (bf16[128,128]{1,0:T(8,128)(2,1)S(1)}, bf16[128,128]{1,0:T(8,128)(2,1)S(1)}, u32[]{:S(2)}, u32[]{:S(2)}) collective-permute-start(bf16[128,128]{1,0:T(8,128)(2,1)S(1)} %add_convert_fusion.part), channel_id=1, source_target_pairs={{0,9},{1,8},{4,13},{5,12},{8,1},{9,0},{12,5},{13,4},{2,11},{3,10},... | collective-permute-start | bytes 98312 | tf_op jit(solution)/shard_map/ppermute | solution.py:367
  13.4 0.0 collective-permute-done.3.from_next.from_previous
  13.4 0.9 %collective-permute-done.2.moved = bf16[128,128]{1,0:T(8,128)(2,1)S(1)} collective-permute-done((bf16[128,128]{1,0:T(8,128)(2,1)S(1)}, bf16[128,128]{1,0:T(8,128)(2,1)S(1)}, u32[]{:S(2)}, u32[]{:S(2)}) %collective-permute-start.2) | collective-permute-done | bytes 32800 | tf_op jit(solution)/shard_map/ppermute | solution.py:367
  14.3 1.9 %backward.1.grad = f32[4,4096]{1,0:T(4,128)S(1)} custom-call(s32[1]{0:T(128)S(6)} %copy.16.count, s32[4,128]{1,0:T(4,128)S(1)} %get-tuple-element.18.indices, bf16[256,64,128]{2,1,0:T(8,128)(2,1)S(1)} %get-tuple-element.19.tiles, bf16[128,128]{1,0:T(8,128)(2,1)S(1)} %add_convert_fusion.part, bf16[128,128]{1,0:T(8,128)(2,1)S(1)} %collective-permute-done.2.moved), custom_call_target="tpu_custom_call" | custom-call | tf_op jit(solution)/shard_map/backward/pallas_call | solution.py:385
  16.3 0.4 %collective-permute-start.4 = (f32[4,4096]{1,0:T(4,128)S(1)}, f32[4,4096]{1,0:T(4,128)S(1)}, u32[]{:S(2)}, u32[]{:S(2)}) collective-permute-start(f32[4,4096]{1,0:T(4,128)S(1)} %backward.1.grad), channel_id=1, source_target_pairs={{0,1},{1,0},{2,3},{3,2},{4,5},{5,4},{6,7},{7,6},{8,9},{9,8},{10,11... | collective-permute-start | bytes 196616 | tf_op jit(solution)/shard_map/ppermute | solution.py:399
  16.7 0.3 %local.1.base = f32[4,4096]{1,0:T(4,128)S(1)} custom-call(f32[1]{0:T(128)S(6)} %copy.17.rho, f32[4,4096]{1,0:T(4,128)S(1)} %copy-done.2, f32[3,4,4096]{2,1,0:T(4,128)S(1)} %copy-done.1, f32[3,4,4096]{2,1,0:T(4,128)S(1)} %copy-done, f32[1,4096]{1,0:T(1,128)S(1)} %get-tuple-element.23.edge, f32[4,4096]{1,0:T(4,128)S(1)} %collective-permute-done.3.from_next.from_previous, ...), custom_call_target="tpu_custom_call" | custom-call | tf_op jit(solution)/shard_map/local/pallas_call | solution.py:376
  17.0 0.6 %collective-permute-done.4.grad_other = f32[4,4096]{1,0:T(4,128)S(1)} collective-permute-done((f32[4,4096]{1,0:T(4,128)S(1)}, f32[4,4096]{1,0:T(4,128)S(1)}, u32[]{:S(2)}, u32[]{:S(2)}) %collective-permute-start.4) | collective-permute-done | bytes 65568 | tf_op jit(solution)/shard_map/ppermute | solution.py:399
  17.6 1.6 %collective-permute-start.5 = (f32[1,4096]{1,0:T(1,128)S(1)}, f32[1,4096]{1,0:T(1,128)S(1)}, u32[]{:S(2)}, u32[]{:S(2)}) collective-permute-start(f32[1,4096]{1,0:T(1,128)S(1)} %fusion.1), channel_id=1, source_target_pairs={{0,3},{1,2},{2,1},{3,0},{4,7},{5,6},{6,5},{7,4},{8,11},{9,10},{10,... | collective-permute-start | bytes 49160 | tf_op jit(solution)/shard_map/ppermute | solution.py:402
  19.2 0.9 %plane.1 = (f32[4,4096]{1,0:T(4,128)S(1)}, f32[4,4096]{1,0:T(4,128)}, f32[3,4,4096]{2,1,0:T(4,128)}, f32[3,4,4096]{2,1,0:T(4,128)}) custom-call(f32[4,4096]{1,0:T(4,128)S(1)} %backward.1.grad, f32[4,4096]{1,0:T(4,128)S(1)} %collective-permute-done.4.grad_other, f32[4,4096]{1,0:T(4,128)S(1)} %local.1.base, f32[3,4,4096]{2,1,0:T(4,128)S(1)} %copy-done, ...), custom_call_target="tpu_custom_call" | custom-call | tf_op jit(solution)/shard_map/plane/pallas_call | solution.py:408
  20.1 0.7 %collective-permute-done.5.ahead = f32[1,4096]{1,0:T(1,128)S(1)} collective-permute-done((f32[1,4096]{1,0:T(1,128)S(1)}, f32[1,4096]{1,0:T(1,128)S(1)}, u32[]{:S(2)}, u32[]{:S(2)}) %collective-permute-start.5) | collective-permute-done | bytes 16416 | tf_op jit(solution)/shard_map/ppermute | solution.py:402
  20.9 0.7 %depth.1 = (f32[3,4,4096]{2,1,0:T(4,128)}, f32[3,4,4096]{2,1,0:T(4,128)}) custom-call(f32[4,4096]{1,0:T(4,128)S(1)} %get-tuple-element.28.field_in, f32[1,4096]{1,0:T(1,128)S(1)} %collective-permute-done.5.ahead, f32[3,4,4096]{2,1,0:T(4,128)S(1)} %copy-done, f32[1,4096]{1,0:T(1,128)S(1)} %broadcast_in_dim.9.limits, ...), custom_call_target="tpu_custom_call", output_to_operand_aliasing={{0}: (4, {}), {1}: (5, {})} | custom-call | tf_op jit(solution)/shard_map/depth/pallas_call | solution.py:418
  (5 shorter events, 0.1 us)
Async XLA Ops:
  0.6 7.6 %copy-start.2 = (f32[4,4096]{1,0:T(4,128)S(1)}, f32[4,4096]{1,0:T(4,128)}, u32[]{:S(2)}) copy-start(f32[4,4096]{1,0:T(4,128)} %vol.3) | copy-start | bytes 196612
  0.6 7.6 %copy-start = (f32[3,4,4096]{2,1,0:T(4,128)S(1)}, f32[3,4,4096]{2,1,0:T(4,128)}, u32[]{:S(2)}) copy-start(f32[3,4,4096]{2,1,0:T(4,128)} %dual.7) | copy-start | bytes 589828
  0.7 7.6 %copy-start.1 = (f32[3,4,4096]{2,1,0:T(4,128)S(1)}, f32[3,4,4096]{2,1,0:T(4,128)}, u32[]{:S(2)}) copy-start(f32[3,4,4096]{2,1,0:T(4,128)} %split.3) | copy-start | bytes 589828
  4.1 1.4 %collective-permute-start = (bf16[128,128]{1,0:T(8,128)(2,1)S(1)}, bf16[128,128]{1,0:T(8,128)(2,1)S(1)}, u32[]{:S(2)}, u32[]{:S(2)}) collective-permute-start(bf16[128,128]{1,0:T(8,128)(2,1)S(1)} %get-tuple-element.20), channel_id=1, source_target_pairs={{0,1},{1,0},{2,3},{3,2},{4,5},{5,4},{6,7},{7,6},{8,9},{9,8},{10,11... | collective-permute-start | bytes 98312 | tf_op jit(solution)/shard_map/ppermute | solution.py:363
  5.5 4.4 %collective-permute-start.1 = (bf16[128,128]{1,0:T(8,128)(2,1)S(1)}, bf16[128,128]{1,0:T(8,128)(2,1)S(1)}, u32[]{:S(2)}, u32[]{:S(2)}) collective-permute-start(bf16[128,128]{1,0:T(8,128)(2,1)S(1)} %add_convert_fusion.1), channel_id=1, source_target_pairs={{0,5},{1,4},{4,1},{5,0},{8,13},{9,12},{12,9},{13,8},{2,7},{3,6},{6... | collective-permute-start | bytes 98312 | tf_op jit(solution)/shard_map/ppermute | solution.py:367
  8.3 5.1 %collective-permute-start.3 = (f32[4,4096]{1,0:T(4,128)S(1)}, f32[4,4096]{1,0:T(4,128)S(1)}, u32[]{:S(2)}, u32[]{:S(2)}) collective-permute-start(f32[4,4096]{1,0:T(4,128)S(1)} %get-tuple-element.21), channel_id=1, source_target_pairs={{0,3},{1,2},{2,1},{3,0},{4,7},{5,6},{6,5},{7,4},{8,11},{9,10},{10,... | collective-permute-start | bytes 196616 | tf_op jit(solution)/shard_map/ppermute | solution.py:358
  9.9 4.4 %collective-permute-start.2 = (bf16[128,128]{1,0:T(8,128)(2,1)S(1)}, bf16[128,128]{1,0:T(8,128)(2,1)S(1)}, u32[]{:S(2)}, u32[]{:S(2)}) collective-permute-start(bf16[128,128]{1,0:T(8,128)(2,1)S(1)} %add_convert_fusion.part), channel_id=1, source_target_pairs={{0,9},{1,8},{4,13},{5,12},{8,1},{9,0},{12,5},{13,4},{2,11},{3,10},... | collective-permute-start | bytes 98312 | tf_op jit(solution)/shard_map/ppermute | solution.py:367
  16.3 1.3 %collective-permute-start.4 = (f32[4,4096]{1,0:T(4,128)S(1)}, f32[4,4096]{1,0:T(4,128)S(1)}, u32[]{:S(2)}, u32[]{:S(2)}) collective-permute-start(f32[4,4096]{1,0:T(4,128)S(1)} %backward.1.grad), channel_id=1, source_target_pairs={{0,1},{1,0},{2,3},{3,2},{4,5},{5,4},{6,7},{7,6},{8,9},{9,8},{10,11... | collective-permute-start | bytes 196616 | tf_op jit(solution)/shard_map/ppermute | solution.py:399
  17.6 3.2 %collective-permute-start.5 = (f32[1,4096]{1,0:T(1,128)S(1)}, f32[1,4096]{1,0:T(1,128)S(1)}, u32[]{:S(2)}, u32[]{:S(2)}) collective-permute-start(f32[1,4096]{1,0:T(1,128)S(1)} %fusion.1), channel_id=1, source_target_pairs={{0,3},{1,2},{2,1},{3,0},{4,7},{5,6},{6,5},{7,4},{8,11},{9,10},{10,... | collective-permute-start | bytes 49160 | tf_op jit(solution)/shard_map/ppermute | solution.py:402

commit v24 on v23

--- a/solution.py
+++ b/solution.py
@@ -361,13 +361,13 @@
         from_previous = lax.ppermute(edge, "slab", [(i - 1, i) for i in range(1, slabs)])
     swap = [(i, i ^ 1) for i in range(reps)]
     moved = lax.ppermute(partial, "rep", swap)
-    step = reps
-    while step < group:
+    step = group // 2
+    while step >= reps:
         partial = (partial.astype(f32) + moved.astype(f32)).astype(bf16)
         moved = lax.ppermute(
             partial, ("tile", "rep"), [(i, i ^ (step + 1)) for i in range(group)]
         )
-        step *= 2
+        step //= 2
     limits = jnp.broadcast_to((1.0 / rho)[:, None], (1, width))
     moved, from_next, from_previous, limits = lax.optimization_barrier(
         (moved, from_next, from_previous, limits)

time: 21.8 us -> 21.8 us (level)
  no operation moved by 1% of the time
where the time goes in v24:
time: 21.8 us; the launch traced here: 21.6 us
  starting transfers between devices  9.55 us (44%)
  Pallas kernels  6.56 us (30%)
  waiting for transfers between devices  3.32 us (15%)
  between operations  2.1 us (10%)
    ppermute x2, starting transfers between devices, shards(): lax.ppermute(partial, ('tile', 'rep'), [(i, i ^ step + 1) for i in range(...  5.46 us
    pallas_call x1, Pallas kernels, shards(): pl.pallas_call(forward_kernel, out_shape=(jax.ShapeDtypeStruct((rays * sl...  2.73 us
    pallas_call x1, Pallas kernels, shards(): pl.pallas_call(backward_kernel, out_shape=jax.ShapeDtypeStruct((slices, w...  1.91 us
    ppermute x1, starting transfers between devices, shards(): ahead = lax.ppermute(ahead, ('slab', 'rep'), across)  1.55 us
    ppermute x1, starting transfers between devices, shards(): from_next = from_previous = lax.ppermute(halo, ('slab', 'rep'), across)  1.51 us
    ppermute x2, waiting for transfers between devices, shards(): lax.ppermute(partial, ('tile', 'rep'), [(i, i ^ step + 1) for i in range(...  1.01 us
    pallas_call x1, Pallas kernels, shards(): pl.pallas_call(plane_kernel, out_shape=(whole, whole, triple, triple), in...  0.89 us
    ppermute x1, waiting for transfers between devices, shards(): moved = lax.ppermute(partial, 'rep', swap)  0.86 us
  transfers between devices with their start and end apart: 6, of which 4 were waited for; matrix products, arithmetic and copies ran while one was open for 0% of the time, Pallas kernels for 6%

profile of v24, /device:TPU:0, one launch (start us, length us, event | category | flops | bytes accessed | tf_op | source)
XLA Modules:
  0.0 21.6 jit_solution(15790514233972199488)
XLA Ops:
  0.6 0.0 copy-start.2
  0.6 0.0 copy-start
  0.7 0.0 copy-start.1
  1.4 2.7 %forward.1 = (bf16[128,128]{1,0:T(8,128)(2,1)S(1)}, s32[4,128]{1,0:T(4,128)S(1)}, bf16[256,64,128]{2,1,0:T(8,128)(2,1)S(1)}) custom-call(s32[1]{0:T(128)S(6)} %copy.16.count, s32[2,128]{1,0:T(2,128)} %bitcast.3, s32[2,128]{1,0:T(2,128)} %bitcast.4, f32[4,4096]{1,0:T(4,128)} %vol.3, f32[4,4,128]{2,1,0:T(4,128)} %sino_hbm.1, bf16[256,64,128]{2,1,0:T(8,128)(2,1)} %proj_hbm.1), custom_call_target="tpu_custom_call" | custom-call | tf_op jit(solution)/shard_map/forward/pallas_call | solution.py:323
  4.1 0.5 %collective-permute-start = (bf16[128,128]{1,0:T(8,128)(2,1)S(1)}, bf16[128,128]{1,0:T(8,128)(2,1)S(1)}, u32[]{:S(2)}, u32[]{:S(2)}) collective-permute-start(bf16[128,128]{1,0:T(8,128)(2,1)S(1)} %get-tuple-element.20), channel_id=1, source_target_pairs={{0,1},{1,0},{2,3},{3,2},{4,5},{5,4},{6,7},{7,6},{8,9},{9,8},{10,11... | collective-permute-start | bytes 98312 | tf_op jit(solution)/shard_map/ppermute | solution.py:363
  4.6 0.9 %collective-permute-done = bf16[128,128]{1,0:T(8,128)(2,1)S(1)} collective-permute-done((bf16[128,128]{1,0:T(8,128)(2,1)S(1)}, bf16[128,128]{1,0:T(8,128)(2,1)S(1)}, u32[]{:S(2)}, u32[]{:S(2)}) %collective-permute-start) | collective-permute-done | bytes 32800 | tf_op jit(solution)/shard_map/ppermute | solution.py:363
  5.5 3.8 %collective-permute-start.1 = (bf16[128,128]{1,0:T(8,128)(2,1)S(1)}, bf16[128,128]{1,0:T(8,128)(2,1)S(1)}, u32[]{:S(2)}, u32[]{:S(2)}) collective-permute-start(bf16[128,128]{1,0:T(8,128)(2,1)S(1)} %add_convert_fusion.1), channel_id=1, source_target_pairs={{0,9},{1,8},{4,13},{5,12},{8,1},{9,0},{12,5},{13,4},{2,11},{3,10},... | collective-permute-start | bytes 98312 | tf_op jit(solution)/shard_map/ppermute | solution.py:367
  9.3 0.0 copy-done.2
  9.3 0.0 copy-done
  9.3 0.0 copy-done.1
  9.3 1.5 %collective-permute-start.3 = (f32[4,4096]{1,0:T(4,128)S(1)}, f32[4,4096]{1,0:T(4,128)S(1)}, u32[]{:S(2)}, u32[]{:S(2)}) collective-permute-start(f32[4,4096]{1,0:T(4,128)S(1)} %get-tuple-element.21), channel_id=1, source_target_pairs={{0,3},{1,2},{2,1},{3,0},{4,7},{5,6},{6,5},{7,4},{8,11},{9,10},{10,... | collective-permute-start | bytes 196616 | tf_op jit(solution)/shard_map/ppermute | solution.py:358
  10.8 0.0 collective-permute-done.1
  10.9 1.7 %collective-permute-start.2 = (bf16[128,128]{1,0:T(8,128)(2,1)S(1)}, bf16[128,128]{1,0:T(8,128)(2,1)S(1)}, u32[]{:S(2)}, u32[]{:S(2)}) collective-permute-start(bf16[128,128]{1,0:T(8,128)(2,1)S(1)} %add_convert_fusion.part), channel_id=1, source_target_pairs={{0,5},{1,4},{4,1},{5,0},{8,13},{9,12},{12,9},{13,8},{2,7},{3,6},{6... | collective-permute-start | bytes 98312 | tf_op jit(solution)/shard_map/ppermute | solution.py:367
  13.3 0.0 collective-permute-done.3.from_next.from_previous
  13.3 1.0 %collective-permute-done.2.moved = bf16[128,128]{1,0:T(8,128)(2,1)S(1)} collective-permute-done((bf16[128,128]{1,0:T(8,128)(2,1)S(1)}, bf16[128,128]{1,0:T(8,128)(2,1)S(1)}, u32[]{:S(2)}, u32[]{:S(2)}) %collective-permute-start.2) | collective-permute-done | bytes 32800 | tf_op jit(solution)/shard_map/ppermute | solution.py:367
  14.3 1.9 %backward.1.grad = f32[4,4096]{1,0:T(4,128)S(1)} custom-call(s32[1]{0:T(128)S(6)} %copy.16.count, s32[4,128]{1,0:T(4,128)S(1)} %get-tuple-element.18.indices, bf16[256,64,128]{2,1,0:T(8,128)(2,1)S(1)} %get-tuple-element.19.tiles, bf16[128,128]{1,0:T(8,128)(2,1)S(1)} %add_convert_fusion.part, bf16[128,128]{1,0:T(8,128)(2,1)S(1)} %collective-permute-done.2.moved), custom_call_target="tpu_custom_call" | custom-call | tf_op jit(solution)/shard_map/backward/pallas_call | solution.py:385
  16.2 0.5 %collective-permute-start.4 = (f32[4,4096]{1,0:T(4,128)S(1)}, f32[4,4096]{1,0:T(4,128)S(1)}, u32[]{:S(2)}, u32[]{:S(2)}) collective-permute-start(f32[4,4096]{1,0:T(4,128)S(1)} %backward.1.grad), channel_id=1, source_target_pairs={{0,1},{1,0},{2,3},{3,2},{4,5},{5,4},{6,7},{7,6},{8,9},{9,8},{10,11... | collective-permute-start | bytes 196616 | tf_op jit(solution)/shard_map/ppermute | solution.py:399
  16.7 0.3 %local.1.base = f32[4,4096]{1,0:T(4,128)S(1)} custom-call(f32[1]{0:T(128)S(6)} %copy.17.rho, f32[4,4096]{1,0:T(4,128)S(1)} %copy-done.2, f32[3,4,4096]{2,1,0:T(4,128)S(1)} %copy-done.1, f32[3,4,4096]{2,1,0:T(4,128)S(1)} %copy-done, f32[1,4096]{1,0:T(1,128)S(1)} %get-tuple-element.23.edge, f32[4,4096]{1,0:T(4,128)S(1)} %collective-permute-done.3.from_next.from_previous, ...), custom_call_target="tpu_custom_call" | custom-call | tf_op jit(solution)/shard_map/local/pallas_call | solution.py:376
  17.0 0.6 %collective-permute-done.4.grad_other = f32[4,4096]{1,0:T(4,128)S(1)} collective-permute-done((f32[4,4096]{1,0:T(4,128)S(1)}, f32[4,4096]{1,0:T(4,128)S(1)}, u32[]{:S(2)}, u32[]{:S(2)}) %collective-permute-start.4) | collective-permute-done | bytes 65568 | tf_op jit(solution)/shard_map/ppermute | solution.py:399
  17.7 1.5 %collective-permute-start.5 = (f32[1,4096]{1,0:T(1,128)S(1)}, f32[1,4096]{1,0:T(1,128)S(1)}, u32[]{:S(2)}, u32[]{:S(2)}) collective-permute-start(f32[1,4096]{1,0:T(1,128)S(1)} %fusion.1), channel_id=1, source_target_pairs={{0,3},{1,2},{2,1},{3,0},{4,7},{5,6},{6,5},{7,4},{8,11},{9,10},{10,... | collective-permute-start | bytes 49160 | tf_op jit(solution)/shard_map/ppermute | solution.py:402
  19.2 0.9 %plane.1 = (f32[4,4096]{1,0:T(4,128)S(1)}, f32[4,4096]{1,0:T(4,128)}, f32[3,4,4096]{2,1,0:T(4,128)}, f32[3,4,4096]{2,1,0:T(4,128)}) custom-call(f32[4,4096]{1,0:T(4,128)S(1)} %backward.1.grad, f32[4,4096]{1,0:T(4,128)S(1)} %collective-permute-done.4.grad_other, f32[4,4096]{1,0:T(4,128)S(1)} %local.1.base, f32[3,4,4096]{2,1,0:T(4,128)S(1)} %copy-done, ...), custom_call_target="tpu_custom_call" | custom-call | tf_op jit(solution)/shard_map/plane/pallas_call | solution.py:408
  20.1 0.8 %collective-permute-done.5.ahead = f32[1,4096]{1,0:T(1,128)S(1)} collective-permute-done((f32[1,4096]{1,0:T(1,128)S(1)}, f32[1,4096]{1,0:T(1,128)S(1)}, u32[]{:S(2)}, u32[]{:S(2)}) %collective-permute-start.5) | collective-permute-done | bytes 16416 | tf_op jit(solution)/shard_map/ppermute | solution.py:402
  20.9 0.7 %depth.1 = (f32[3,4,4096]{2,1,0:T(4,128)}, f32[3,4,4096]{2,1,0:T(4,128)}) custom-call(f32[4,4096]{1,0:T(4,128)S(1)} %get-tuple-element.28.field_in, f32[1,4096]{1,0:T(1,128)S(1)} %collective-permute-done.5.ahead, f32[3,4,4096]{2,1,0:T(4,128)S(1)} %copy-done, f32[1,4096]{1,0:T(1,128)S(1)} %broadcast_in_dim.9.limits, ...), custom_call_target="tpu_custom_call", output_to_operand_aliasing={{0}: (4, {}), {1}: (5, {})} | custom-call | tf_op jit(solution)/shard_map/depth/pallas_call | solution.py:418
  (5 shorter events, 0.1 us)
Async XLA Ops:
  0.6 8.6 %copy-start.2 = (f32[4,4096]{1,0:T(4,128)S(1)}, f32[4,4096]{1,0:T(4,128)}, u32[]{:S(2)}) copy-start(f32[4,4096]{1,0:T(4,128)} %vol.3) | copy-start | bytes 196612
  0.6 8.6 %copy-start = (f32[3,4,4096]{2,1,0:T(4,128)S(1)}, f32[3,4,4096]{2,1,0:T(4,128)}, u32[]{:S(2)}) copy-start(f32[3,4,4096]{2,1,0:T(4,128)} %dual.7) | copy-start | bytes 589828
  0.7 8.6 %copy-start.1 = (f32[3,4,4096]{2,1,0:T(4,128)S(1)}, f32[3,4,4096]{2,1,0:T(4,128)}, u32[]{:S(2)}) copy-start(f32[3,4,4096]{2,1,0:T(4,128)} %split.3) | copy-start | bytes 589828
  4.1 1.4 %collective-permute-start = (bf16[128,128]{1,0:T(8,128)(2,1)S(1)}, bf16[128,128]{1,0:T(8,128)(2,1)S(1)}, u32[]{:S(2)}, u32[]{:S(2)}) collective-permute-start(bf16[128,128]{1,0:T(8,128)(2,1)S(1)} %get-tuple-element.20), channel_id=1, source_target_pairs={{0,1},{1,0},{2,3},{3,2},{4,5},{5,4},{6,7},{7,6},{8,9},{9,8},{10,11... | collective-permute-start | bytes 98312 | tf_op jit(solution)/shard_map/ppermute | solution.py:363
  5.5 5.4 %collective-permute-start.1 = (bf16[128,128]{1,0:T(8,128)(2,1)S(1)}, bf16[128,128]{1,0:T(8,128)(2,1)S(1)}, u32[]{:S(2)}, u32[]{:S(2)}) collective-permute-start(bf16[128,128]{1,0:T(8,128)(2,1)S(1)} %add_convert_fusion.1), channel_id=1, source_target_pairs={{0,9},{1,8},{4,13},{5,12},{8,1},{9,0},{12,5},{13,4},{2,11},{3,10},... | collective-permute-start | bytes 98312 | tf_op jit(solution)/shard_map/ppermute | solution.py:367
  9.3 4.0 %collective-permute-start.3 = (f32[4,4096]{1,0:T(4,128)S(1)}, f32[4,4096]{1,0:T(4,128)S(1)}, u32[]{:S(2)}, u32[]{:S(2)}) collective-permute-start(f32[4,4096]{1,0:T(4,128)S(1)} %get-tuple-element.21), channel_id=1, source_target_pairs={{0,3},{1,2},{2,1},{3,0},{4,7},{5,6},{6,5},{7,4},{8,11},{9,10},{10,... | collective-permute-start | bytes 196616 | tf_op jit(solution)/shard_map/ppermute | solution.py:358
  10.9 3.4 %collective-permute-start.2 = (bf16[128,128]{1,0:T(8,128)(2,1)S(1)}, bf16[128,128]{1,0:T(8,128)(2,1)S(1)}, u32[]{:S(2)}, u32[]{:S(2)}) collective-permute-start(bf16[128,128]{1,0:T(8,128)(2,1)S(1)} %add_convert_fusion.part), channel_id=1, source_target_pairs={{0,5},{1,4},{4,1},{5,0},{8,13},{9,12},{12,9},{13,8},{2,7},{3,6},{6... | collective-permute-start | bytes 98312 | tf_op jit(solution)/shard_map/ppermute | solution.py:367
  16.2 1.4 %collective-permute-start.4 = (f32[4,4096]{1,0:T(4,128)S(1)}, f32[4,4096]{1,0:T(4,128)S(1)}, u32[]{:S(2)}, u32[]{:S(2)}) collective-permute-start(f32[4,4096]{1,0:T(4,128)S(1)} %backward.1.grad), channel_id=1, source_target_pairs={{0,1},{1,0},{2,3},{3,2},{4,5},{5,4},{6,7},{7,6},{8,9},{9,8},{10,11... | collective-permute-start | bytes 196616 | tf_op jit(solution)/shard_map/ppermute | solution.py:399
  17.7 3.2 %collective-permute-start.5 = (f32[1,4096]{1,0:T(1,128)S(1)}, f32[1,4096]{1,0:T(1,128)S(1)}, u32[]{:S(2)}, u32[]{:S(2)}) collective-permute-start(f32[1,4096]{1,0:T(1,128)S(1)} %fusion.1), channel_id=1, source_target_pairs={{0,3},{1,2},{2,1},{3,0},{4,7},{5,6},{6,5},{7,4},{8,11},{9,10},{10,... | collective-permute-start | bytes 49160 | tf_op jit(solution)/shard_map/ppermute | solution.py:402

commit v25 on v23

--- a/solution.py
+++ b/solution.py
@@ -1,3 +1,5 @@
+import functools
+
 import jax
 import jax.numpy as jnp
 from jax import lax
@@ -67,9 +69,10 @@
     loads[0].start()
     copies[0].start()
     loads[1].start()
+    used = count[0]
     for n in copies:
         if n > 0:
-            copies[n].start()
+            pl.when(used > n)(copies[n].start)
     for load in loads[3:]:
         load.start()
     accs = (acc0, acc1, acc2, acc3)
@@ -94,29 +97,35 @@
 
     loads[0].wait()
     loads[1].wait()
-    used = count[0]
-    for n in range(0, slots, GROUP):
-        if n in copies:
-            copies[n].wait()
-        at = [divmod(n + i, 128) for i in range(GROUP)]
-        picked = [table[rows8(voxel[line, place] * 8), :] for line, place in at]
-        pairs = [jnp.where(top, picked[2 * i], picked[2 * i + 1]) for i in range(2)]
-        zero = jnp.zeros_like(pairs[0])
-        left = jnp.concatenate([pairs[0], zero], axis=0).astype(jnp.bfloat16)
-        right = jnp.concatenate([zero, pairs[1]], axis=0).astype(jnp.bfloat16)
-        sums = jnp.dot(
-            jnp.concatenate([left, right], axis=1),
-            tiles[n:n + GROUP].reshape(GROUP * TV, TR),
-            preferred_element_type=jnp.float32,
-        )
-        add_rows(
-            accs,
-            [
-                jnp.where(n + i < used, ray[line, place], rays) * 8
-                for i, (line, place) in enumerate(at)
-            ],
-            [sums[0:8], sums[0:8], sums[8:16], sums[8:16]],
-        )
+
+    def add_part(low, high):
+        copies[low].wait()
+        for n in range(low, high, GROUP):
+            at = [divmod(n + i, 128) for i in range(GROUP)]
+            picked = [table[rows8(voxel[line, place] * 8), :] for line, place in at]
+            pairs = [jnp.where(top, picked[2 * i], picked[2 * i + 1]) for i in range(2)]
+            zero = jnp.zeros_like(pairs[0])
+            left = jnp.concatenate([pairs[0], zero], axis=0).astype(jnp.bfloat16)
+            right = jnp.concatenate([zero, pairs[1]], axis=0).astype(jnp.bfloat16)
+            sums = jnp.dot(
+                jnp.concatenate([left, right], axis=1),
+                tiles[n:n + GROUP].reshape(GROUP * TV, TR),
+                preferred_element_type=jnp.float32,
+            )
+            add_rows(
+                accs,
+                [
+                    jnp.where(n + i < used, ray[line, place], rays) * 8
+                    for i, (line, place) in enumerate(at)
+                ],
+                [sums[0:8], sums[0:8], sums[8:16], sums[8:16]],
+            )
+
+    lows = [*copies, slots]
+    add_part(0, lows[1])
+    for low, high in zip(lows[1:], lows[2:]):
+        pl.when(used > low)(functools.partial(add_part, low, high))
+
     loads[3].wait()
     mine = (lax.axis_index("tile") * lax.axis_size("rep") + lax.axis_index("rep")) * owned
     for r in range(owned):

time: 21.8 us -> 21.5 us (0.986)
  Pallas kernels: 6.62 us -> 6.1 us
  waiting for transfers between devices: 3.15 us -> 3.6 us
    ppermute x1, starting transfers between devices: 0.52 us -> 1.02 us  [shards(): moved = lax.ppermute(partial, 'rep', swap)]
    pallas_call x1, Pallas kernels: 2.74 us -> 2.24 us  [shards(): pl.pallas_call(forward_kernel, out_shape=(jax.ShapeDtypeStruct((rays * sl...]
    ppermute x2, starting transfers between devices: 5.58 us -> 5.34 us  [shards(): lax.ppermute(partial, ('tile', 'rep'), [(i, i ^ step + 1) for i in range(...]
  transfers between devices with their start and end apart: 6 -> 6, of which waited for: 4 -> 5; matrix products, arithmetic and copies ran while one was open for 0% -> 0% of each run, Pallas kernels for 6% -> 6%
where the time goes in v25:
time: 21.5 us; the launch traced here: 21.3 us
  starting transfers between devices  9.45 us (44%)
  Pallas kernels  6.1 us (28%)
  waiting for transfers between devices  3.6 us (17%)
  between operations  2.11 us (10%)
    ppermute x2, starting transfers between devices, shards(): lax.ppermute(partial, ('tile', 'rep'), [(i, i ^ step + 1) for i in range(...  5.34 us
    pallas_call x1, Pallas kernels, shards(): pl.pallas_call(forward_kernel, out_shape=(jax.ShapeDtypeStruct((rays * sl...  2.24 us
    pallas_call x1, Pallas kernels, shards(): pl.pallas_call(backward_kernel, out_shape=jax.ShapeDtypeStruct((slices, w...  1.93 us
    ppermute x1, starting transfers between devices, shards(): ahead = lax.ppermute(ahead, ('slab', 'rep'), across)  1.5 us
    ppermute x1, starting transfers between devices, shards(): from_next = from_previous = lax.ppermute(halo, ('slab', 'rep'), across)  1.36 us
    ppermute x2, waiting for transfers between devices, shards(): lax.ppermute(partial, ('tile', 'rep'), [(i, i ^ step + 1) for i in range(...  1.09 us
    ppermute x1, starting transfers between devices, shards(): moved = lax.ppermute(partial, 'rep', swap)  1.02 us
    pallas_call x1, Pallas kernels, shards(): pl.pallas_call(plane_kernel, out_shape=(whole, whole, triple, triple), in...  0.89 us
  transfers between devices with their start and end apart: 6, of which 5 were waited for; matrix products, arithmetic and copies ran while one was open for 0% of the time, Pallas kernels for 6%

profile of v25, /device:TPU:0, one launch (start us, length us, event | category | flops | bytes accessed | tf_op | source)
XLA Modules:
  0.0 21.3 jit_solution(18388351265268334916)
XLA Ops:
  0.6 0.0 copy-start.2
  0.6 0.0 copy-start
  0.7 0.0 copy-start.1
  1.4 2.2 %forward.1 = (bf16[128,128]{1,0:T(8,128)(2,1)S(1)}, s32[4,128]{1,0:T(4,128)S(1)}, bf16[256,64,128]{2,1,0:T(8,128)(2,1)S(1)}) custom-call(s32[1]{0:T(128)S(6)} %copy.16.count, s32[2,128]{1,0:T(2,128)} %bitcast.3, s32[2,128]{1,0:T(2,128)} %bitcast.4, f32[4,4096]{1,0:T(4,128)} %vol.3, f32[4,4,128]{2,1,0:T(4,128)} %sino_hbm.1, bf16[256,64,128]{2,1,0:T(8,128)(2,1)} %proj_hbm.1), custom_call_target="tpu_custom_call" | custom-call | tf_op jit(solution)/shard_map/forward/pallas_call | solution.py:332
  3.6 1.0 %collective-permute-start = (bf16[128,128]{1,0:T(8,128)(2,1)S(1)}, bf16[128,128]{1,0:T(8,128)(2,1)S(1)}, u32[]{:S(2)}, u32[]{:S(2)}) collective-permute-start(bf16[128,128]{1,0:T(8,128)(2,1)S(1)} %get-tuple-element.20), channel_id=1, source_target_pairs={{0,1},{1,0},{2,3},{3,2},{4,5},{5,4},{6,7},{7,6},{8,9},{9,8},{10,11... | collective-permute-start | bytes 98312 | tf_op jit(solution)/shard_map/ppermute | solution.py:372
  4.6 0.9 %collective-permute-done = bf16[128,128]{1,0:T(8,128)(2,1)S(1)} collective-permute-done((bf16[128,128]{1,0:T(8,128)(2,1)S(1)}, bf16[128,128]{1,0:T(8,128)(2,1)S(1)}, u32[]{:S(2)}, u32[]{:S(2)}) %collective-permute-start) | collective-permute-done | bytes 32800 | tf_op jit(solution)/shard_map/ppermute | solution.py:372
  5.5 2.4 %collective-permute-start.1 = (bf16[128,128]{1,0:T(8,128)(2,1)S(1)}, bf16[128,128]{1,0:T(8,128)(2,1)S(1)}, u32[]{:S(2)}, u32[]{:S(2)}) collective-permute-start(bf16[128,128]{1,0:T(8,128)(2,1)S(1)} %add_convert_fusion.1), channel_id=1, source_target_pairs={{0,5},{1,4},{4,1},{5,0},{8,13},{9,12},{12,9},{13,8},{2,7},{3,6},{6... | collective-permute-start | bytes 98312 | tf_op jit(solution)/shard_map/ppermute | solution.py:376
  7.9 0.0 copy-done.2
  7.9 0.0 copy-done
  7.9 0.0 copy-done.1
  8.0 1.4 %collective-permute-start.3 = (f32[4,4096]{1,0:T(4,128)S(1)}, f32[4,4096]{1,0:T(4,128)S(1)}, u32[]{:S(2)}, u32[]{:S(2)}) collective-permute-start(f32[4,4096]{1,0:T(4,128)S(1)} %get-tuple-element.21), channel_id=1, source_target_pairs={{0,3},{1,2},{2,1},{3,0},{4,7},{5,6},{6,5},{7,4},{8,11},{9,10},{10,... | collective-permute-start | bytes 196616 | tf_op jit(solution)/shard_map/ppermute | solution.py:367
  9.3 0.2 collective-permute-done.1
  9.5 2.9 %collective-permute-start.2 = (bf16[128,128]{1,0:T(8,128)(2,1)S(1)}, bf16[128,128]{1,0:T(8,128)(2,1)S(1)}, u32[]{:S(2)}, u32[]{:S(2)}) collective-permute-start(bf16[128,128]{1,0:T(8,128)(2,1)S(1)} %add_convert_fusion.part), channel_id=1, source_target_pairs={{0,9},{1,8},{4,13},{5,12},{8,1},{9,0},{12,5},{13,4},{2,11},{3,10},... | collective-permute-start | bytes 98312 | tf_op jit(solution)/shard_map/ppermute | solution.py:376
  13.2 0.0 collective-permute-done.3.from_next.from_previous
  13.2 0.9 %collective-permute-done.2.moved = bf16[128,128]{1,0:T(8,128)(2,1)S(1)} collective-permute-done((bf16[128,128]{1,0:T(8,128)(2,1)S(1)}, bf16[128,128]{1,0:T(8,128)(2,1)S(1)}, u32[]{:S(2)}, u32[]{:S(2)}) %collective-permute-start.2) | collective-permute-done | bytes 32800 | tf_op jit(solution)/shard_map/ppermute | solution.py:376
  14.1 1.9 %backward.1.grad = f32[4,4096]{1,0:T(4,128)S(1)} custom-call(s32[1]{0:T(128)S(6)} %copy.16.count, s32[4,128]{1,0:T(4,128)S(1)} %get-tuple-element.18.indices, bf16[256,64,128]{2,1,0:T(8,128)(2,1)S(1)} %get-tuple-element.19.tiles, bf16[128,128]{1,0:T(8,128)(2,1)S(1)} %add_convert_fusion.part, bf16[128,128]{1,0:T(8,128)(2,1)S(1)} %collective-permute-done.2.moved), custom_call_target="tpu_custom_call" | custom-call | tf_op jit(solution)/shard_map/backward/pallas_call | solution.py:394
  16.0 0.2 %collective-permute-start.4 = (f32[4,4096]{1,0:T(4,128)S(1)}, f32[4,4096]{1,0:T(4,128)S(1)}, u32[]{:S(2)}, u32[]{:S(2)}) collective-permute-start(f32[4,4096]{1,0:T(4,128)S(1)} %backward.1.grad), channel_id=1, source_target_pairs={{0,1},{1,0},{2,3},{3,2},{4,5},{5,4},{6,7},{7,6},{8,9},{9,8},{10,11... | collective-permute-start | bytes 196616 | tf_op jit(solution)/shard_map/ppermute | solution.py:408
  16.3 0.3 %local.1.base = f32[4,4096]{1,0:T(4,128)S(1)} custom-call(f32[1]{0:T(128)S(6)} %copy.17.rho, f32[4,4096]{1,0:T(4,128)S(1)} %copy-done.2, f32[3,4,4096]{2,1,0:T(4,128)S(1)} %copy-done.1, f32[3,4,4096]{2,1,0:T(4,128)S(1)} %copy-done, f32[1,4096]{1,0:T(1,128)S(1)} %get-tuple-element.23.edge, f32[4,4096]{1,0:T(4,128)S(1)} %collective-permute-done.3.from_next.from_previous, ...), custom_call_target="tpu_custom_call" | custom-call | tf_op jit(solution)/shard_map/local/pallas_call | solution.py:385
  16.5 0.8 %collective-permute-done.4.grad_other = f32[4,4096]{1,0:T(4,128)S(1)} collective-permute-done((f32[4,4096]{1,0:T(4,128)S(1)}, f32[4,4096]{1,0:T(4,128)S(1)}, u32[]{:S(2)}, u32[]{:S(2)}) %collective-permute-start.4) | collective-permute-done | bytes 65568 | tf_op jit(solution)/shard_map/ppermute | solution.py:408
  17.4 1.5 %collective-permute-start.5 = (f32[1,4096]{1,0:T(1,128)S(1)}, f32[1,4096]{1,0:T(1,128)S(1)}, u32[]{:S(2)}, u32[]{:S(2)}) collective-permute-start(f32[1,4096]{1,0:T(1,128)S(1)} %fusion.1), channel_id=1, source_target_pairs={{0,3},{1,2},{2,1},{3,0},{4,7},{5,6},{6,5},{7,4},{8,11},{9,10},{10,... | collective-permute-start | bytes 49160 | tf_op jit(solution)/shard_map/ppermute | solution.py:411
  18.9 0.9 %plane.1 = (f32[4,4096]{1,0:T(4,128)S(1)}, f32[4,4096]{1,0:T(4,128)}, f32[3,4,4096]{2,1,0:T(4,128)}, f32[3,4,4096]{2,1,0:T(4,128)}) custom-call(f32[4,4096]{1,0:T(4,128)S(1)} %backward.1.grad, f32[4,4096]{1,0:T(4,128)S(1)} %collective-permute-done.4.grad_other, f32[4,4096]{1,0:T(4,128)S(1)} %local.1.base, f32[3,4,4096]{2,1,0:T(4,128)S(1)} %copy-done, ...), custom_call_target="tpu_custom_call" | custom-call | tf_op jit(solution)/shard_map/plane/pallas_call | solution.py:417
  19.8 0.8 %collective-permute-done.5.ahead = f32[1,4096]{1,0:T(1,128)S(1)} collective-permute-done((f32[1,4096]{1,0:T(1,128)S(1)}, f32[1,4096]{1,0:T(1,128)S(1)}, u32[]{:S(2)}, u32[]{:S(2)}) %collective-permute-start.5) | collective-permute-done | bytes 16416 | tf_op jit(solution)/shard_map/ppermute | solution.py:411
  20.6 0.7 %depth.1 = (f32[3,4,4096]{2,1,0:T(4,128)}, f32[3,4,4096]{2,1,0:T(4,128)}) custom-call(f32[4,4096]{1,0:T(4,128)S(1)} %get-tuple-element.28.field_in, f32[1,4096]{1,0:T(1,128)S(1)} %collective-permute-done.5.ahead, f32[3,4,4096]{2,1,0:T(4,128)S(1)} %copy-done, f32[1,4096]{1,0:T(1,128)S(1)} %broadcast_in_dim.9.limits, ...), custom_call_target="tpu_custom_call", output_to_operand_aliasing={{0}: (4, {}), {1}: (5, {})} | custom-call | tf_op jit(solution)/shard_map/depth/pallas_call | solution.py:427
  (5 shorter events, 0.1 us)
Async XLA Ops:
  0.6 7.3 %copy-start.2 = (f32[4,4096]{1,0:T(4,128)S(1)}, f32[4,4096]{1,0:T(4,128)}, u32[]{:S(2)}) copy-start(f32[4,4096]{1,0:T(4,128)} %vol.3) | copy-start | bytes 196612
  0.6 7.3 %copy-start = (f32[3,4,4096]{2,1,0:T(4,128)S(1)}, f32[3,4,4096]{2,1,0:T(4,128)}, u32[]{:S(2)}) copy-start(f32[3,4,4096]{2,1,0:T(4,128)} %dual.7) | copy-start | bytes 589828
  0.7 7.3 %copy-start.1 = (f32[3,4,4096]{2,1,0:T(4,128)S(1)}, f32[3,4,4096]{2,1,0:T(4,128)}, u32[]{:S(2)}) copy-start(f32[3,4,4096]{2,1,0:T(4,128)} %split.3) | copy-start | bytes 589828
  3.6 1.9 %collective-permute-start = (bf16[128,128]{1,0:T(8,128)(2,1)S(1)}, bf16[128,128]{1,0:T(8,128)(2,1)S(1)}, u32[]{:S(2)}, u32[]{:S(2)}) collective-permute-start(bf16[128,128]{1,0:T(8,128)(2,1)S(1)} %get-tuple-element.20), channel_id=1, source_target_pairs={{0,1},{1,0},{2,3},{3,2},{4,5},{5,4},{6,7},{7,6},{8,9},{9,8},{10,11... | collective-permute-start | bytes 98312 | tf_op jit(solution)/shard_map/ppermute | solution.py:372
  5.5 4.0 %collective-permute-start.1 = (bf16[128,128]{1,0:T(8,128)(2,1)S(1)}, bf16[128,128]{1,0:T(8,128)(2,1)S(1)}, u32[]{:S(2)}, u32[]{:S(2)}) collective-permute-start(bf16[128,128]{1,0:T(8,128)(2,1)S(1)} %add_convert_fusion.1), channel_id=1, source_target_pairs={{0,5},{1,4},{4,1},{5,0},{8,13},{9,12},{12,9},{13,8},{2,7},{3,6},{6... | collective-permute-start | bytes 98312 | tf_op jit(solution)/shard_map/ppermute | solution.py:376
  8.0 5.2 %collective-permute-start.3 = (f32[4,4096]{1,0:T(4,128)S(1)}, f32[4,4096]{1,0:T(4,128)S(1)}, u32[]{:S(2)}, u32[]{:S(2)}) collective-permute-start(f32[4,4096]{1,0:T(4,128)S(1)} %get-tuple-element.21), channel_id=1, source_target_pairs={{0,3},{1,2},{2,1},{3,0},{4,7},{5,6},{6,5},{7,4},{8,11},{9,10},{10,... | collective-permute-start | bytes 196616 | tf_op jit(solution)/shard_map/ppermute | solution.py:367
  9.5 4.5 %collective-permute-start.2 = (bf16[128,128]{1,0:T(8,128)(2,1)S(1)}, bf16[128,128]{1,0:T(8,128)(2,1)S(1)}, u32[]{:S(2)}, u32[]{:S(2)}) collective-permute-start(bf16[128,128]{1,0:T(8,128)(2,1)S(1)} %add_convert_fusion.part), channel_id=1, source_target_pairs={{0,9},{1,8},{4,13},{5,12},{8,1},{9,0},{12,5},{13,4},{2,11},{3,10},... | collective-permute-start | bytes 98312 | tf_op jit(solution)/shard_map/ppermute | solution.py:376
  16.0 1.3 %collective-permute-start.4 = (f32[4,4096]{1,0:T(4,128)S(1)}, f32[4,4096]{1,0:T(4,128)S(1)}, u32[]{:S(2)}, u32[]{:S(2)}) collective-permute-start(f32[4,4096]{1,0:T(4,128)S(1)} %backward.1.grad), channel_id=1, source_target_pairs={{0,1},{1,0},{2,3},{3,2},{4,5},{5,4},{6,7},{7,6},{8,9},{9,8},{10,11... | collective-permute-start | bytes 196616 | tf_op jit(solution)/shard_map/ppermute | solution.py:408
  17.4 3.2 %collective-permute-start.5 = (f32[1,4096]{1,0:T(1,128)S(1)}, f32[1,4096]{1,0:T(1,128)S(1)}, u32[]{:S(2)}, u32[]{:S(2)}) collective-permute-start(f32[1,4096]{1,0:T(1,128)S(1)} %fusion.1), channel_id=1, source_target_pairs={{0,3},{1,2},{2,1},{3,0},{4,7},{5,6},{6,5},{7,4},{8,11},{9,10},{10,... | collective-permute-start | bytes 49160 | tf_op jit(solution)/shard_map/ppermute | solution.py:411

commit v26 on v25

--- a/solution.py
+++ b/solution.py
@@ -48,19 +48,15 @@
 
 def forward_kernel(
     count, ray_hbm, voxel_hbm, vol_hbm, sino_hbm, proj_hbm,
-    partial_out, index_out, tiles,
+    partial_out, tiles,
     ray, voxel, vol, sino, double, table, acc0, acc1, acc2, acc3,
     sems, tile_sems,
 ):
     slots = proj_hbm.shape[0]
-    lines = ray.shape[0]
     rays = acc0.shape[0] // 8 - 1
     owned = sino.shape[0]
     width = vol.shape[1]
-    pairs = [
-        (voxel_hbm, voxel), (ray_hbm, ray), (vol_hbm, vol), (sino_hbm, sino),
-        (voxel_hbm, index_out.at[pl.ds(0, lines)]), (ray_hbm, index_out.at[pl.ds(lines, lines)]),
-    ]
+    pairs = [(voxel_hbm, voxel), (ray_hbm, ray), (vol_hbm, vol), (sino_hbm, sino)]
     loads = [
         pltpu.make_async_copy(source, target, sems.at[i]) for i, (source, target) in enumerate(pairs)
     ]
@@ -131,8 +127,6 @@
     for r in range(owned):
         at = pl.ds(pl.multiple_of((mine + r) * 8, 8), 4)
         acc0[at, :] = acc0[at, :] - sino[r]
-    loads[4].wait()
-    loads[5].wait()
     for q in range(rays // 4):
         halves = []
         for r in (4 * q, 4 * q + 2):
@@ -144,6 +138,18 @@
                 + pltpu.roll(jnp.where(top, even[1], odd[0]), 4, axis=0)
             )
         partial_out[16 * q:16 * q + 16, :] = jnp.concatenate(halves, axis=0).astype(jnp.bfloat16)
+
+
+def index_kernel(ray_hbm, voxel_hbm, index_out, sems):
+    lines = ray_hbm.shape[0]
+    copies = [
+        pltpu.make_async_copy(voxel_hbm, index_out.at[pl.ds(0, lines)], sems.at[0]),
+        pltpu.make_async_copy(ray_hbm, index_out.at[pl.ds(lines, lines)], sems.at[1]),
+    ]
+    for copy in copies:
+        copy.start()
+    for copy in copies:
+        copy.wait()
 
 
 def edges_kernel(vol, split, dual, edge_out, halo_out):
@@ -329,15 +335,14 @@
         for x in (ray_index, voxel_index, volume, sinogram, proj_tiles)
     ]
 
-    partial, indices, tiles = pl.pallas_call(
+    partial, tiles = pl.pallas_call(
         forward_kernel,
         out_shape=(
             jax.ShapeDtypeStruct((rays * slices, TR), bf16),
-            jax.ShapeDtypeStruct((2 * lines, 128), jnp.int32),
             jax.ShapeDtypeStruct(proj_tiles.shape, bf16),
         ),
         in_specs=[smem()] + [hbm()] * 5,
-        out_specs=(vmem(),) * 3,
+        out_specs=(vmem(),) * 2,
         scratch_shapes=[
             pltpu.SMEM((lines, 128), jnp.int32),
             pltpu.SMEM((lines, 128), jnp.int32),
@@ -347,7 +352,7 @@
             pltpu.VMEM((voxel_tiles * 8, 128), f32),
         ]
         + [pltpu.VMEM((rays * 8 + 8, 128), f32)] * 4
-        + [pltpu.SemaphoreType.DMA((6,)), pltpu.SemaphoreType.DMA((len(CUTS) - 1,))],
+        + [pltpu.SemaphoreType.DMA((4,)), pltpu.SemaphoreType.DMA((len(CUTS) - 1,))],
         compiler_params=params(),
         name="forward",
     )(tile_count, *sources)
@@ -377,9 +382,18 @@
             partial, ("tile", "rep"), [(i, i ^ (step + 1)) for i in range(group)]
         )
         step *= 2
+    indices = pl.pallas_call(
+        index_kernel,
+        out_shape=jax.ShapeDtypeStruct((2 * lines, 128), jnp.int32),
+        in_specs=[hbm()] * 2,
+        out_specs=vmem(),
+        scratch_shapes=[pltpu.SemaphoreType.DMA((2,))],
+        compiler_params=params(),
+        name="indices",
+    )(*sources[:2])
     limits = jnp.broadcast_to((1.0 / rho)[:, None], (1, width))
-    moved, from_next, from_previous, limits = lax.optimization_barrier(
-        (moved, from_next, from_previous, limits)
+    moved, from_next, from_previous, limits, indices = lax.optimization_barrier(
+        (moved, from_next, from_previous, limits, indices)
     )
 
     base = pl.pallas_call(

time: 21.5 us -> 21.6 us (level)
  Pallas kernels: 6.1 us -> 7.23 us
  waiting for transfers between devices: 3.6 us -> 2.69 us
    ppermute x1, starting transfers between devices: 1.02 us -> 0.07 us  [shards(): moved = lax.ppermute(partial, 'rep', swap)]
    ppermute x2, waiting for transfers between devices: 1.09 us -> 0.31 us  [shards(): lax.ppermute(partial, ('tile', 'rep'), [(i, i ^ step + 1) for i in range(...]
    ppermute x1, starting transfers between devices: 1.5 us -> 2.22 us  [shards(): ahead = lax.ppermute(ahead, ('slab', 'rep'), across)]
    pallas_call x0 -> x1, Pallas kernels: none -> 0.71 us  [shards(): pl.pallas_call(index_kernel, out_shape=jax.ShapeDtypeStruct((2 * lines, 1...]
    pallas_call x1, Pallas kernels: 2.24 us -> 2.68 us  [shards(): pl.pallas_call(forward_kernel, out_shape=(jax.ShapeDtypeStruct((rays * sl...]
    ppermute x2, starting transfers between devices: 5.34 us -> 5 us  [shards(): lax.ppermute(partial, ('tile', 'rep'), [(i, i ^ step + 1) for i in range(...]
    ppermute x1, waiting for transfers between devices: 0.86 us -> 1.19 us  [shards(): moved = lax.ppermute(partial, 'rep', swap)]
    ppermute x1, waiting for transfers between devices: 0.84 us -> 0.55 us  [shards(): ahead = lax.ppermute(ahead, ('slab', 'rep'), across)]
  transfers between devices with their start and end apart: 6 -> 6, of which waited for: 5 -> 4; matrix products, arithmetic and copies ran while one was open for 0% -> 0% of each run, Pallas kernels for 6% -> 9%
where the time goes in v26:
time: 21.6 us; the launch traced here: 21.4 us
  starting transfers between devices  9.26 us (43%)
  Pallas kernels  7.23 us (33%)
  waiting for transfers between devices  2.69 us (12%)
  between operations  2.12 us (10%)
    ppermute x2, starting transfers between devices, shards(): lax.ppermute(partial, ('tile', 'rep'), [(i, i ^ step + 1) for i in range(...  5 us
    pallas_call x1, Pallas kernels, shards(): pl.pallas_call(forward_kernel, out_shape=(jax.ShapeDtypeStruct((rays * sl...  2.68 us
    ppermute x1, starting transfers between devices, shards(): ahead = lax.ppermute(ahead, ('slab', 'rep'), across)  2.22 us
    pallas_call x1, Pallas kernels, shards(): pl.pallas_call(backward_kernel, out_shape=jax.ShapeDtypeStruct((slices, w...  1.91 us
    ppermute x1, starting transfers between devices, shards(): from_next = from_previous = lax.ppermute(halo, ('slab', 'rep'), across)  1.51 us
    ppermute x1, waiting for transfers between devices, shards(): moved = lax.ppermute(partial, 'rep', swap)  1.19 us
    pallas_call x1, Pallas kernels, shards(): pl.pallas_call(plane_kernel, out_shape=(whole, whole, triple, triple), in...  0.89 us
    pallas_call x1, Pallas kernels, shards(): pl.pallas_call(depth_kernel, out_shape=(triple, triple), in_specs=[vmem()...  0.73 us
  transfers between devices with their start and end apart: 6, of which 4 were waited for; matrix products, arithmetic and copies ran while one was open for 0% of the time, Pallas kernels for 9%

profile of v26, /device:TPU:0, one launch (start us, length us, event | category | flops | bytes accessed | tf_op | source)
XLA Modules:
  0.0 21.4 jit_solution(17617119404292450226)
XLA Ops:
  0.6 0.0 copy-start.2
  0.6 0.0 copy-start
  0.7 0.0 copy-start.1
  1.4 2.7 %forward.1 = (bf16[128,128]{1,0:T(8,128)(2,1)S(1)}, bf16[256,64,128]{2,1,0:T(8,128)(2,1)S(1)}) custom-call(s32[1]{0:T(128)S(6)} %copy.16.count, s32[2,128]{1,0:T(2,128)} %bitcast.3, s32[2,128]{1,0:T(2,128)} %bitcast.5, f32[4,4096]{1,0:T(4,128)} %vol.3, f32[4,4,128]{2,1,0:T(4,128)} %sino_hbm.1, bf16[256,64,128]{2,1,0:T(8,128)(2,1)} %proj_hbm.1), custom_call_target="tpu_custom_call" | custom-call | tf_op jit(solution)/shard_map/forward/pallas_call | solution.py:338
  4.0 0.1 collective-permute-start
  4.1 1.2 %collective-permute-done = bf16[128,128]{1,0:T(8,128)(2,1)S(1)} collective-permute-done((bf16[128,128]{1,0:T(8,128)(2,1)S(1)}, bf16[128,128]{1,0:T(8,128)(2,1)S(1)}, u32[]{:S(2)}, u32[]{:S(2)}) %collective-permute-start) | collective-permute-done | bytes 32800 | tf_op jit(solution)/shard_map/ppermute | solution.py:377
  5.3 2.4 %collective-permute-start.1 = (bf16[128,128]{1,0:T(8,128)(2,1)S(1)}, bf16[128,128]{1,0:T(8,128)(2,1)S(1)}, u32[]{:S(2)}, u32[]{:S(2)}) collective-permute-start(bf16[128,128]{1,0:T(8,128)(2,1)S(1)} %add_convert_fusion.1), channel_id=1, source_target_pairs={{0,5},{1,4},{4,1},{5,0},{8,13},{9,12},{12,9},{13,8},{2,7},{3,6},{6... | collective-permute-start | bytes 98312 | tf_op jit(solution)/shard_map/ppermute | solution.py:381
  7.7 0.0 copy-done.2
  7.7 0.0 copy-done
  7.7 0.0 copy-done.1
  7.8 1.5 %collective-permute-start.3 = (f32[4,4096]{1,0:T(4,128)S(1)}, f32[4,4096]{1,0:T(4,128)S(1)}, u32[]{:S(2)}, u32[]{:S(2)}) collective-permute-start(f32[4,4096]{1,0:T(4,128)S(1)} %get-tuple-element.19), channel_id=1, source_target_pairs={{0,3},{1,2},{2,1},{3,0},{4,7},{5,6},{6,5},{7,4},{8,11},{9,10},{10,... | collective-permute-start | bytes 196616 | tf_op jit(solution)/shard_map/ppermute | solution.py:372
  9.3 0.0 collective-permute-done.1
  9.3 2.6 %collective-permute-start.2 = (bf16[128,128]{1,0:T(8,128)(2,1)S(1)}, bf16[128,128]{1,0:T(8,128)(2,1)S(1)}, u32[]{:S(2)}, u32[]{:S(2)}) collective-permute-start(bf16[128,128]{1,0:T(8,128)(2,1)S(1)} %add_convert_fusion.part), channel_id=1, source_target_pairs={{0,9},{1,8},{4,13},{5,12},{8,1},{9,0},{12,5},{13,4},{2,11},{3,10},... | collective-permute-start | bytes 98312 | tf_op jit(solution)/shard_map/ppermute | solution.py:381
  12.0 0.7 %indices.1 = s32[4,128]{1,0:T(4,128)S(1)} custom-call(s32[2,128]{1,0:T(2,128)} %bitcast.4, s32[2,128]{1,0:T(2,128)} %bitcast.6), custom_call_target="tpu_custom_call" | custom-call | tf_op jit(solution)/shard_map/indices/pallas_call | solution.py:385
  13.4 0.0 collective-permute-done.3.from_next.from_previous
  13.4 0.3 %collective-permute-done.2.moved = bf16[128,128]{1,0:T(8,128)(2,1)S(1)} collective-permute-done((bf16[128,128]{1,0:T(8,128)(2,1)S(1)}, bf16[128,128]{1,0:T(8,128)(2,1)S(1)}, u32[]{:S(2)}, u32[]{:S(2)}) %collective-permute-start.2) | collective-permute-done | bytes 32800 | tf_op jit(solution)/shard_map/ppermute | solution.py:381
  13.7 1.9 %backward.1.grad = f32[4,4096]{1,0:T(4,128)S(1)} custom-call(s32[1]{0:T(128)S(6)} %copy.16.count, s32[4,128]{1,0:T(4,128)S(1)} %indices.1, bf16[256,64,128]{2,1,0:T(8,128)(2,1)S(1)} %get-tuple-element.21.tiles, bf16[128,128]{1,0:T(8,128)(2,1)S(1)} %add_convert_fusion.part, bf16[128,128]{1,0:T(8,128)(2,1)S(1)} %collective-permute-done.2.moved), custom_call_target="tpu_custom_call" | custom-call | tf_op jit(solution)/shard_map/backward/pallas_call | solution.py:408
  15.6 0.5 %collective-permute-start.4 = (f32[4,4096]{1,0:T(4,128)S(1)}, f32[4,4096]{1,0:T(4,128)S(1)}, u32[]{:S(2)}, u32[]{:S(2)}) collective-permute-start(f32[4,4096]{1,0:T(4,128)S(1)} %backward.1.grad), channel_id=1, source_target_pairs={{0,1},{1,0},{2,3},{3,2},{4,5},{5,4},{6,7},{7,6},{8,9},{9,8},{10,11... | collective-permute-start | bytes 196616 | tf_op jit(solution)/shard_map/ppermute | solution.py:422
  16.0 0.3 %local.1.base = f32[4,4096]{1,0:T(4,128)S(1)} custom-call(f32[1]{0:T(128)S(6)} %copy.17.rho, f32[4,4096]{1,0:T(4,128)S(1)} %copy-done.2, f32[3,4,4096]{2,1,0:T(4,128)S(1)} %copy-done.1, f32[3,4,4096]{2,1,0:T(4,128)S(1)} %copy-done, f32[1,4096]{1,0:T(1,128)S(1)} %get-tuple-element.23.edge, f32[4,4096]{1,0:T(4,128)S(1)} %collective-permute-done.3.from_next.from_previous, ...), custom_call_target="tpu_custom_call" | custom-call | tf_op jit(solution)/shard_map/local/pallas_call | solution.py:399
  16.3 0.6 %collective-permute-done.4.grad_other = f32[4,4096]{1,0:T(4,128)S(1)} collective-permute-done((f32[4,4096]{1,0:T(4,128)S(1)}, f32[4,4096]{1,0:T(4,128)S(1)}, u32[]{:S(2)}, u32[]{:S(2)}) %collective-permute-start.4) | collective-permute-done | bytes 65568 | tf_op jit(solution)/shard_map/ppermute | solution.py:422
  17.0 2.2 %collective-permute-start.5 = (f32[1,4096]{1,0:T(1,128)S(1)}, f32[1,4096]{1,0:T(1,128)S(1)}, u32[]{:S(2)}, u32[]{:S(2)}) collective-permute-start(f32[1,4096]{1,0:T(1,128)S(1)} %fusion.1), channel_id=1, source_target_pairs={{0,3},{1,2},{2,1},{3,0},{4,7},{5,6},{6,5},{7,4},{8,11},{9,10},{10,... | collective-permute-start | bytes 49160 | tf_op jit(solution)/shard_map/ppermute | solution.py:425
  19.2 0.9 %plane.1 = (f32[4,4096]{1,0:T(4,128)S(1)}, f32[4,4096]{1,0:T(4,128)}, f32[3,4,4096]{2,1,0:T(4,128)}, f32[3,4,4096]{2,1,0:T(4,128)}) custom-call(f32[4,4096]{1,0:T(4,128)S(1)} %backward.1.grad, f32[4,4096]{1,0:T(4,128)S(1)} %collective-permute-done.4.grad_other, f32[4,4096]{1,0:T(4,128)S(1)} %local.1.base, f32[3,4,4096]{2,1,0:T(4,128)S(1)} %copy-done, ...), custom_call_target="tpu_custom_call" | custom-call | tf_op jit(solution)/shard_map/plane/pallas_call | solution.py:431
  20.1 0.6 %collective-permute-done.5.ahead = f32[1,4096]{1,0:T(1,128)S(1)} collective-permute-done((f32[1,4096]{1,0:T(1,128)S(1)}, f32[1,4096]{1,0:T(1,128)S(1)}, u32[]{:S(2)}, u32[]{:S(2)}) %collective-permute-start.5) | collective-permute-done | bytes 16416 | tf_op jit(solution)/shard_map/ppermute | solution.py:425
  20.6 0.7 %depth.1 = (f32[3,4,4096]{2,1,0:T(4,128)}, f32[3,4,4096]{2,1,0:T(4,128)}) custom-call(f32[4,4096]{1,0:T(4,128)S(1)} %get-tuple-element.28.field_in, f32[1,4096]{1,0:T(1,128)S(1)} %collective-permute-done.5.ahead, f32[3,4,4096]{2,1,0:T(4,128)S(1)} %copy-done, f32[1,4096]{1,0:T(1,128)S(1)} %broadcast_in_dim.9.limits, ...), custom_call_target="tpu_custom_call", output_to_operand_aliasing={{0}: (4, {}), {1}: (5, {})} | custom-call | tf_op jit(solution)/shard_map/depth/pallas_call | solution.py:441
  (5 shorter events, 0.1 us)
Async XLA Ops:
  0.6 7.1 %copy-start.2 = (f32[4,4096]{1,0:T(4,128)S(1)}, f32[4,4096]{1,0:T(4,128)}, u32[]{:S(2)}) copy-start(f32[4,4096]{1,0:T(4,128)} %vol.3) | copy-start | bytes 196612
  0.6 7.1 %copy-start = (f32[3,4,4096]{2,1,0:T(4,128)S(1)}, f32[3,4,4096]{2,1,0:T(4,128)}, u32[]{:S(2)}) copy-start(f32[3,4,4096]{2,1,0:T(4,128)} %dual.7) | copy-start | bytes 589828
  0.7 7.1 %copy-start.1 = (f32[3,4,4096]{2,1,0:T(4,128)S(1)}, f32[3,4,4096]{2,1,0:T(4,128)}, u32[]{:S(2)}) copy-start(f32[3,4,4096]{2,1,0:T(4,128)} %split.3) | copy-start | bytes 589828
  4.0 1.3 %collective-permute-start = (bf16[128,128]{1,0:T(8,128)(2,1)S(1)}, bf16[128,128]{1,0:T(8,128)(2,1)S(1)}, u32[]{:S(2)}, u32[]{:S(2)}) collective-permute-start(bf16[128,128]{1,0:T(8,128)(2,1)S(1)} %get-tuple-element.18), channel_id=1, source_target_pairs={{0,1},{1,0},{2,3},{3,2},{4,5},{5,4},{6,7},{7,6},{8,9},{9,8},{10,11... | collective-permute-start | bytes 98312 | tf_op jit(solution)/shard_map/ppermute | solution.py:377
  5.3 4.0 %collective-permute-start.1 = (bf16[128,128]{1,0:T(8,128)(2,1)S(1)}, bf16[128,128]{1,0:T(8,128)(2,1)S(1)}, u32[]{:S(2)}, u32[]{:S(2)}) collective-permute-start(bf16[128,128]{1,0:T(8,128)(2,1)S(1)} %add_convert_fusion.1), channel_id=1, source_target_pairs={{0,5},{1,4},{4,1},{5,0},{8,13},{9,12},{12,9},{13,8},{2,7},{3,6},{6... | collective-permute-start | bytes 98312 | tf_op jit(solution)/shard_map/ppermute | solution.py:381
  7.8 5.6 %collective-permute-start.3 = (f32[4,4096]{1,0:T(4,128)S(1)}, f32[4,4096]{1,0:T(4,128)S(1)}, u32[]{:S(2)}, u32[]{:S(2)}) collective-permute-start(f32[4,4096]{1,0:T(4,128)S(1)} %get-tuple-element.19), channel_id=1, source_target_pairs={{0,3},{1,2},{2,1},{3,0},{4,7},{5,6},{6,5},{7,4},{8,11},{9,10},{10,... | collective-permute-start | bytes 196616 | tf_op jit(solution)/shard_map/ppermute | solution.py:372
  9.3 4.3 %collective-permute-start.2 = (bf16[128,128]{1,0:T(8,128)(2,1)S(1)}, bf16[128,128]{1,0:T(8,128)(2,1)S(1)}, u32[]{:S(2)}, u32[]{:S(2)}) collective-permute-start(bf16[128,128]{1,0:T(8,128)(2,1)S(1)} %add_convert_fusion.part), channel_id=1, source_target_pairs={{0,9},{1,8},{4,13},{5,12},{8,1},{9,0},{12,5},{13,4},{2,11},{3,10},... | collective-permute-start | bytes 98312 | tf_op jit(solution)/shard_map/ppermute | solution.py:381
  15.6 1.4 %collective-permute-start.4 = (f32[4,4096]{1,0:T(4,128)S(1)}, f32[4,4096]{1,0:T(4,128)S(1)}, u32[]{:S(2)}, u32[]{:S(2)}) collective-permute-start(f32[4,4096]{1,0:T(4,128)S(1)} %backward.1.grad), channel_id=1, source_target_pairs={{0,1},{1,0},{2,3},{3,2},{4,5},{5,4},{6,7},{7,6},{8,9},{9,8},{10,11... | collective-permute-start | bytes 196616 | tf_op jit(solution)/shard_map/ppermute | solution.py:422
  17.0 3.7 %collective-permute-start.5 = (f32[1,4096]{1,0:T(1,128)S(1)}, f32[1,4096]{1,0:T(1,128)S(1)}, u32[]{:S(2)}, u32[]{:S(2)}) collective-permute-start(f32[1,4096]{1,0:T(1,128)S(1)} %fusion.1), channel_id=1, source_target_pairs={{0,3},{1,2},{2,1},{3,0},{4,7},{5,6},{6,5},{7,4},{8,11},{9,10},{10,... | collective-permute-start | bytes 49160 | tf_op jit(solution)/shard_map/ppermute | solution.py:425

commit v27 on v25

--- a/solution.py
+++ b/solution.py
@@ -11,7 +11,7 @@
 TR = 128
 TAU = 0.5
 GROUP = 4
-CUTS = (0, 2, 5, 8)
+CUTS = (0, 2, 4, 6, 8)
 VMEM_LIMIT = 16 * 1024 * 1024
 
 

time: 21.5 us -> 21.5 us (level)
  starting transfers between devices: 9.45 us -> 8.99 us
  Pallas kernels: 6.1 us -> 6.49 us
    ppermute x1, starting transfers between devices: 1.02 us -> 0.19 us  [shards(): moved = lax.ppermute(partial, 'rep', swap)]
    pallas_call x1, Pallas kernels: 2.24 us -> 2.64 us  [shards(): pl.pallas_call(forward_kernel, out_shape=(jax.ShapeDtypeStruct((rays * sl...]
    ppermute x2, waiting for transfers between devices: 1.09 us -> 1.35 us  [shards(): lax.ppermute(partial, ('tile', 'rep'), [(i, i ^ step + 1) for i in range(...]
    ppermute x1, waiting for transfers between devices: 0.84 us -> 0.6 us  [shards(): ahead = lax.ppermute(ahead, ('slab', 'rep'), across)]
    ppermute x1, starting transfers between devices: 1.5 us -> 1.74 us  [shards(): ahead = lax.ppermute(ahead, ('slab', 'rep'), across)]
    ppermute x1, waiting for transfers between devices: 0.86 us -> 1.08 us  [shards(): moved = lax.ppermute(partial, 'rep', swap)]
  transfers between devices with their start and end apart: 6 -> 6, of which waited for: 5 -> 4; matrix products, arithmetic and copies ran while one was open for 0% -> 0% of each run, Pallas kernels for 6% -> 6%
where the time goes in v27:
time: 21.5 us; the launch traced here: 21.3 us
  starting transfers between devices  8.99 us (42%)
  Pallas kernels  6.49 us (30%)
  waiting for transfers between devices  3.67 us (17%)
  between operations  2.11 us (10%)
    ppermute x2, starting transfers between devices, shards(): lax.ppermute(partial, ('tile', 'rep'), [(i, i ^ step + 1) for i in range(...  5.14 us
    pallas_call x1, Pallas kernels, shards(): pl.pallas_call(forward_kernel, out_shape=(jax.ShapeDtypeStruct((rays * sl...  2.64 us
    pallas_call x1, Pallas kernels, shards(): pl.pallas_call(backward_kernel, out_shape=jax.ShapeDtypeStruct((slices, w...  1.93 us
    ppermute x1, starting transfers between devices, shards(): ahead = lax.ppermute(ahead, ('slab', 'rep'), across)  1.74 us
    ppermute x1, starting transfers between devices, shards(): from_next = from_previous = lax.ppermute(halo, ('slab', 'rep'), across)  1.51 us
    ppermute x2, waiting for transfers between devices, shards(): lax.ppermute(partial, ('tile', 'rep'), [(i, i ^ step + 1) for i in range(...  1.35 us
    ppermute x1, waiting for transfers between devices, shards(): moved = lax.ppermute(partial, 'rep', swap)  1.08 us
    pallas_call x1, Pallas kernels, shards(): pl.pallas_call(plane_kernel, out_shape=(whole, whole, triple, triple), in...  0.89 us
  transfers between devices with their start and end apart: 6, of which 4 were waited for; matrix products, arithmetic and copies ran while one was open for 0% of the time, Pallas kernels for 6%

profile of v27, /device:TPU:0, one launch (start us, length us, event | category | flops | bytes accessed | tf_op | source)
XLA Modules:
  0.0 21.3 jit_solution(6823901657888688283)
XLA Ops:
  0.6 0.0 copy-start.2
  0.6 0.0 copy-start
  0.7 0.0 copy-start.1
  1.4 2.6 %forward.1 = (bf16[128,128]{1,0:T(8,128)(2,1)S(1)}, s32[4,128]{1,0:T(4,128)S(1)}, bf16[256,64,128]{2,1,0:T(8,128)(2,1)S(1)}) custom-call(s32[1]{0:T(128)S(6)} %copy.16.count, s32[2,128]{1,0:T(2,128)} %bitcast.3, s32[2,128]{1,0:T(2,128)} %bitcast.4, f32[4,4096]{1,0:T(4,128)} %vol.3, f32[4,4,128]{2,1,0:T(4,128)} %sino_hbm.1, bf16[256,64,128]{2,1,0:T(8,128)(2,1)} %proj_hbm.1), custom_call_target="tpu_custom_call" | custom-call | tf_op jit(solution)/shard_map/forward/pallas_call | solution.py:332
  4.0 0.2 collective-permute-start
  4.2 1.1 %collective-permute-done = bf16[128,128]{1,0:T(8,128)(2,1)S(1)} collective-permute-done((bf16[128,128]{1,0:T(8,128)(2,1)S(1)}, bf16[128,128]{1,0:T(8,128)(2,1)S(1)}, u32[]{:S(2)}, u32[]{:S(2)}) %collective-permute-start) | collective-permute-done | bytes 32800 | tf_op jit(solution)/shard_map/ppermute | solution.py:372
  5.3 2.9 %collective-permute-start.1 = (bf16[128,128]{1,0:T(8,128)(2,1)S(1)}, bf16[128,128]{1,0:T(8,128)(2,1)S(1)}, u32[]{:S(2)}, u32[]{:S(2)}) collective-permute-start(bf16[128,128]{1,0:T(8,128)(2,1)S(1)} %add_convert_fusion.1), channel_id=1, source_target_pairs={{0,5},{1,4},{4,1},{5,0},{8,13},{9,12},{12,9},{13,8},{2,7},{3,6},{6... | collective-permute-start | bytes 98312 | tf_op jit(solution)/shard_map/ppermute | solution.py:376
  8.1 0.0 copy-done.2
  8.2 0.0 copy-done
  8.2 0.0 copy-done.1
  8.2 1.5 %collective-permute-start.3 = (f32[4,4096]{1,0:T(4,128)S(1)}, f32[4,4096]{1,0:T(4,128)S(1)}, u32[]{:S(2)}, u32[]{:S(2)}) collective-permute-start(f32[4,4096]{1,0:T(4,128)S(1)} %get-tuple-element.21), channel_id=1, source_target_pairs={{0,3},{1,2},{2,1},{3,0},{4,7},{5,6},{6,5},{7,4},{8,11},{9,10},{10,... | collective-permute-start | bytes 196616 | tf_op jit(solution)/shard_map/ppermute | solution.py:367
  9.7 0.0 collective-permute-done.1
  9.8 2.3 %collective-permute-start.2 = (bf16[128,128]{1,0:T(8,128)(2,1)S(1)}, bf16[128,128]{1,0:T(8,128)(2,1)S(1)}, u32[]{:S(2)}, u32[]{:S(2)}) collective-permute-start(bf16[128,128]{1,0:T(8,128)(2,1)S(1)} %add_convert_fusion.part), channel_id=1, source_target_pairs={{0,9},{1,8},{4,13},{5,12},{8,1},{9,0},{12,5},{13,4},{2,11},{3,10},... | collective-permute-start | bytes 98312 | tf_op jit(solution)/shard_map/ppermute | solution.py:376
  12.7 0.0 collective-permute-done.3.from_next.from_previous
  12.8 1.3 %collective-permute-done.2.moved = bf16[128,128]{1,0:T(8,128)(2,1)S(1)} collective-permute-done((bf16[128,128]{1,0:T(8,128)(2,1)S(1)}, bf16[128,128]{1,0:T(8,128)(2,1)S(1)}, u32[]{:S(2)}, u32[]{:S(2)}) %collective-permute-start.2) | collective-permute-done | bytes 32800 | tf_op jit(solution)/shard_map/ppermute | solution.py:376
  14.1 1.9 %backward.1.grad = f32[4,4096]{1,0:T(4,128)S(1)} custom-call(s32[1]{0:T(128)S(6)} %copy.16.count, s32[4,128]{1,0:T(4,128)S(1)} %get-tuple-element.18.indices, bf16[256,64,128]{2,1,0:T(8,128)(2,1)S(1)} %get-tuple-element.19.tiles, bf16[128,128]{1,0:T(8,128)(2,1)S(1)} %add_convert_fusion.part, bf16[128,128]{1,0:T(8,128)(2,1)S(1)} %collective-permute-done.2.moved), custom_call_target="tpu_custom_call" | custom-call | tf_op jit(solution)/shard_map/backward/pallas_call | solution.py:394
  16.0 0.4 %collective-permute-start.4 = (f32[4,4096]{1,0:T(4,128)S(1)}, f32[4,4096]{1,0:T(4,128)S(1)}, u32[]{:S(2)}, u32[]{:S(2)}) collective-permute-start(f32[4,4096]{1,0:T(4,128)S(1)} %backward.1.grad), channel_id=1, source_target_pairs={{0,1},{1,0},{2,3},{3,2},{4,5},{5,4},{6,7},{7,6},{8,9},{9,8},{10,11... | collective-permute-start | bytes 196616 | tf_op jit(solution)/shard_map/ppermute | solution.py:408
  16.4 0.3 %local.1.base = f32[4,4096]{1,0:T(4,128)S(1)} custom-call(f32[1]{0:T(128)S(6)} %copy.17.rho, f32[4,4096]{1,0:T(4,128)S(1)} %copy-done.2, f32[3,4,4096]{2,1,0:T(4,128)S(1)} %copy-done.1, f32[3,4,4096]{2,1,0:T(4,128)S(1)} %copy-done, f32[1,4096]{1,0:T(1,128)S(1)} %get-tuple-element.23.edge, f32[4,4096]{1,0:T(4,128)S(1)} %collective-permute-done.3.from_next.from_previous, ...), custom_call_target="tpu_custom_call" | custom-call | tf_op jit(solution)/shard_map/local/pallas_call | solution.py:385
  16.7 0.6 %collective-permute-done.4.grad_other = f32[4,4096]{1,0:T(4,128)S(1)} collective-permute-done((f32[4,4096]{1,0:T(4,128)S(1)}, f32[4,4096]{1,0:T(4,128)S(1)}, u32[]{:S(2)}, u32[]{:S(2)}) %collective-permute-start.4) | collective-permute-done | bytes 65568 | tf_op jit(solution)/shard_map/ppermute | solution.py:408
  17.4 1.7 %collective-permute-start.5 = (f32[1,4096]{1,0:T(1,128)S(1)}, f32[1,4096]{1,0:T(1,128)S(1)}, u32[]{:S(2)}, u32[]{:S(2)}) collective-permute-start(f32[1,4096]{1,0:T(1,128)S(1)} %fusion.1), channel_id=1, source_target_pairs={{0,3},{1,2},{2,1},{3,0},{4,7},{5,6},{6,5},{7,4},{8,11},{9,10},{10,... | collective-permute-start | bytes 49160 | tf_op jit(solution)/shard_map/ppermute | solution.py:411
  19.1 0.9 %plane.1 = (f32[4,4096]{1,0:T(4,128)S(1)}, f32[4,4096]{1,0:T(4,128)}, f32[3,4,4096]{2,1,0:T(4,128)}, f32[3,4,4096]{2,1,0:T(4,128)}) custom-call(f32[4,4096]{1,0:T(4,128)S(1)} %backward.1.grad, f32[4,4096]{1,0:T(4,128)S(1)} %collective-permute-done.4.grad_other, f32[4,4096]{1,0:T(4,128)S(1)} %local.1.base, f32[3,4,4096]{2,1,0:T(4,128)S(1)} %copy-done, ...), custom_call_target="tpu_custom_call" | custom-call | tf_op jit(solution)/shard_map/plane/pallas_call | solution.py:417
  20.0 0.6 %collective-permute-done.5.ahead = f32[1,4096]{1,0:T(1,128)S(1)} collective-permute-done((f32[1,4096]{1,0:T(1,128)S(1)}, f32[1,4096]{1,0:T(1,128)S(1)}, u32[]{:S(2)}, u32[]{:S(2)}) %collective-permute-start.5) | collective-permute-done | bytes 16416 | tf_op jit(solution)/shard_map/ppermute | solution.py:411
  20.6 0.7 %depth.1 = (f32[3,4,4096]{2,1,0:T(4,128)}, f32[3,4,4096]{2,1,0:T(4,128)}) custom-call(f32[4,4096]{1,0:T(4,128)S(1)} %get-tuple-element.28.field_in, f32[1,4096]{1,0:T(1,128)S(1)} %collective-permute-done.5.ahead, f32[3,4,4096]{2,1,0:T(4,128)S(1)} %copy-done, f32[1,4096]{1,0:T(1,128)S(1)} %broadcast_in_dim.9.limits, ...), custom_call_target="tpu_custom_call", output_to_operand_aliasing={{0}: (4, {}), {1}: (5, {})} | custom-call | tf_op jit(solution)/shard_map/depth/pallas_call | solution.py:427
  (5 shorter events, 0.1 us)
Async XLA Ops:
  0.6 7.5 %copy-start.2 = (f32[4,4096]{1,0:T(4,128)S(1)}, f32[4,4096]{1,0:T(4,128)}, u32[]{:S(2)}) copy-start(f32[4,4096]{1,0:T(4,128)} %vol.3) | copy-start | bytes 196612
  0.6 7.5 %copy-start = (f32[3,4,4096]{2,1,0:T(4,128)S(1)}, f32[3,4,4096]{2,1,0:T(4,128)}, u32[]{:S(2)}) copy-start(f32[3,4,4096]{2,1,0:T(4,128)} %dual.7) | copy-start | bytes 589828
  0.7 7.5 %copy-start.1 = (f32[3,4,4096]{2,1,0:T(4,128)S(1)}, f32[3,4,4096]{2,1,0:T(4,128)}, u32[]{:S(2)}) copy-start(f32[3,4,4096]{2,1,0:T(4,128)} %split.3) | copy-start | bytes 589828
  4.0 1.3 %collective-permute-start = (bf16[128,128]{1,0:T(8,128)(2,1)S(1)}, bf16[128,128]{1,0:T(8,128)(2,1)S(1)}, u32[]{:S(2)}, u32[]{:S(2)}) collective-permute-start(bf16[128,128]{1,0:T(8,128)(2,1)S(1)} %get-tuple-element.20), channel_id=1, source_target_pairs={{0,1},{1,0},{2,3},{3,2},{4,5},{5,4},{6,7},{7,6},{8,9},{9,8},{10,11... | collective-permute-start | bytes 98312 | tf_op jit(solution)/shard_map/ppermute | solution.py:372
  5.3 4.5 %collective-permute-start.1 = (bf16[128,128]{1,0:T(8,128)(2,1)S(1)}, bf16[128,128]{1,0:T(8,128)(2,1)S(1)}, u32[]{:S(2)}, u32[]{:S(2)}) collective-permute-start(bf16[128,128]{1,0:T(8,128)(2,1)S(1)} %add_convert_fusion.1), channel_id=1, source_target_pairs={{0,5},{1,4},{4,1},{5,0},{8,13},{9,12},{12,9},{13,8},{2,7},{3,6},{6... | collective-permute-start | bytes 98312 | tf_op jit(solution)/shard_map/ppermute | solution.py:376
  8.2 4.5 %collective-permute-start.3 = (f32[4,4096]{1,0:T(4,128)S(1)}, f32[4,4096]{1,0:T(4,128)S(1)}, u32[]{:S(2)}, u32[]{:S(2)}) collective-permute-start(f32[4,4096]{1,0:T(4,128)S(1)} %get-tuple-element.21), channel_id=1, source_target_pairs={{0,3},{1,2},{2,1},{3,0},{4,7},{5,6},{6,5},{7,4},{8,11},{9,10},{10,... | collective-permute-start | bytes 196616 | tf_op jit(solution)/shard_map/ppermute | solution.py:367
  9.8 4.3 %collective-permute-start.2 = (bf16[128,128]{1,0:T(8,128)(2,1)S(1)}, bf16[128,128]{1,0:T(8,128)(2,1)S(1)}, u32[]{:S(2)}, u32[]{:S(2)}) collective-permute-start(bf16[128,128]{1,0:T(8,128)(2,1)S(1)} %add_convert_fusion.part), channel_id=1, source_target_pairs={{0,9},{1,8},{4,13},{5,12},{8,1},{9,0},{12,5},{13,4},{2,11},{3,10},... | collective-permute-start | bytes 98312 | tf_op jit(solution)/shard_map/ppermute | solution.py:376
  16.0 1.3 %collective-permute-start.4 = (f32[4,4096]{1,0:T(4,128)S(1)}, f32[4,4096]{1,0:T(4,128)S(1)}, u32[]{:S(2)}, u32[]{:S(2)}) collective-permute-start(f32[4,4096]{1,0:T(4,128)S(1)} %backward.1.grad), channel_id=1, source_target_pairs={{0,1},{1,0},{2,3},{3,2},{4,5},{5,4},{6,7},{7,6},{8,9},{9,8},{10,11... | collective-permute-start | bytes 196616 | tf_op jit(solution)/shard_map/ppermute | solution.py:408
  17.4 3.2 %collective-permute-start.5 = (f32[1,4096]{1,0:T(1,128)S(1)}, f32[1,4096]{1,0:T(1,128)S(1)}, u32[]{:S(2)}, u32[]{:S(2)}) collective-permute-start(f32[1,4096]{1,0:T(1,128)S(1)} %fusion.1), channel_id=1, source_target_pairs={{0,3},{1,2},{2,1},{3,0},{4,7},{5,6},{6,5},{7,4},{8,11},{9,10},{10,... | collective-permute-start | bytes 49160 | tf_op jit(solution)/shard_map/ppermute | solution.py:411

commit v28 on v27

--- a/solution.py
+++ b/solution.py
@@ -11,7 +11,7 @@
 TR = 128
 TAU = 0.5
 GROUP = 4
-CUTS = (0, 2, 4, 6, 8)
+CUTS = (0, 2, 4, 8)
 VMEM_LIMIT = 16 * 1024 * 1024
 
 

time: 21.5 us -> 21.8 us (1.014)
  starting transfers between devices: 8.99 us -> 10.7 us
  Pallas kernels: 6.49 us -> 5.53 us
  waiting for transfers between devices: 3.67 us -> 3.3 us
    ppermute x1, starting transfers between devices: 0.19 us -> 1.71 us  [shards(): moved = lax.ppermute(partial, 'rep', swap)]
    pallas_call x1, Pallas kernels: 2.64 us -> 1.65 us  [shards(): pl.pallas_call(forward_kernel, out_shape=(jax.ShapeDtypeStruct((rays * sl...]
    ppermute x2, starting transfers between devices: 5.14 us -> 5.57 us  [shards(): lax.ppermute(partial, ('tile', 'rep'), [(i, i ^ step + 1) for i in range(...]
    ppermute x2, waiting for transfers between devices: 1.35 us -> 0.93 us  [shards(): lax.ppermute(partial, ('tile', 'rep'), [(i, i ^ step + 1) for i in range(...]
    ppermute x1, waiting for transfers between devices: 0.6 us -> 0.85 us  [shards(): ahead = lax.ppermute(ahead, ('slab', 'rep'), across)]
    ppermute x1, starting transfers between devices: 1.74 us -> 1.48 us  [shards(): ahead = lax.ppermute(ahead, ('slab', 'rep'), across)]
    ppermute x1, waiting for transfers between devices: 1.08 us -> 0.86 us  [shards(): moved = lax.ppermute(partial, 'rep', swap)]
where the time goes in v28:
time: 21.8 us; the launch traced here: 21.7 us
  starting transfers between devices  10.7 us (49%)
  Pallas kernels  5.53 us (25%)
  waiting for transfers between devices  3.3 us (15%)
  between operations  2.11 us (10%)
    ppermute x2, starting transfers between devices, shards(): lax.ppermute(partial, ('tile', 'rep'), [(i, i ^ step + 1) for i in range(...  5.57 us
    pallas_call x1, Pallas kernels, shards(): pl.pallas_call(backward_kernel, out_shape=jax.ShapeDtypeStruct((slices, w...  1.95 us
    ppermute x1, starting transfers between devices, shards(): moved = lax.ppermute(partial, 'rep', swap)  1.71 us
    pallas_call x1, Pallas kernels, shards(): pl.pallas_call(forward_kernel, out_shape=(jax.ShapeDtypeStruct((rays * sl...  1.65 us
    ppermute x1, starting transfers between devices, shards(): from_next = from_previous = lax.ppermute(halo, ('slab', 'rep'), across)  1.51 us
    ppermute x1, starting transfers between devices, shards(): ahead = lax.ppermute(ahead, ('slab', 'rep'), across)  1.48 us
    ppermute x2, waiting for transfers between devices, shards(): lax.ppermute(partial, ('tile', 'rep'), [(i, i ^ step + 1) for i in range(...  0.93 us
    pallas_call x1, Pallas kernels, shards(): pl.pallas_call(plane_kernel, out_shape=(whole, whole, triple, triple), in...  0.89 us
  transfers between devices with their start and end apart: 6, of which 4 were waited for; matrix products, arithmetic and copies ran while one was open for 0% of the time, Pallas kernels for 6%

profile of v28, /device:TPU:0, one launch (start us, length us, event | category | flops | bytes accessed | tf_op | source)
XLA Modules:
  0.0 21.7 jit_solution(7981157159708869775)
XLA Ops:
  0.6 0.0 copy-start.2
  0.6 0.0 copy-start
  0.7 0.0 copy-start.1
  1.4 1.7 %forward.1 = (bf16[128,128]{1,0:T(8,128)(2,1)S(1)}, s32[4,128]{1,0:T(4,128)S(1)}, bf16[256,64,128]{2,1,0:T(8,128)(2,1)S(1)}) custom-call(s32[1]{0:T(128)S(6)} %copy.16.count, s32[2,128]{1,0:T(2,128)} %bitcast.3, s32[2,128]{1,0:T(2,128)} %bitcast.4, f32[4,4096]{1,0:T(4,128)} %vol.3, f32[4,4,128]{2,1,0:T(4,128)} %sino_hbm.1, bf16[256,64,128]{2,1,0:T(8,128)(2,1)} %proj_hbm.1), custom_call_target="tpu_custom_call" | custom-call | tf_op jit(solution)/shard_map/forward/pallas_call | solution.py:332
  3.0 1.7 %collective-permute-start = (bf16[128,128]{1,0:T(8,128)(2,1)S(1)}, bf16[128,128]{1,0:T(8,128)(2,1)S(1)}, u32[]{:S(2)}, u32[]{:S(2)}) collective-permute-start(bf16[128,128]{1,0:T(8,128)(2,1)S(1)} %get-tuple-element.20), channel_id=1, source_target_pairs={{0,1},{1,0},{2,3},{3,2},{4,5},{5,4},{6,7},{7,6},{8,9},{9,8},{10,11... | collective-permute-start | bytes 98312 | tf_op jit(solution)/shard_map/ppermute | solution.py:372
  4.7 0.9 %collective-permute-done = bf16[128,128]{1,0:T(8,128)(2,1)S(1)} collective-permute-done((bf16[128,128]{1,0:T(8,128)(2,1)S(1)}, bf16[128,128]{1,0:T(8,128)(2,1)S(1)}, u32[]{:S(2)}, u32[]{:S(2)}) %collective-permute-start) | collective-permute-done | bytes 32800 | tf_op jit(solution)/shard_map/ppermute | solution.py:372
  5.6 1.9 %collective-permute-start.1 = (bf16[128,128]{1,0:T(8,128)(2,1)S(1)}, bf16[128,128]{1,0:T(8,128)(2,1)S(1)}, u32[]{:S(2)}, u32[]{:S(2)}) collective-permute-start(bf16[128,128]{1,0:T(8,128)(2,1)S(1)} %add_convert_fusion.1), channel_id=1, source_target_pairs={{0,5},{1,4},{4,1},{5,0},{8,13},{9,12},{12,9},{13,8},{2,7},{3,6},{6... | collective-permute-start | bytes 98312 | tf_op jit(solution)/shard_map/ppermute | solution.py:376
  7.5 0.0 copy-done.2
  7.5 0.0 copy-done
  7.5 0.0 copy-done.1
  7.6 1.5 %collective-permute-start.3 = (f32[4,4096]{1,0:T(4,128)S(1)}, f32[4,4096]{1,0:T(4,128)S(1)}, u32[]{:S(2)}, u32[]{:S(2)}) collective-permute-start(f32[4,4096]{1,0:T(4,128)S(1)} %get-tuple-element.21), channel_id=1, source_target_pairs={{0,3},{1,2},{2,1},{3,0},{4,7},{5,6},{6,5},{7,4},{8,11},{9,10},{10,... | collective-permute-start | bytes 196616 | tf_op jit(solution)/shard_map/ppermute | solution.py:367
  9.1 0.0 collective-permute-done.1
  9.1 3.7 %collective-permute-start.2 = (bf16[128,128]{1,0:T(8,128)(2,1)S(1)}, bf16[128,128]{1,0:T(8,128)(2,1)S(1)}, u32[]{:S(2)}, u32[]{:S(2)}) collective-permute-start(bf16[128,128]{1,0:T(8,128)(2,1)S(1)} %add_convert_fusion.part), channel_id=1, source_target_pairs={{0,9},{1,8},{4,13},{5,12},{8,1},{9,0},{12,5},{13,4},{2,11},{3,10},... | collective-permute-start | bytes 98312 | tf_op jit(solution)/shard_map/ppermute | solution.py:376
  13.5 0.0 collective-permute-done.3.from_next.from_previous
  13.5 0.9 %collective-permute-done.2.moved = bf16[128,128]{1,0:T(8,128)(2,1)S(1)} collective-permute-done((bf16[128,128]{1,0:T(8,128)(2,1)S(1)}, bf16[128,128]{1,0:T(8,128)(2,1)S(1)}, u32[]{:S(2)}, u32[]{:S(2)}) %collective-permute-start.2) | collective-permute-done | bytes 32800 | tf_op jit(solution)/shard_map/ppermute | solution.py:376
  14.4 2.0 %backward.1.grad = f32[4,4096]{1,0:T(4,128)S(1)} custom-call(s32[1]{0:T(128)S(6)} %copy.16.count, s32[4,128]{1,0:T(4,128)S(1)} %get-tuple-element.18.indices, bf16[256,64,128]{2,1,0:T(8,128)(2,1)S(1)} %get-tuple-element.19.tiles, bf16[128,128]{1,0:T(8,128)(2,1)S(1)} %add_convert_fusion.part, bf16[128,128]{1,0:T(8,128)(2,1)S(1)} %collective-permute-done.2.moved), custom_call_target="tpu_custom_call" | custom-call | tf_op jit(solution)/shard_map/backward/pallas_call | solution.py:394
  16.4 0.4 %collective-permute-start.4 = (f32[4,4096]{1,0:T(4,128)S(1)}, f32[4,4096]{1,0:T(4,128)S(1)}, u32[]{:S(2)}, u32[]{:S(2)}) collective-permute-start(f32[4,4096]{1,0:T(4,128)S(1)} %backward.1.grad), channel_id=1, source_target_pairs={{0,1},{1,0},{2,3},{3,2},{4,5},{5,4},{6,7},{7,6},{8,9},{9,8},{10,11... | collective-permute-start | bytes 196616 | tf_op jit(solution)/shard_map/ppermute | solution.py:408
  16.8 0.3 %local.1.base = f32[4,4096]{1,0:T(4,128)S(1)} custom-call(f32[1]{0:T(128)S(6)} %copy.17.rho, f32[4,4096]{1,0:T(4,128)S(1)} %copy-done.2, f32[3,4,4096]{2,1,0:T(4,128)S(1)} %copy-done.1, f32[3,4,4096]{2,1,0:T(4,128)S(1)} %copy-done, f32[1,4096]{1,0:T(1,128)S(1)} %get-tuple-element.23.edge, f32[4,4096]{1,0:T(4,128)S(1)} %collective-permute-done.3.from_next.from_previous, ...), custom_call_target="tpu_custom_call" | custom-call | tf_op jit(solution)/shard_map/local/pallas_call | solution.py:385
  17.0 0.7 %collective-permute-done.4.grad_other = f32[4,4096]{1,0:T(4,128)S(1)} collective-permute-done((f32[4,4096]{1,0:T(4,128)S(1)}, f32[4,4096]{1,0:T(4,128)S(1)}, u32[]{:S(2)}, u32[]{:S(2)}) %collective-permute-start.4) | collective-permute-done | bytes 65568 | tf_op jit(solution)/shard_map/ppermute | solution.py:408
  17.7 1.5 %collective-permute-start.5 = (f32[1,4096]{1,0:T(1,128)S(1)}, f32[1,4096]{1,0:T(1,128)S(1)}, u32[]{:S(2)}, u32[]{:S(2)}) collective-permute-start(f32[1,4096]{1,0:T(1,128)S(1)} %fusion.1), channel_id=1, source_target_pairs={{0,3},{1,2},{2,1},{3,0},{4,7},{5,6},{6,5},{7,4},{8,11},{9,10},{10,... | collective-permute-start | bytes 49160 | tf_op jit(solution)/shard_map/ppermute | solution.py:411
  19.2 0.9 %plane.1 = (f32[4,4096]{1,0:T(4,128)S(1)}, f32[4,4096]{1,0:T(4,128)}, f32[3,4,4096]{2,1,0:T(4,128)}, f32[3,4,4096]{2,1,0:T(4,128)}) custom-call(f32[4,4096]{1,0:T(4,128)S(1)} %backward.1.grad, f32[4,4096]{1,0:T(4,128)S(1)} %collective-permute-done.4.grad_other, f32[4,4096]{1,0:T(4,128)S(1)} %local.1.base, f32[3,4,4096]{2,1,0:T(4,128)S(1)} %copy-done, ...), custom_call_target="tpu_custom_call" | custom-call | tf_op jit(solution)/shard_map/plane/pallas_call | solution.py:417
  20.1 0.9 %collective-permute-done.5.ahead = f32[1,4096]{1,0:T(1,128)S(1)} collective-permute-done((f32[1,4096]{1,0:T(1,128)S(1)}, f32[1,4096]{1,0:T(1,128)S(1)}, u32[]{:S(2)}, u32[]{:S(2)}) %collective-permute-start.5) | collective-permute-done | bytes 16416 | tf_op jit(solution)/shard_map/ppermute | solution.py:411
  21.0 0.7 %depth.1 = (f32[3,4,4096]{2,1,0:T(4,128)}, f32[3,4,4096]{2,1,0:T(4,128)}) custom-call(f32[4,4096]{1,0:T(4,128)S(1)} %get-tuple-element.28.field_in, f32[1,4096]{1,0:T(1,128)S(1)} %collective-permute-done.5.ahead, f32[3,4,4096]{2,1,0:T(4,128)S(1)} %copy-done, f32[1,4096]{1,0:T(1,128)S(1)} %broadcast_in_dim.9.limits, ...), custom_call_target="tpu_custom_call", output_to_operand_aliasing={{0}: (4, {}), {1}: (5, {})} | custom-call | tf_op jit(solution)/shard_map/depth/pallas_call | solution.py:427
  (5 shorter events, 0.1 us)
Async XLA Ops:
  0.6 6.9 %copy-start.2 = (f32[4,4096]{1,0:T(4,128)S(1)}, f32[4,4096]{1,0:T(4,128)}, u32[]{:S(2)}) copy-start(f32[4,4096]{1,0:T(4,128)} %vol.3) | copy-start | bytes 196612
  0.6 6.9 %copy-start = (f32[3,4,4096]{2,1,0:T(4,128)S(1)}, f32[3,4,4096]{2,1,0:T(4,128)}, u32[]{:S(2)}) copy-start(f32[3,4,4096]{2,1,0:T(4,128)} %dual.7) | copy-start | bytes 589828
  0.7 6.9 %copy-start.1 = (f32[3,4,4096]{2,1,0:T(4,128)S(1)}, f32[3,4,4096]{2,1,0:T(4,128)}, u32[]{:S(2)}) copy-start(f32[3,4,4096]{2,1,0:T(4,128)} %split.3) | copy-start | bytes 589828
  3.0 2.6 %collective-permute-start = (bf16[128,128]{1,0:T(8,128)(2,1)S(1)}, bf16[128,128]{1,0:T(8,128)(2,1)S(1)}, u32[]{:S(2)}, u32[]{:S(2)}) collective-permute-start(bf16[128,128]{1,0:T(8,128)(2,1)S(1)} %get-tuple-element.20), channel_id=1, source_target_pairs={{0,1},{1,0},{2,3},{3,2},{4,5},{5,4},{6,7},{7,6},{8,9},{9,8},{10,11... | collective-permute-start | bytes 98312 | tf_op jit(solution)/shard_map/ppermute | solution.py:372
  5.6 3.5 %collective-permute-start.1 = (bf16[128,128]{1,0:T(8,128)(2,1)S(1)}, bf16[128,128]{1,0:T(8,128)(2,1)S(1)}, u32[]{:S(2)}, u32[]{:S(2)}) collective-permute-start(bf16[128,128]{1,0:T(8,128)(2,1)S(1)} %add_convert_fusion.1), channel_id=1, source_target_pairs={{0,5},{1,4},{4,1},{5,0},{8,13},{9,12},{12,9},{13,8},{2,7},{3,6},{6... | collective-permute-start | bytes 98312 | tf_op jit(solution)/shard_map/ppermute | solution.py:376
  7.6 5.9 %collective-permute-start.3 = (f32[4,4096]{1,0:T(4,128)S(1)}, f32[4,4096]{1,0:T(4,128)S(1)}, u32[]{:S(2)}, u32[]{:S(2)}) collective-permute-start(f32[4,4096]{1,0:T(4,128)S(1)} %get-tuple-element.21), channel_id=1, source_target_pairs={{0,3},{1,2},{2,1},{3,0},{4,7},{5,6},{6,5},{7,4},{8,11},{9,10},{10,... | collective-permute-start | bytes 196616 | tf_op jit(solution)/shard_map/ppermute | solution.py:367
  9.1 5.3 %collective-permute-start.2 = (bf16[128,128]{1,0:T(8,128)(2,1)S(1)}, bf16[128,128]{1,0:T(8,128)(2,1)S(1)}, u32[]{:S(2)}, u32[]{:S(2)}) collective-permute-start(bf16[128,128]{1,0:T(8,128)(2,1)S(1)} %add_convert_fusion.part), channel_id=1, source_target_pairs={{0,9},{1,8},{4,13},{5,12},{8,1},{9,0},{12,5},{13,4},{2,11},{3,10},... | collective-permute-start | bytes 98312 | tf_op jit(solution)/shard_map/ppermute | solution.py:376
  16.4 1.3 %collective-permute-start.4 = (f32[4,4096]{1,0:T(4,128)S(1)}, f32[4,4096]{1,0:T(4,128)S(1)}, u32[]{:S(2)}, u32[]{:S(2)}) collective-permute-start(f32[4,4096]{1,0:T(4,128)S(1)} %backward.1.grad), channel_id=1, source_target_pairs={{0,1},{1,0},{2,3},{3,2},{4,5},{5,4},{6,7},{7,6},{8,9},{9,8},{10,11... | collective-permute-start | bytes 196616 | tf_op jit(solution)/shard_map/ppermute | solution.py:408
  17.7 3.2 %collective-permute-start.5 = (f32[1,4096]{1,0:T(1,128)S(1)}, f32[1,4096]{1,0:T(1,128)S(1)}, u32[]{:S(2)}, u32[]{:S(2)}) collective-permute-start(f32[1,4096]{1,0:T(1,128)S(1)} %fusion.1), channel_id=1, source_target_pairs={{0,3},{1,2},{2,1},{3,0},{4,7},{5,6},{6,5},{7,4},{8,11},{9,10},{10,... | collective-permute-start | bytes 49160 | tf_op jit(solution)/shard_map/ppermute | solution.py:411
